TPU v7x, 256 devices: a whole 4x4x8 slice. The times are simulated.
256 devices in a mesh: section: 4 (over y_lo, core), dp: 64 (over z, x, y_hi).
Axes of the slice: x: 4, y: 4 (y_hi: 2, y_lo: 2; y = y_hi * 2 + y_lo), z: 8, core: 2. Of those that a mesh axis runs over, the one named last changes fastest.
Arguments:
- token_ids: int32 [8192], P('dp'), may hold values from 0 to 64511, as said below
- embed_table: bfloat16 [64512, 8192], P('dp', 'section'), may hold values from -6 to 6
- subspace: bfloat16 [4, 8192, 256], P('section'), may hold values from -0.0625 to 0.0625
- adapter_in: bfloat16 [4, 8192, 128], P('section'), may hold values from -0.0625 to 0.0625
- adapter_out: bfloat16 [4, 128, 8192], P('section'), may hold values from -0.5 to 0.5
- norm_gain: float32 [4, 8192], P('section'), may hold values from 0.1 to 1.9
- coef_cotangent: bfloat16 [8192, 256], P('dp'), may hold values from -0.059814453 to 0.059814453
Outputs:
- sent_coefs: bfloat16 [4, 8192, 256], P('section', 'dp')
- grad_adapter_in: float32 [4, 8192, 128], P('section', 'dp')
- grad_adapter_out: float32 [4, 128, 8192], P('section', None, 'dp')
- grad_norm_gain: float32 [4, 8192], P('section', 'dp')
Inputs may be any that keep to these rules, and one draw needn't show every extreme that they name: `token_ids`: an id i lies in table shard i // 1008. In each aligned block of 128 ids (the ids of one device) no shard is named by more than 4 ids; one shard is named by exactly 4 ids in every block, and in most blocks a second shard as well.
All inputs are finite; a program needn't handle non-finite values.
Results may differ from a plain program's by a relative error of at most 0.017.
Values may be sent and summed in bfloat16 or wider, within the bound.
No kernel may reach another device: no remote copies, remote signals or barrier semaphores. Data moves between devices by JAX's collectives and lax.ppermute only.
A program may use at most 128 MiB of HBM per device.

v0:
```python
import jax
import jax.numpy as jnp
from jax import lax
from jax.sharding import PartitionSpec as P

VOC_DEV = 1008


EPSILON = 1e-05


def shifted(x, axis, by):
    count = lax.axis_size(axis)
    pairs = [(i, i + by) for i in range(count) if 0 <= i + by < count]
    return lax.ppermute(x, axis, pairs)


def contract_last(left, right):
    return lax.dot_general(
        left, right, (((1,), (1,)), ((), ())), preferred_element_type=jnp.float32
    )


def contract_first(left, right):
    return lax.dot_general(
        left, right, (((0,), (0,)), ((), ())), preferred_element_type=jnp.float32
    )


def contract_first_exact(left, right):
    return lax.dot_general(
        left.astype(jnp.float32),
        right,
        (((0,), (0,)), ((), ())),
        precision=lax.Precision.HIGHEST,
        preferred_element_type=jnp.float32,
    )


def layer_pieces(hidden, scale, weight_in):
    inverse_rms = lax.rsqrt(jnp.mean(hidden * hidden, axis=-1, keepdims=True) + EPSILON)
    normal_hat = hidden * inverse_rms
    normed = (normal_hat * scale).astype(jnp.bfloat16)
    preact = jnp.dot(normed, weight_in, preferred_element_type=jnp.float32)
    return (inverse_rms, normal_hat, normed, preact)


def unchanged(state):
    return state


def per_device(
    token_ids, embed_table, subspace, adapter_in, adapter_out, norm_gain, coef_cotangent
):
    token_count = token_ids.shape[0]
    shard_count = lax.axis_size("dp")
    section_count = lax.axis_size("section")
    section_index = lax.axis_index("section")
    capacity = 2 * token_count // shard_count
    column_count = embed_table.shape[1]
    owner = token_ids // VOC_DEV
    local_row = token_ids - owner * VOC_DEV
    matches = (owner[:, None] == jnp.arange(shard_count, dtype=jnp.int32)[None, :]).astype(
        jnp.int32
    )
    position = jnp.sum(jnp.cumsum(matches, axis=0) * matches, axis=1) - 1
    place = owner * capacity + position
    requests = (
        jnp.zeros((shard_count * capacity,), jnp.int32)
        .at[place]
        .set(local_row)
        .reshape(shard_count, capacity)
    )
    found = jnp.take(
        embed_table, lax.all_to_all(requests, "dp", split_axis=0, concat_axis=0, tiled=True), axis=0
    )
    answered = lax.all_to_all(found, "dp", split_axis=0, concat_axis=0, tiled=True)
    base_part = jnp.take(answered.reshape(shard_count * capacity, column_count), place, axis=0)
    base = lax.all_gather(base_part, "section", axis=1, tiled=True)
    own_basis = subspace[0]
    prev_basis = shifted(subspace, "section", 1)[0]
    weight_in = adapter_in[0]
    weight_out = adapter_out[0]
    scale = norm_gain[0]
    width = base.shape[1]
    rank = weight_in.shape[1]
    coef_width = own_basis.shape[1]
    micro_count = 2
    block_rows = token_count // micro_count
    tick_count = micro_count + section_count - 1
    hidden_store = jnp.zeros((token_count, width), jnp.float32)
    sent_store = jnp.zeros((token_count, coef_width), jnp.bfloat16)
    incoming = jnp.zeros((block_rows, coef_width), jnp.bfloat16)
    for tick in range(tick_count):
        micro = tick - section_index
        active_now = (micro >= 0) & (micro < micro_count)
        start_row = jnp.clip(micro, 0, micro_count - 1) * block_rows

        def run_forward(state):
            hidden_all, sent_all = state
            base_rows = lax.dynamic_slice_in_dim(base, start_row, block_rows, 0).astype(jnp.float32)
            rebuilt = base_rows + contract_last(incoming, prev_basis)
            hidden = jnp.where(section_index == 0, base_rows, rebuilt)
            inverse_rms, normal_hat, normed, preact = layer_pieces(hidden, scale, weight_in)
            activation = jax.nn.silu(preact).astype(jnp.bfloat16)
            output = hidden + jnp.dot(activation, weight_out, preferred_element_type=jnp.float32)
            sent = jnp.dot(
                (output - base_rows).astype(jnp.bfloat16),
                own_basis,
                preferred_element_type=jnp.float32,
            ).astype(jnp.bfloat16)
            return (
                lax.dynamic_update_slice_in_dim(hidden_all, hidden, start_row, 0),
                lax.dynamic_update_slice_in_dim(sent_all, sent, start_row, 0),
            )

        hidden_store, sent_store = lax.cond(
            active_now, run_forward, unchanged, (hidden_store, sent_store)
        )
        if tick + 1 < tick_count:
            latest = lax.dynamic_slice_in_dim(sent_store, start_row, block_rows, 0)
            incoming = shifted(latest, "section", 1)
    store = (jnp.zeros((width, rank), jnp.float32), jnp.zeros((rank, width), jnp.float32))
    gain_total = jnp.zeros((width,), jnp.float32)
    returning = jnp.zeros((block_rows, coef_width), jnp.bfloat16)
    outgoing = jnp.zeros((block_rows, coef_width), jnp.bfloat16)
    for tick in range(tick_count):
        micro = tick - (section_count - 1 - section_index)
        active_now = (micro >= 0) & (micro < micro_count)
        start_row = jnp.clip(micro, 0, micro_count - 1) * block_rows

        def run_backward(state):
            gain_sum, buffers, unused_out = state
            hidden = lax.dynamic_slice_in_dim(hidden_store, start_row, block_rows, 0)
            cot_rows = lax.dynamic_slice_in_dim(coef_cotangent, start_row, block_rows, 0)
            arrived = jnp.where(section_index == section_count - 1, cot_rows, returning)
            slope = contract_last(arrived, own_basis)
            inverse_rms, normal_hat, normed, preact = layer_pieces(hidden, scale, weight_in)
            activation = jax.nn.silu(preact).astype(jnp.bfloat16)
            slope_half = slope.astype(jnp.bfloat16)
            grad_branch = contract_last(slope_half, weight_out)
            sigmoid_value = jax.nn.sigmoid(preact)
            grad_preact = (
                grad_branch * sigmoid_value * (1.0 + preact * (1.0 - sigmoid_value))
            ).astype(jnp.bfloat16)
            grad_normed = contract_last(grad_preact, weight_in)
            grad_hat = grad_normed * scale
            gain_term = jnp.sum(grad_normed * normal_hat, axis=0)
            grad_hidden = slope + inverse_rms * (
                grad_hat - normal_hat * jnp.mean(grad_hat * normal_hat, axis=-1, keepdims=True)
            )
            sent_back = jnp.dot(
                grad_hidden.astype(jnp.bfloat16), prev_basis, preferred_element_type=jnp.float32
            ).astype(jnp.bfloat16)
            buffers = (
                buffers[0] + contract_first(normed, grad_preact),
                buffers[1] + contract_first_exact(activation, slope),
            )
            return (gain_sum + gain_term, buffers, sent_back)

        gain_total, store, outgoing = lax.cond(
            active_now, run_backward, unchanged, (gain_total, store, outgoing)
        )
        if tick + 1 < tick_count:
            returning = shifted(outgoing, "section", -1)
    grad_in, grad_out, grad_gain = (
        lax.psum_scatter(store[0], "dp", scatter_dimension=0, tiled=True),
        lax.psum_scatter(store[1], "dp", scatter_dimension=1, tiled=True),
        lax.psum_scatter(gain_total, "dp", scatter_dimension=0, tiled=True),
    )
    return (sent_store[None], grad_in[None], grad_out[None], grad_gain[None])


def solution(mesh):
    return jax.shard_map(
        per_device,
        mesh=mesh,
        in_specs=(
            P("dp"),
            P("dp", "section"),
            P("section", None, None),
            P("section", None, None),
            P("section", None, None),
            P("section", None),
            P("dp", None),
        ),
        out_specs=(
            P("section", "dp", None),
            P("section", "dp", None),
            P("section", None, "dp"),
            P("section", "dp"),
        ),
        check_vma=False,
    )
```

profile of v0, /device:TPU:8, one launch (start us, length us, event | category | flops | bytes accessed | tf_op | source)
XLA Modules:
  0.0 1112.5 jit_solution(7979449877300892687)
XLA Ops:
  8.3 1.0 scatter_custom_fusion
  9.4 25.4 %all_to_all.20 = s32[64,1,4]{2,1,0:T(1,128)S(1)} all-to-all(s32[64,1,4]{2,1,0:T(1,128)S(1)} %bitcast.153), channel_id=1, replica_groups=mesh['section'=4,'dp'=64] {'dp'}, dimensions={0} | all-to-all | bytes 2048 | tf_op jit(solution)/shard_map/all_to_all | solution.py:75
  34.9 5.1 gather_fusion
  40.5 1.5 broadcast_select_fusion
  42.0 4.7 all-to-all-start.1
  46.7 1.9 collective-permute-start
  48.7 27.3 %all-to-all-done.1 = bf16[64,4,2048]{2,1,0:T(4,128)(2,1)S(1)} async-done(((bf16[64,4,2048]{2,1,0:T(4,128)(2,1)}), bf16[64,4,2048]{2,1,0:T(4,128)(2,1)S(1)}, u32[]{:S(2)}, u32[]{:S(2)}) %all-to-all-start.1) | async-done | bytes 1048608 | tf_op jit(solution)/shard_map/all_to_all | solution.py:77
  76.2 1.7 gather_fusion.1
  78.0 2.0 broadcast_select_fusion.1
  80.0 42.9 %collective-permute-done = bf16[1,8192,256]{2,1,0:T(8,128)(2,1)} collective-permute-done((bf16[1,8192,256]{2,1,0:T(8,128)(2,1)}, bf16[1,8192,256]{2,1,0:T(8,128)(2,1)}, u32[]{:S(2)}, u32[]{:S(2)}) %collective-permute-start) | collective-permute-done | bytes 4194336 | tf_op jit(solution)/shard_map/ppermute | solution.py:15
  122.9 3.0 conditional.10
  122.9 2.4 broadcast.243
  126.7 1.9 collective-permute-start.1
  128.7 3.3 collective-permute-done.1
  132.9 1.9 collective-permute-start.2
  134.8 27.9 %collective-permute-done.2 = bf16[64,256]{1,0:T(8,128)(2,1)S(1)} collective-permute-done((bf16[64,256]{1,0:T(8,128)(2,1)S(1)}, bf16[64,256]{1,0:T(8,128)(2,1)S(1)}, u32[]{:S(2)}, u32[]{:S(2)}) %collective-permute-start.2) | collective-permute-done | bytes 32800 | tf_op jit(solution)/shard_map/ppermute | solution.py:15
  162.8 19.0 %conditional.12 = ((f32[128,8192]{1,0:T(8,128)}, bf16[128,256]{1,0:T(8,128)(2,1)})) conditional(s32[]{:T(128)} %convert_element_type.205, (f32[128,8192]{1,0:T(8,128)}, bf16[128,256]{1,0:T(8,128)(2,1)}) %get-tuple-element.594, (s32[]{:T(128)}, s32[]{:T(128)}, bf16[128,8192]{1,0:T(8,128)(2,1)}, bf16[64,256]{1,0:T(8,128)(2,1)S(1)}, ...), branch_computations={%region_9.10_spmd, %region_10.12_spmd} | conditional | flops 811655232 | bytes 33752176 | solution.py:117
  162.8 4.0 multiply_reduce_fusion.2
  168.2 5.1 fusion.26
  173.2 1.5 dynamic_update_slice.26
  174.7 7.1 dynamic_update_slice.25
  182.5 1.9 collective-permute-start.3
  184.4 3.3 collective-permute-done.3
  187.7 18.2 %conditional.13 = ((f32[128,8192]{1,0:T(8,128)}, bf16[128,256]{1,0:T(8,128)(2,1)})) conditional(s32[]{:T(128)} %convert_element_type.204, (f32[128,8192]{1,0:T(8,128)}, bf16[128,256]{1,0:T(8,128)(2,1)}) %get-tuple-element.595, (s32[]{:T(128)}, s32[]{:T(128)}, bf16[128,8192]{1,0:T(8,128)(2,1)}, bf16[64,256]{1,0:T(8,128)(2,1)S(1)}, ...), branch_computations={%region_12.13_spmd, %region_13.15_spmd} | conditional | flops 811655232 | bytes 33752176 | solution.py:117
  187.7 4.0 multiply_reduce_fusion.3
  192.3 0.8 copy-done.9
  193.1 5.0 fusion.36
  198.1 1.4 dynamic_update_slice.28
  199.5 6.4 dynamic_update_slice.27
  206.7 1.9 collective-permute-start.4
  208.7 3.3 collective-permute-done.4
  212.0 0.8 copy-done.12
  212.8 4.9 conditional.15
  212.8 2.4 broadcast.256
  215.2 2.2 broadcast_in_dim.54
  217.7 1.9 collective-permute-start.5
  219.6 28.6 %collective-permute-done.5 = bf16[64,256]{1,0:T(8,128)(2,1)S(1)} collective-permute-done((bf16[64,256]{1,0:T(8,128)(2,1)S(1)}, bf16[64,256]{1,0:T(8,128)(2,1)S(1)}, u32[]{:S(2)}, u32[]{:S(2)}) %collective-permute-start.5) | collective-permute-done | bytes 32800 | tf_op jit(solution)/shard_map/ppermute | solution.py:15
  248.3 27.7 %conditional.16 = ((f32[8192]{0:T(1024)S(1)}, f32[8192,128]{1,0:T(8,128)}, f32[128,8192]{1,0:T(8,128)}, bf16[64,256]{1,0:T(8,128)(2,1)S(1)})) conditional(s32[]{:T(128)} %convert_element_type.212, (f32[8192]{0:T(1024)S(1)}, f32[8192,128]{1,0:T(8,128)}, f32[128,8192]{1,0:T(8,128)}, bf16[64,256]{1,0:T(8,128)(2,1)S(1)}) %conditional.15, (s32[]{:T(128)}, ...), branch_computations={%region_23.24_spmd, %region_24.28_spmd} | conditional | flops 1892827136 | bytes 63425416 | solution.py:161
  248.5 2.0 multiply_reduce_fusion.10
  250.6 2.3 fusion.87
  252.8 3.7 fusion.79
  256.6 0.8 fusion.74
  257.4 2.7 multiply_reduce_fusion.8
  260.1 4.0 convolution_convert_fusion.1
  264.1 5.7 convolution_add_fusion.11
  269.8 6.1 convolution_add_fusion.10
  275.9 1.9 collective-permute-start.6
  277.9 1.6 collective-permute-done.6
  279.4 27.5 %conditional.17 = ((f32[8192]{0:T(1024)S(1)}, f32[8192,128]{1,0:T(8,128)}, f32[128,8192]{1,0:T(8,128)}, bf16[64,256]{1,0:T(8,128)(2,1)S(1)})) conditional(s32[]{:T(128)} %convert_element_type.211, (f32[8192]{0:T(1024)S(1)}, f32[8192,128]{1,0:T(8,128)}, f32[128,8192]{1,0:T(8,128)}, bf16[64,256]{1,0:T(8,128)(2,1)S(1)}) %get-tuple-element.597, ...), branch_computations={%region_28.29_spmd, %region_29.33_spmd} | conditional | flops 1892827136 | bytes 63425416 | solution.py:161
  279.9 2.0 multiply_reduce_fusion.13
  281.9 2.2 fusion.102
  284.1 3.7 fusion.94
  287.8 0.8 fusion.89
  288.6 2.6 multiply_reduce_fusion.11
  291.3 3.9 convolution_convert_fusion.2
  295.2 5.7 convolution_add_fusion.13
  300.8 6.1 convolution_add_fusion.12
  306.9 4.0 collective-permute-start.7
  311.0 1.6 collective-permute-done.7
  312.7 30.4 %collective-permute-start.8 = (bf16[64,256]{1,0:T(8,128)(2,1)S(1)}, bf16[64,256]{1,0:T(8,128)(2,1)S(1)}, u32[]{:S(2)}, u32[]{:S(2)}) collective-permute-start(bf16[64,256]{1,0:T(8,128)(2,1)S(1)} %get-tuple-element.492), channel_id=1, source_target_pairs={{64,0},{128,64},{192,128},{65,1},{129,65},{193,129},{66,2},{130,66... | collective-permute-start | bytes 98312 | tf_op jit(solution)/shard_map/ppermute | solution.py:15
  343.1 1.6 collective-permute-done.8
  346.7 358.8 %all-reduce = f32[8192]{0:T(1024)S(1)} all-reduce(f32[8192]{0:T(1024)S(1)} %get-tuple-element.495), channel_id=4, replica_groups=mesh['section'=4,'dp'=64] {'dp'}, use_global_device_ids=true, to_apply=%region_44.45.clone | all-reduce | flops 8192 | bytes 65536
  706.1 31.5 %reduce-scatter.3.cloned.1.call-done = f32[128,128]{1,0:T(8,128)} async-done(((f32[8192,128]{1,0:T(8,128)}), f32[128,128]{1,0:T(8,128)}) %reduce-scatter.3.cloned.1.call-update) | async-done | bytes 65552 | tf_op jit(solution)/shard_map/reduce_scatter | solution.py:167
  737.6 368.2 %reduce-scatter.5.cloned.1.call-done = f32[128,128]{1,0:T(8,128)} async-done(((f32[128,8192]{1,0:T(8,128)}), f32[128,128]{1,0:T(8,128)}) %reduce-scatter.5.cloned.1.call-update) | async-done | bytes 65552 | tf_op jit(solution)/shard_map/reduce_scatter | solution.py:168
  (57 shorter events, 10.0 us)
Async XLA Ops:
  42.0 33.9 %all-to-all-start.1 = ((bf16[64,4,2048]{2,1,0:T(4,128)(2,1)}), bf16[64,4,2048]{2,1,0:T(4,128)(2,1)S(1)}, u32[]{:S(2)}, u32[]{:S(2)}) async-start(bf16[64,4,2048]{2,1,0:T(4,128)(2,1)} %broadcast_select_fusion), calls=%async_computation.1 | async-start | bytes 2097152 | tf_op jit(solution)/shard_map/all_to_all | solution.py:77
  46.7 76.3 %all-gather.2.cloned.1.call-start = ((), (), s32[]{:S(2)}) async-start(), calls=%async_computation.4 | async-start | bytes 2621440 | tf_op jit(solution)/shard_map/all_gather | solution.py:79
  46.7 76.2 %collective-permute-start = (bf16[1,8192,256]{2,1,0:T(8,128)(2,1)}, bf16[1,8192,256]{2,1,0:T(8,128)(2,1)}, u32[]{:S(2)}, u32[]{:S(2)}) collective-permute-start(bf16[1,8192,256]{2,1,0:T(8,128)(2,1)} %param.29), channel_id=1, source_target_pairs={{0,64},{64,128},{128,192},{1,65},{65,129},{129,193},{2,66},{66,130... | collective-permute-start | bytes 12582920 | tf_op jit(solution)/shard_map/ppermute | solution.py:15
  76.2 46.7 %copy-start = (bf16[1,8192,128]{2,1,0:T(8,128)(2,1)S(1)}, bf16[1,8192,128]{2,1,0:T(8,128)(2,1)}, u32[]{:S(2)}) copy-start(bf16[1,8192,128]{2,1,0:T(8,128)(2,1)} %param.30) | copy-start | bytes 6291460
  76.2 46.7 %copy-start.11 = (f32[1,8192]{1,0:T(1,128)S(1)}, f32[1,8192]{1,0:T(1,128)}, u32[]{:S(2)}) copy-start(f32[1,8192]{1,0:T(1,128)} %param.32) | copy-start | bytes 98308
  80.0 657.6 %reduce-scatter.3.cloned.1.call-start = ((), (), s32[]{:S(2)}) async-start(), calls=%async_computation.5 | async-start | bytes 4259840 | tf_op jit(solution)/shard_map/reduce_scatter | solution.py:167
  126.7 5.2 collective-permute-start.1
  132.9 29.9 %collective-permute-start.2 = (bf16[64,256]{1,0:T(8,128)(2,1)S(1)}, bf16[64,256]{1,0:T(8,128)(2,1)S(1)}, u32[]{:S(2)}, u32[]{:S(2)}) collective-permute-start(bf16[64,256]{1,0:T(8,128)(2,1)S(1)} %constant_dynamic-slice_fusion.2), channel_id=1, source_target_pairs={{0,64},{64,128},{128,192},{1,65},{65,129},{129,193},{2,66},{66,130... | collective-permute-start | bytes 98312 | tf_op jit(solution)/shard_map/ppermute | solution.py:15
  166.8 1.4 copy-start.8
  182.5 5.2 collective-permute-start.3
  191.7 1.4 copy-start.9
  206.7 5.2 collective-permute-start.4
  212.0 0.8 copy-start.12
  217.7 30.6 %collective-permute-start.5 = (bf16[64,256]{1,0:T(8,128)(2,1)S(1)}, bf16[64,256]{1,0:T(8,128)(2,1)S(1)}, u32[]{:S(2)}, u32[]{:S(2)}) collective-permute-start(bf16[64,256]{1,0:T(8,128)(2,1)S(1)} %get-tuple-element.477), channel_id=1, source_target_pairs={{64,0},{128,64},{192,128},{65,1},{129,65},{193,129},{66,2},{130,66... | collective-permute-start | bytes 98312 | tf_op jit(solution)/shard_map/ppermute | solution.py:15
  252.8 3.7 copy-start.2
  275.9 3.5 collective-permute-start.6
  284.1 3.7 copy-start.3
  306.9 5.6 collective-permute-start.7
  312.7 32.0 %collective-permute-start.8 = (bf16[64,256]{1,0:T(8,128)(2,1)S(1)}, bf16[64,256]{1,0:T(8,128)(2,1)S(1)}, u32[]{:S(2)}, u32[]{:S(2)}) collective-permute-start(bf16[64,256]{1,0:T(8,128)(2,1)S(1)} %get-tuple-element.492), channel_id=1, source_target_pairs={{64,0},{128,64},{192,128},{65,1},{129,65},{193,129},{66,2},{130,66... | collective-permute-start | bytes 98312 | tf_op jit(solution)/shard_map/ppermute | solution.py:15
  344.7 761.1 %reduce-scatter.5.cloned.1.call-start = ((), (), s32[]{:S(2)}) async-start(), calls=%async_computation.6 | async-start | bytes 4259840 | tf_op jit(solution)/shard_map/reduce_scatter | solution.py:168
  344.7 0.7 copy-start.13
Sparse Core Ops, SparseCore 0:
  80.1 33.9 all-gather.1
  344.8 392.7 reduce-scatter.2
  740.8 364.8 reduce-scatter.4
where the time goes:
time: 1120 us; the launch traced here: 1110 us
  waiting for transfers between devices  542 us (48%)
  blocking collectives  384 us (34%)
  matrix products  69.5 us (6%)
  starting transfers between devices  52.6 us (5%)
  local copies, waits for them, and re-layouts  39.4 us (4%)
  between operations  14.9 us (1%)
    reduce_scatter x1, waiting for transfers between devices, per_device(): lax.psum_scatter(store[1], 'dp', scatter_dimension=1, tiled=True)  368 us
    unnamed x1, blocking collectives  359 us
    ppermute x9, waiting for transfers between devices, shifted(): return lax.ppermute(x, axis, pairs)  114 us
    ppermute x9, starting transfers between devices, shifted(): return lax.ppermute(x, axis, pairs)  47.8 us
    reduce_scatter x1, waiting for transfers between devices, per_device(): lax.psum_scatter(store[0], 'dp', scatter_dimension=0, tiled=True)  31.5 us
    all_to_all x1, waiting for transfers between devices, per_device(): lax.all_to_all(found, 'dp', split_axis=0, concat_axis=0, tiled=True)  27.3 us
    all_to_all x1, blocking collectives, per_device(): lax.all_to_all(requests, 'dp', split_axis=0, concat_axis=0, tiled=True)  25.4 us
    dot_general x8, matrix products, contract_last(): lax.dot_general(left, right, (((1,), (1,)), ((), ())), preferred_element_...  22.5 us
  transfers between devices with their start and end apart: 13, of which 12 were waited for; matrix products, arithmetic and copies ran while one was open for 0% of the time, Pallas kernels for 0%

commit v1 on v0

v1 whole, which is shorter than its diff:
```python
import jax
import jax.numpy as jnp
from jax import lax
from jax.experimental import pallas as pl
from jax.experimental.pallas import tpu as pltpu
from jax.sharding import Mesh, PartitionSpec as P

CAP = 4
EPSILON = 1e-05
F32, BF16 = jnp.float32, jnp.bfloat16
YL, CO, Z, X, YH = "yl", "co", "z", "x", "yh"
DP = (Z, X, YH)
SEC = (YL, CO)
XY = (X, YH)


def dot_nn(a, b):
    return lax.dot_general(a, b, (((1,), (0,)), ((), ())), preferred_element_type=F32)


def dot_nt(a, b):
    return lax.dot_general(a, b, (((1,), (1,)), ((), ())), preferred_element_type=F32)


def dot_tn(a, b):
    return lax.dot_general(a, b, (((0,), (0,)), ((), ())), preferred_element_type=F32)


def swap(x, axis):
    return lax.ppermute(x, axis, [(0, 1), (1, 0)])


def gather_peers(x):
    across = swap(x, YL)
    beside = swap(x, CO)
    return x, beside, across, swap(across, CO)


def full(shape):
    return pl.BlockSpec(shape, lambda *_: (0,) * len(shape))


def prep_kernel(basis, prev, gained, weight_out, mats, acc):
    step = pl.program_id(0)
    r, h = basis.shape[1], gained.shape[1]

    @pl.when(step == 0)
    def _():
        acc[...] = jnp.zeros_like(acc)

    own, before = basis[...], prev[...]
    acc[0:r, :] += dot_tn(before, own)
    acc[r : r + h, :] += dot_tn(gained[...], before)
    acc[r + h : r + 2 * h, :] += dot_nn(weight_out[...], own)
    acc[r + 2 * h : 2 * r + 2 * h, :] += dot_tn(own, own)

    @pl.when(step == pl.num_programs(0) - 1)
    def _():
        top = 2 * r + 2 * h
        high = acc[...].astype(BF16)
        mats[0:top, :] = high
        gram = acc[r + 2 * h : top, :]
        mats[top : top + r, :] = (gram - high[r + 2 * h : top, :].astype(F32)).astype(BF16)


def prep(basis, prev, gained, weight_out):
    d, r = basis.shape
    h = gained.shape[1]
    steps = 8
    rows = d // steps
    return pl.pallas_call(
        prep_kernel,
        grid=(steps,),
        in_specs=[
            pl.BlockSpec((rows, r), lambda k: (k, 0)),
            pl.BlockSpec((rows, r), lambda k: (k, 0)),
            pl.BlockSpec((rows, h), lambda k: (k, 0)),
            pl.BlockSpec((h, rows), lambda k: (0, k)),
        ],
        out_specs=full((3 * r + 2 * h, r)),
        out_shape=jax.ShapeDtypeStruct((3 * r + 2 * h, r), BF16),
        scratch_shapes=[pltpu.VMEM((2 * r + 2 * h, r), F32)],
        compiler_params=pltpu.CompilerParams(vmem_limit_bytes=24 * 2**20),
        cost_estimate=pl.CostEstimate(
            flops=2 * d * r * (2 * r + 2 * h), bytes_accessed=4 * d * (r + h), transcendentals=0
        ),
        name="prep",
    )(basis, prev, gained, weight_out)


def project_kernel(me, p0, p1, p2, p3, basis, gained, out, square):
    step = pl.program_id(0)
    r = basis.shape[1]
    for k, piece in enumerate((p0, p1, p2, p3)):

        @pl.when(step == k)
        def _(k=k, piece=piece):
            x = piece[...]
            xf = x.astype(F32)
            q = jnp.broadcast_to(jnp.sum(xf * xf, axis=1, keepdims=True), square.shape)
            a, b = dot_nn(x, basis[...]), dot_nn(x, gained[...])
            if k == 0:
                out[:, 0:r] = a
                out[:, r:] = b
                square[...] = q
            else:
                out[:, 0:r] += a
                out[:, r:] += b
                square[...] += q


def project(me, pieces, basis, gained):
    tokens, cols = pieces[0].shape
    r, h = basis.shape[1], gained.shape[1]
    return pl.pallas_call(
        project_kernel,
        grid_spec=pltpu.PrefetchScalarGridSpec(
            num_scalar_prefetch=1,
            grid=(4,),
            in_specs=[full((tokens, cols))] * 4
            + [
                pl.BlockSpec((cols, r), lambda k, me: (k ^ me[0], 0)),
                pl.BlockSpec((cols, h), lambda k, me: (k ^ me[0], 0)),
            ],
            out_specs=[full((tokens, r + h)), full((tokens, 128))],
        ),
        out_shape=[
            jax.ShapeDtypeStruct((tokens, r + h), F32),
            jax.ShapeDtypeStruct((tokens, 128), F32),
        ],
        compiler_params=pltpu.CompilerParams(vmem_limit_bytes=24 * 2**20),
        cost_estimate=pl.CostEstimate(
            flops=8 * tokens * cols * (r + h), bytes_accessed=8 * cols * (r + h + tokens), transcendentals=0
        ),
        name="project",
    )(me, *pieces, basis, gained)


def chain_kernel(width, me_ref, cot, square, q0, q1, q2, q3, m0, m1, m2, m3, sent, packed,
                 pq, mats, pres, acts, coefs, spans, invs, ins, ws):
    me = me_ref[0]
    r = cot.shape[1]
    h = q0.shape[1] - r
    for k, (q, m) in enumerate(((q0, m0), (q1, m1), (q2, m2), (q3, m3))):
        pq[k ^ me] = q[...]
        mats[k ^ me] = m[...]
    o_k, o_n, o_g, o_l = r, r + h, r + 2 * h, 2 * r + 2 * h
    squares = square[:, 0:1]
    coefs[0] = jnp.zeros_like(coefs[0])
    for s in range(4):
        base_in = pq[s, :, r:]
        if s == 0:
            inv = lax.rsqrt(squares * (1.0 / width) + EPSILON)
            pre = inv * base_in
        else:
            c = coefs[s]
            base_sub = pq[s - 1, :, 0:r]
            span = base_sub + dot_nn(c, mats[s - 1, o_g:o_l, :]) + dot_nn(c, mats[s - 1, o_l:, :])
            total = squares + jnp.sum(c.astype(F32) * (base_sub + span), axis=1, keepdims=True)
            inv = lax.rsqrt(jnp.maximum(total, 0.0) * (1.0 / width) + EPSILON)
            pre = inv * (base_in + dot_nt(c, mats[s, o_k:o_n, :]))
            spans[s] = span
        invs[s] = jnp.broadcast_to(inv, invs.shape[1:])
        pres[s] = pre
        act = (pre / (1.0 + jnp.exp(-pre))).astype(BF16)
        acts[s] = act
        new = dot_nn(act, mats[s, o_n:o_g, :])
        if s > 0:
            new = new + dot_nn(c, mats[s, 0:r, :])
        coefs[s + 1] = new.astype(BF16)
    arrived = cot[...]
    for s in (3, 2, 1, 0):
        ins[s] = arrived
        pre = pres[s]
        sg = 1.0 / (1.0 + jnp.exp(-pre))
        gp = dot_nt(arrived, mats[s, o_n:o_g, :]) * sg * (1.0 + pre * (1.0 - sg))
        inv = invs[s, :, 0:1]
        ws[s] = (gp * inv).astype(BF16)
        if s > 0:
            mean = jnp.sum(gp * pre, axis=1, keepdims=True) * (1.0 / width)
            back = dot_nn(gp.astype(BF16), mats[s, o_k:o_n, :]) - (inv * mean) * spans[s]
            arrived = (dot_nt(arrived, mats[s, 0:r, :]) + inv * back).astype(BF16)
    sent[...] = coefs[me + 1]
    row = (ws[me], acts[me], ins[me], coefs[me])
    for t in range(packed.shape[0]):
        at = 0
        for v in row:
            packed[t, :, at : at + v.shape[1]] = v
            at += v.shape[1]


def chain(me, cot, square, pq, mats, width, copies):
    tokens, r = cot.shape
    h = pq[0].shape[1] - r
    vmem = pl.BlockSpec(memory_space=pltpu.VMEM)
    return pl.pallas_call(
        lambda *refs: chain_kernel(width, *refs),
        in_specs=[pl.BlockSpec(memory_space=pltpu.SMEM)] + [vmem] * 10,
        out_specs=[vmem, vmem],
        out_shape=[
            jax.ShapeDtypeStruct((tokens, r), BF16),
            jax.ShapeDtypeStruct((copies, tokens, 2 * h + 2 * r), BF16),
        ],
        scratch_shapes=[
            pltpu.VMEM((4, tokens, r + h), F32),
            pltpu.VMEM((4,) + mats[0].shape, BF16),
            pltpu.VMEM((4, tokens, h), F32),
            pltpu.VMEM((4, tokens, h), BF16),
            pltpu.VMEM((5, tokens, r), BF16),
            pltpu.VMEM((4, tokens, r), F32),
            pltpu.VMEM((4, tokens, 128), F32),
            pltpu.VMEM((4, tokens, r), BF16),
            pltpu.VMEM((4, tokens, h), BF16),
        ],
        compiler_params=pltpu.CompilerParams(vmem_limit_bytes=32 * 2**20),
        cost_estimate=pl.CostEstimate(flops=4 * 10**9, bytes_accessed=6 * 2**20, transcendentals=10**6),
        name="chain",
    )(me, cot, square, *pq, *mats)


def share_kernel(me_ref, packed, t0, t1, t2, t3, rows_own, rows_prev, out):
    me = me_ref[0]
    r = rows_own.shape[2]
    h = (packed.shape[1] - 2 * r) // 2
    w = packed[:, 0:h]
    act = packed[:, h : 2 * h]
    arrived = packed[:, 2 * h : 2 * h + r]
    coef = packed[:, 2 * h + r :]
    v = dot_tn(act, arrived)
    u = dot_tn(w, coef)
    vh, uh = v.astype(BF16), u.astype(BF16)
    vl = (v - vh.astype(F32)).astype(BF16)
    wt = w.astype(F32).T.astype(BF16)
    for k, piece in enumerate((t0, t1, t2, t3)):
        c = k ^ me
        xs = dot_nn(wt, piece[...])
        n = xs.shape[1] // 2
        for e in range(2):
            z = 2 * c + e
            own = rows_own[z]
            out[z, 0:h, :] = (xs[:, e * n : (e + 1) * n] + dot_nt(uh, rows_prev[z])).astype(BF16)
            out[z, h:, :] = (dot_nt(vh, own) + dot_nt(vl, own)).astype(BF16)


def share(me, packed, pieces, rows_own, rows_prev):
    h = (packed.shape[1] - 2 * rows_own.shape[2]) // 2
    zs, n, _ = rows_own.shape
    vmem = pl.BlockSpec(memory_space=pltpu.VMEM)
    return pl.pallas_call(
        share_kernel,
        in_specs=[pl.BlockSpec(memory_space=pltpu.SMEM)] + [vmem] * 7,
        out_specs=vmem,
        out_shape=jax.ShapeDtypeStruct((zs, 2 * h, n), BF16),
        compiler_params=pltpu.CompilerParams(vmem_limit_bytes=32 * 2**20),
        cost_estimate=pl.CostEstimate(flops=2 * 10**9, bytes_accessed=6 * 2**20, transcendentals=0),
        name="share",
    )(me, packed, *pieces, rows_own, rows_prev)


def per_device(
    token_ids, embed_table, subspace, adapter_in, adapter_out, norm_gain, coef_cotangent
):
    tokens = token_ids.shape[0]
    shards = lax.axis_size(Z) * lax.axis_size(X) * lax.axis_size(YH)
    nz, nxy = lax.axis_size(Z), lax.axis_size(X) * lax.axis_size(YH)
    section = lax.axis_index(YL) * lax.axis_size(CO) + lax.axis_index(CO)
    me = jnp.reshape(section, (1,)).astype(jnp.int32)
    xy = lax.axis_index(X) * lax.axis_size(YH) + lax.axis_index(YH)
    dp = lax.axis_index(Z) * nxy + xy
    vocab, cols = embed_table.shape
    basis, weight_in, weight_out, gain = subspace[0], adapter_in[0], adapter_out[0], norm_gain[0]
    d, r = basis.shape
    h = weight_in.shape[1]
    block = d // shards

    prev = lax.ppermute(subspace, SEC, [(0, 1), (1, 2), (2, 3)])[0]

    owner = token_ids // vocab
    local_row = token_ids - owner * vocab
    matches = (owner[:, None] == jnp.arange(shards, dtype=jnp.int32)[None, :]).astype(jnp.int32)
    position = jnp.sum(jnp.cumsum(matches, axis=0) * matches, axis=1) - 1
    place = owner * CAP + position
    requests = jnp.zeros((shards * CAP,), jnp.int32).at[place].set(local_row).reshape(shards, CAP)
    asked = lax.all_to_all(requests, DP, split_axis=0, concat_axis=0, tiled=True).reshape(-1)
    pick = (asked[:, None] == jnp.arange(vocab, dtype=jnp.int32)[None, :]).astype(BF16)
    found = dot_nn(pick, embed_table).astype(BF16).reshape(shards, CAP, cols)
    answered = lax.all_to_all(found, DP, split_axis=0, concat_axis=0, tiled=True)
    put = (place[:, None] == jnp.arange(shards * CAP, dtype=jnp.int32)[None, :]).astype(BF16)
    part = dot_nn(put, answered.reshape(shards * CAP, cols)).astype(BF16)

    pieces = gather_peers(part)
    gained = (gain[:, None] * weight_in.astype(F32)).astype(BF16)
    pq, square = project(me, pieces, basis, gained)
    pqs = gather_peers(pq)
    mats = gather_peers(prep(basis, prev, gained, weight_out))

    turned = jnp.transpose(part.reshape(tokens, 2, nxy, block), (2, 0, 1, 3)).reshape(nxy, tokens, 2 * block)
    turned = lax.all_to_all(turned, XY, split_axis=0, concat_axis=0, tiled=True)
    turned = gather_peers(turned.reshape(nxy * tokens, 2 * block))

    sent, packed = chain(me, coef_cotangent, square, pqs, mats, d, nxy)
    packed = lax.all_to_all(packed, XY, split_axis=0, concat_axis=0, tiled=True)
    packed = packed.reshape(nxy * tokens, 2 * h + 2 * r)
    rows_own = lax.dynamic_index_in_dim(basis.reshape(nz, nxy, block, r), xy, 1, False)
    rows_prev = lax.dynamic_index_in_dim(prev.reshape(nz, nxy, block, r), xy, 1, False)
    shares = share(me, packed, turned, rows_own, rows_prev)
    shares = lax.all_to_all(shares, Z, split_axis=0, concat_axis=0, tiled=True)
    total = jnp.sum(shares.astype(F32), axis=0)
    plain = total[0:h].T
    gain_block = lax.dynamic_slice_in_dim(gain, dp * block, block, 0)
    in_block = lax.dynamic_slice_in_dim(weight_in, dp * block, block, 0)
    grad_in = gain_block[:, None] * plain
    grad_gain = jnp.sum(in_block.astype(F32) * plain, axis=1)
    return sent[None], grad_in[None], total[h:][None], grad_gain[None]


def solution(mesh):
    fine = Mesh(mesh.devices.reshape(2, 2, 8, 4, 2), (YL, CO, Z, X, YH))
    return jax.shard_map(
        per_device,
        mesh=fine,
        in_specs=(
            P(DP),
            P(DP, SEC),
            P(SEC, None, None),
            P(SEC, None, None),
            P(SEC, None, None),
            P(SEC, None),
            P(DP, None),
        ),
        out_specs=(
            P(SEC, DP, None),
            P(SEC, DP, None),
            P(SEC, None, DP),
            P(SEC, DP),
        ),
        check_vma=False,
    )
```

time: 1120 us -> 224 us (0.20)
  the two profiles are of different devices: /device:TPU:8 before, /device:TPU:33 now
where the time goes in v1:
time: 224 us; the launch traced here: 220 us
  waiting for transfers between devices  119 us (53%)
  starting transfers between devices  35.3 us (16%)
  blocking collectives  23.6 us (11%)
  Pallas kernels  19.2 us (9%)
  local copies, waits for them, and re-layouts  13 us (6%)
  other arithmetic  5.32 us (2%)
  matrix products  3.82 us (2%)
    ppermute x12, waiting for transfers between devices, swap(): return lax.ppermute(x, axis, [(0, 1), (1, 0)])  42 us
    ppermute x1, waiting for transfers between devices, per_device(): prev = lax.ppermute(subspace, SEC, [(0, 1), (1, 2), (2, 3)])[0]  33.5 us
    all_to_all x1, blocking collectives, per_device(): lax.all_to_all(requests, DP, split_axis=0, concat_axis=0, tiled=True)  23.6 us
    all_to_all x1, waiting for transfers between devices, per_device(): lax.all_to_all(found, DP, split_axis=0, concat_axis=0, tiled=True)  23 us
    all_to_all x1, waiting for transfers between devices, per_device(): shares = lax.all_to_all(shares, Z, split_axis=0, concat_axis=0, tiled=True)  14.9 us
    ppermute x12, starting transfers between devices, swap(): return lax.ppermute(x, axis, [(0, 1), (1, 0)])  9.81 us
    pallas_call x1, Pallas kernels, prep(): pl.pallas_call(prep_kernel, grid=(steps,), in_specs=[pl.BlockSpec((rows,...  7.59 us
    all_to_all x1, starting transfers between devices, per_device(): shares = lax.all_to_all(shares, Z, split_axis=0, concat_axis=0, tiled=True)  6.2 us
  transfers between devices with their start and end apart: 17, of which 7 were waited for; matrix products, arithmetic and copies ran while one was open for 4% of the time, Pallas kernels for 7%

profile of v1, /device:TPU:33, one launch (start us, length us, event | category | flops | bytes accessed | tf_op | source)
XLA Modules:
  0.0 219.9 jit_solution(5189414725324834184)
XLA Ops:
  0.6 0.7 multiply_subtract_fusion
  1.3 0.1 fusion.4
  1.4 0.2 reduce_window_sum.11
  1.6 0.2 select_reduce_fusion
  1.8 1.0 scatter_custom_fusion
  2.7 0.1 all_to_all.18
  2.8 23.6 %all_to_all.29 = s32[64,1,4]{2,1,0:T(1,128)S(1)} all-to-all(s32[64,1,4]{2,1,0:T(1,128)S(1)} %bitcast.54), channel_id=1, replica_groups=mesh['yl'=2,'co'=2,'z'=8,'x'=4,'yh'=2] {'z','x','yh'}, dimensions={0} | all-to-all | bytes 2048 | tf_op jit(solution)/shard_map/all_to_all | solution.py:284
  26.4 0.5 broadcast.17
  26.9 0.7 reduce.3
  27.7 0.1 eq.47
  27.8 3.5 %convolution_convert_fusion = bf16[256,2048]{1,0:T(8,128)(2,1)S(1)} fusion(bf16[1008,2048]{1,0:T(8,128)(2,1)} %param.8, s32[256]{0:T(256)S(1)} %eq.47), kind=kOutput, calls=%fused_computation.3 | convolution fusion | flops 1057746944 | bytes 5178368 | tf_op jit(solution)/shard_map/dot_general | solution.py:18
  31.3 0.0 copy-start.4
  31.3 1.2 reshape.47
  32.5 5.3 %all-to-all-start.1 = ((bf16[64,4,2048]{2,1,0:T(4,128)(2,1)}), bf16[64,4,2048]{2,1,0:T(4,128)(2,1)S(1)}, u32[]{:S(2)}, u32[]{:S(2)}) async-start(bf16[64,4,2048]{2,1,0:T(4,128)(2,1)} %reshape.47), calls=%async_computation.1 | async-start | bytes 2097152 | tf_op jit(solution)/shard_map/all_to_all | solution.py:287
  37.8 4.6 %collective-permute-start.6 = (bf16[1,8192,256]{2,1,0:T(8,128)(2,1)}, bf16[1,8192,256]{2,1,0:T(8,128)(2,1)}, u32[]{:S(2)}, u32[]{:S(2)}) collective-permute-start(bf16[1,8192,256]{2,1,0:T(8,128)(2,1)} %param.9), channel_id=1, source_target_pairs={{0,64},{64,128},{128,192},{1,65},{65,129},{129,193},{2,66},{66,130... | collective-permute-start | bytes 12582920 | tf_op jit(solution)/shard_map/ppermute | solution.py:276
  42.4 23.0 %all-to-all-done.1 = bf16[64,4,2048]{2,1,0:T(4,128)(2,1)S(1)} async-done(((bf16[64,4,2048]{2,1,0:T(4,128)(2,1)}), bf16[64,4,2048]{2,1,0:T(4,128)(2,1)S(1)}, u32[]{:S(2)}, u32[]{:S(2)}) %all-to-all-start.1) | async-done | bytes 1048608 | tf_op jit(solution)/shard_map/all_to_all | solution.py:287
  65.3 0.3 reshape.48
  65.6 0.0 copy-start
  65.6 0.3 convolution_convert_fusion.1.p0
  66.0 0.5 collective-permute-start.1
  66.5 2.9 %fusion.gained = bf16[8192,128]{1,0:T(8,128)(2,1)S(1)} fusion(bf16[1,8192,128]{2,1,0:T(8,128)(2,1)} %param.10, f32[8192]{0:T(1024)S(1)} %bitcast.56), kind=kLoop, calls=%fused_computation.2 | loop fusion | flops 3145728 | bytes 4227072 | tf_op jit(solution)/shard_map/convert_element_type | solution.py:292
  69.3 33.5 %collective-permute-done.6 = bf16[1,8192,256]{2,1,0:T(8,128)(2,1)} collective-permute-done((bf16[1,8192,256]{2,1,0:T(8,128)(2,1)}, bf16[1,8192,256]{2,1,0:T(8,128)(2,1)}, u32[]{:S(2)}, u32[]{:S(2)}) %collective-permute-start.6) | collective-permute-done | bytes 4194336 | tf_op jit(solution)/shard_map/ppermute | solution.py:276
  102.8 1.6 copy-done.2
  104.4 7.6 %prep.1.refs_7_ = bf16[1024,256]{1,0:T(8,128)(2,1)S(1)} custom-call(bf16[8192,256]{1,0:T(8,128)(2,1)S(1)} %bitcast.45, bf16[8192,256]{1,0:T(8,128)(2,1)} %bitcast.5.prev, bf16[8192,128]{1,0:T(8,128)(2,1)S(1)} %fusion.gained, bf16[128,8192]{1,0:T(8,128)(2,1)S(1)} %bitcast.48), custom_call_target="tpu_custom_call" | custom-call | flops 3221225472 | bytes 12582912 | tf_op jit(solution)/shard_map/prep/pallas_call | solution.py:71
  112.0 0.1 collective-permute-start.8
  112.1 2.9 %collective-permute-start = (bf16[128,2048]{1,0:T(8,128)(2,1)S(1)}, bf16[128,2048]{1,0:T(8,128)(2,1)}, u32[]{:S(2)}, u32[]{:S(2)}) collective-permute-start(bf16[128,2048]{1,0:T(8,128)(2,1)S(1)} %convolution_convert_fusion.1.p0), channel_id=1, source_target_pairs={{0,64},{64,0},{1,65},{65,1},{2,66},{66,2},{3,67},{67,3},{4,68},{68... | collective-permute-start | bytes 1572872 | tf_op jit(solution)/shard_map/ppermute | solution.py:30
  115.0 0.0 collective-permute-done.1.p2
  115.0 0.0 collective-permute-start.2
  115.0 0.5 collective-permute-start.7
  115.5 9.3 %collective-permute-done.8.refs_9_ = bf16[1024,256]{1,0:T(8,128)(2,1)} collective-permute-done((bf16[1024,256]{1,0:T(8,128)(2,1)S(1)}, bf16[1024,256]{1,0:T(8,128)(2,1)}, u32[]{:S(2)}, u32[]{:S(2)}) %collective-permute-start.8) | collective-permute-done | bytes 524320 | tf_op jit(solution)/shard_map/ppermute | solution.py:30
  124.8 1.8 collective-permute-start.9
  126.6 0.0 collective-permute-done.p1
  126.6 0.0 collective-permute-done.2.p3
  126.6 2.2 copy-done.1
  128.8 3.2 %project.1 = (f32[128,384]{1,0:T(8,128)S(1)}, f32[128,128]{1,0:T(8,128)S(1)}) custom-call(s32[1]{0:T(128)} %bitcast.me.refs_0_.me_ref, bf16[128,2048]{1,0:T(8,128)(2,1)S(1)} %convolution_convert_fusion.1.p0, bf16[128,2048]{1,0:T(8,128)(2,1)} %collective-permute-done.p1, bf16[128,2048]{1,0:T(8,128)(2,1)} %collective-permute-done.1.p2, ...), custom_call_target="tpu_custom_call" | custom-call | flops 805306368 | bytes 8388608 | tf_op jit(solution)/shard_map/project/pallas_call | solution.py:115
  132.0 0.0 copy-start.3
  132.0 0.1 collective-permute-start.4
  132.1 0.3 collective-permute-start.3
  132.4 6.2 %collective-permute-done.4.refs_5_ = f32[128,384]{1,0:T(8,128)S(1)} collective-permute-done((f32[128,384]{1,0:T(8,128)S(1)}, f32[128,384]{1,0:T(8,128)S(1)}, u32[]{:S(2)}, u32[]{:S(2)}) %collective-permute-start.4) | collective-permute-done | bytes 196640 | tf_op jit(solution)/shard_map/ppermute | solution.py:30
  138.6 0.8 collective-permute-start.5
  139.4 0.1 copy.28
  139.5 0.4 copy.20
  139.9 1.1 reshape.51
  141.1 5.9 %all-to-all-start.3 = ((bf16[8,128,256]{2,1,0:T(8,128)(2,1)}), bf16[8,128,256]{2,1,0:T(8,128)(2,1)S(1)}, u32[]{:S(2)}, u32[]{:S(2)}) async-start(bf16[8,128,256]{2,1,0:T(8,128)(2,1)} %reshape.51), calls=%async_computation.3 | async-start | bytes 1048576 | tf_op jit(solution)/shard_map/all_to_all | solution.py:298
  146.9 0.0 collective-permute-done.3.refs_4_
  146.9 0.0 collective-permute-done.9.refs_10_
  147.0 5.2 %chain.1 = (bf16[128,256]{1,0:T(8,128)(2,1)}, bf16[8,128,768]{2,1,0:T(8,128)(2,1)}) custom-call(s32[1]{0:T(128)} %bitcast.me.refs_0_.me_ref, bf16[128,256]{1,0:T(8,128)(2,1)S(1)} %copy-done.3, f32[128,128]{1,0:T(8,128)S(1)} %get-tuple-element.8.refs_2_, f32[128,384]{1,0:T(8,128)S(1)} %get-tuple-element.9.refs_3_, ...), custom_call_target="tpu_custom_call" | custom-call | flops 4000000000 | bytes 6291456 | tf_op jit(solution)/shard_map/chain/pallas_call | solution.py:196
  152.1 5.3 %all-to-all-done.3 = bf16[8,128,256]{2,1,0:T(8,128)(2,1)S(1)} async-done(((bf16[8,128,256]{2,1,0:T(8,128)(2,1)}), bf16[8,128,256]{2,1,0:T(8,128)(2,1)S(1)}, u32[]{:S(2)}, u32[]{:S(2)}) %all-to-all-start.3) | async-done | bytes 524320 | tf_op jit(solution)/shard_map/all_to_all | solution.py:298
  157.4 3.6 %all-to-all-start.2 = ((bf16[8,128,768]{2,1,0:T(8,128)(2,1)}), bf16[8,128,768]{2,1,0:T(8,128)(2,1)S(1)}, u32[]{:S(2)}, u32[]{:S(2)}) async-start(bf16[8,128,768]{2,1,0:T(8,128)(2,1)} %get-tuple-element.11), calls=%async_computation.2 | async-start | bytes 3145728 | tf_op jit(solution)/shard_map/all_to_all | solution.py:302
  161.0 0.1 collective-permute-start.11
  161.1 1.2 collective-permute-start.10
  162.3 26.5 %collective-permute-done.11.t2 = bf16[1024,256]{1,0:T(8,128)(2,1)} collective-permute-done((bf16[1024,256]{1,0:T(8,128)(2,1)S(1)}, bf16[1024,256]{1,0:T(8,128)(2,1)}, u32[]{:S(2)}, u32[]{:S(2)}) %collective-permute-start.11) | collective-permute-done | bytes 524320 | tf_op jit(solution)/shard_map/ppermute | solution.py:30
  188.8 1.6 collective-permute-start.12
  190.4 1.1 dynamic-slice_bitcast_fusion.1.rows_own
  191.5 1.1 dynamic-slice_bitcast_fusion.rows_prev
  192.6 3.2 %share.1 = bf16[8,256,128]{2,1,0:T(8,128)(2,1)} custom-call(s32[1]{0:T(128)} %bitcast.me.refs_0_.me_ref, bf16[1024,768]{1,0:T(8,128)(2,1)S(1)} %bitcast.49, bf16[1024,256]{1,0:T(8,128)(2,1)S(1)} %bitcast.52, bf16[1024,256]{1,0:T(8,128)(2,1)} %collective-permute-done.10.t1, bf16[1024,256]{1,0:T(8,128)(2,1)} %collective-permute-done.11.t2, ...), custom_call_target="tpu_custom_call" | custom-call | flops 2000000000 | bytes 6291456 | tf_op jit(solution)/shard_map/share/pallas_call | solution.py:249
  195.9 6.2 %all-to-all-start.4 = ((bf16[8,256,128]{2,1,0:T(8,128)(2,1)}), bf16[8,256,128]{2,1,0:T(8,128)(2,1)S(1)}, u32[]{:S(2)}, u32[]{:S(2)}) async-start(bf16[8,256,128]{2,1,0:T(8,128)(2,1)} %share.1), calls=%async_computation.4 | async-start | bytes 1048576 | tf_op jit(solution)/shard_map/all_to_all | solution.py:307
  202.1 0.8 constant_dynamic-slice_fusion
  202.8 0.1 copy.27
  203.0 14.9 %all-to-all-done.4 = bf16[8,256,128]{2,1,0:T(8,128)(2,1)S(1)} async-done(((bf16[8,256,128]{2,1,0:T(8,128)(2,1)}), bf16[8,256,128]{2,1,0:T(8,128)(2,1)S(1)}, u32[]{:S(2)}, u32[]{:S(2)}) %all-to-all-start.4) | async-done | bytes 524320 | tf_op jit(solution)/shard_map/all_to_all | solution.py:307
  217.9 0.1 convert_reduce_fusion
  218.0 0.6 slice_bitcast_fusion
  218.6 0.5 fusion.2
  219.1 0.7 copy.23
  (12 shorter events, 0.0 us)
Async XLA Ops:
  31.3 35.2 %copy-start.4 = (f32[1,8192]{1,0:T(1,128)S(1)}, f32[1,8192]{1,0:T(1,128)}, u32[]{:S(2)}) copy-start(f32[1,8192]{1,0:T(1,128)} %param.12) | copy-start | bytes 98308
  32.5 32.9 %all-to-all-start.1 = ((bf16[64,4,2048]{2,1,0:T(4,128)(2,1)}), bf16[64,4,2048]{2,1,0:T(4,128)(2,1)S(1)}, u32[]{:S(2)}, u32[]{:S(2)}) async-start(bf16[64,4,2048]{2,1,0:T(4,128)(2,1)} %reshape.47), calls=%async_computation.1 | async-start | bytes 2097152 | tf_op jit(solution)/shard_map/all_to_all | solution.py:287
  37.8 65.1 %collective-permute-start.6 = (bf16[1,8192,256]{2,1,0:T(8,128)(2,1)}, bf16[1,8192,256]{2,1,0:T(8,128)(2,1)}, u32[]{:S(2)}, u32[]{:S(2)}) collective-permute-start(bf16[1,8192,256]{2,1,0:T(8,128)(2,1)} %param.9), channel_id=1, source_target_pairs={{0,64},{64,128},{128,192},{1,65},{65,129},{129,193},{2,66},{66,130... | collective-permute-start | bytes 12582920 | tf_op jit(solution)/shard_map/ppermute | solution.py:276
  65.6 37.2 %copy-start = (bf16[1,8192,256]{2,1,0:T(8,128)(2,1)S(1)}, bf16[1,8192,256]{2,1,0:T(8,128)(2,1)}, u32[]{:S(2)}) copy-start(bf16[1,8192,256]{2,1,0:T(8,128)(2,1)} %param.9) | copy-start | bytes 12582916
  66.0 49.0 %collective-permute-start.1 = (bf16[128,2048]{1,0:T(8,128)(2,1)S(1)}, bf16[128,2048]{1,0:T(8,128)(2,1)}, u32[]{:S(2)}, u32[]{:S(2)}) collective-permute-start(bf16[128,2048]{1,0:T(8,128)(2,1)S(1)} %convolution_convert_fusion.1.p0), channel_id=1, source_target_pairs={{0,128},{128,0},{1,129},{129,1},{2,130},{130,2},{3,131},{131,3},{4... | collective-permute-start | bytes 1572872 | tf_op jit(solution)/shard_map/ppermute | solution.py:30
  102.8 1.6 copy-start.2
  112.0 12.8 %collective-permute-start.8 = (bf16[1024,256]{1,0:T(8,128)(2,1)S(1)}, bf16[1024,256]{1,0:T(8,128)(2,1)}, u32[]{:S(2)}, u32[]{:S(2)}) collective-permute-start(bf16[1024,256]{1,0:T(8,128)(2,1)S(1)} %prep.1.refs_7_), channel_id=1, source_target_pairs={{0,128},{128,0},{1,129},{129,1},{2,130},{130,2},{3,131},{131,3},{4... | collective-permute-start | bytes 1572872 | tf_op jit(solution)/shard_map/ppermute | solution.py:30
  112.1 14.4 %collective-permute-start = (bf16[128,2048]{1,0:T(8,128)(2,1)S(1)}, bf16[128,2048]{1,0:T(8,128)(2,1)}, u32[]{:S(2)}, u32[]{:S(2)}) collective-permute-start(bf16[128,2048]{1,0:T(8,128)(2,1)S(1)} %convolution_convert_fusion.1.p0), channel_id=1, source_target_pairs={{0,64},{64,0},{1,65},{65,1},{2,66},{66,2},{3,67},{67,3},{4,68},{68... | collective-permute-start | bytes 1572872 | tf_op jit(solution)/shard_map/ppermute | solution.py:30
  115.0 11.6 %collective-permute-start.2 = (bf16[128,2048]{1,0:T(8,128)(2,1)}, bf16[128,2048]{1,0:T(8,128)(2,1)}, u32[]{:S(2)}, u32[]{:S(2)}) collective-permute-start(bf16[128,2048]{1,0:T(8,128)(2,1)} %collective-permute-done.1.p2), channel_id=1, source_target_pairs={{0,64},{64,0},{1,65},{65,1},{2,66},{66,2},{3,67},{67,3},{4,68},{68... | collective-permute-start | bytes 1572872 | tf_op jit(solution)/shard_map/ppermute | solution.py:30
  115.0 31.9 %collective-permute-start.7 = (bf16[1024,256]{1,0:T(8,128)(2,1)S(1)}, bf16[1024,256]{1,0:T(8,128)(2,1)}, u32[]{:S(2)}, u32[]{:S(2)}) collective-permute-start(bf16[1024,256]{1,0:T(8,128)(2,1)S(1)} %prep.1.refs_7_), channel_id=1, source_target_pairs={{0,64},{64,0},{1,65},{65,1},{2,66},{66,2},{3,67},{67,3},{4,68},{68... | collective-permute-start | bytes 1572872 | tf_op jit(solution)/shard_map/ppermute | solution.py:30
  124.8 22.1 %collective-permute-start.9 = (bf16[1024,256]{1,0:T(8,128)(2,1)}, bf16[1024,256]{1,0:T(8,128)(2,1)}, u32[]{:S(2)}, u32[]{:S(2)}) collective-permute-start(bf16[1024,256]{1,0:T(8,128)(2,1)} %collective-permute-done.8.refs_9_), channel_id=1, source_target_pairs={{0,64},{64,0},{1,65},{65,1},{2,66},{66,2},{3,67},{67,3},{4,68},{68... | collective-permute-start | bytes 1572872 | tf_op jit(solution)/shard_map/ppermute | solution.py:30
  126.6 2.2 copy-start.1
  132.0 15.0 %copy-start.3 = (bf16[128,256]{1,0:T(8,128)(2,1)S(1)}, bf16[128,256]{1,0:T(8,128)(2,1)}, u32[]{:S(2)}) copy-start(bf16[128,256]{1,0:T(8,128)(2,1)} %refs_1_.1) | copy-start | bytes 196612
  132.0 6.6 %collective-permute-start.4 = (f32[128,384]{1,0:T(8,128)S(1)}, f32[128,384]{1,0:T(8,128)S(1)}, u32[]{:S(2)}, u32[]{:S(2)}) collective-permute-start(f32[128,384]{1,0:T(8,128)S(1)} %get-tuple-element.9.refs_3_), channel_id=1, source_target_pairs={{0,128},{128,0},{1,129},{129,1},{2,130},{130,2},{3,131},{131,3},{4... | collective-permute-start | bytes 589832 | tf_op jit(solution)/shard_map/ppermute | solution.py:30
  132.1 14.8 %collective-permute-start.3 = (f32[128,384]{1,0:T(8,128)S(1)}, f32[128,384]{1,0:T(8,128)S(1)}, u32[]{:S(2)}, u32[]{:S(2)}) collective-permute-start(f32[128,384]{1,0:T(8,128)S(1)} %get-tuple-element.9.refs_3_), channel_id=1, source_target_pairs={{0,64},{64,0},{1,65},{65,1},{2,66},{66,2},{3,67},{67,3},{4,68},{68... | collective-permute-start | bytes 589832 | tf_op jit(solution)/shard_map/ppermute | solution.py:30
  138.6 8.3 %collective-permute-start.5 = (f32[128,384]{1,0:T(8,128)S(1)}, f32[128,384]{1,0:T(8,128)S(1)}, u32[]{:S(2)}, u32[]{:S(2)}) collective-permute-start(f32[128,384]{1,0:T(8,128)S(1)} %collective-permute-done.4.refs_5_), channel_id=1, source_target_pairs={{0,64},{64,0},{1,65},{65,1},{2,66},{66,2},{3,67},{67,3},{4,68},{68... | collective-permute-start | bytes 589832 | tf_op jit(solution)/shard_map/ppermute | solution.py:30
  141.1 16.3 %all-to-all-start.3 = ((bf16[8,128,256]{2,1,0:T(8,128)(2,1)}), bf16[8,128,256]{2,1,0:T(8,128)(2,1)S(1)}, u32[]{:S(2)}, u32[]{:S(2)}) async-start(bf16[8,128,256]{2,1,0:T(8,128)(2,1)} %reshape.51), calls=%async_computation.3 | async-start | bytes 1048576 | tf_op jit(solution)/shard_map/all_to_all | solution.py:298
  157.4 35.2 %all-to-all-start.2 = ((bf16[8,128,768]{2,1,0:T(8,128)(2,1)}), bf16[8,128,768]{2,1,0:T(8,128)(2,1)S(1)}, u32[]{:S(2)}, u32[]{:S(2)}) async-start(bf16[8,128,768]{2,1,0:T(8,128)(2,1)} %get-tuple-element.11), calls=%async_computation.2 | async-start | bytes 3145728 | tf_op jit(solution)/shard_map/all_to_all | solution.py:302
  161.0 27.8 %collective-permute-start.11 = (bf16[1024,256]{1,0:T(8,128)(2,1)S(1)}, bf16[1024,256]{1,0:T(8,128)(2,1)}, u32[]{:S(2)}, u32[]{:S(2)}) collective-permute-start(bf16[1024,256]{1,0:T(8,128)(2,1)S(1)} %bitcast.50), channel_id=1, source_target_pairs={{0,128},{128,0},{1,129},{129,1},{2,130},{130,2},{3,131},{131,3},{4... | collective-permute-start | bytes 1572872 | tf_op jit(solution)/shard_map/ppermute | solution.py:30
  161.1 31.5 %collective-permute-start.10 = (bf16[1024,256]{1,0:T(8,128)(2,1)S(1)}, bf16[1024,256]{1,0:T(8,128)(2,1)}, u32[]{:S(2)}, u32[]{:S(2)}) collective-permute-start(bf16[1024,256]{1,0:T(8,128)(2,1)S(1)} %bitcast.51), channel_id=1, source_target_pairs={{0,64},{64,0},{1,65},{65,1},{2,66},{66,2},{3,67},{67,3},{4,68},{68... | collective-permute-start | bytes 1572872 | tf_op jit(solution)/shard_map/ppermute | solution.py:30
  188.8 3.8 %collective-permute-start.12 = (bf16[1024,256]{1,0:T(8,128)(2,1)}, bf16[1024,256]{1,0:T(8,128)(2,1)}, u32[]{:S(2)}, u32[]{:S(2)}) collective-permute-start(bf16[1024,256]{1,0:T(8,128)(2,1)} %collective-permute-done.11.t2), channel_id=1, source_target_pairs={{0,64},{64,0},{1,65},{65,1},{2,66},{66,2},{3,67},{67,3},{4,68},{68... | collective-permute-start | bytes 1572872 | tf_op jit(solution)/shard_map/ppermute | solution.py:30
  195.9 22.0 %all-to-all-start.4 = ((bf16[8,256,128]{2,1,0:T(8,128)(2,1)}), bf16[8,256,128]{2,1,0:T(8,128)(2,1)S(1)}, u32[]{:S(2)}, u32[]{:S(2)}) async-start(bf16[8,256,128]{2,1,0:T(8,128)(2,1)} %share.1), calls=%async_computation.4 | async-start | bytes 1048576 | tf_op jit(solution)/shard_map/all_to_all | solution.py:307

commit v2 on v1

v2 whole, which is shorter than its diff:
```python
import jax
import jax.numpy as jnp
from jax import lax
from jax.experimental import pallas as pl
from jax.experimental.pallas import tpu as pltpu
from jax.sharding import Mesh, PartitionSpec as P

CAP = 4
EPSILON = 1e-05
F32, BF16 = jnp.float32, jnp.bfloat16
YL, CO, ZH, ZL, X, YH = "yl", "co", "zh", "zl", "x", "yh"
DP = (ZH, ZL, X, YH)
SEC = (YL, CO)
GATHER = (ZL, X)
REDUCE = (ZH, YH)


def dot_nn(a, b):
    return lax.dot_general(a, b, (((1,), (0,)), ((), ())), preferred_element_type=F32)


def dot_nt(a, b):
    return lax.dot_general(a, b, (((1,), (1,)), ((), ())), preferred_element_type=F32)


def dot_tn(a, b):
    return lax.dot_general(a, b, (((0,), (0,)), ((), ())), preferred_element_type=F32)


def swap(x, axis):
    return lax.ppermute(x, axis, [(0, 1), (1, 0)])


def gather_peers(x):
    across = swap(x, YL)
    beside = swap(x, CO)
    return x, beside, across, swap(across, CO)


def full(shape):
    return pl.BlockSpec(shape, lambda *_: (0,) * len(shape))


def own_kernel(basis, weight_out, out, acc):
    step = pl.program_id(0)
    r, h = basis.shape[1], weight_out.shape[0]

    @pl.when(step == 0)
    def _():
        acc[...] = jnp.zeros_like(acc)

    own = basis[...]
    acc[0:h, :] += dot_nn(weight_out[...], own)
    acc[h:, :] += dot_tn(own, own)

    @pl.when(step == pl.num_programs(0) - 1)
    def _():
        high = acc[...].astype(BF16)
        out[0 : h + r, :] = high
        out[h + r :, :] = (acc[h:, :] - high[h:, :].astype(F32)).astype(BF16)


def own_products(basis, weight_out):
    d, r = basis.shape
    h = weight_out.shape[0]
    steps = 4
    rows = d // steps
    return pl.pallas_call(
        own_kernel,
        grid=(steps,),
        in_specs=[
            pl.BlockSpec((rows, r), lambda k: (k, 0)),
            pl.BlockSpec((h, rows), lambda k: (0, k)),
        ],
        out_specs=full((2 * r + h, r)),
        out_shape=jax.ShapeDtypeStruct((2 * r + h, r), BF16),
        scratch_shapes=[pltpu.VMEM((r + h, r), F32)],
        compiler_params=pltpu.CompilerParams(vmem_limit_bytes=24 * 2**20),
        cost_estimate=pl.CostEstimate(
            flops=2 * d * r * (r + h), bytes_accessed=2 * d * (r + h), transcendentals=0
        ),
        name="own_products",
    )(basis, weight_out)


def cross_kernel(at, basis, prev, gained, out):
    r, h = basis.shape[1], gained.shape[1]

    @pl.when(pl.program_id(0) == 0)
    def _():
        out[...] = jnp.zeros_like(out)

    before = prev[0]
    out[0:r, :] += dot_tn(before, basis[...])
    out[r:, :] += dot_tn(gained[...], before)


def cross_products(at, basis, prev, gained):
    r, h = basis.shape[1], gained.shape[1]
    blocks, rows, _ = prev.shape
    return pl.pallas_call(
        cross_kernel,
        grid_spec=pltpu.PrefetchScalarGridSpec(
            num_scalar_prefetch=1,
            grid=(blocks,),
            in_specs=[
                pl.BlockSpec((rows, r), lambda k, at: (k * 4 + at[0], 0)),
                pl.BlockSpec((1, rows, r), lambda k, at: (k, 0, 0)),
                pl.BlockSpec((rows, h), lambda k, at: (k * 4 + at[0], 0)),
            ],
            out_specs=full((r + h, r)),
        ),
        out_shape=jax.ShapeDtypeStruct((r + h, r), F32),
        compiler_params=pltpu.CompilerParams(vmem_limit_bytes=24 * 2**20),
        cost_estimate=pl.CostEstimate(
            flops=2 * blocks * rows * r * (r + h),
            bytes_accessed=2 * blocks * rows * (2 * r + h),
            transcendentals=0,
        ),
        name="cross_products",
    )(at, basis, prev, gained)


def sum_over_x(v):
    v = v + lax.ppermute(v, X, [(0, 1), (1, 0), (2, 3), (3, 2)])
    return v + lax.ppermute(v, X, [(0, 3), (3, 0), (1, 2), (2, 1)])


def column_of(row, n):
    return jnp.broadcast_to(row, (8, n)).T[:, 0:1]


def pick_kernel(asked, table, first, out):
    slots, vocab = asked.shape[1], table.shape[0]
    lanes = lax.broadcasted_iota(jnp.int32, (slots, vocab), 1)
    pick = (column_of(asked[...], slots) == lanes).astype(F32).astype(BF16)
    out[...] = dot_nn(pick, table[...]).astype(BF16)


def pick_rows(asked, table, first):
    slots = asked.shape[1]
    vocab, cols = table.shape
    steps = 4
    return pl.pallas_call(
        pick_kernel,
        grid=(steps,),
        in_specs=[
            full(asked.shape),
            pl.BlockSpec((vocab, cols // steps), lambda k: (0, k)),
            pl.BlockSpec(memory_space=pl.ANY),
        ],
        out_specs=pl.BlockSpec((slots, cols // steps), lambda k: (0, k)),
        out_shape=jax.ShapeDtypeStruct((slots, cols), BF16),
        compiler_params=pltpu.CompilerParams(vmem_limit_bytes=24 * 2**20),
        cost_estimate=pl.CostEstimate(
            flops=2 * slots * vocab * cols, bytes_accessed=2 * cols * (vocab + slots), transcendentals=0
        ),
        name="pick_rows",
    )(asked, table, first)


def place_kernel(place, answered, *refs):
    part, turned = refs[-2:]
    tokens, slots = part.shape[0], answered.shape[0]
    width = turned.shape[2]
    lanes = lax.broadcasted_iota(jnp.int32, (tokens, slots), 1)
    put = (column_of(place[...], tokens) == lanes).astype(F32).astype(BF16)
    for t in range(turned.shape[0]):
        rows = dot_nn(put, answered[:, t * width : (t + 1) * width]).astype(BF16)
        part[:, t * width : (t + 1) * width] = rows
        turned[t] = rows


def place_rows(place, answered, copies, firsts):
    tokens = place.shape[1]
    slots, cols = answered.shape
    vmem = pl.BlockSpec(memory_space=pltpu.VMEM)
    return pl.pallas_call(
        place_kernel,
        in_specs=[vmem, vmem] + [pl.BlockSpec(memory_space=pl.ANY)] * len(firsts),
        out_specs=[vmem, vmem],
        out_shape=[
            jax.ShapeDtypeStruct((tokens, cols), BF16),
            jax.ShapeDtypeStruct((copies, tokens, cols // copies), BF16),
        ],
        compiler_params=pltpu.CompilerParams(vmem_limit_bytes=16 * 2**20),
        cost_estimate=pl.CostEstimate(
            flops=2 * slots * tokens * cols, bytes_accessed=2 * cols * (slots + 2 * tokens), transcendentals=0
        ),
        name="place_rows",
    )(place, answered, *firsts)


def project_kernel(me, p0, p1, p2, p3, basis, gained, first, out, square):
    step = pl.program_id(0)
    r = basis.shape[1]
    for k, piece in enumerate((p0, p1, p2, p3)):

        @pl.when(step == k)
        def _(k=k, piece=piece):
            x = piece[...]
            xf = x.astype(F32)
            q = jnp.broadcast_to(jnp.sum(xf * xf, axis=1, keepdims=True), square.shape)
            a, b = dot_nn(x, basis[...]), dot_nn(x, gained[...])
            if k == 0:
                out[:, 0:r] = a
                out[:, r:] = b
                square[...] = q
            else:
                out[:, 0:r] += a
                out[:, r:] += b
                square[...] += q


def project(me, pieces, basis, gained, first):
    tokens, cols = pieces[0].shape
    r, h = basis.shape[1], gained.shape[1]
    return pl.pallas_call(
        project_kernel,
        grid_spec=pltpu.PrefetchScalarGridSpec(
            num_scalar_prefetch=1,
            grid=(4,),
            in_specs=[full((tokens, cols))] * 4
            + [
                pl.BlockSpec((cols, r), lambda k, me: (k ^ me[0], 0)),
                pl.BlockSpec((cols, h), lambda k, me: (k ^ me[0], 0)),
                pl.BlockSpec(memory_space=pl.ANY),
            ],
            out_specs=[full((tokens, r + h)), full((tokens, 128))],
        ),
        out_shape=[
            jax.ShapeDtypeStruct((tokens, r + h), F32),
            jax.ShapeDtypeStruct((tokens, 128), F32),
        ],
        compiler_params=pltpu.CompilerParams(vmem_limit_bytes=24 * 2**20),
        cost_estimate=pl.CostEstimate(
            flops=8 * tokens * cols * (r + h), bytes_accessed=8 * cols * (r + h + tokens), transcendentals=0
        ),
        name="project",
    )(me, *pieces, basis, gained, first)


def chain_kernel(width, me_ref, cot, square, q0, q1, q2, q3, g0, g1, g2, g3, m0, m1, m2, m3, sent, packed,
                 pq, owns, mats, pres, acts, coefs, spans, invs, ins, ws):
    me = me_ref[0]
    r = cot.shape[1]
    h = q0.shape[1] - r
    for k, (q, g, m) in enumerate(((q0, g0, m0), (q1, g1, m1), (q2, g2, m2), (q3, g3, m3))):
        pq[k ^ me] = q[...]
        owns[k ^ me] = g[...]
        mats[k ^ me] = m[...]
    squares = square[:, 0:1]
    coefs[0] = jnp.zeros_like(coefs[0])
    for s in range(4):
        base_in = pq[s, :, r:]
        if s == 0:
            inv = lax.rsqrt(squares * (1.0 / width) + EPSILON)
            pre = inv * base_in
        else:
            c = coefs[s]
            base_sub = pq[s - 1, :, 0:r]
            span = base_sub + dot_nn(c, owns[s - 1, h : h + r, :]) + dot_nn(c, owns[s - 1, h + r :, :])
            total = squares + jnp.sum(c.astype(F32) * (base_sub + span), axis=1, keepdims=True)
            inv = lax.rsqrt(jnp.maximum(total, 0.0) * (1.0 / width) + EPSILON)
            pre = inv * (base_in + dot_nt(c, mats[s, r:, :]))
            spans[s] = span
        invs[s] = jnp.broadcast_to(inv, invs.shape[1:])
        pres[s] = pre
        act = (pre / (1.0 + jnp.exp(-pre))).astype(BF16)
        acts[s] = act
        new = dot_nn(act, owns[s, 0:h, :])
        if s > 0:
            new = new + dot_nn(c, mats[s, 0:r, :])
        coefs[s + 1] = new.astype(BF16)
    arrived = cot[...]
    for s in (3, 2, 1, 0):
        ins[s] = arrived
        pre = pres[s]
        sg = 1.0 / (1.0 + jnp.exp(-pre))
        gp = dot_nt(arrived, owns[s, 0:h, :]) * sg * (1.0 + pre * (1.0 - sg))
        inv = invs[s, :, 0:1]
        ws[s] = (gp * inv).astype(BF16)
        if s > 0:
            mean = jnp.sum(gp * pre, axis=1, keepdims=True) * (1.0 / width)
            back = dot_nn(gp.astype(BF16), mats[s, r:, :]) - (inv * mean) * spans[s]
            arrived = (dot_nt(arrived, mats[s, 0:r, :]) + inv * back).astype(BF16)
    sent[...] = coefs[me + 1]
    row = (ws[me], acts[me], ins[me], coefs[me])
    for t in range(packed.shape[0]):
        at = 0
        for v in row:
            packed[t, :, at : at + v.shape[1]] = v
            at += v.shape[1]


def chain(me, cot, square, pq, owns, mats, width, copies):
    tokens, r = cot.shape
    h = pq[0].shape[1] - r
    vmem = pl.BlockSpec(memory_space=pltpu.VMEM)
    return pl.pallas_call(
        lambda *refs: chain_kernel(width, *refs),
        in_specs=[pl.BlockSpec(memory_space=pltpu.SMEM)] + [vmem] * 14,
        out_specs=[vmem, vmem],
        out_shape=[
            jax.ShapeDtypeStruct((tokens, r), BF16),
            jax.ShapeDtypeStruct((copies, tokens, 2 * h + 2 * r), BF16),
        ],
        scratch_shapes=[
            pltpu.VMEM((4, tokens, r + h), F32),
            pltpu.VMEM((4,) + owns[0].shape, BF16),
            pltpu.VMEM((4,) + mats[0].shape, BF16),
            pltpu.VMEM((4, tokens, h), F32),
            pltpu.VMEM((4, tokens, h), BF16),
            pltpu.VMEM((5, tokens, r), BF16),
            pltpu.VMEM((4, tokens, r), F32),
            pltpu.VMEM((4, tokens, 128), F32),
            pltpu.VMEM((4, tokens, r), BF16),
            pltpu.VMEM((4, tokens, h), BF16),
        ],
        compiler_params=pltpu.CompilerParams(vmem_limit_bytes=32 * 2**20),
        cost_estimate=pl.CostEstimate(flops=4 * 10**9, bytes_accessed=6 * 2**20, transcendentals=10**6),
        name="chain",
    )(me, cot, square, *pq, *owns, *mats)


def share_kernel(me_ref, packed, t0, t1, t2, t3, rows_own, rows_prev, out):
    me = me_ref[0]
    r = rows_own.shape[2]
    h = (packed.shape[1] - 2 * r) // 2
    w = packed[:, 0:h]
    act = packed[:, h : 2 * h]
    arrived = packed[:, 2 * h : 2 * h + r]
    coef = packed[:, 2 * h + r :]
    v = dot_tn(act, arrived)
    u = dot_tn(w, coef)
    vh, uh = v.astype(BF16), u.astype(BF16)
    vl = (v - vh.astype(F32)).astype(BF16)
    wt = w.astype(F32).T.astype(BF16)
    for k, piece in enumerate((t0, t1, t2, t3)):
        c = k ^ me
        xs = (dot_nn(wt, piece[...]) + dot_nt(uh, rows_prev[c])).astype(BF16)
        own = rows_own[c]
        os = (dot_nt(vh, own) + dot_nt(vl, own)).astype(BF16)
        n = xs.shape[1] // 2
        for e in range(2):
            out[2 * c + e, 0:h, :] = xs[:, e * n : (e + 1) * n]
            out[2 * c + e, h:, :] = os[:, e * n : (e + 1) * n]


def share(me, packed, pieces, rows_own, rows_prev):
    h = (packed.shape[1] - 2 * rows_own.shape[2]) // 2
    cs, n, _ = rows_own.shape
    vmem = pl.BlockSpec(memory_space=pltpu.VMEM)
    return pl.pallas_call(
        share_kernel,
        in_specs=[pl.BlockSpec(memory_space=pltpu.SMEM)] + [vmem] * 7,
        out_specs=vmem,
        out_shape=jax.ShapeDtypeStruct((2 * cs, 2 * h, n // 2), BF16),
        compiler_params=pltpu.CompilerParams(vmem_limit_bytes=32 * 2**20),
        cost_estimate=pl.CostEstimate(flops=2 * 10**9, bytes_accessed=6 * 2**20, transcendentals=0),
        name="share",
    )(me, packed, *pieces, rows_own, rows_prev)


def per_device(
    token_ids, embed_table, subspace, adapter_in, adapter_out, norm_gain, coef_cotangent
):
    tokens = token_ids.shape[0]
    zl, x = lax.axis_index(ZL), lax.axis_index(X)
    shards = lax.axis_size(DP)
    group = lax.axis_size(GATHER)
    section = lax.axis_index(SEC)
    me = jnp.reshape(section, (1,)).astype(jnp.int32)
    dp = lax.axis_index(DP)
    vocab, cols = embed_table.shape
    basis, weight_in, weight_out, gain = subspace[0], adapter_in[0], adapter_out[0], norm_gain[0]
    d, r = basis.shape
    h = weight_in.shape[1]
    block = d // shards

    rows_x = lax.dynamic_index_in_dim(basis.reshape(8, 4, 2 * block, r), x, 1, False)
    prev_x = lax.ppermute(rows_x, SEC, [(0, 1), (1, 2), (2, 3)])

    owner = token_ids // vocab
    local_row = token_ids - owner * vocab
    matches = (owner[:, None] == jnp.arange(shards, dtype=jnp.int32)[None, :]).astype(jnp.int32)
    position = jnp.sum(jnp.cumsum(matches, axis=0) * matches, axis=1) - 1
    place = owner * CAP + position
    requests = jnp.zeros((shards * CAP,), jnp.int32).at[place].set(local_row).reshape(shards, CAP)
    asked = lax.all_to_all(requests, DP, split_axis=0, concat_axis=0, tiled=True)
    found = pick_rows(asked.reshape(1, shards * CAP), embed_table, prev_x)
    answered = lax.all_to_all(
        found.reshape(shards, CAP, cols), DP, split_axis=0, concat_axis=0, tiled=True
    )

    gained = (gain[:, None] * weight_in.astype(F32)).astype(BF16)
    owns = gather_peers(own_products(basis, weight_out))
    crossed = sum_over_x(cross_products(jnp.reshape(x, (1,)), basis, prev_x, gained)).astype(BF16)
    rows_own = lax.dynamic_index_in_dim(rows_x.reshape(4, 2, 2 * block, r), zl, 1, False)
    rows_prev = lax.dynamic_index_in_dim(prev_x.reshape(4, 2, 2 * block, r), zl, 1, False)

    part, turned = place_rows(
        place.reshape(1, tokens),
        answered.reshape(shards * CAP, cols),
        group,
        (*owns, crossed, rows_own, rows_prev, gained),
    )
    pieces = gather_peers(part)
    turned = lax.all_to_all(turned, GATHER, split_axis=0, concat_axis=0, tiled=True)
    pq, square = project(me, pieces, basis, gained, turned)
    pqs = gather_peers(pq)
    mats = gather_peers(crossed)
    turned = gather_peers(turned.reshape(group * tokens, cols // group))

    sent, packed = chain(me, coef_cotangent, square, pqs, owns, mats, d, group)
    packed = lax.all_to_all(packed, GATHER, split_axis=0, concat_axis=0, tiled=True)
    packed = packed.reshape(group * tokens, 2 * h + 2 * r)
    shares = share(me, packed, turned, rows_own, rows_prev)
    shares = lax.all_to_all(shares, REDUCE, split_axis=0, concat_axis=0, tiled=True)
    total = jnp.sum(shares.astype(F32), axis=0)
    plain = total[0:h].T
    gain_block = lax.dynamic_slice_in_dim(gain, dp * block, block, 0)
    in_block = lax.dynamic_slice_in_dim(weight_in, dp * block, block, 0)
    grad_in = gain_block[:, None] * plain
    grad_gain = jnp.sum(in_block.astype(F32) * plain, axis=1)
    return sent[None], grad_in[None], total[h:][None], grad_gain[None]


def solution(mesh):
    fine = Mesh(mesh.devices.reshape(2, 2, 4, 2, 4, 2), (YL, CO, ZH, ZL, X, YH))
    return jax.shard_map(
        per_device,
        mesh=fine,
        in_specs=(
            P(DP),
            P(DP, SEC),
            P(SEC, None, None),
            P(SEC, None, None),
            P(SEC, None, None),
            P(SEC, None),
            P(DP, None),
        ),
        out_specs=(
            P(SEC, DP, None),
            P(SEC, DP, None),
            P(SEC, None, DP),
            P(SEC, DP),
        ),
        check_vma=False,
    )
```

time: 224 us -> 180 us (0.80); the launches traced: 220 us -> 179 us
  waiting for transfers between devices: 119 us -> 67.3 us
  local copies, waits for them, and re-layouts: 13 us -> 20.3 us
  starting transfers between devices: 35.3 us -> 40.6 us
  matrix products: 3.82 us -> 0 us
    all_to_all x4, waiting for transfers between devices: 43.2 us -> 22.3 us  [the longest x1 17.7 us: per_device(): lax.all_to_all(shares, REDUCE, split_axis=0, concat_axis=0, tiled=True)]
    ppermute x12 -> x15, waiting for transfers between devices: 42 us -> 26.8 us  [swap(): return lax.ppermute(x, axis, [(0, 1), (1, 0)])]
    ppermute x1 -> x3, waiting for transfers between devices: 33.5 us -> 18.3 us  [the longest x1 13.3 us: sum_over_x(): v = v + lax.ppermute(v, X, [(0, 1), (1, 0), (2, 3), (3, 2)])]
    unnamed x12 -> x31, local copies, waits for them, and re-layouts: 4.02 us -> 9.61 us
    dot_general x2 -> x0, matrix products: 3.82 us -> none  [dot_nn(): lax.dot_general(a, b, (((1,), (0,)), ((), ())), preferred_element_type=F32)]
    ppermute x1 -> x3, starting transfers between devices: 4.58 us -> 7.31 us  [the longest x1 3.77 us: per_device(): prev_x = lax.ppermute(rows_x, SEC, [(0, 1), (1, 2), (2, 3)])]
    ppermute x12 -> x15, starting transfers between devices: 9.81 us -> 11.4 us  [swap(): return lax.ppermute(x, axis, [(0, 1), (1, 0)])]
    pallas_call x1 -> x4, Pallas kernels: 7.59 us -> 8.89 us  [the longest x1 2.96 us: pick_rows(): pl.pallas_call(pick_kernel, grid=(steps,), in_specs=[full(asked.shape), p...]
  transfers between devices with their start and end apart: 17 -> 22, of which waited for: 7 -> 10; matrix products, arithmetic and copies ran while one was open for 4% -> 7% of each run, Pallas kernels for 7% -> 4%
where the time goes in v2:
time: 180 us; the launch traced here: 179 us
  waiting for transfers between devices  67.3 us (37%)
  starting transfers between devices  40.6 us (23%)
  blocking collectives  23.5 us (13%)
  local copies, waits for them, and re-layouts  20.3 us (11%)
  Pallas kernels  19.3 us (11%)
  other arithmetic  7.09 us (4%)
    ppermute x15, waiting for transfers between devices, swap(): return lax.ppermute(x, axis, [(0, 1), (1, 0)])  26.8 us
    all_to_all x1, blocking collectives, per_device(): lax.all_to_all(requests, DP, split_axis=0, concat_axis=0, tiled=True)  23.5 us
    all_to_all x1, waiting for transfers between devices, per_device(): lax.all_to_all(shares, REDUCE, split_axis=0, concat_axis=0, tiled=True)  17.7 us
    ppermute x1, waiting for transfers between devices, sum_over_x(): v = v + lax.ppermute(v, X, [(0, 1), (1, 0), (2, 3), (3, 2)])  13.3 us
    ppermute x15, starting transfers between devices, swap(): return lax.ppermute(x, axis, [(0, 1), (1, 0)])  11.4 us
    unnamed x31, local copies, waits for them, and re-layouts  9.61 us
    all_to_all x1, starting transfers between devices, per_device(): lax.all_to_all(shares, REDUCE, split_axis=0, concat_axis=0, tiled=True)  7.36 us
    all_to_all x1, starting transfers between devices, per_device(): lax.all_to_all(found.reshape(shards, CAP, cols), DP, split_axis=0, concat...  5.97 us
  transfers between devices with their start and end apart: 22, of which 10 were waited for; matrix products, arithmetic and copies ran while one was open for 7% of the time, Pallas kernels for 4%

profile of v2, /device:TPU:33, one launch (start us, length us, event | category | flops | bytes accessed | tf_op | source)
XLA Modules:
  0.0 179.0 jit_solution(14983006872017862602)
XLA Ops:
  0.6 1.3 fusion.8
  1.9 3.8 %collective-permute-start = (bf16[8,256,256]{2,1,0:T(8,128)(2,1)S(1)}, bf16[8,256,256]{2,1,0:T(8,128)(2,1)S(1)}, u32[]{:S(2)}, u32[]{:S(2)}) collective-permute-start(bf16[8,256,256]{2,1,0:T(8,128)(2,1)S(1)} %fusion.8), channel_id=1, source_target_pairs={{0,64},{64,128},{128,192},{1,65},{65,129},{129,193},{2,66},{66,130... | collective-permute-start | bytes 3145736 | tf_op jit(solution)/shard_map/ppermute | solution.py:382
  5.8 0.2 reduce_window_sum.11
  6.0 0.2 select_reduce_fusion
  6.2 1.0 scatter_custom_fusion
  7.2 0.1 all_to_all.18
  7.3 23.5 %all_to_all.29 = s32[64,1,4]{2,1,0:T(1,128)S(1)} all-to-all(s32[64,1,4]{2,1,0:T(1,128)S(1)} %bitcast.51), channel_id=1, replica_groups=mesh['yl'=2,'co'=2,'zh'=4,'zl'=2,'x'=4,'yh'=2] {'zh','zl','x','yh'}, dimensions={0} | all-to-all | bytes 2048 | tf_op jit(solution)/shard_map/all_to_all | solution.py:390
  30.8 0.5 broadcast.20
  31.3 0.7 reduce.3
  32.0 0.1 reshape.56.asked
  32.2 2.2 %copy-done.2 = bf16[1008,2048]{1,0:T(8,128)(2,1)S(1)} copy-done((bf16[1008,2048]{1,0:T(8,128)(2,1)S(1)}, bf16[1008,2048]{1,0:T(8,128)(2,1)}, u32[]{:S(2)}) %copy-start.2) | copy-done | bytes 4128792
  34.3 3.0 %pick_rows.1 = bf16[256,2048]{1,0:T(8,128)(2,1)S(1)} custom-call(s32[1,256]{1,0:T(1,128)S(1)} %reshape.56.asked, bf16[1008,2048]{1,0:T(8,128)(2,1)S(1)} %copy-done.2, bf16[8,256,256]{2,1,0:T(8,128)(2,1)S(1)} %collective-permute-done.first.prev), custom_call_target="tpu_custom_call" | custom-call | flops 1056964608 | bytes 5177344 | tf_op jit(solution)/shard_map/pick_rows/pallas_call | solution.py:144
  37.3 1.2 reshape.57
  38.5 6.0 %all-to-all-start.1 = ((bf16[64,4,2048]{2,1,0:T(4,128)(2,1)}), bf16[64,4,2048]{2,1,0:T(4,128)(2,1)}, u32[]{:S(2)}, u32[]{:S(2)}) async-start(bf16[64,4,2048]{2,1,0:T(4,128)(2,1)} %reshape.57), calls=%async_computation.1 | async-start | bytes 2097152 | tf_op jit(solution)/shard_map/all_to_all | solution.py:392
  44.5 2.6 %fusion.gained.refs_7_ = bf16[8192,128]{1,0:T(8,128)(2,1)S(1)} fusion(bf16[1,8192,128]{2,1,0:T(8,128)(2,1)} %param.10, f32[8192]{0:T(1024)S(1)} %bitcast.53), kind=kLoop, calls=%fused_computation.2 | loop fusion | flops 3145728 | bytes 4227072 | tf_op jit(solution)/shard_map/convert_element_type | solution.py:396
  47.2 0.2 copy-done
  47.3 2.0 %cross_products.1 = f32[384,256]{1,0:T(8,128)S(1)} custom-call(s32[1]{0:T(128)} %bitcast.7.at, bf16[8192,256]{1,0:T(8,128)(2,1)S(1)} %bitcast.42, bf16[8,256,256]{2,1,0:T(8,128)(2,1)S(1)} %collective-permute-done.first.prev, bf16[8192,128]{1,0:T(8,128)(2,1)S(1)} %fusion.gained.refs_7_), custom_call_target="tpu_custom_call" | custom-call | flops 402653184 | bytes 2621440 | tf_op jit(solution)/shard_map/cross_products/pallas_call | solution.py:101
  49.4 1.3 collective-permute-start.4
  50.7 2.7 %own_products.1.refs_0_.refs_7_ = bf16[640,256]{1,0:T(8,128)(2,1)S(1)} custom-call(bf16[8192,256]{1,0:T(8,128)(2,1)S(1)} %bitcast.43, bf16[128,8192]{1,0:T(8,128)(2,1)S(1)} %bitcast.46), custom_call_target="tpu_custom_call" | custom-call | flops 1610612736 | bytes 6291456 | tf_op jit(solution)/shard_map/own_products/pallas_call | solution.py:68
  53.3 0.1 collective-permute-start.2
  53.4 13.3 %collective-permute-done.4 = f32[384,256]{1,0:T(8,128)S(1)} collective-permute-done((f32[384,256]{1,0:T(8,128)S(1)}, f32[384,256]{1,0:T(8,128)S(1)}, u32[]{:S(2)}, u32[]{:S(2)}) %collective-permute-start.4) | collective-permute-done | bytes 393248 | tf_op jit(solution)/shard_map/ppermute | solution.py:125
  66.7 0.8 add.47
  67.5 2.3 %collective-permute-start.5 = (f32[384,256]{1,0:T(8,128)}, f32[384,256]{1,0:T(8,128)}, u32[]{:S(2)}, u32[]{:S(2)}) collective-permute-start(f32[384,256]{1,0:T(8,128)} %add.47), channel_id=1, source_target_pairs={{0,6},{6,0},{2,4},{4,2},{1,7},{7,1},{3,5},{5,3},{8,14},{14,8},{10,... | collective-permute-start | bytes 1179656 | tf_op jit(solution)/shard_map/ppermute | solution.py:126
  69.8 1.6 collective-permute-start.1
  71.3 1.3 constant_dynamic-slice_fusion.2
  72.6 0.9 dynamic-slice_bitcast_fusion.1.refs_5_.rows_own
  73.5 0.8 dynamic-slice_bitcast_fusion.refs_6_.rows_prev
  74.4 5.0 %collective-permute-done.5 = f32[384,256]{1,0:T(8,128)} collective-permute-done((f32[384,256]{1,0:T(8,128)}, f32[384,256]{1,0:T(8,128)}, u32[]{:S(2)}, u32[]{:S(2)}) %collective-permute-start.5) | collective-permute-done | bytes 393248 | tf_op jit(solution)/shard_map/ppermute | solution.py:126
  79.4 1.8 %add_convert_fusion.refs_4_.refs_11_ = bf16[384,256]{1,0:T(8,128)(2,1)} fusion(f32[384,256]{1,0:T(8,128)} %add.47, f32[384,256]{1,0:T(8,128)} %collective-permute-done.5), kind=kLoop, calls=%fused_computation.6 | loop fusion | flops 196608 | bytes 983040 | tf_op jit(solution)/shard_map/convert_element_type | solution.py:398
  81.2 1.3 reshape.58.answered
  82.6 1.0 copy-done.4
  83.6 1.0 copy-done.6
  84.7 0.9 copy-done.9
  85.6 1.2 place_rows.1
  86.8 0.8 copy-done.11
  87.6 4.1 %all-to-all-start.2 = ((bf16[8,128,256]{2,1,0:T(8,128)(2,1)}), bf16[8,128,256]{2,1,0:T(8,128)(2,1)S(1)}, u32[]{:S(2)}, u32[]{:S(2)}) async-start(bf16[8,128,256]{2,1,0:T(8,128)(2,1)} %copy-done.11), calls=%async_computation.2 | async-start | bytes 1048576 | tf_op jit(solution)/shard_map/all_to_all | solution.py:409
  91.7 2.6 %collective-permute-start.6 = (bf16[128,2048]{1,0:T(8,128)(2,1)}, bf16[128,2048]{1,0:T(8,128)(2,1)}, u32[]{:S(2)}, u32[]{:S(2)}) collective-permute-start(bf16[128,2048]{1,0:T(8,128)(2,1)} %get-tuple-element.10.p0), channel_id=1, source_target_pairs={{0,64},{64,0},{1,65},{65,1},{2,66},{66,2},{3,67},{67,3},{4,68},{68... | collective-permute-start | bytes 1572872 | tf_op jit(solution)/shard_map/ppermute | solution.py:31
  94.3 5.6 %collective-permute-done.7.p2 = bf16[128,2048]{1,0:T(8,128)(2,1)S(1)} collective-permute-done((bf16[128,2048]{1,0:T(8,128)(2,1)}, bf16[128,2048]{1,0:T(8,128)(2,1)S(1)}, u32[]{:S(2)}, u32[]{:S(2)}) %collective-permute-start.7) | collective-permute-done | bytes 524320 | tf_op jit(solution)/shard_map/ppermute | solution.py:31
  99.9 2.3 %collective-permute-start.8 = (bf16[128,2048]{1,0:T(8,128)(2,1)S(1)}, bf16[128,2048]{1,0:T(8,128)(2,1)}, u32[]{:S(2)}, u32[]{:S(2)}) collective-permute-start(bf16[128,2048]{1,0:T(8,128)(2,1)S(1)} %collective-permute-done.7.p2), channel_id=1, source_target_pairs={{0,64},{64,0},{1,65},{65,1},{2,66},{66,2},{3,67},{67,3},{4,68},{68... | collective-permute-start | bytes 1572872 | tf_op jit(solution)/shard_map/ppermute | solution.py:31
  102.2 1.7 collective-permute-done.8.p3
  103.8 2.2 %copy-done.1 = bf16[1,8192,256]{2,1,0:T(8,128)(2,1)S(1)} copy-done((bf16[1,8192,256]{2,1,0:T(8,128)(2,1)S(1)}, bf16[1,8192,256]{2,1,0:T(8,128)(2,1)}, u32[]{:S(2)}) %copy-start.1) | copy-done | bytes 4194328
  106.0 3.2 %project.1 = (f32[128,384]{1,0:T(8,128)S(1)}, f32[128,128]{1,0:T(8,128)S(1)}) custom-call(s32[1]{0:T(128)} %bitcast.me.refs_0_.me_ref, bf16[128,2048]{1,0:T(8,128)(2,1)} %get-tuple-element.10.p0, bf16[128,2048]{1,0:T(8,128)(2,1)} %collective-permute-done.6.p1, bf16[128,2048]{1,0:T(8,128)(2,1)S(1)} %collective-permute-done.7.p2, ...), custom_call_target="tpu_custom_call" | custom-call | flops 805306368 | bytes 8388608 | tf_op jit(solution)/shard_map/project/pallas_call | solution.py:218
  109.3 0.1 collective-permute-start.10
  109.4 0.6 collective-permute-start.12
  110.1 0.4 collective-permute-start.9
  110.6 4.9 %collective-permute-done.10.refs_5_ = f32[128,384]{1,0:T(8,128)S(1)} collective-permute-done((f32[128,384]{1,0:T(8,128)S(1)}, f32[128,384]{1,0:T(8,128)S(1)}, u32[]{:S(2)}, u32[]{:S(2)}) %collective-permute-start.10) | collective-permute-done | bytes 196640 | tf_op jit(solution)/shard_map/ppermute | solution.py:31
  115.5 1.2 collective-permute-start.11
  116.7 1.1 collective-permute-done.11.refs_6_
  117.8 3.8 %chain.1 = (bf16[128,256]{1,0:T(8,128)(2,1)}, bf16[8,128,768]{2,1,0:T(8,128)(2,1)S(1)}) custom-call(s32[1]{0:T(128)} %bitcast.me.refs_0_.me_ref, bf16[128,256]{1,0:T(8,128)(2,1)S(1)} %copy-done.12, f32[128,128]{1,0:T(8,128)S(1)} %get-tuple-element.12.refs_2_, f32[128,384]{1,0:T(8,128)S(1)} %get-tuple-element.13.refs_3_, ...), custom_call_target="tpu_custom_call" | custom-call | flops 4000000000 | bytes 6291456 | tf_op jit(solution)/shard_map/chain/pallas_call | solution.py:300
  121.6 1.1 copy-done.8
  122.7 4.5 %all-to-all-start.3 = ((bf16[8,128,768]{2,1,0:T(8,128)(2,1)}), bf16[8,128,768]{2,1,0:T(8,128)(2,1)}, u32[]{:S(2)}, u32[]{:S(2)}) async-start(bf16[8,128,768]{2,1,0:T(8,128)(2,1)} %copy-done.8), calls=%async_computation.3 | async-start | bytes 3145728 | tf_op jit(solution)/shard_map/all_to_all | solution.py:416
  127.3 0.9 collective-permute-start.15
  128.2 12.0 %collective-permute-done.16.t2 = bf16[1024,256]{1,0:T(8,128)(2,1)S(1)} collective-permute-done((bf16[1024,256]{1,0:T(8,128)(2,1)S(1)}, bf16[1024,256]{1,0:T(8,128)(2,1)S(1)}, u32[]{:S(2)}, u32[]{:S(2)}) %collective-permute-start.16) | collective-permute-done | bytes 524320 | tf_op jit(solution)/shard_map/ppermute | solution.py:31
  140.2 1.4 collective-permute-start.17
  141.6 1.5 collective-permute-done.17.t3
  143.1 4.6 %all-to-all-done.3 = bf16[8,128,768]{2,1,0:T(8,128)(2,1)} async-done(((bf16[8,128,768]{2,1,0:T(8,128)(2,1)}), bf16[8,128,768]{2,1,0:T(8,128)(2,1)}, u32[]{:S(2)}, u32[]{:S(2)}) %all-to-all-start.3) | async-done | bytes 1572896 | tf_op jit(solution)/shard_map/all_to_all | solution.py:416
  147.7 3.3 %share.1 = bf16[8,256,128]{2,1,0:T(8,128)(2,1)} custom-call(s32[1]{0:T(128)} %bitcast.me.refs_0_.me_ref, bf16[1024,768]{1,0:T(8,128)(2,1)} %bitcast.16.packed, bf16[1024,256]{1,0:T(8,128)(2,1)S(1)} %bitcast.49, bf16[1024,256]{1,0:T(8,128)(2,1)S(1)} %collective-permute-done.15.t1, bf16[1024,256]{1,0:T(8,128)(2,1)S(1)} %collective-permute-done.16.t2, ...), custom_call_target="tpu_custom_call" | custom-call | flops 2000000000 | bytes 6291456 | tf_op jit(solution)/shard_map/share/pallas_call | solution.py:354
  151.1 7.4 %all-to-all-start.4 = ((bf16[8,256,128]{2,1,0:T(8,128)(2,1)}), bf16[8,256,128]{2,1,0:T(8,128)(2,1)S(1)}, u32[]{:S(2)}, u32[]{:S(2)}) async-start(bf16[8,256,128]{2,1,0:T(8,128)(2,1)} %share.1), calls=%async_computation.4 | async-start | bytes 1048576 | tf_op jit(solution)/shard_map/all_to_all | solution.py:419
  158.4 0.8 constant_dynamic-slice_fusion
  159.2 0.1 copy.23
  159.3 17.7 %all-to-all-done.4 = bf16[8,256,128]{2,1,0:T(8,128)(2,1)S(1)} async-done(((bf16[8,256,128]{2,1,0:T(8,128)(2,1)}), bf16[8,256,128]{2,1,0:T(8,128)(2,1)S(1)}, u32[]{:S(2)}, u32[]{:S(2)}) %all-to-all-start.4) | async-done | bytes 524320 | tf_op jit(solution)/shard_map/all_to_all | solution.py:419
  177.1 0.6 slice_bitcast_fusion
  177.7 0.5 fusion.1
  178.2 0.7 copy.20
  (44 shorter events, 0.4 us)
Async XLA Ops:
  0.6 5.1 %copy-start.14 = (s32[128]{0:T(128)S(1)}, s32[128]{0:T(128)}, u32[]{:S(2)}) copy-start(s32[128]{0:T(128)} %param.7) | copy-start | bytes 1540
  1.9 30.2 %collective-permute-start = (bf16[8,256,256]{2,1,0:T(8,128)(2,1)S(1)}, bf16[8,256,256]{2,1,0:T(8,128)(2,1)S(1)}, u32[]{:S(2)}, u32[]{:S(2)}) collective-permute-start(bf16[8,256,256]{2,1,0:T(8,128)(2,1)S(1)} %fusion.8), channel_id=1, source_target_pairs={{0,64},{64,128},{128,192},{1,65},{65,129},{129,193},{2,66},{66,130... | collective-permute-start | bytes 3145736 | tf_op jit(solution)/shard_map/ppermute | solution.py:382
  32.1 2.2 %copy-start.2 = (bf16[1008,2048]{1,0:T(8,128)(2,1)S(1)}, bf16[1008,2048]{1,0:T(8,128)(2,1)}, u32[]{:S(2)}) copy-start(bf16[1008,2048]{1,0:T(8,128)(2,1)} %table.1) | copy-start | bytes 12386308
  37.3 7.2 %copy-start.13 = (f32[1,8192]{1,0:T(1,128)S(1)}, f32[1,8192]{1,0:T(1,128)}, u32[]{:S(2)}) copy-start(f32[1,8192]{1,0:T(1,128)} %param.12) | copy-start | bytes 98308
  38.5 42.7 %all-to-all-start.1 = ((bf16[64,4,2048]{2,1,0:T(4,128)(2,1)}), bf16[64,4,2048]{2,1,0:T(4,128)(2,1)}, u32[]{:S(2)}, u32[]{:S(2)}) async-start(bf16[64,4,2048]{2,1,0:T(4,128)(2,1)} %reshape.57), calls=%async_computation.1 | async-start | bytes 2097152 | tf_op jit(solution)/shard_map/all_to_all | solution.py:392
  44.5 2.8 %copy-start = (bf16[1,8192,256]{2,1,0:T(8,128)(2,1)S(1)}, bf16[1,8192,256]{2,1,0:T(8,128)(2,1)}, u32[]{:S(2)}) copy-start(bf16[1,8192,256]{2,1,0:T(8,128)(2,1)} %param.9) | copy-start | bytes 12582916
  47.3 3.3 %copy-start.3 = (bf16[1,128,8192]{2,1,0:T(8,128)(2,1)S(1)}, bf16[1,128,8192]{2,1,0:T(8,128)(2,1)}, u32[]{:S(2)}) copy-start(bf16[1,128,8192]{2,1,0:T(8,128)(2,1)} %param.11) | copy-start | bytes 6291460
  49.4 17.3 %collective-permute-start.4 = (f32[384,256]{1,0:T(8,128)S(1)}, f32[384,256]{1,0:T(8,128)S(1)}, u32[]{:S(2)}, u32[]{:S(2)}) collective-permute-start(f32[384,256]{1,0:T(8,128)S(1)} %cross_products.1), channel_id=1, source_target_pairs={{0,2},{2,0},{4,6},{6,4},{1,3},{3,1},{5,7},{7,5},{8,10},{10,8},{12,... | collective-permute-start | bytes 1179656 | tf_op jit(solution)/shard_map/ppermute | solution.py:125
  53.3 20.2 %collective-permute-start.2 = (bf16[640,256]{1,0:T(8,128)(2,1)S(1)}, bf16[640,256]{1,0:T(8,128)(2,1)}, u32[]{:S(2)}, u32[]{:S(2)}) collective-permute-start(bf16[640,256]{1,0:T(8,128)(2,1)S(1)} %own_products.1.refs_0_.refs_7_), channel_id=1, source_target_pairs={{0,128},{128,0},{1,129},{129,1},{2,130},{130,2},{3,131},{131,3},{4... | collective-permute-start | bytes 983048 | tf_op jit(solution)/shard_map/ppermute | solution.py:31
  67.5 11.8 %collective-permute-start.5 = (f32[384,256]{1,0:T(8,128)}, f32[384,256]{1,0:T(8,128)}, u32[]{:S(2)}, u32[]{:S(2)}) collective-permute-start(f32[384,256]{1,0:T(8,128)} %add.47), channel_id=1, source_target_pairs={{0,6},{6,0},{2,4},{4,2},{1,7},{7,1},{3,5},{5,3},{8,14},{14,8},{10,... | collective-permute-start | bytes 1179656 | tf_op jit(solution)/shard_map/ppermute | solution.py:126
  69.8 12.8 %collective-permute-start.1 = (bf16[640,256]{1,0:T(8,128)(2,1)S(1)}, bf16[640,256]{1,0:T(8,128)(2,1)}, u32[]{:S(2)}, u32[]{:S(2)}) collective-permute-start(bf16[640,256]{1,0:T(8,128)(2,1)S(1)} %own_products.1.refs_0_.refs_7_), channel_id=1, source_target_pairs={{0,64},{64,0},{1,65},{65,1},{2,66},{66,2},{3,67},{67,3},{4,68},{68... | collective-permute-start | bytes 983048 | tf_op jit(solution)/shard_map/ppermute | solution.py:31
  73.5 9.1 %collective-permute-start.3 = (bf16[640,256]{1,0:T(8,128)(2,1)}, bf16[640,256]{1,0:T(8,128)(2,1)}, u32[]{:S(2)}, u32[]{:S(2)}) collective-permute-start(bf16[640,256]{1,0:T(8,128)(2,1)} %collective-permute-done.2.refs_2_.refs_9_), channel_id=1, source_target_pairs={{0,64},{64,0},{1,65},{65,1},{2,66},{66,2},{3,67},{67,3},{4,68},{68... | collective-permute-start | bytes 983048 | tf_op jit(solution)/shard_map/ppermute | solution.py:31
  82.6 1.0 copy-start.4
  83.6 1.0 copy-start.6
  84.7 0.9 copy-start.9
  86.8 0.8 copy-start.11
  87.6 12.2 %collective-permute-start.7 = (bf16[128,2048]{1,0:T(8,128)(2,1)}, bf16[128,2048]{1,0:T(8,128)(2,1)S(1)}, u32[]{:S(2)}, u32[]{:S(2)}) collective-permute-start(bf16[128,2048]{1,0:T(8,128)(2,1)} %get-tuple-element.10.p0), channel_id=1, source_target_pairs={{0,128},{128,0},{1,129},{129,1},{2,130},{130,2},{3,131},{131,3},{4... | collective-permute-start | bytes 1572872 | tf_op jit(solution)/shard_map/ppermute | solution.py:31
  87.6 14.6 %all-to-all-start.2 = ((bf16[8,128,256]{2,1,0:T(8,128)(2,1)}), bf16[8,128,256]{2,1,0:T(8,128)(2,1)S(1)}, u32[]{:S(2)}, u32[]{:S(2)}) async-start(bf16[8,128,256]{2,1,0:T(8,128)(2,1)} %copy-done.11), calls=%async_computation.2 | async-start | bytes 1048576 | tf_op jit(solution)/shard_map/all_to_all | solution.py:409
  91.7 10.5 %collective-permute-start.6 = (bf16[128,2048]{1,0:T(8,128)(2,1)}, bf16[128,2048]{1,0:T(8,128)(2,1)}, u32[]{:S(2)}, u32[]{:S(2)}) collective-permute-start(bf16[128,2048]{1,0:T(8,128)(2,1)} %get-tuple-element.10.p0), channel_id=1, source_target_pairs={{0,64},{64,0},{1,65},{65,1},{2,66},{66,2},{3,67},{67,3},{4,68},{68... | collective-permute-start | bytes 1572872 | tf_op jit(solution)/shard_map/ppermute | solution.py:31
  99.9 4.0 %collective-permute-start.8 = (bf16[128,2048]{1,0:T(8,128)(2,1)S(1)}, bf16[128,2048]{1,0:T(8,128)(2,1)}, u32[]{:S(2)}, u32[]{:S(2)}) collective-permute-start(bf16[128,2048]{1,0:T(8,128)(2,1)S(1)} %collective-permute-done.7.p2), channel_id=1, source_target_pairs={{0,64},{64,0},{1,65},{65,1},{2,66},{66,2},{3,67},{67,3},{4,68},{68... | collective-permute-start | bytes 1572872 | tf_op jit(solution)/shard_map/ppermute | solution.py:31
  102.2 7.9 %collective-permute-start.13 = (bf16[384,256]{1,0:T(8,128)(2,1)}, bf16[384,256]{1,0:T(8,128)(2,1)}, u32[]{:S(2)}, u32[]{:S(2)}) collective-permute-start(bf16[384,256]{1,0:T(8,128)(2,1)} %add_convert_fusion.refs_4_.refs_11_), channel_id=1, source_target_pairs={{0,128},{128,0},{1,129},{129,1},{2,130},{130,2},{3,131},{131,3},{4... | collective-permute-start | bytes 589832 | tf_op jit(solution)/shard_map/ppermute | solution.py:31
  103.8 2.2 %copy-start.1 = (bf16[1,8192,256]{2,1,0:T(8,128)(2,1)S(1)}, bf16[1,8192,256]{2,1,0:T(8,128)(2,1)}, u32[]{:S(2)}) copy-start(bf16[1,8192,256]{2,1,0:T(8,128)(2,1)} %param.9) | copy-start | bytes 12582916
  106.0 3.4 %copy-start.10 = (bf16[384,256]{1,0:T(8,128)(2,1)S(1)}, bf16[384,256]{1,0:T(8,128)(2,1)}, u32[]{:S(2)}) copy-start(bf16[384,256]{1,0:T(8,128)(2,1)} %add_convert_fusion.refs_4_.refs_11_) | copy-start | bytes 589828
  106.0 11.7 %copy-start.12 = (bf16[128,256]{1,0:T(8,128)(2,1)S(1)}, bf16[128,256]{1,0:T(8,128)(2,1)}, u32[]{:S(2)}) copy-start(bf16[128,256]{1,0:T(8,128)(2,1)} %refs_1_.1) | copy-start | bytes 196612
  109.3 6.2 %collective-permute-start.10 = (f32[128,384]{1,0:T(8,128)S(1)}, f32[128,384]{1,0:T(8,128)S(1)}, u32[]{:S(2)}, u32[]{:S(2)}) collective-permute-start(f32[128,384]{1,0:T(8,128)S(1)} %get-tuple-element.13.refs_3_), channel_id=1, source_target_pairs={{0,128},{128,0},{1,129},{129,1},{2,130},{130,2},{3,131},{131,3},{4... | collective-permute-start | bytes 589832 | tf_op jit(solution)/shard_map/ppermute | solution.py:31
  109.4 7.3 %collective-permute-start.12 = (bf16[384,256]{1,0:T(8,128)(2,1)S(1)}, bf16[384,256]{1,0:T(8,128)(2,1)S(1)}, u32[]{:S(2)}, u32[]{:S(2)}) collective-permute-start(bf16[384,256]{1,0:T(8,128)(2,1)S(1)} %copy-done.10), channel_id=1, source_target_pairs={{0,64},{64,0},{1,65},{65,1},{2,66},{66,2},{3,67},{67,3},{4,68},{68... | collective-permute-start | bytes 589832 | tf_op jit(solution)/shard_map/ppermute | solution.py:31
  110.0 6.7 %collective-permute-start.14 = (bf16[384,256]{1,0:T(8,128)(2,1)}, bf16[384,256]{1,0:T(8,128)(2,1)S(1)}, u32[]{:S(2)}, u32[]{:S(2)}) collective-permute-start(bf16[384,256]{1,0:T(8,128)(2,1)} %collective-permute-done.13.refs_13_), channel_id=1, source_target_pairs={{0,64},{64,0},{1,65},{65,1},{2,66},{66,2},{3,67},{67,3},{4,68},{68... | collective-permute-start | bytes 589832 | tf_op jit(solution)/shard_map/ppermute | solution.py:31
  110.1 6.6 %collective-permute-start.9 = (f32[128,384]{1,0:T(8,128)S(1)}, f32[128,384]{1,0:T(8,128)S(1)}, u32[]{:S(2)}, u32[]{:S(2)}) collective-permute-start(f32[128,384]{1,0:T(8,128)S(1)} %get-tuple-element.13.refs_3_), channel_id=1, source_target_pairs={{0,64},{64,0},{1,65},{65,1},{2,66},{66,2},{3,67},{67,3},{4,68},{68... | collective-permute-start | bytes 589832 | tf_op jit(solution)/shard_map/ppermute | solution.py:31
  115.5 2.3 %collective-permute-start.11 = (f32[128,384]{1,0:T(8,128)S(1)}, f32[128,384]{1,0:T(8,128)S(1)}, u32[]{:S(2)}, u32[]{:S(2)}) collective-permute-start(f32[128,384]{1,0:T(8,128)S(1)} %collective-permute-done.10.refs_5_), channel_id=1, source_target_pairs={{0,64},{64,0},{1,65},{65,1},{2,66},{66,2},{3,67},{67,3},{4,68},{68... | collective-permute-start | bytes 589832 | tf_op jit(solution)/shard_map/ppermute | solution.py:31
  121.6 1.1 copy-start.8
  122.7 25.0 %copy-start.5 = (bf16[4,256,256]{2,1,0:T(8,128)(2,1)S(1)}, bf16[4,256,256]{2,1,0:T(8,128)(2,1)}, u32[]{:S(2)}) copy-start(bf16[4,256,256]{2,1,0:T(8,128)(2,1)} %dynamic-slice_bitcast_fusion.1.refs_5_.rows_own) | copy-start | bytes 1572868
  122.7 25.0 %copy-start.7 = (bf16[4,256,256]{2,1,0:T(8,128)(2,1)S(1)}, bf16[4,256,256]{2,1,0:T(8,128)(2,1)}, u32[]{:S(2)}) copy-start(bf16[4,256,256]{2,1,0:T(8,128)(2,1)} %dynamic-slice_bitcast_fusion.refs_6_.rows_prev) | copy-start | bytes 1572868
  122.7 25.0 %all-to-all-start.3 = ((bf16[8,128,768]{2,1,0:T(8,128)(2,1)}), bf16[8,128,768]{2,1,0:T(8,128)(2,1)}, u32[]{:S(2)}, u32[]{:S(2)}) async-start(bf16[8,128,768]{2,1,0:T(8,128)(2,1)} %copy-done.8), calls=%async_computation.3 | async-start | bytes 3145728 | tf_op jit(solution)/shard_map/all_to_all | solution.py:416
  127.3 12.9 %collective-permute-start.16 = (bf16[1024,256]{1,0:T(8,128)(2,1)S(1)}, bf16[1024,256]{1,0:T(8,128)(2,1)S(1)}, u32[]{:S(2)}, u32[]{:S(2)}) collective-permute-start(bf16[1024,256]{1,0:T(8,128)(2,1)S(1)} %bitcast.47), channel_id=1, source_target_pairs={{0,128},{128,0},{1,129},{129,1},{2,130},{130,2},{3,131},{131,3},{4... | collective-permute-start | bytes 1572872 | tf_op jit(solution)/shard_map/ppermute | solution.py:31
  127.3 14.3 %collective-permute-start.15 = (bf16[1024,256]{1,0:T(8,128)(2,1)S(1)}, bf16[1024,256]{1,0:T(8,128)(2,1)S(1)}, u32[]{:S(2)}, u32[]{:S(2)}) collective-permute-start(bf16[1024,256]{1,0:T(8,128)(2,1)S(1)} %bitcast.48), channel_id=1, source_target_pairs={{0,64},{64,0},{1,65},{65,1},{2,66},{66,2},{3,67},{67,3},{4,68},{68... | collective-permute-start | bytes 1572872 | tf_op jit(solution)/shard_map/ppermute | solution.py:31
  140.2 3.0 %collective-permute-start.17 = (bf16[1024,256]{1,0:T(8,128)(2,1)S(1)}, bf16[1024,256]{1,0:T(8,128)(2,1)S(1)}, u32[]{:S(2)}, u32[]{:S(2)}) collective-permute-start(bf16[1024,256]{1,0:T(8,128)(2,1)S(1)} %collective-permute-done.16.t2), channel_id=1, source_target_pairs={{0,64},{64,0},{1,65},{65,1},{2,66},{66,2},{3,67},{67,3},{4,68},{68... | collective-permute-start | bytes 1572872 | tf_op jit(solution)/shard_map/ppermute | solution.py:31
  151.1 25.9 %all-to-all-start.4 = ((bf16[8,256,128]{2,1,0:T(8,128)(2,1)}), bf16[8,256,128]{2,1,0:T(8,128)(2,1)S(1)}, u32[]{:S(2)}, u32[]{:S(2)}) async-start(bf16[8,256,128]{2,1,0:T(8,128)(2,1)} %share.1), calls=%async_computation.4 | async-start | bytes 1048576 | tf_op jit(solution)/shard_map/all_to_all | solution.py:419

commit v3 on v2

v3 whole, which is shorter than its diff:
```python
import functools

import jax
import jax.numpy as jnp
from jax import lax
from jax.experimental import pallas as pl
from jax.experimental.pallas import tpu as pltpu
from jax.sharding import Mesh, PartitionSpec as P

CAP = 4
EPSILON = 1e-05
GRANT = 63 * 2**20
F32, BF16 = jnp.float32, jnp.bfloat16
YL, CO, ZH, ZL, X, YH = "yl", "co", "zh", "zl", "x", "yh"
DP = (ZH, ZL, X, YH)
SEC = (YL, CO)
GATHER = (ZL, X)
REDUCE = (ZH, YH)


def dot_nn(a, b):
    return lax.dot_general(a, b, (((1,), (0,)), ((), ())), preferred_element_type=F32)


def dot_nt(a, b):
    return lax.dot_general(a, b, (((1,), (1,)), ((), ())), preferred_element_type=F32)


def dot_tn(a, b):
    return lax.dot_general(a, b, (((0,), (0,)), ((), ())), preferred_element_type=F32)


def swap(x, axis):
    return lax.ppermute(x, axis, [(0, 1), (1, 0)])


def gather_peers(x):
    across = swap(x, YL)
    beside = swap(x, CO)
    return x, beside, across, swap(across, CO)


def full(shape):
    return pl.BlockSpec(shape, lambda *_: (0,) * len(shape))


def weights_kernel(basis, weight_in, gain, weight_out, after, gained, own, acc):
    step = pl.program_id(0)
    h = weight_in.shape[1]

    @pl.when(step == 0)
    def _():
        acc[...] = jnp.zeros_like(acc)

    part = basis[...]
    gained[...] = scaled(weight_in[...], gain[...])
    acc[0:h, :] += dot_nn(weight_out[...], part)
    acc[h:, :] += dot_tn(part, part)

    @pl.when(step == pl.num_programs(0) - 1)
    def _():
        own[...] = acc[...].astype(BF16)


def weights(basis, weight_in, gain, weight_out, after):
    d, r = basis.shape
    h = weight_in.shape[1]
    steps = 4
    rows = d // steps
    return pl.pallas_call(
        weights_kernel,
        grid=(steps,),
        in_specs=[
            pl.BlockSpec((rows, r), lambda k: (k, 0)),
            pl.BlockSpec((rows, h), lambda k: (k, 0)),
            pl.BlockSpec((1, rows), lambda k: (0, k)),
            pl.BlockSpec((h, rows), lambda k: (0, k)),
            pl.BlockSpec(memory_space=pl.ANY),
        ],
        out_specs=[pl.BlockSpec((rows, h), lambda k: (k, 0)), full((r + h, r))],
        out_shape=[
            jax.ShapeDtypeStruct((d, h), BF16),
            jax.ShapeDtypeStruct((r + h, r), BF16),
        ],
        scratch_shapes=[pltpu.VMEM((r + h, r), F32)],
        compiler_params=pltpu.CompilerParams(vmem_limit_bytes=GRANT),
        cost_estimate=pl.CostEstimate(
            flops=2 * d * r * (r + h), bytes_accessed=4 * d * (r + h), transcendentals=0
        ),
        name="weights",
    )(basis, weight_in, gain, weight_out, after)


def scaled(rows, gain):
    column = jnp.broadcast_to(gain, (8, rows.shape[0])).T[:, 0:1]
    return (rows.astype(F32) * column).astype(BF16)


def cross_kernel(at, basis, weight_in, gain, prev, after, out, mine, ins, theirs, sems):
    blocks, rows, r = mine.shape
    copies = [
        start_all(
            [
                pltpu.make_async_copy(prev.at[k], theirs.at[k], sems.at[0, k]),
                pltpu.make_async_copy(basis.at[k, at[0]], mine.at[k], sems.at[1, k]),
                pltpu.make_async_copy(weight_in.at[k, at[0]], ins.at[k], sems.at[2, k]),
            ]
        )
        for k in range(blocks)
    ]
    first, second = 0.0, 0.0
    for k in range(blocks):
        start = pl.multiple_of((k * 4 + at[0]) * rows, rows)
        wait_all(copies[k])
        first = first + dot_tn(theirs[k], mine[k])
        second = second + dot_tn(theirs[k], scaled(ins[k], gain[:, pl.ds(start, rows)]))
    out[:, 0:r] = first.astype(BF16)
    out[:, r:] = second.astype(BF16)


def cross_products(at, basis, weight_in, gain, prev, after):
    blocks, rows, r = prev.shape
    h = weight_in.shape[1]
    hbm = pl.BlockSpec(memory_space=pl.ANY)
    return pl.pallas_call(
        cross_kernel,
        in_specs=[pl.BlockSpec(memory_space=pltpu.SMEM), hbm, hbm, full(gain.shape), hbm, hbm],
        out_specs=full((r, r + h)),
        out_shape=jax.ShapeDtypeStruct((r, r + h), BF16),
        scratch_shapes=[
            pltpu.VMEM((blocks, rows, r), BF16),
            pltpu.VMEM((blocks, rows, h), BF16),
            pltpu.VMEM((blocks, rows, r), BF16),
            pltpu.SemaphoreType.DMA((3, blocks)),
        ],
        compiler_params=pltpu.CompilerParams(vmem_limit_bytes=GRANT),
        cost_estimate=pl.CostEstimate(
            flops=2 * blocks * rows * r * (r + h),
            bytes_accessed=2 * blocks * rows * (2 * r + h),
            transcendentals=0,
        ),
        name="cross_products",
    )(at, basis.reshape(blocks, 4, rows, r), weight_in.reshape(blocks, 4, rows, h), gain, prev, after)


def sum_over_x(v):
    total = v.astype(F32)
    for k in (1, 2, 3):
        total = total + lax.ppermute(v, X, [(i, (i + k) % 4) for i in range(4)]).astype(F32)
    return total.astype(BF16)


def start_all(copies):
    for copy in copies:
        copy.start()
    return copies


def wait_all(copies):
    for copy in copies:
        copy.wait()


def one_hot(column, n):
    lanes = lax.broadcasted_iota(jnp.int32, (column.shape[0], n), 1)
    return (column == lanes).astype(F32)


def split_int(v):
    return (v // 128).astype(F32).astype(BF16), (v % 128).astype(F32).astype(BF16)


def request_kernel(vocab, at, ids, basis, place, requests, rows, sem):
    copy = pltpu.make_async_copy(basis.at[:, at[0]], rows, sem)
    copy.start()
    tokens, shards = ids.shape[1], requests.shape[0]
    column = jnp.broadcast_to(ids[...], (8, tokens)).T[:, 0:1]
    first = lax.broadcasted_iota(jnp.int32, (tokens, shards), 1) * vocab
    mine = (column >= first) & (column < first + vocab)
    matches = mine.astype(F32)
    local = jnp.sum(jnp.where(mine, column - first, 0), axis=1, keepdims=True)
    owner = jnp.sum(jnp.where(mine, first // vocab, 0), axis=1, keepdims=True)
    earlier = lax.broadcasted_iota(jnp.int32, (tokens, tokens), 0) > lax.broadcasted_iota(
        jnp.int32, (tokens, tokens), 1
    )
    half = matches.astype(BF16)
    before = dot_nn(earlier.astype(F32).astype(BF16), half)
    position = jnp.sum(matches * before, axis=1, keepdims=True).astype(jnp.int32)
    place[...] = owner * CAP + position
    slot = one_hot(position, 128)
    high, low = split_int(local)
    found = 128.0 * dot_tn(half, (slot * high.astype(F32)).astype(BF16))
    found = found + dot_tn(half, (slot * low.astype(F32)).astype(BF16))
    requests[...] = found[:, 0:CAP].astype(jnp.int32)
    copy.wait()


def request(at, ids, basis, vocab, shards):
    tokens = ids.shape[1]
    blocks, _, rows, r = basis.shape
    hbm = pl.BlockSpec(memory_space=pl.ANY)
    return pl.pallas_call(
        functools.partial(request_kernel, vocab),
        in_specs=[pl.BlockSpec(memory_space=pltpu.SMEM), full(ids.shape), hbm],
        out_specs=[full((tokens, 1)), full((shards, CAP)), full((blocks, rows, r))],
        out_shape=[
            jax.ShapeDtypeStruct((tokens, 1), jnp.int32),
            jax.ShapeDtypeStruct((shards, CAP), jnp.int32),
            jax.ShapeDtypeStruct((blocks, rows, r), BF16),
        ],
        scratch_shapes=[pltpu.SemaphoreType.DMA],
        compiler_params=pltpu.CompilerParams(vmem_limit_bytes=GRANT),
        cost_estimate=pl.CostEstimate(flops=10**7, bytes_accessed=2**21, transcendentals=0),
        name="request",
    )(at, ids, basis)


def pick_kernel(asked, table, *refs):
    out, hot, rows, found, in_sems, out_sems = refs[-6:]
    shards, cap = asked.shape
    slots, vocab = hot.shape
    steps, _, width = rows.shape
    ins = [
        pltpu.make_async_copy(table.at[:, pl.ds(k * width, width)], rows.at[k], in_sems.at[k])
        for k in range(steps)
    ]
    outs = [
        pltpu.make_async_copy(found.at[k], out.at[:, :, pl.ds(k * width, width)], out_sems.at[k])
        for k in range(steps)
    ]
    for copy in ins:
        copy.start()
    peer = lax.broadcasted_iota(jnp.int32, (slots, shards), 0) // cap
    peer = (peer == lax.broadcasted_iota(jnp.int32, (slots, shards), 1)).astype(F32).astype(BF16)
    high, low = split_int(asked[...])
    spread = 128.0 * dot_nn(peer, high) + dot_nn(peer, low)
    slot = lax.broadcasted_iota(jnp.int32, (slots, cap), 0) % cap
    keep = slot == lax.broadcasted_iota(jnp.int32, (slots, cap), 1)
    column = jnp.sum(jnp.where(keep, spread, 0.0), axis=1, keepdims=True)
    hot[...] = one_hot(column.astype(jnp.int32), vocab).astype(BF16)
    for k in range(steps):
        ins[k].wait()
        found[k] = dot_nn(hot[...], rows[k]).astype(BF16).reshape(shards, cap, width)
        outs[k].start()
    for copy in outs:
        copy.wait()


def pick_rows(asked, table, firsts):
    shards, cap = asked.shape
    vocab, cols = table.shape
    slots = shards * cap
    steps = 4
    width = cols // steps
    return pl.pallas_call(
        pick_kernel,
        in_specs=[full(asked.shape), pl.BlockSpec(memory_space=pl.ANY)]
        + [pl.BlockSpec(memory_space=pl.ANY)] * len(firsts),
        out_specs=pl.BlockSpec(memory_space=pl.ANY),
        out_shape=jax.ShapeDtypeStruct((shards, cap, cols), BF16),
        scratch_shapes=[
            pltpu.VMEM((slots, vocab), BF16),
            pltpu.VMEM((steps, vocab, width), BF16),
            pltpu.VMEM((steps, shards, cap, width), BF16),
            pltpu.SemaphoreType.DMA((steps,)),
            pltpu.SemaphoreType.DMA((steps,)),
        ],
        compiler_params=pltpu.CompilerParams(vmem_limit_bytes=GRANT),
        cost_estimate=pl.CostEstimate(
            flops=2 * slots * vocab * cols, bytes_accessed=2 * cols * (vocab + slots), transcendentals=0
        ),
        name="pick_rows",
    )(asked, table, *firsts)


def place_kernel(place, answered, *refs):
    part, turned = refs[-2:]
    tokens, slots = part.shape[0], answered.shape[0]
    width = turned.shape[2]
    put = one_hot(place[...], slots).astype(BF16)
    for t in range(turned.shape[0]):
        rows = dot_nn(put, answered[:, t * width : (t + 1) * width]).astype(BF16)
        part[:, t * width : (t + 1) * width] = rows
        turned[t] = rows


def place_rows(place, answered, copies, firsts):
    tokens = place.shape[0]
    slots, cols = answered.shape
    vmem = pl.BlockSpec(memory_space=pltpu.VMEM)
    return pl.pallas_call(
        place_kernel,
        in_specs=[vmem, vmem] + [pl.BlockSpec(memory_space=pl.ANY)] * len(firsts),
        out_specs=[vmem, vmem],
        out_shape=[
            jax.ShapeDtypeStruct((tokens, cols), BF16),
            jax.ShapeDtypeStruct((copies, tokens, cols // copies), BF16),
        ],
        compiler_params=pltpu.CompilerParams(vmem_limit_bytes=16 * 2**20),
        cost_estimate=pl.CostEstimate(
            flops=2 * slots * tokens * cols, bytes_accessed=2 * cols * (slots + 2 * tokens), transcendentals=0
        ),
        name="place_rows",
    )(place, answered, *firsts)


def project_kernel(me, p0, p1, p2, p3, basis, gained, first, second, out, square):
    step = pl.program_id(0)
    r = basis.shape[1]
    for k, piece in enumerate((p0, p1, p2, p3)):

        @pl.when(step == k)
        def _(k=k, piece=piece):
            x = piece[...]
            xf = x.astype(F32)
            q = jnp.broadcast_to(jnp.sum(xf * xf, axis=1, keepdims=True), square.shape)
            a, b = dot_nn(x, basis[...]), dot_nn(x, gained[...])
            if k == 0:
                out[:, 0:r] = a
                out[:, r:] = b
                square[...] = q
            else:
                out[:, 0:r] += a
                out[:, r:] += b
                square[...] += q


def project(me, pieces, basis, gained, first, second):
    tokens, cols = pieces[0].shape
    r, h = basis.shape[1], gained.shape[1]
    return pl.pallas_call(
        project_kernel,
        grid_spec=pltpu.PrefetchScalarGridSpec(
            num_scalar_prefetch=1,
            grid=(4,),
            in_specs=[full((tokens, cols))] * 4
            + [
                pl.BlockSpec((cols, r), lambda k, me: (k ^ me[0], 0)),
                pl.BlockSpec((cols, h), lambda k, me: (k ^ me[0], 0)),
                pl.BlockSpec(memory_space=pl.ANY),
                pl.BlockSpec(memory_space=pl.ANY),
            ],
            out_specs=[full((tokens, r + h)), full((tokens, 128))],
        ),
        out_shape=[
            jax.ShapeDtypeStruct((tokens, r + h), F32),
            jax.ShapeDtypeStruct((tokens, 128), F32),
        ],
        compiler_params=pltpu.CompilerParams(vmem_limit_bytes=24 * 2**20),
        cost_estimate=pl.CostEstimate(
            flops=8 * tokens * cols * (r + h), bytes_accessed=8 * cols * (r + h + tokens), transcendentals=0
        ),
        name="project",
    )(me, *pieces, basis, gained, first, second)


def chain_kernel(width, me_ref, cot, square, q0, q1, q2, q3, g0, g1, g2, g3, m0, m1, m2, m3, sent, packed,
                 pq, owns, mats, pres, acts, coefs, spans, invs, ins, ws):
    me = me_ref[0]
    r = cot.shape[1]
    h = q0.shape[1] - r
    for k, (q, g, m) in enumerate(((q0, g0, m0), (q1, g1, m1), (q2, g2, m2), (q3, g3, m3))):
        pq[k ^ me] = q[...]
        owns[k ^ me] = g[...]
        mats[k ^ me] = m[...]
    squares = square[:, 0:1]
    coefs[0] = jnp.zeros_like(coefs[0])
    for s in range(4):
        base_in = pq[s, :, r:]
        if s == 0:
            inv = lax.rsqrt(squares * (1.0 / width) + EPSILON)
            pre = inv * base_in
        else:
            c = coefs[s]
            base_sub = pq[s - 1, :, 0:r]
            span = base_sub + dot_nn(c, owns[s - 1, h:, :])
            total = squares + jnp.sum(c.astype(F32) * (base_sub + span), axis=1, keepdims=True)
            inv = lax.rsqrt(jnp.maximum(total, 0.0) * (1.0 / width) + EPSILON)
            pre = inv * (base_in + dot_nn(c, mats[s, :, r:]))
            spans[s] = span
        invs[s] = jnp.broadcast_to(inv, invs.shape[1:])
        pres[s] = pre
        act = (pre / (1.0 + jnp.exp(-pre))).astype(BF16)
        acts[s] = act
        new = dot_nn(act, owns[s, 0:h, :])
        if s > 0:
            new = new + dot_nn(c, mats[s, :, 0:r])
        coefs[s + 1] = new.astype(BF16)
    arrived = cot[...]
    for s in (3, 2, 1, 0):
        ins[s] = arrived
        pre = pres[s]
        sg = 1.0 / (1.0 + jnp.exp(-pre))
        gp = dot_nt(arrived, owns[s, 0:h, :]) * sg * (1.0 + pre * (1.0 - sg))
        inv = invs[s, :, 0:1]
        ws[s] = (gp * inv).astype(BF16)
        if s > 0:
            mean = jnp.sum(gp * pre, axis=1, keepdims=True) * (1.0 / width)
            back = dot_nt(gp.astype(BF16), mats[s, :, r:]) - (inv * mean) * spans[s]
            arrived = (dot_nt(arrived, mats[s, :, 0:r]) + inv * back).astype(BF16)
    sent[...] = coefs[me + 1]
    row = (ws[me], acts[me], ins[me], coefs[me])
    for t in range(packed.shape[0]):
        at = 0
        for v in row:
            packed[t, :, at : at + v.shape[1]] = v
            at += v.shape[1]


def chain(me, cot, square, pq, owns, mats, width, copies):
    tokens, r = cot.shape
    h = pq[0].shape[1] - r
    vmem = pl.BlockSpec(memory_space=pltpu.VMEM)
    return pl.pallas_call(
        functools.partial(chain_kernel, width),
        in_specs=[pl.BlockSpec(memory_space=pltpu.SMEM)] + [vmem] * 14,
        out_specs=[vmem, vmem],
        out_shape=[
            jax.ShapeDtypeStruct((tokens, r), BF16),
            jax.ShapeDtypeStruct((copies, tokens, 2 * h + 2 * r), BF16),
        ],
        scratch_shapes=[
            pltpu.VMEM((4, tokens, r + h), F32),
            pltpu.VMEM((4,) + owns[0].shape, BF16),
            pltpu.VMEM((4,) + mats[0].shape, BF16),
            pltpu.VMEM((4, tokens, h), F32),
            pltpu.VMEM((4, tokens, h), BF16),
            pltpu.VMEM((5, tokens, r), BF16),
            pltpu.VMEM((4, tokens, r), F32),
            pltpu.VMEM((4, tokens, 128), F32),
            pltpu.VMEM((4, tokens, r), BF16),
            pltpu.VMEM((4, tokens, h), BF16),
        ],
        compiler_params=pltpu.CompilerParams(vmem_limit_bytes=32 * 2**20),
        cost_estimate=pl.CostEstimate(flops=4 * 10**9, bytes_accessed=6 * 2**20, transcendentals=10**6),
        name="chain",
    )(me, cot, square, *pq, *owns, *mats)


def share_kernel(at, packed_in, t0, t1, t2, t3, basis, prev, out, packed, turned, rows_own, rows_prev, sems, t_sems, p_sems):
    me = at[0]
    r = rows_own.shape[2]
    h = (packed.shape[1] - 2 * r) // 2
    tokens = packed_in.shape[1]
    first = start_all(
        [
            pltpu.make_async_copy(packed_in.at[k], packed.at[pl.ds(k * tokens, tokens)], p_sems.at[k])
            for k in range(packed_in.shape[0])
        ]
    )
    rest = start_all(
        [
            pltpu.make_async_copy(prev.at[:, at[1]], rows_prev, sems.at[0]),
            pltpu.make_async_copy(basis.at[:, at[1], at[2]], rows_own, sems.at[1]),
        ]
    )
    pieces = start_all(
        [pltpu.make_async_copy(t, turned.at[k], t_sems.at[k]) for k, t in enumerate((t0, t1, t2, t3))]
    )
    wait_all(first)
    w = packed[:, 0:h]
    act = packed[:, h : 2 * h]
    arrived = packed[:, 2 * h : 2 * h + r]
    coef = packed[:, 2 * h + r :]
    v = dot_tn(act, arrived)
    wt = w.astype(F32).T.astype(BF16)
    uh = dot_nn(wt, coef).astype(BF16)
    vh = v.astype(BF16)
    vl = (v - vh.astype(F32)).astype(BF16)
    wait_all(rest)
    for k, piece in enumerate(pieces):
        c = k ^ me
        own = rows_own[c]
        os = (dot_nt(vh, own) + dot_nt(vl, own)).astype(BF16)
        low = dot_nt(uh, rows_prev[c])
        piece.wait()
        xs = (dot_nn(wt, turned[k]) + low).astype(BF16)
        n = xs.shape[1] // 2
        for e in range(2):
            out[2 * c + e, 0:h, :] = xs[:, e * n : (e + 1) * n]
            out[2 * c + e, h:, :] = os[:, e * n : (e + 1) * n]


def share(at, packed, pieces, basis, prev):
    cs, _, _, n, r = basis.shape
    group, tokens, wide = packed.shape
    h = (wide - 2 * r) // 2
    hbm = pl.BlockSpec(memory_space=pl.ANY)
    return pl.pallas_call(
        share_kernel,
        in_specs=[pl.BlockSpec(memory_space=pltpu.SMEM)] + [hbm] * 7,
        out_specs=full((2 * cs, 2 * h, n // 2)),
        out_shape=jax.ShapeDtypeStruct((2 * cs, 2 * h, n // 2), BF16),
        scratch_shapes=[
            pltpu.VMEM((group * tokens, wide), BF16),
            pltpu.VMEM((4,) + pieces[0].shape, BF16),
            pltpu.VMEM((cs, n, r), BF16),
            pltpu.VMEM((cs, n, r), BF16),
            pltpu.SemaphoreType.DMA((2,)),
            pltpu.SemaphoreType.DMA((4,)),
            pltpu.SemaphoreType.DMA((group,)),
        ],
        compiler_params=pltpu.CompilerParams(vmem_limit_bytes=GRANT),
        cost_estimate=pl.CostEstimate(flops=2 * 10**9, bytes_accessed=6 * 2**20, transcendentals=0),
        name="share",
    )(at, packed, *pieces, basis, prev)


def finish_kernel(arrived, weight_in, gain, grad_in, grad_out, grad_gain, shares, sem):
    h = shares.shape[1] // 2
    copy = pltpu.make_async_copy(arrived, shares, sem)
    copy.start()
    copy.wait()
    total = jnp.sum(shares[...].astype(F32), axis=0)
    plain = total[0:h]
    grad_out[...] = total[h:]
    grad_in[...] = (plain * gain[...]).T
    grad_gain[...] = jnp.sum(plain * weight_in[...].astype(F32).T, axis=0, keepdims=True)


def finish(shares, weight_in, gain):
    _, twice, n = shares.shape
    h = twice // 2
    return pl.pallas_call(
        finish_kernel,
        in_specs=[pl.BlockSpec(memory_space=pl.ANY), full((n, h)), full((1, n))],
        out_specs=[full((n, h)), full((h, n)), full((1, n))],
        out_shape=[
            jax.ShapeDtypeStruct((n, h), F32),
            jax.ShapeDtypeStruct((h, n), F32),
            jax.ShapeDtypeStruct((1, n), F32),
        ],
        scratch_shapes=[pltpu.VMEM(shares.shape, BF16), pltpu.SemaphoreType.DMA],
        compiler_params=pltpu.CompilerParams(vmem_limit_bytes=16 * 2**20),
        cost_estimate=pl.CostEstimate(flops=10**6, bytes_accessed=2**20, transcendentals=0),
        name="finish",
    )(shares, weight_in, gain)


def per_device(
    token_ids, embed_table, subspace, adapter_in, adapter_out, norm_gain, coef_cotangent
):
    tokens = token_ids.shape[0]
    zl, x = lax.axis_index(ZL), lax.axis_index(X)
    shards = lax.axis_size(DP)
    group = lax.axis_size(GATHER)
    section = lax.axis_index(SEC)
    me = jnp.reshape(section, (1,)).astype(jnp.int32)
    dp = lax.axis_index(DP)
    vocab, cols = embed_table.shape
    basis, weight_in, weight_out = subspace[0], adapter_in[0], adapter_out[0]
    d, r = basis.shape
    h = weight_in.shape[1]
    block = d // shards

    x_at = jnp.reshape(x, (1,)).astype(jnp.int32)
    place, requests, rows_x = request(
        x_at, token_ids.reshape(1, tokens), basis.reshape(8, 4, 2 * block, r), vocab, shards
    )
    prev_x = lax.ppermute(rows_x, SEC, [(0, 1), (1, 2), (2, 3)])
    asked = lax.all_to_all(requests, DP, split_axis=0, concat_axis=0, tiled=True)
    found = pick_rows(asked, embed_table, (prev_x,))
    answered = lax.all_to_all(found, DP, split_axis=0, concat_axis=0, tiled=True)

    crossed = cross_products(x_at, basis, weight_in, norm_gain, prev_x, found)
    gained, own = weights(basis, weight_in, norm_gain, weight_out, crossed)
    owns = gather_peers(own)
    mats = gather_peers(sum_over_x(crossed))

    part, turned = place_rows(
        place,
        answered.reshape(shards * CAP, cols),
        group,
        (*owns[1:], mats[2]),
    )
    pieces = gather_peers(part)
    turned = lax.all_to_all(turned, GATHER, split_axis=0, concat_axis=0, tiled=True)
    pq, square = project(me, pieces, basis, gained, turned, mats[2])
    pqs = gather_peers(pq)
    turned = gather_peers(turned.reshape(group * tokens, cols // group))

    sent, packed = chain(me, coef_cotangent, square, pqs, owns, mats, d, group)
    packed = lax.all_to_all(packed, GATHER, split_axis=0, concat_axis=0, tiled=True)
    at = jnp.stack([section, zl, x]).astype(jnp.int32)
    shares = share(
        at, packed, turned, basis.reshape(4, 2, 4, 2 * block, r), prev_x.reshape(4, 2, 2 * block, r)
    )
    shares = lax.all_to_all(shares, REDUCE, split_axis=0, concat_axis=0, tiled=True)
    in_block = lax.dynamic_slice_in_dim(weight_in, dp * block, block, 0)
    gain_block = lax.dynamic_slice_in_dim(norm_gain, dp * block, block, 1)
    grad_in, grad_out, grad_gain = finish(shares, in_block, gain_block)
    return sent[None], grad_in[None], grad_out[None], grad_gain


def solution(mesh):
    fine = Mesh(mesh.devices.reshape(2, 2, 4, 2, 4, 2), (YL, CO, ZH, ZL, X, YH))
    return jax.shard_map(
        per_device,
        mesh=fine,
        in_specs=(
            P(DP),
            P(DP, SEC),
            P(SEC, None, None),
            P(SEC, None, None),
            P(SEC, None, None),
            P(SEC, None),
            P(DP, None),
        ),
        out_specs=(
            P(SEC, DP, None),
            P(SEC, DP, None),
            P(SEC, None, DP),
            P(SEC, DP),
        ),
        check_vma=False,
    )
```

time: 180 us -> 167 us (0.928)
  waiting for transfers between devices: 67.3 us -> 44.8 us
  starting transfers between devices: 40.6 us -> 55.5 us
  Pallas kernels: 19.3 us -> 33.7 us
  local copies, waits for them, and re-layouts: 20.3 us -> 6.56 us
  other arithmetic: 7.09 us -> 0.69 us
    ppermute x2 -> x3, waiting for transfers between devices: 18.3 us -> 3.93 us  [sum_over_x(): lax.ppermute(v, X, [(i, (i + k) % 4) for i in range(4)]).astype(F32)]
    pallas_call x4 -> x6, Pallas kernels: 11.5 us -> 25.2 us  [the longest x1 7.14 us: weights(): pl.pallas_call(weights_kernel, grid=(steps,), in_specs=[pl.BlockSpec((row...]
    ppermute x15, starting transfers between devices: 11.4 us -> 20.8 us  [swap(): return lax.ppermute(x, axis, [(0, 1), (1, 0)])]
    ppermute x15, waiting for transfers between devices: 26.8 us -> 18.4 us  [swap(): return lax.ppermute(x, axis, [(0, 1), (1, 0)])]
    unnamed x31 -> x24, local copies, waits for them, and re-layouts: 9.61 us -> 3.82 us
    convert_element_type x3 -> x1, other arithmetic: 4.55 us -> 0.1 us  [sum_over_x(): return total.astype(BF16)]
    squeeze x3 -> x0, local copies, waits for them, and re-layouts: 3.01 us -> none  [the longest x1 1.3 us: per_device(): lax.dynamic_index_in_dim(basis.reshape(8, 4, 2 * block, r), x, 1, False)]
    pallas_call x1, Pallas kernels: 3.34 us -> 5.56 us  [share(): pl.pallas_call(share_kernel, in_specs=[pl.BlockSpec(memory_space=pltpu.SM...]
  transfers between devices with their start and end apart: 22 -> 23, of which waited for: 10 -> 11; matrix products, arithmetic and copies ran while one was open for 7% -> 2% of each run, Pallas kernels for 4% -> 8%
where the time goes in v3:
time: 167 us; the launch traced here: 166 us
  starting transfers between devices  55.5 us (33%)
  waiting for transfers between devices  44.8 us (27%)
  Pallas kernels  33.7 us (20%)
  blocking collectives  23.5 us (14%)
  local copies, waits for them, and re-layouts  6.56 us (4%)
    all_to_all x1, blocking collectives, per_device(): lax.all_to_all(requests, DP, split_axis=0, concat_axis=0, tiled=True)  23.5 us
    ppermute x15, starting transfers between devices, swap(): return lax.ppermute(x, axis, [(0, 1), (1, 0)])  20.8 us
    ppermute x15, waiting for transfers between devices, swap(): return lax.ppermute(x, axis, [(0, 1), (1, 0)])  18.4 us
    all_to_all x1, waiting for transfers between devices, per_device(): lax.all_to_all(shares, REDUCE, split_axis=0, concat_axis=0, tiled=True)  17.1 us
    all_to_all x1, starting transfers between devices, per_device(): lax.all_to_all(shares, REDUCE, split_axis=0, concat_axis=0, tiled=True)  7.55 us
    pallas_call x1, Pallas kernels, weights(): pl.pallas_call(weights_kernel, grid=(steps,), in_specs=[pl.BlockSpec((row...  7.14 us
    all_to_all x1, starting transfers between devices, per_device(): lax.all_to_all(packed, GATHER, split_axis=0, concat_axis=0, tiled=True)  6.62 us
    all_to_all x1, starting transfers between devices, per_device(): lax.all_to_all(found, DP, split_axis=0, concat_axis=0, tiled=True)  6.21 us
  transfers between devices with their start and end apart: 23, of which 11 were waited for; matrix products, arithmetic and copies ran while one was open for 2% of the time, Pallas kernels for 8%

profile of v3, /device:TPU:33, one launch (start us, length us, event | category | flops | bytes accessed | tf_op | source)
XLA Modules:
  0.0 165.7 jit_solution(14536493380114999639)
XLA Ops:
  0.6 2.9 %request.1 = (s32[128,1]{1,0:T(8,128)}, s32[64,4]{1,0:T(8,128)}, bf16[8,256,256]{2,1,0:T(8,128)(2,1)}) custom-call(s32[1]{0:T(128)} %bitcast.1.at, s32[1,128]{1,0:T(1,128)} %bitcast.34, bf16[8,4,256,256]{3,2,1,0:T(8,128)(2,1)} %bitcast.21), custom_call_target="tpu_custom_call" | custom-call | flops 10000000 | bytes 2097152 | tf_op jit(solution)/shard_map/request/pallas_call | solution.py:202
  3.6 3.8 %collective-permute-start = (bf16[8,256,256]{2,1,0:T(8,128)(2,1)}, bf16[8,256,256]{2,1,0:T(8,128)(2,1)}, u32[]{:S(2)}, u32[]{:S(2)}) collective-permute-start(bf16[8,256,256]{2,1,0:T(8,128)(2,1)} %get-tuple-element.20), channel_id=1, source_target_pairs={{0,64},{64,128},{128,192},{1,65},{65,129},{129,193},{2,66},{66,130... | collective-permute-start | bytes 3145736 | tf_op jit(solution)/shard_map/ppermute | solution.py:560
  7.3 23.5 %all_to_all.31 = s32[64,1,4]{2,1,0:T(1,128)} all-to-all(s32[64,1,4]{2,1,0:T(1,128)} %bitcast.33), channel_id=1, replica_groups=mesh['yl'=2,'co'=2,'zh'=4,'zl'=2,'x'=4,'yh'=2] {'zh','zl','x','yh'}, dimensions={0} | all-to-all | bytes 2048 | tf_op jit(solution)/shard_map/all_to_all | solution.py:561
  30.8 0.0 collective-permute-done.refs_0_.prev
  30.8 4.5 %pick_rows.1.after = bf16[64,4,2048]{2,1,0:T(4,128)(2,1)} custom-call(s32[64,4]{1,0:T(8,128)} %bitcast.32, bf16[1008,2048]{1,0:T(8,128)(2,1)} %table.1, bf16[8,256,256]{2,1,0:T(8,128)(2,1)} %collective-permute-done.refs_0_.prev), custom_call_target="tpu_custom_call" | custom-call | flops 1056964608 | bytes 5177344 | tf_op jit(solution)/shard_map/pick_rows/pallas_call | solution.py:255
  35.3 6.2 %all-to-all-start.1 = ((bf16[64,4,2048]{2,1,0:T(4,128)(2,1)}), bf16[64,4,2048]{2,1,0:T(4,128)(2,1)}, u32[]{:S(2)}, u32[]{:S(2)}) async-start(bf16[64,4,2048]{2,1,0:T(4,128)(2,1)} %pick_rows.1.after), calls=%async_computation.1 | async-start | bytes 2097152 | tf_op jit(solution)/shard_map/all_to_all | solution.py:563
  41.5 6.2 %cross_products.1.after = bf16[256,384]{1,0:T(8,128)(2,1)} custom-call(s32[1]{0:T(128)} %bitcast.1.at, bf16[8,4,256,256]{3,2,1,0:T(8,128)(2,1)} %bitcast.22, bf16[8,4,256,128]{3,2,1,0:T(8,128)(2,1)} %bitcast.29, f32[1,8192]{1,0:T(1,128)} %gain.3, bf16[8,256,256]{2,1,0:T(8,128)(2,1)} %collective-permute-done.refs_0_.prev, bf16[64,4,2048]{2,1,0:T(4,128)(2,1)} %pick_rows.1.after), custom_call_target="tpu_custom_call" | custom-call | flops 402653184 | bytes 2621440 | tf_op jit(solution)/shard_map/cross_products/pallas_call | solution.py:125
  47.7 1.3 collective-permute-start.4
  49.0 2.4 %collective-permute-start.5 = (bf16[256,384]{1,0:T(8,128)(2,1)}, bf16[256,384]{1,0:T(8,128)(2,1)S(1)}, u32[]{:S(2)}, u32[]{:S(2)}) collective-permute-start(bf16[256,384]{1,0:T(8,128)(2,1)} %cross_products.1.after), channel_id=1, source_target_pairs={{0,4},{2,6},{4,0},{6,2},{1,5},{3,7},{5,1},{7,3},{8,12},{10,14},{12... | collective-permute-start | bytes 589832 | tf_op jit(solution)/shard_map/ppermute | solution.py:149
  51.4 1.2 collective-permute-start.6
  52.6 7.1 %weights.1 = (bf16[8192,128]{1,0:T(8,128)(2,1)}, bf16[384,256]{1,0:T(8,128)(2,1)}) custom-call(bf16[8192,256]{1,0:T(8,128)(2,1)} %bitcast.23, bf16[8192,128]{1,0:T(8,128)(2,1)} %bitcast.30, f32[1,8192]{1,0:T(1,128)} %gain.3, bf16[128,8192]{1,0:T(8,128)(2,1)} %bitcast.31, bf16[256,384]{1,0:T(8,128)(2,1)} %cross_products.1.after), custom_call_target="tpu_custom_call" | custom-call | flops 1610612736 | bytes 12582912 | tf_op jit(solution)/shard_map/weights/pallas_call | solution.py:70
  59.7 0.1 collective-permute-start.2
  59.8 2.4 %collective-permute-start.1 = (bf16[384,256]{1,0:T(8,128)(2,1)}, bf16[384,256]{1,0:T(8,128)(2,1)S(1)}, u32[]{:S(2)}, u32[]{:S(2)}) collective-permute-start(bf16[384,256]{1,0:T(8,128)(2,1)} %get-tuple-element.21.g0), channel_id=1, source_target_pairs={{0,64},{64,0},{1,65},{65,1},{2,66},{66,2},{3,67},{67,3},{4,68},{68... | collective-permute-start | bytes 589832 | tf_op jit(solution)/shard_map/ppermute | solution.py:34
  62.2 0.0 collective-permute-done.4
  62.2 3.9 %collective-permute-done.5 = bf16[256,384]{1,0:T(8,128)(2,1)S(1)} collective-permute-done((bf16[256,384]{1,0:T(8,128)(2,1)}, bf16[256,384]{1,0:T(8,128)(2,1)S(1)}, u32[]{:S(2)}, u32[]{:S(2)}) %collective-permute-start.5) | collective-permute-done | bytes 196640 | tf_op jit(solution)/shard_map/ppermute | solution.py:149
  66.2 0.0 collective-permute-done.6
  66.2 0.1 add_convert_fusion.m0
  66.3 0.1 collective-permute-start.7
  66.4 0.0 collective-permute-done.2.refs_1_.g2
  66.4 2.4 %collective-permute-start.3 = (bf16[384,256]{1,0:T(8,128)(2,1)S(1)}, bf16[384,256]{1,0:T(8,128)(2,1)S(1)}, u32[]{:S(2)}, u32[]{:S(2)}) collective-permute-start(bf16[384,256]{1,0:T(8,128)(2,1)S(1)} %collective-permute-done.2.refs_1_.g2), channel_id=1, source_target_pairs={{0,64},{64,0},{1,65},{65,1},{2,66},{66,2},{3,67},{67,3},{4,68},{68... | collective-permute-start | bytes 589832 | tf_op jit(solution)/shard_map/ppermute | solution.py:34
  68.8 0.8 all-to-all-done.1
  69.6 1.3 reshape.32.answered
  70.9 0.0 collective-permute-done.1.refs_0_.g1
  70.9 0.3 collective-permute-done.7.refs_3_.second.m2
  71.3 0.0 collective-permute-done.3.refs_2_.g3
  71.3 1.2 place_rows.1
  72.5 1.3 collective-permute-start.9
  73.7 0.0 copy-done.3
  73.7 5.7 %all-to-all-start.2 = ((bf16[8,128,256]{2,1,0:T(8,128)(2,1)}), bf16[8,128,256]{2,1,0:T(8,128)(2,1)S(1)}, u32[]{:S(2)}, u32[]{:S(2)}) async-start(bf16[8,128,256]{2,1,0:T(8,128)(2,1)} %get-tuple-element.24), calls=%async_computation.2 | async-start | bytes 1048576 | tf_op jit(solution)/shard_map/all_to_all | solution.py:577
  79.4 2.3 %collective-permute-start.8 = (bf16[128,2048]{1,0:T(8,128)(2,1)S(1)}, bf16[128,2048]{1,0:T(8,128)(2,1)S(1)}, u32[]{:S(2)}, u32[]{:S(2)}) collective-permute-start(bf16[128,2048]{1,0:T(8,128)(2,1)S(1)} %get-tuple-element.22.p0), channel_id=1, source_target_pairs={{0,64},{64,0},{1,65},{65,1},{2,66},{66,2},{3,67},{67,3},{4,68},{68... | collective-permute-start | bytes 1572872 | tf_op jit(solution)/shard_map/ppermute | solution.py:34
  81.7 1.3 collective-permute-done.9.p2
  83.0 3.9 %collective-permute-start.10 = (bf16[128,2048]{1,0:T(8,128)(2,1)S(1)}, bf16[128,2048]{1,0:T(8,128)(2,1)S(1)}, u32[]{:S(2)}, u32[]{:S(2)}) collective-permute-start(bf16[128,2048]{1,0:T(8,128)(2,1)S(1)} %collective-permute-done.9.p2), channel_id=1, source_target_pairs={{0,64},{64,0},{1,65},{65,1},{2,66},{66,2},{3,67},{67,3},{4,68},{68... | collective-permute-start | bytes 1572872 | tf_op jit(solution)/shard_map/ppermute | solution.py:34
  86.8 0.0 collective-permute-done.8.p1
  86.8 0.0 all-to-all-done.2.first
  86.8 1.5 collective-permute-done.10.p3
  88.3 2.2 %copy-done = bf16[1,8192,256]{2,1,0:T(8,128)(2,1)S(1)} copy-done((bf16[1,8192,256]{2,1,0:T(8,128)(2,1)S(1)}, bf16[1,8192,256]{2,1,0:T(8,128)(2,1)}, u32[]{:S(2)}) %copy-start) | copy-done | bytes 4194328
  90.5 1.6 copy-done.2
  92.1 1.8 %project.1 = (f32[128,384]{1,0:T(8,128)S(1)}, f32[128,128]{1,0:T(8,128)S(1)}) custom-call(s32[1]{0:T(128)} %bitcast.me.me_ref, bf16[128,2048]{1,0:T(8,128)(2,1)S(1)} %get-tuple-element.22.p0, bf16[128,2048]{1,0:T(8,128)(2,1)S(1)} %collective-permute-done.8.p1, bf16[128,2048]{1,0:T(8,128)(2,1)S(1)} %collective-permute-done.9.p2, ...), custom_call_target="tpu_custom_call" | custom-call | flops 805306368 | bytes 8388608 | tf_op jit(solution)/shard_map/project/pallas_call | solution.py:331
  94.0 1.4 collective-permute-start.12
  95.3 1.3 collective-permute-start.14
  96.6 0.0 collective-permute-start.15
  96.6 0.5 collective-permute-start.11
  97.1 2.2 %collective-permute-done.12.q2 = f32[128,384]{1,0:T(8,128)S(1)} collective-permute-done((f32[128,384]{1,0:T(8,128)S(1)}, f32[128,384]{1,0:T(8,128)S(1)}, u32[]{:S(2)}, u32[]{:S(2)}) %collective-permute-start.12) | collective-permute-done | bytes 196640 | tf_op jit(solution)/shard_map/ppermute | solution.py:34
  99.3 2.0 %collective-permute-start.13 = (f32[128,384]{1,0:T(8,128)S(1)}, f32[128,384]{1,0:T(8,128)S(1)}, u32[]{:S(2)}, u32[]{:S(2)}) collective-permute-start(f32[128,384]{1,0:T(8,128)S(1)} %collective-permute-done.12.q2), channel_id=1, source_target_pairs={{0,64},{64,0},{1,65},{65,1},{2,66},{66,2},{3,67},{67,3},{4,68},{68... | collective-permute-start | bytes 589832 | tf_op jit(solution)/shard_map/ppermute | solution.py:34
  101.4 0.0 collective-permute-done.14.m1
  101.4 0.0 collective-permute-done.15.m3
  101.4 0.0 collective-permute-done.11.q1
  101.4 1.1 collective-permute-done.13.q3
  102.5 3.6 %chain.1 = (bf16[128,256]{1,0:T(8,128)(2,1)}, bf16[8,128,768]{2,1,0:T(8,128)(2,1)}) custom-call(s32[1]{0:T(128)} %bitcast.me.me_ref, bf16[128,256]{1,0:T(8,128)(2,1)S(1)} %copy-done.7, f32[128,128]{1,0:T(8,128)S(1)} %get-tuple-element.25.square, f32[128,384]{1,0:T(8,128)S(1)} %get-tuple-element.26.q0, f32[128,384]{1,0:T(8,128)S(1)} %collective-permute-done.11.q1, ...), custom_call_target="tpu_custom_call" | custom-call | flops 4000000000 | bytes 6291456 | tf_op jit(solution)/shard_map/chain/pallas_call | solution.py:414
  106.1 6.6 %all-to-all-start.3 = ((bf16[8,128,768]{2,1,0:T(8,128)(2,1)}), bf16[8,128,768]{2,1,0:T(8,128)(2,1)}, u32[]{:S(2)}, u32[]{:S(2)}) async-start(bf16[8,128,768]{2,1,0:T(8,128)(2,1)} %get-tuple-element.28), calls=%async_computation.3 | async-start | bytes 3145728 | tf_op jit(solution)/shard_map/all_to_all | solution.py:583
  112.7 0.3 collective-permute-start.17
  113.0 1.2 collective-permute-start.16
  114.2 11.1 %collective-permute-done.17.t2 = bf16[1024,256]{1,0:T(8,128)(2,1)S(1)} collective-permute-done((bf16[1024,256]{1,0:T(8,128)(2,1)S(1)}, bf16[1024,256]{1,0:T(8,128)(2,1)S(1)}, u32[]{:S(2)}, u32[]{:S(2)}) %collective-permute-start.17) | collective-permute-done | bytes 524320 | tf_op jit(solution)/shard_map/ppermute | solution.py:34
  125.3 1.7 %collective-permute-start.18 = (bf16[1024,256]{1,0:T(8,128)(2,1)S(1)}, bf16[1024,256]{1,0:T(8,128)(2,1)S(1)}, u32[]{:S(2)}, u32[]{:S(2)}) collective-permute-start(bf16[1024,256]{1,0:T(8,128)(2,1)S(1)} %collective-permute-done.17.t2), channel_id=1, source_target_pairs={{0,64},{64,0},{1,65},{65,1},{2,66},{66,2},{3,67},{67,3},{4,68},{68... | collective-permute-start | bytes 1572872 | tf_op jit(solution)/shard_map/ppermute | solution.py:34
  127.0 0.6 pad_add_fusion.at
  127.6 0.0 collective-permute-done.16.t1
  127.6 0.9 collective-permute-done.18.t3
  128.6 4.5 %all-to-all-done.3.packed_in = bf16[8,128,768]{2,1,0:T(8,128)(2,1)} async-done(((bf16[8,128,768]{2,1,0:T(8,128)(2,1)}), bf16[8,128,768]{2,1,0:T(8,128)(2,1)}, u32[]{:S(2)}, u32[]{:S(2)}) %all-to-all-start.3) | async-done | bytes 1572896 | tf_op jit(solution)/shard_map/all_to_all | solution.py:583
  133.1 5.6 %share.1 = bf16[8,256,128]{2,1,0:T(8,128)(2,1)} custom-call(s32[3]{0:T(128)} %pad_add_fusion.at, bf16[8,128,768]{2,1,0:T(8,128)(2,1)} %all-to-all-done.3.packed_in, bf16[1024,256]{1,0:T(8,128)(2,1)} %bitcast.28, bf16[1024,256]{1,0:T(8,128)(2,1)} %copy-done.10, bf16[1024,256]{1,0:T(8,128)(2,1)} %copy-done.9, bf16[1024,256]{1,0:T(8,128)(2,1)} %copy-done.11, ...), custom_call_target="tpu_custom_call" | custom-call | flops 2000000000 | bytes 6291456 | tf_op jit(solution)/shard_map/share/pallas_call | solution.py:489
  138.6 7.5 %all-to-all-start.4 = ((bf16[8,256,128]{2,1,0:T(8,128)(2,1)}), bf16[8,256,128]{2,1,0:T(8,128)(2,1)S(1)}, u32[]{:S(2)}, u32[]{:S(2)}) async-start(bf16[8,256,128]{2,1,0:T(8,128)(2,1)} %share.1), calls=%async_computation.4 | async-start | bytes 1048576 | tf_op jit(solution)/shard_map/all_to_all | solution.py:588
  146.2 0.7 constant_dynamic-slice_fusion.gain
  146.9 0.8 dynamic-slice_bitcast_fusion.weight_in
  147.6 17.1 %all-to-all-done.4.arrived = bf16[8,256,128]{2,1,0:T(8,128)(2,1)S(1)} async-done(((bf16[8,256,128]{2,1,0:T(8,128)(2,1)}), bf16[8,256,128]{2,1,0:T(8,128)(2,1)S(1)}, u32[]{:S(2)}, u32[]{:S(2)}) %all-to-all-start.4) | async-done | bytes 524320 | tf_op jit(solution)/shard_map/all_to_all | solution.py:588
  164.8 0.8 finish.1
  (21 shorter events, 0.0 us)
Async XLA Ops:
  3.6 27.2 %collective-permute-start = (bf16[8,256,256]{2,1,0:T(8,128)(2,1)}, bf16[8,256,256]{2,1,0:T(8,128)(2,1)}, u32[]{:S(2)}, u32[]{:S(2)}) collective-permute-start(bf16[8,256,256]{2,1,0:T(8,128)(2,1)} %get-tuple-element.20), channel_id=1, source_target_pairs={{0,64},{64,128},{128,192},{1,65},{65,129},{129,193},{2,66},{66,130... | collective-permute-start | bytes 3145736 | tf_op jit(solution)/shard_map/ppermute | solution.py:560
  35.3 34.3 %all-to-all-start.1 = ((bf16[64,4,2048]{2,1,0:T(4,128)(2,1)}), bf16[64,4,2048]{2,1,0:T(4,128)(2,1)}, u32[]{:S(2)}, u32[]{:S(2)}) async-start(bf16[64,4,2048]{2,1,0:T(4,128)(2,1)} %pick_rows.1.after), calls=%async_computation.1 | async-start | bytes 2097152 | tf_op jit(solution)/shard_map/all_to_all | solution.py:563
  47.7 14.5 %collective-permute-start.4 = (bf16[256,384]{1,0:T(8,128)(2,1)}, bf16[256,384]{1,0:T(8,128)(2,1)S(1)}, u32[]{:S(2)}, u32[]{:S(2)}) collective-permute-start(bf16[256,384]{1,0:T(8,128)(2,1)} %cross_products.1.after), channel_id=1, source_target_pairs={{0,2},{2,4},{4,6},{6,0},{1,3},{3,5},{5,7},{7,1},{8,10},{10,12},{12... | collective-permute-start | bytes 589832 | tf_op jit(solution)/shard_map/ppermute | solution.py:149
  49.0 17.2 %collective-permute-start.5 = (bf16[256,384]{1,0:T(8,128)(2,1)}, bf16[256,384]{1,0:T(8,128)(2,1)S(1)}, u32[]{:S(2)}, u32[]{:S(2)}) collective-permute-start(bf16[256,384]{1,0:T(8,128)(2,1)} %cross_products.1.after), channel_id=1, source_target_pairs={{0,4},{2,6},{4,0},{6,2},{1,5},{3,7},{5,1},{7,3},{8,12},{10,14},{12... | collective-permute-start | bytes 589832 | tf_op jit(solution)/shard_map/ppermute | solution.py:149
  51.4 14.8 %collective-permute-start.6 = (bf16[256,384]{1,0:T(8,128)(2,1)}, bf16[256,384]{1,0:T(8,128)(2,1)S(1)}, u32[]{:S(2)}, u32[]{:S(2)}) collective-permute-start(bf16[256,384]{1,0:T(8,128)(2,1)} %cross_products.1.after), channel_id=1, source_target_pairs={{0,6},{2,0},{4,2},{6,4},{1,7},{3,1},{5,3},{7,5},{8,14},{10,8},{12,... | collective-permute-start | bytes 589832 | tf_op jit(solution)/shard_map/ppermute | solution.py:149
  52.6 13.6 %copy-start.8 = (bf16[256,384]{1,0:T(8,128)(2,1)S(1)}, bf16[256,384]{1,0:T(8,128)(2,1)}, u32[]{:S(2)}) copy-start(bf16[256,384]{1,0:T(8,128)(2,1)} %cross_products.1.after) | copy-start | bytes 589828
  59.7 11.6 %copy-start.5 = (s32[128,1]{1,0:T(8,128)S(1)}, s32[128,1]{1,0:T(8,128)}, u32[]{:S(2)}) copy-start(s32[128,1]{1,0:T(8,128)} %get-tuple-element.18.place) | copy-start | bytes 1540
  59.7 6.7 %collective-permute-start.2 = (bf16[384,256]{1,0:T(8,128)(2,1)}, bf16[384,256]{1,0:T(8,128)(2,1)S(1)}, u32[]{:S(2)}, u32[]{:S(2)}) collective-permute-start(bf16[384,256]{1,0:T(8,128)(2,1)} %get-tuple-element.21.g0), channel_id=1, source_target_pairs={{0,128},{128,0},{1,129},{129,1},{2,130},{130,2},{3,131},{131,3},{4... | collective-permute-start | bytes 589832 | tf_op jit(solution)/shard_map/ppermute | solution.py:34
  59.8 11.1 %collective-permute-start.1 = (bf16[384,256]{1,0:T(8,128)(2,1)}, bf16[384,256]{1,0:T(8,128)(2,1)S(1)}, u32[]{:S(2)}, u32[]{:S(2)}) collective-permute-start(bf16[384,256]{1,0:T(8,128)(2,1)} %get-tuple-element.21.g0), channel_id=1, source_target_pairs={{0,64},{64,0},{1,65},{65,1},{2,66},{66,2},{3,67},{67,3},{4,68},{68... | collective-permute-start | bytes 589832 | tf_op jit(solution)/shard_map/ppermute | solution.py:34
  66.3 7.5 %copy-start.3 = (bf16[256,384]{1,0:T(8,128)(2,1)}, bf16[256,384]{1,0:T(8,128)(2,1)S(1)}, u32[]{:S(2)}) copy-start(bf16[256,384]{1,0:T(8,128)(2,1)S(1)} %add_convert_fusion.m0) | copy-start | bytes 589828
  66.3 5.0 %collective-permute-start.7 = (bf16[256,384]{1,0:T(8,128)(2,1)S(1)}, bf16[256,384]{1,0:T(8,128)(2,1)S(1)}, u32[]{:S(2)}, u32[]{:S(2)}) collective-permute-start(bf16[256,384]{1,0:T(8,128)(2,1)S(1)} %add_convert_fusion.m0), channel_id=1, source_target_pairs={{0,128},{128,0},{1,129},{129,1},{2,130},{130,2},{3,131},{131,3},{4... | collective-permute-start | bytes 589832 | tf_op jit(solution)/shard_map/ppermute | solution.py:34
  66.4 4.9 %collective-permute-start.3 = (bf16[384,256]{1,0:T(8,128)(2,1)S(1)}, bf16[384,256]{1,0:T(8,128)(2,1)S(1)}, u32[]{:S(2)}, u32[]{:S(2)}) collective-permute-start(bf16[384,256]{1,0:T(8,128)(2,1)S(1)} %collective-permute-done.2.refs_1_.g2), channel_id=1, source_target_pairs={{0,64},{64,0},{1,65},{65,1},{2,66},{66,2},{3,67},{67,3},{4,68},{68... | collective-permute-start | bytes 589832 | tf_op jit(solution)/shard_map/ppermute | solution.py:34
  72.5 10.5 %collective-permute-start.9 = (bf16[128,2048]{1,0:T(8,128)(2,1)S(1)}, bf16[128,2048]{1,0:T(8,128)(2,1)S(1)}, u32[]{:S(2)}, u32[]{:S(2)}) collective-permute-start(bf16[128,2048]{1,0:T(8,128)(2,1)S(1)} %get-tuple-element.22.p0), channel_id=1, source_target_pairs={{0,128},{128,0},{1,129},{129,1},{2,130},{130,2},{3,131},{131,3},{4... | collective-permute-start | bytes 1572872 | tf_op jit(solution)/shard_map/ppermute | solution.py:34
  73.7 13.1 %all-to-all-start.2 = ((bf16[8,128,256]{2,1,0:T(8,128)(2,1)}), bf16[8,128,256]{2,1,0:T(8,128)(2,1)S(1)}, u32[]{:S(2)}, u32[]{:S(2)}) async-start(bf16[8,128,256]{2,1,0:T(8,128)(2,1)} %get-tuple-element.24), calls=%async_computation.2 | async-start | bytes 1048576 | tf_op jit(solution)/shard_map/all_to_all | solution.py:577
  79.4 7.4 %collective-permute-start.8 = (bf16[128,2048]{1,0:T(8,128)(2,1)S(1)}, bf16[128,2048]{1,0:T(8,128)(2,1)S(1)}, u32[]{:S(2)}, u32[]{:S(2)}) collective-permute-start(bf16[128,2048]{1,0:T(8,128)(2,1)S(1)} %get-tuple-element.22.p0), channel_id=1, source_target_pairs={{0,64},{64,0},{1,65},{65,1},{2,66},{66,2},{3,67},{67,3},{4,68},{68... | collective-permute-start | bytes 1572872 | tf_op jit(solution)/shard_map/ppermute | solution.py:34
  83.0 5.4 %collective-permute-start.10 = (bf16[128,2048]{1,0:T(8,128)(2,1)S(1)}, bf16[128,2048]{1,0:T(8,128)(2,1)S(1)}, u32[]{:S(2)}, u32[]{:S(2)}) collective-permute-start(bf16[128,2048]{1,0:T(8,128)(2,1)S(1)} %collective-permute-done.9.p2), channel_id=1, source_target_pairs={{0,64},{64,0},{1,65},{65,1},{2,66},{66,2},{3,67},{67,3},{4,68},{68... | collective-permute-start | bytes 1572872 | tf_op jit(solution)/shard_map/ppermute | solution.py:34
  86.8 26.2 %copy-start.1 = (bf16[8,128,256]{2,1,0:T(8,128)(2,1)}, bf16[8,128,256]{2,1,0:T(8,128)(2,1)S(1)}, u32[]{:S(2)}) copy-start(bf16[8,128,256]{2,1,0:T(8,128)(2,1)S(1)} %all-to-all-done.2.first) | copy-start | bytes 1572868
  88.3 2.2 %copy-start = (bf16[1,8192,256]{2,1,0:T(8,128)(2,1)S(1)}, bf16[1,8192,256]{2,1,0:T(8,128)(2,1)}, u32[]{:S(2)}) copy-start(bf16[1,8192,256]{2,1,0:T(8,128)(2,1)} %param.9) | copy-start | bytes 12582916
  90.5 1.6 copy-start.2
  92.1 3.2 %copy-start.4 = (bf16[256,384]{1,0:T(8,128)(2,1)S(1)}, bf16[256,384]{1,0:T(8,128)(2,1)}, u32[]{:S(2)}) copy-start(bf16[256,384]{1,0:T(8,128)(2,1)} %copy-done.3) | copy-start | bytes 589828
  92.1 10.3 %copy-start.6 = (bf16[384,256]{1,0:T(8,128)(2,1)S(1)}, bf16[384,256]{1,0:T(8,128)(2,1)}, u32[]{:S(2)}) copy-start(bf16[384,256]{1,0:T(8,128)(2,1)} %get-tuple-element.21.g0) | copy-start | bytes 589828
  92.1 10.3 %copy-start.7 = (bf16[128,256]{1,0:T(8,128)(2,1)S(1)}, bf16[128,256]{1,0:T(8,128)(2,1)}, u32[]{:S(2)}) copy-start(bf16[128,256]{1,0:T(8,128)(2,1)} %cot.1) | copy-start | bytes 196612
  94.0 5.4 %collective-permute-start.12 = (f32[128,384]{1,0:T(8,128)S(1)}, f32[128,384]{1,0:T(8,128)S(1)}, u32[]{:S(2)}, u32[]{:S(2)}) collective-permute-start(f32[128,384]{1,0:T(8,128)S(1)} %get-tuple-element.26.q0), channel_id=1, source_target_pairs={{0,128},{128,0},{1,129},{129,1},{2,130},{130,2},{3,131},{131,3},{4... | collective-permute-start | bytes 589832 | tf_op jit(solution)/shard_map/ppermute | solution.py:34
  95.3 6.0 %collective-permute-start.14 = (bf16[256,384]{1,0:T(8,128)(2,1)S(1)}, bf16[256,384]{1,0:T(8,128)(2,1)S(1)}, u32[]{:S(2)}, u32[]{:S(2)}) collective-permute-start(bf16[256,384]{1,0:T(8,128)(2,1)S(1)} %copy-done.4), channel_id=1, source_target_pairs={{0,64},{64,0},{1,65},{65,1},{2,66},{66,2},{3,67},{67,3},{4,68},{68... | collective-permute-start | bytes 589832 | tf_op jit(solution)/shard_map/ppermute | solution.py:34
  96.6 4.8 %collective-permute-start.15 = (bf16[256,384]{1,0:T(8,128)(2,1)S(1)}, bf16[256,384]{1,0:T(8,128)(2,1)S(1)}, u32[]{:S(2)}, u32[]{:S(2)}) collective-permute-start(bf16[256,384]{1,0:T(8,128)(2,1)S(1)} %collective-permute-done.7.refs_3_.second.m2), channel_id=1, source_target_pairs={{0,64},{64,0},{1,65},{65,1},{2,66},{66,2},{3,67},{67,3},{4,68},{68... | collective-permute-start | bytes 589832 | tf_op jit(solution)/shard_map/ppermute | solution.py:34
  96.6 4.8 %collective-permute-start.11 = (f32[128,384]{1,0:T(8,128)S(1)}, f32[128,384]{1,0:T(8,128)S(1)}, u32[]{:S(2)}, u32[]{:S(2)}) collective-permute-start(f32[128,384]{1,0:T(8,128)S(1)} %get-tuple-element.26.q0), channel_id=1, source_target_pairs={{0,64},{64,0},{1,65},{65,1},{2,66},{66,2},{3,67},{67,3},{4,68},{68... | collective-permute-start | bytes 589832 | tf_op jit(solution)/shard_map/ppermute | solution.py:34
  99.3 3.1 %collective-permute-start.13 = (f32[128,384]{1,0:T(8,128)S(1)}, f32[128,384]{1,0:T(8,128)S(1)}, u32[]{:S(2)}, u32[]{:S(2)}) collective-permute-start(f32[128,384]{1,0:T(8,128)S(1)} %collective-permute-done.12.q2), channel_id=1, source_target_pairs={{0,64},{64,0},{1,65},{65,1},{2,66},{66,2},{3,67},{67,3},{4,68},{68... | collective-permute-start | bytes 589832 | tf_op jit(solution)/shard_map/ppermute | solution.py:34
  106.1 27.0 %all-to-all-start.3 = ((bf16[8,128,768]{2,1,0:T(8,128)(2,1)}), bf16[8,128,768]{2,1,0:T(8,128)(2,1)}, u32[]{:S(2)}, u32[]{:S(2)}) async-start(bf16[8,128,768]{2,1,0:T(8,128)(2,1)} %get-tuple-element.28), calls=%async_computation.3 | async-start | bytes 3145728 | tf_op jit(solution)/shard_map/all_to_all | solution.py:583
  112.7 12.6 %collective-permute-start.17 = (bf16[1024,256]{1,0:T(8,128)(2,1)S(1)}, bf16[1024,256]{1,0:T(8,128)(2,1)S(1)}, u32[]{:S(2)}, u32[]{:S(2)}) collective-permute-start(bf16[1024,256]{1,0:T(8,128)(2,1)S(1)} %bitcast.26), channel_id=1, source_target_pairs={{0,128},{128,0},{1,129},{129,1},{2,130},{130,2},{3,131},{131,3},{4... | collective-permute-start | bytes 1572872 | tf_op jit(solution)/shard_map/ppermute | solution.py:34
  113.0 14.6 %collective-permute-start.16 = (bf16[1024,256]{1,0:T(8,128)(2,1)S(1)}, bf16[1024,256]{1,0:T(8,128)(2,1)S(1)}, u32[]{:S(2)}, u32[]{:S(2)}) collective-permute-start(bf16[1024,256]{1,0:T(8,128)(2,1)S(1)} %bitcast.27), channel_id=1, source_target_pairs={{0,64},{64,0},{1,65},{65,1},{2,66},{66,2},{3,67},{67,3},{4,68},{68... | collective-permute-start | bytes 1572872 | tf_op jit(solution)/shard_map/ppermute | solution.py:34
  125.3 7.8 %copy-start.9 = (bf16[1024,256]{1,0:T(8,128)(2,1)}, bf16[1024,256]{1,0:T(8,128)(2,1)S(1)}, u32[]{:S(2)}) copy-start(bf16[1024,256]{1,0:T(8,128)(2,1)S(1)} %collective-permute-done.17.t2) | copy-start | bytes 1572868
  125.3 3.3 %collective-permute-start.18 = (bf16[1024,256]{1,0:T(8,128)(2,1)S(1)}, bf16[1024,256]{1,0:T(8,128)(2,1)S(1)}, u32[]{:S(2)}, u32[]{:S(2)}) collective-permute-start(bf16[1024,256]{1,0:T(8,128)(2,1)S(1)} %collective-permute-done.17.t2), channel_id=1, source_target_pairs={{0,64},{64,0},{1,65},{65,1},{2,66},{66,2},{3,67},{67,3},{4,68},{68... | collective-permute-start | bytes 1572872 | tf_op jit(solution)/shard_map/ppermute | solution.py:34
  127.6 0.9 copy-start.10
  128.6 4.5 %copy-start.11 = (bf16[1024,256]{1,0:T(8,128)(2,1)}, bf16[1024,256]{1,0:T(8,128)(2,1)S(1)}, u32[]{:S(2)}) copy-start(bf16[1024,256]{1,0:T(8,128)(2,1)S(1)} %collective-permute-done.18.t3) | copy-start | bytes 1572868
  138.6 26.1 %all-to-all-start.4 = ((bf16[8,256,128]{2,1,0:T(8,128)(2,1)}), bf16[8,256,128]{2,1,0:T(8,128)(2,1)S(1)}, u32[]{:S(2)}, u32[]{:S(2)}) async-start(bf16[8,256,128]{2,1,0:T(8,128)(2,1)} %share.1), calls=%async_computation.4 | async-start | bytes 1048576 | tf_op jit(solution)/shard_map/all_to_all | solution.py:588

commit v4 on v3

--- a/solution.py
+++ b/solution.py
@@ -44,7 +44,20 @@
     return pl.BlockSpec(shape, lambda *_: (0,) * len(shape))
 
 
-def weights_kernel(basis, weight_in, gain, weight_out, after, gained, own, acc):
+def ordered(x, after):
+    hbm = pl.BlockSpec(memory_space=pl.ANY)
+    return pl.pallas_call(
+        lambda *refs: None,
+        in_specs=[hbm, hbm],
+        out_specs=hbm,
+        out_shape=jax.ShapeDtypeStruct(x.shape, x.dtype),
+        input_output_aliases={0: 0},
+        name="ordered",
+    )(x, after)
+
+
+def weights_kernel(basis, weight_in, gain, weight_out, *refs):
+    gained, own, acc = refs[-3:]
     step = pl.program_id(0)
     h = weight_in.shape[1]
 
@@ -62,7 +75,7 @@
         own[...] = acc[...].astype(BF16)
 
 
-def weights(basis, weight_in, gain, weight_out, after):
+def weights(basis, weight_in, gain, weight_out, afters):
     d, r = basis.shape
     h = weight_in.shape[1]
     steps = 4
@@ -75,20 +88,20 @@
             pl.BlockSpec((rows, h), lambda k: (k, 0)),
             pl.BlockSpec((1, rows), lambda k: (0, k)),
             pl.BlockSpec((h, rows), lambda k: (0, k)),
-            pl.BlockSpec(memory_space=pl.ANY),
-        ],
+        ]
+        + [pl.BlockSpec(memory_space=pl.ANY)] * len(afters),
         out_specs=[pl.BlockSpec((rows, h), lambda k: (k, 0)), full((r + h, r))],
         out_shape=[
             jax.ShapeDtypeStruct((d, h), BF16),
             jax.ShapeDtypeStruct((r + h, r), BF16),
         ],
         scratch_shapes=[pltpu.VMEM((r + h, r), F32)],
-        compiler_params=pltpu.CompilerParams(vmem_limit_bytes=GRANT),
+        compiler_params=pltpu.CompilerParams(vmem_limit_bytes=24 * 2**20),
         cost_estimate=pl.CostEstimate(
             flops=2 * d * r * (r + h), bytes_accessed=4 * d * (r + h), transcendentals=0
         ),
         name="weights",
-    )(basis, weight_in, gain, weight_out, after)
+    )(basis, weight_in, gain, weight_out, *afters)
 
 
 def scaled(rows, gain):
@@ -97,21 +110,19 @@
 
 
 def cross_kernel(at, basis, weight_in, gain, prev, after, out, mine, ins, theirs, sems):
-    blocks, rows, r = mine.shape
-    copies = [
+    blocks, rows, r = theirs.shape
+    wait_all(
         start_all(
             [
-                pltpu.make_async_copy(prev.at[k], theirs.at[k], sems.at[0, k]),
-                pltpu.make_async_copy(basis.at[k, at[0]], mine.at[k], sems.at[1, k]),
-                pltpu.make_async_copy(weight_in.at[k, at[0]], ins.at[k], sems.at[2, k]),
+                pltpu.make_async_copy(prev, theirs, sems.at[0]),
+                pltpu.make_async_copy(basis.at[:, at[0]], mine, sems.at[1]),
+                pltpu.make_async_copy(weight_in.at[:, at[0]], ins, sems.at[2]),
             ]
         )
-        for k in range(blocks)
-    ]
+    )
     first, second = 0.0, 0.0
     for k in range(blocks):
         start = pl.multiple_of((k * 4 + at[0]) * rows, rows)
-        wait_all(copies[k])
         first = first + dot_tn(theirs[k], mine[k])
         second = second + dot_tn(theirs[k], scaled(ins[k], gain[:, pl.ds(start, rows)]))
     out[:, 0:r] = first.astype(BF16)
@@ -131,7 +142,7 @@
             pltpu.VMEM((blocks, rows, r), BF16),
             pltpu.VMEM((blocks, rows, h), BF16),
             pltpu.VMEM((blocks, rows, r), BF16),
-            pltpu.SemaphoreType.DMA((3, blocks)),
+            pltpu.SemaphoreType.DMA((3,)),
         ],
         compiler_params=pltpu.CompilerParams(vmem_limit_bytes=GRANT),
         cost_estimate=pl.CostEstimate(
@@ -399,7 +410,8 @@
             back = dot_nt(gp.astype(BF16), mats[s, :, r:]) - (inv * mean) * spans[s]
             arrived = (dot_nt(arrived, mats[s, :, 0:r]) + inv * back).astype(BF16)
     sent[...] = coefs[me + 1]
-    row = (ws[me], acts[me], ins[me], coefs[me])
+    w = ws[me]
+    row = (w, dot_tn(acts[me], ins[me]).astype(BF16), dot_tn(w, coefs[me]).astype(BF16))
     for t in range(packed.shape[0]):
         at = 0
         for v in row:
@@ -417,7 +429,7 @@
         out_specs=[vmem, vmem],
         out_shape=[
             jax.ShapeDtypeStruct((tokens, r), BF16),
-            jax.ShapeDtypeStruct((copies, tokens, 2 * h + 2 * r), BF16),
+            jax.ShapeDtypeStruct((copies, tokens, h + 2 * r), BF16),
         ],
         scratch_shapes=[
             pltpu.VMEM((4, tokens, r + h), F32),
@@ -437,73 +449,42 @@
     )(me, cot, square, *pq, *owns, *mats)
 
 
-def share_kernel(at, packed_in, t0, t1, t2, t3, basis, prev, out, packed, turned, rows_own, rows_prev, sems, t_sems, p_sems):
-    me = at[0]
+def share_kernel(me_ref, packed, t0, t1, t2, t3, rows_own, rows_prev, out):
+    me = me_ref[0]
+    group, tokens, wide = packed.shape
     r = rows_own.shape[2]
-    h = (packed.shape[1] - 2 * r) // 2
-    tokens = packed_in.shape[1]
-    first = start_all(
-        [
-            pltpu.make_async_copy(packed_in.at[k], packed.at[pl.ds(k * tokens, tokens)], p_sems.at[k])
-            for k in range(packed_in.shape[0])
-        ]
-    )
-    rest = start_all(
-        [
-            pltpu.make_async_copy(prev.at[:, at[1]], rows_prev, sems.at[0]),
-            pltpu.make_async_copy(basis.at[:, at[1], at[2]], rows_own, sems.at[1]),
-        ]
-    )
-    pieces = start_all(
-        [pltpu.make_async_copy(t, turned.at[k], t_sems.at[k]) for k, t in enumerate((t0, t1, t2, t3))]
-    )
-    wait_all(first)
-    w = packed[:, 0:h]
-    act = packed[:, h : 2 * h]
-    arrived = packed[:, 2 * h : 2 * h + r]
-    coef = packed[:, 2 * h + r :]
-    v = dot_tn(act, arrived)
-    wt = w.astype(F32).T.astype(BF16)
-    uh = dot_nn(wt, coef).astype(BF16)
+    h = wide - 2 * r
+    both = packed[0, :, h:].astype(F32)
+    for g in range(1, group):
+        both = both + packed[g, :, h:].astype(F32)
+    v, uh = both[:, 0:r], both[:, r:].astype(BF16)
     vh = v.astype(BF16)
     vl = (v - vh.astype(F32)).astype(BF16)
-    wait_all(rest)
-    for k, piece in enumerate(pieces):
+    wt = jnp.concatenate([packed[g, :, 0:h].astype(F32).T.astype(BF16) for g in range(group)], axis=1)
+    for k, piece in enumerate((t0, t1, t2, t3)):
         c = k ^ me
+        xs = (dot_nn(wt, piece[...]) + dot_nt(uh, rows_prev[c])).astype(BF16)
         own = rows_own[c]
         os = (dot_nt(vh, own) + dot_nt(vl, own)).astype(BF16)
-        low = dot_nt(uh, rows_prev[c])
-        piece.wait()
-        xs = (dot_nn(wt, turned[k]) + low).astype(BF16)
         n = xs.shape[1] // 2
         for e in range(2):
             out[2 * c + e, 0:h, :] = xs[:, e * n : (e + 1) * n]
             out[2 * c + e, h:, :] = os[:, e * n : (e + 1) * n]
 
 
-def share(at, packed, pieces, basis, prev):
-    cs, _, _, n, r = basis.shape
-    group, tokens, wide = packed.shape
-    h = (wide - 2 * r) // 2
-    hbm = pl.BlockSpec(memory_space=pl.ANY)
+def share(me, packed, pieces, rows_own, rows_prev):
+    h = packed.shape[2] - 2 * rows_own.shape[2]
+    cs, n, _ = rows_own.shape
+    vmem = pl.BlockSpec(memory_space=pltpu.VMEM)
     return pl.pallas_call(
         share_kernel,
-        in_specs=[pl.BlockSpec(memory_space=pltpu.SMEM)] + [hbm] * 7,
-        out_specs=full((2 * cs, 2 * h, n // 2)),
+        in_specs=[pl.BlockSpec(memory_space=pltpu.SMEM)] + [vmem] * 7,
+        out_specs=vmem,
         out_shape=jax.ShapeDtypeStruct((2 * cs, 2 * h, n // 2), BF16),
-        scratch_shapes=[
-            pltpu.VMEM((group * tokens, wide), BF16),
-            pltpu.VMEM((4,) + pieces[0].shape, BF16),
-            pltpu.VMEM((cs, n, r), BF16),
-            pltpu.VMEM((cs, n, r), BF16),
-            pltpu.SemaphoreType.DMA((2,)),
-            pltpu.SemaphoreType.DMA((4,)),
-            pltpu.SemaphoreType.DMA((group,)),
-        ],
-        compiler_params=pltpu.CompilerParams(vmem_limit_bytes=GRANT),
+        compiler_params=pltpu.CompilerParams(vmem_limit_bytes=32 * 2**20),
         cost_estimate=pl.CostEstimate(flops=2 * 10**9, bytes_accessed=6 * 2**20, transcendentals=0),
         name="share",
-    )(at, packed, *pieces, basis, prev)
+    )(me, packed, *pieces, rows_own, rows_prev)
 
 
 def finish_kernel(arrived, weight_in, gain, grad_in, grad_out, grad_gain, shares, sem):
@@ -563,16 +544,13 @@
     answered = lax.all_to_all(found, DP, split_axis=0, concat_axis=0, tiled=True)
 
     crossed = cross_products(x_at, basis, weight_in, norm_gain, prev_x, found)
-    gained, own = weights(basis, weight_in, norm_gain, weight_out, crossed)
+    crossed = sum_over_x(crossed)
+    mats = gather_peers(crossed)
+
+    part, turned = place_rows(place, answered.reshape(shards * CAP, cols), group, (crossed,))
+    gained, own = weights(basis, weight_in, norm_gain, weight_out, (part,))
     owns = gather_peers(own)
-    mats = gather_peers(sum_over_x(crossed))
-
-    part, turned = place_rows(
-        place,
-        answered.reshape(shards * CAP, cols),
-        group,
-        (*owns[1:], mats[2]),
-    )
+    turned = ordered(turned, mats[2])
     pieces = gather_peers(part)
     turned = lax.all_to_all(turned, GATHER, split_axis=0, concat_axis=0, tiled=True)
     pq, square = project(me, pieces, basis, gained, turned, mats[2])
@@ -581,10 +559,9 @@
 
     sent, packed = chain(me, coef_cotangent, square, pqs, owns, mats, d, group)
     packed = lax.all_to_all(packed, GATHER, split_axis=0, concat_axis=0, tiled=True)
-    at = jnp.stack([section, zl, x]).astype(jnp.int32)
-    shares = share(
-        at, packed, turned, basis.reshape(4, 2, 4, 2 * block, r), prev_x.reshape(4, 2, 2 * block, r)
-    )
+    rows_own = lax.dynamic_index_in_dim(rows_x.reshape(4, 2, 2 * block, r), zl, 1, False)
+    rows_prev = lax.dynamic_index_in_dim(prev_x.reshape(4, 2, 2 * block, r), zl, 1, False)
+    shares = share(me, packed, turned, rows_own, rows_prev)
     shares = lax.all_to_all(shares, REDUCE, split_axis=0, concat_axis=0, tiled=True)
     in_block = lax.dynamic_slice_in_dim(weight_in, dp * block, block, 0)
     gain_block = lax.dynamic_slice_in_dim(norm_gain, dp * block, block, 1)

time: 167 us -> 173 us (1.036)
  local copies, waits for them, and re-layouts: 6.56 us -> 19.2 us
  starting transfers between devices: 55.5 us -> 48.1 us
  waiting for transfers between devices: 44.8 us -> 50.4 us
  Pallas kernels: 33.7 us -> 28.3 us
    unnamed x24 -> x28, local copies, waits for them, and re-layouts: 3.82 us -> 14.2 us
    ppermute x3, waiting for transfers between devices: 3.93 us -> 13.7 us  [sum_over_x(): lax.ppermute(v, X, [(i, (i + k) % 4) for i in range(4)]).astype(F32)]
    all_to_all x1, waiting for transfers between devices: 4.51 us -> 0.17 us  [per_device(): lax.all_to_all(packed, GATHER, split_axis=0, concat_axis=0, tiled=True)]
    ppermute x15, starting transfers between devices: 20.8 us -> 16.9 us  [swap(): return lax.ppermute(x, axis, [(0, 1), (1, 0)])]
    ppermute x15, waiting for transfers between devices: 18.4 us -> 15.1 us  [swap(): return lax.ppermute(x, axis, [(0, 1), (1, 0)])]
    pallas_call x1, Pallas kernels: 7.14 us -> 3.87 us  [weights(): pl.pallas_call(weights_kernel, grid=(steps,), in_specs=[pl.BlockSpec((row...]
    squeeze x0 -> x2, local copies, waits for them, and re-layouts: none -> 2.96 us  [the longest x1 1.89 us: per_device(): lax.dynamic_index_in_dim(prev_x.reshape(4, 2, 2 * block, r), zl, 1, False)]
    all_to_all x1, waiting for transfers between devices: 0.82 us -> 3.5 us  [per_device(): lax.all_to_all(found, DP, split_axis=0, concat_axis=0, tiled=True)]
  transfers between devices with their start and end apart: 23 -> 23, of which waited for: 11 -> 9; matrix products, arithmetic and copies ran while one was open for 2% -> 3% of each run, Pallas kernels for 8% -> 8%
where the time goes in v4:
time: 173 us; the launch traced here: 171 us
  waiting for transfers between devices  50.4 us (29%)
  starting transfers between devices  48.1 us (28%)
  Pallas kernels  28.3 us (16%)
  blocking collectives  23.5 us (14%)
  local copies, waits for them, and re-layouts  19.2 us (11%)
    all_to_all x1, blocking collectives, per_device(): lax.all_to_all(requests, DP, split_axis=0, concat_axis=0, tiled=True)  23.5 us
    all_to_all x1, waiting for transfers between devices, per_device(): lax.all_to_all(shares, REDUCE, split_axis=0, concat_axis=0, tiled=True)  17.9 us
    ppermute x15, starting transfers between devices, swap(): return lax.ppermute(x, axis, [(0, 1), (1, 0)])  16.9 us
    ppermute x15, waiting for transfers between devices, swap(): return lax.ppermute(x, axis, [(0, 1), (1, 0)])  15.1 us
    unnamed x28, local copies, waits for them, and re-layouts  14.2 us
    ppermute x3, waiting for transfers between devices, sum_over_x(): lax.ppermute(v, X, [(i, (i + k) % 4) for i in range(4)]).astype(F32)  13.7 us
    all_to_all x1, starting transfers between devices, per_device(): lax.all_to_all(shares, REDUCE, split_axis=0, concat_axis=0, tiled=True)  6.55 us
    all_to_all x1, starting transfers between devices, per_device(): lax.all_to_all(found, DP, split_axis=0, concat_axis=0, tiled=True)  6.06 us
  transfers between devices with their start and end apart: 23, of which 9 were waited for; matrix products, arithmetic and copies ran while one was open for 3% of the time, Pallas kernels for 8%

profile of v4, /device:TPU:33, one launch (start us, length us, event | category | flops | bytes accessed | tf_op | source)
XLA Modules:
  0.0 171.4 jit_solution(14085025000354006016)
XLA Ops:
  0.6 2.9 %request.1 = (s32[128,1]{1,0:T(8,128)}, s32[64,4]{1,0:T(8,128)}, bf16[8,256,256]{2,1,0:T(8,128)(2,1)}) custom-call(s32[1]{0:T(128)} %bitcast.1.at, s32[1,128]{1,0:T(1,128)} %bitcast.41, bf16[8,4,256,256]{3,2,1,0:T(8,128)(2,1)} %bitcast.28), custom_call_target="tpu_custom_call" | custom-call | flops 10000000 | bytes 2097152 | tf_op jit(solution)/shard_map/request/pallas_call | solution.py:213
  3.5 3.8 %collective-permute-start = (bf16[8,256,256]{2,1,0:T(8,128)(2,1)}, bf16[8,256,256]{2,1,0:T(8,128)(2,1)}, u32[]{:S(2)}, u32[]{:S(2)}) collective-permute-start(bf16[8,256,256]{2,1,0:T(8,128)(2,1)} %get-tuple-element.20), channel_id=1, source_target_pairs={{0,64},{64,128},{128,192},{1,65},{65,129},{129,193},{2,66},{66,130... | collective-permute-start | bytes 3145736 | tf_op jit(solution)/shard_map/ppermute | solution.py:541
  7.3 23.5 %all_to_all.31 = s32[64,1,4]{2,1,0:T(1,128)} all-to-all(s32[64,1,4]{2,1,0:T(1,128)} %bitcast.40), channel_id=1, replica_groups=mesh['yl'=2,'co'=2,'zh'=4,'zl'=2,'x'=4,'yh'=2] {'zh','zl','x','yh'}, dimensions={0} | all-to-all | bytes 2048 | tf_op jit(solution)/shard_map/all_to_all | solution.py:542
  30.8 4.5 %pick_rows.1.after = bf16[64,4,2048]{2,1,0:T(4,128)(2,1)} custom-call(s32[64,4]{1,0:T(8,128)} %bitcast.39, bf16[1008,2048]{1,0:T(8,128)(2,1)} %table.1, bf16[8,256,256]{2,1,0:T(8,128)(2,1)} %collective-permute-done.refs_0_.prev), custom_call_target="tpu_custom_call" | custom-call | flops 1056964608 | bytes 5177344 | tf_op jit(solution)/shard_map/pick_rows/pallas_call | solution.py:266
  35.3 6.1 %all-to-all-start.1 = ((bf16[64,4,2048]{2,1,0:T(4,128)(2,1)}), bf16[64,4,2048]{2,1,0:T(4,128)(2,1)}, u32[]{:S(2)}, u32[]{:S(2)}) async-start(bf16[64,4,2048]{2,1,0:T(4,128)(2,1)} %pick_rows.1.after), calls=%async_computation.1 | async-start | bytes 2097152 | tf_op jit(solution)/shard_map/all_to_all | solution.py:544
  41.4 4.7 %cross_products.1 = bf16[256,384]{1,0:T(8,128)(2,1)} custom-call(s32[1]{0:T(128)} %bitcast.1.at, bf16[8,4,256,256]{3,2,1,0:T(8,128)(2,1)} %bitcast.29, bf16[8,4,256,128]{3,2,1,0:T(8,128)(2,1)} %bitcast.32, f32[1,8192]{1,0:T(1,128)} %gain.3, bf16[8,256,256]{2,1,0:T(8,128)(2,1)} %collective-permute-done.refs_0_.prev, bf16[64,4,2048]{2,1,0:T(4,128)(2,1)} %pick_rows.1.after), custom_call_target="tpu_custom_call" | custom-call | flops 402653184 | bytes 2621440 | tf_op jit(solution)/shard_map/cross_products/pallas_call | solution.py:136
  46.0 1.3 collective-permute-start.1
  47.3 2.4 %collective-permute-start.2 = (bf16[256,384]{1,0:T(8,128)(2,1)}, bf16[256,384]{1,0:T(8,128)(2,1)S(1)}, u32[]{:S(2)}, u32[]{:S(2)}) collective-permute-start(bf16[256,384]{1,0:T(8,128)(2,1)} %cross_products.1), channel_id=1, source_target_pairs={{0,4},{2,6},{4,0},{6,2},{1,5},{3,7},{5,1},{7,3},{8,12},{10,14},{12... | collective-permute-start | bytes 589832 | tf_op jit(solution)/shard_map/ppermute | solution.py:160
  49.7 1.2 collective-permute-start.3
  50.9 6.5 %collective-permute-done.1 = bf16[256,384]{1,0:T(8,128)(2,1)S(1)} collective-permute-done((bf16[256,384]{1,0:T(8,128)(2,1)}, bf16[256,384]{1,0:T(8,128)(2,1)S(1)}, u32[]{:S(2)}, u32[]{:S(2)}) %collective-permute-start.1) | collective-permute-done | bytes 196640 | tf_op jit(solution)/shard_map/ppermute | solution.py:160
  57.4 7.2 %collective-permute-done.2 = bf16[256,384]{1,0:T(8,128)(2,1)S(1)} collective-permute-done((bf16[256,384]{1,0:T(8,128)(2,1)}, bf16[256,384]{1,0:T(8,128)(2,1)S(1)}, u32[]{:S(2)}, u32[]{:S(2)}) %collective-permute-start.2) | collective-permute-done | bytes 196640 | tf_op jit(solution)/shard_map/ppermute | solution.py:160
  64.6 0.0 collective-permute-done.3
  64.6 1.0 add_convert_fusion.refs_0_.m0
  65.6 0.1 collective-permute-start.7
  65.7 3.5 %all-to-all-done.1 = bf16[64,4,2048]{2,1,0:T(4,128)(2,1)} async-done(((bf16[64,4,2048]{2,1,0:T(4,128)(2,1)}), bf16[64,4,2048]{2,1,0:T(4,128)(2,1)}, u32[]{:S(2)}, u32[]{:S(2)}) %all-to-all-start.1) | async-done | bytes 1048608 | tf_op jit(solution)/shard_map/all_to_all | solution.py:544
  69.2 1.3 reshape.35.answered
  70.6 0.0 copy-start.2
  70.6 0.0 copy-start.12
  70.6 1.0 copy-done.12
  71.6 1.2 place_rows.1
  72.7 0.8 copy-done.6
  73.5 0.7 copy-done.8
  74.2 4.9 %all-to-all-start.2 = ((bf16[8,128,256]{2,1,0:T(8,128)(2,1)}), bf16[8,128,256]{2,1,0:T(8,128)(2,1)S(1)}, u32[]{:S(2)}, u32[]{:S(2)}) async-start(bf16[8,128,256]{2,1,0:T(8,128)(2,1)} %ordered.1), calls=%async_computation.2 | async-start | bytes 1048576 | tf_op jit(solution)/shard_map/all_to_all | solution.py:555
  79.2 3.0 %collective-permute-start.4 = (bf16[128,2048]{1,0:T(8,128)(2,1)}, bf16[128,2048]{1,0:T(8,128)(2,1)}, u32[]{:S(2)}, u32[]{:S(2)}) collective-permute-start(bf16[128,2048]{1,0:T(8,128)(2,1)} %get-tuple-element.21.refs_0_.p0), channel_id=1, source_target_pairs={{0,64},{64,0},{1,65},{65,1},{2,66},{66,2},{3,67},{67,3},{4,68},{68... | collective-permute-start | bytes 1572872 | tf_op jit(solution)/shard_map/ppermute | solution.py:34
  82.1 1.6 collective-permute-done.5.p2
  83.7 4.5 %collective-permute-start.6 = (bf16[128,2048]{1,0:T(8,128)(2,1)}, bf16[128,2048]{1,0:T(8,128)(2,1)}, u32[]{:S(2)}, u32[]{:S(2)}) collective-permute-start(bf16[128,2048]{1,0:T(8,128)(2,1)} %collective-permute-done.5.p2), channel_id=1, source_target_pairs={{0,64},{64,0},{1,65},{65,1},{2,66},{66,2},{3,67},{67,3},{4,68},{68... | collective-permute-start | bytes 1572872 | tf_op jit(solution)/shard_map/ppermute | solution.py:34
  88.2 0.0 collective-permute-start.14
  88.2 2.2 %copy-done = bf16[1,8192,256]{2,1,0:T(8,128)(2,1)S(1)} copy-done((bf16[1,8192,256]{2,1,0:T(8,128)(2,1)S(1)}, bf16[1,8192,256]{2,1,0:T(8,128)(2,1)}, u32[]{:S(2)}) %copy-start) | copy-done | bytes 4194328
  90.4 1.6 copy-done.3
  92.0 0.8 copy-done.11
  92.7 3.9 %weights.1 = (bf16[8192,128]{1,0:T(8,128)(2,1)S(1)}, bf16[384,256]{1,0:T(8,128)(2,1)S(1)}) custom-call(bf16[8192,256]{1,0:T(8,128)(2,1)S(1)} %bitcast.30, bf16[8192,128]{1,0:T(8,128)(2,1)S(1)} %bitcast.33, f32[1,8192]{1,0:T(1,128)S(1)} %copy-done.11, bf16[128,8192]{1,0:T(8,128)(2,1)S(1)} %bitcast.34, bf16[128,2048]{1,0:T(8,128)(2,1)} %get-tuple-element.21.refs_0_.p0), custom_call_target="tpu_custom_call" | custom-call | flops 1610612736 | bytes 12582912 | tf_op jit(solution)/shard_map/weights/pallas_call | solution.py:83
  96.6 1.3 copy-done.4
  98.0 0.0 collective-permute-start.12
  98.0 0.0 collective-permute-done.6.p3
  98.0 0.0 copy-start.1
  98.0 2.2 %copy-done.1 = bf16[1,8192,256]{2,1,0:T(8,128)(2,1)S(1)} copy-done((bf16[1,8192,256]{2,1,0:T(8,128)(2,1)S(1)}, bf16[1,8192,256]{2,1,0:T(8,128)(2,1)}, u32[]{:S(2)}) %copy-start.1) | copy-done | bytes 4194328
  100.2 1.6 copy-done.5
  101.8 3.4 %project.1 = (f32[128,384]{1,0:T(8,128)S(1)}, f32[128,128]{1,0:T(8,128)S(1)}) custom-call(s32[1]{0:T(128)} %bitcast.me.me_ref, bf16[128,2048]{1,0:T(8,128)(2,1)} %get-tuple-element.21.refs_0_.p0, bf16[128,2048]{1,0:T(8,128)(2,1)} %collective-permute-done.4.p1, bf16[128,2048]{1,0:T(8,128)(2,1)} %collective-permute-done.5.p2, ...), custom_call_target="tpu_custom_call" | custom-call | flops 805306368 | bytes 8388608 | tf_op jit(solution)/shard_map/project/pallas_call | solution.py:342
  105.2 1.5 collective-permute-start.9
  106.7 1.1 collective-permute-start.15
  107.8 0.0 collective-permute-start.11
  107.8 0.0 collective-permute-done.12.g2
  107.8 0.5 collective-permute-start.13
  108.3 0.1 collective-permute-start.8
  108.4 2.5 %collective-permute-done.9.q2 = f32[128,384]{1,0:T(8,128)S(1)} collective-permute-done((f32[128,384]{1,0:T(8,128)S(1)}, f32[128,384]{1,0:T(8,128)S(1)}, u32[]{:S(2)}, u32[]{:S(2)}) %collective-permute-start.9) | collective-permute-done | bytes 196640 | tf_op jit(solution)/shard_map/ppermute | solution.py:34
  110.9 1.7 collective-permute-start.10
  112.6 0.0 collective-permute-done.15.m3
  112.6 1.0 collective-permute-done.10.q3
  113.7 3.5 %chain.1 = (bf16[128,256]{1,0:T(8,128)(2,1)}, bf16[8,128,640]{2,1,0:T(8,128)(2,1)S(1)}) custom-call(s32[1]{0:T(128)} %bitcast.me.me_ref, bf16[128,256]{1,0:T(8,128)(2,1)S(1)} %copy-done.13, f32[128,128]{1,0:T(8,128)S(1)} %get-tuple-element.24.square, f32[128,384]{1,0:T(8,128)S(1)} %get-tuple-element.25.q0, f32[128,384]{1,0:T(8,128)S(1)} %collective-permute-done.8.q1, ...), custom_call_target="tpu_custom_call" | custom-call | flops 4000000000 | bytes 6291456 | tf_op jit(solution)/shard_map/chain/pallas_call | solution.py:426
  117.2 1.1 copy-done.7
  118.3 4.9 %all-to-all-start.3 = ((bf16[8,128,640]{2,1,0:T(8,128)(2,1)}), bf16[8,128,640]{2,1,0:T(8,128)(2,1)}, u32[]{:S(2)}, u32[]{:S(2)}) async-start(bf16[8,128,640]{2,1,0:T(8,128)(2,1)} %copy-done.7), calls=%async_computation.3 | async-start | bytes 2621440 | tf_op jit(solution)/shard_map/all_to_all | solution.py:561
  123.2 1.5 collective-permute-start.17
  124.7 1.2 collective-permute-start.16
  125.9 9.9 %collective-permute-done.17.t2 = bf16[1024,256]{1,0:T(8,128)(2,1)} collective-permute-done((bf16[1024,256]{1,0:T(8,128)(2,1)S(1)}, bf16[1024,256]{1,0:T(8,128)(2,1)}, u32[]{:S(2)}, u32[]{:S(2)}) %collective-permute-start.17) | collective-permute-done | bytes 524320 | tf_op jit(solution)/shard_map/ppermute | solution.py:34
  135.8 1.8 %collective-permute-start.18 = (bf16[1024,256]{1,0:T(8,128)(2,1)}, bf16[1024,256]{1,0:T(8,128)(2,1)}, u32[]{:S(2)}, u32[]{:S(2)}) collective-permute-start(bf16[1024,256]{1,0:T(8,128)(2,1)} %collective-permute-done.17.t2), channel_id=1, source_target_pairs={{0,64},{64,0},{1,65},{65,1},{2,66},{66,2},{3,67},{67,3},{4,68},{68... | collective-permute-start | bytes 1572872 | tf_op jit(solution)/shard_map/ppermute | solution.py:34
  137.6 1.1 dynamic-slice_bitcast_fusion.1.rows_own
  138.7 1.9 %dynamic-slice_bitcast_fusion.rows_prev = bf16[4,256,256]{2,1,0:T(8,128)(2,1)} fusion(bf16[4,2,256,256]{3,2,1,0:T(8,128)(2,1)} %bitcast.15, s32[]{:T(128)S(6)} %select_n.9), kind=kLoop, calls=%fused_computation | loop fusion | bytes 1048580 | tf_op jit(solution)/shard_map/jit(dynamic_index_in_dim)/squeeze | solution.py:563
  140.6 0.2 all-to-all-done.3.packed
  140.8 1.0 copy-done.10
  141.8 3.5 %share.1 = bf16[8,256,128]{2,1,0:T(8,128)(2,1)} custom-call(s32[1]{0:T(128)} %bitcast.me.me_ref, bf16[8,128,640]{2,1,0:T(8,128)(2,1)} %all-to-all-done.3.packed, bf16[1024,256]{1,0:T(8,128)(2,1)S(1)} %bitcast.37, bf16[1024,256]{1,0:T(8,128)(2,1)} %collective-permute-done.16.t1, bf16[1024,256]{1,0:T(8,128)(2,1)} %collective-permute-done.17.t2, ...), custom_call_target="tpu_custom_call" | custom-call | flops 2000000000 | bytes 6291456 | tf_op jit(solution)/shard_map/share/pallas_call | solution.py:479
  145.3 6.6 %all-to-all-start.4 = ((bf16[8,256,128]{2,1,0:T(8,128)(2,1)}), bf16[8,256,128]{2,1,0:T(8,128)(2,1)S(1)}, u32[]{:S(2)}, u32[]{:S(2)}) async-start(bf16[8,256,128]{2,1,0:T(8,128)(2,1)} %share.1), calls=%async_computation.4 | async-start | bytes 1048576 | tf_op jit(solution)/shard_map/all_to_all | solution.py:565
  151.9 0.7 constant_dynamic-slice_fusion.gain
  152.6 17.9 %all-to-all-done.4.arrived = bf16[8,256,128]{2,1,0:T(8,128)(2,1)S(1)} async-done(((bf16[8,256,128]{2,1,0:T(8,128)(2,1)}), bf16[8,256,128]{2,1,0:T(8,128)(2,1)S(1)}, u32[]{:S(2)}, u32[]{:S(2)}) %all-to-all-start.4) | async-done | bytes 524320 | tf_op jit(solution)/shard_map/all_to_all | solution.py:565
  170.5 0.8 finish.1
  (27 shorter events, 0.1 us)
Async XLA Ops:
  3.5 27.2 %collective-permute-start = (bf16[8,256,256]{2,1,0:T(8,128)(2,1)}, bf16[8,256,256]{2,1,0:T(8,128)(2,1)}, u32[]{:S(2)}, u32[]{:S(2)}) collective-permute-start(bf16[8,256,256]{2,1,0:T(8,128)(2,1)} %get-tuple-element.20), channel_id=1, source_target_pairs={{0,64},{64,128},{128,192},{1,65},{65,129},{129,193},{2,66},{66,130... | collective-permute-start | bytes 3145736 | tf_op jit(solution)/shard_map/ppermute | solution.py:541
  35.3 33.9 %all-to-all-start.1 = ((bf16[64,4,2048]{2,1,0:T(4,128)(2,1)}), bf16[64,4,2048]{2,1,0:T(4,128)(2,1)}, u32[]{:S(2)}, u32[]{:S(2)}) async-start(bf16[64,4,2048]{2,1,0:T(4,128)(2,1)} %pick_rows.1.after), calls=%async_computation.1 | async-start | bytes 2097152 | tf_op jit(solution)/shard_map/all_to_all | solution.py:544
  46.0 11.3 %collective-permute-start.1 = (bf16[256,384]{1,0:T(8,128)(2,1)}, bf16[256,384]{1,0:T(8,128)(2,1)S(1)}, u32[]{:S(2)}, u32[]{:S(2)}) collective-permute-start(bf16[256,384]{1,0:T(8,128)(2,1)} %cross_products.1), channel_id=1, source_target_pairs={{0,2},{2,4},{4,6},{6,0},{1,3},{3,5},{5,7},{7,1},{8,10},{10,12},{12... | collective-permute-start | bytes 589832 | tf_op jit(solution)/shard_map/ppermute | solution.py:160
  47.3 17.3 %collective-permute-start.2 = (bf16[256,384]{1,0:T(8,128)(2,1)}, bf16[256,384]{1,0:T(8,128)(2,1)S(1)}, u32[]{:S(2)}, u32[]{:S(2)}) collective-permute-start(bf16[256,384]{1,0:T(8,128)(2,1)} %cross_products.1), channel_id=1, source_target_pairs={{0,4},{2,6},{4,0},{6,2},{1,5},{3,7},{5,1},{7,3},{8,12},{10,14},{12... | collective-permute-start | bytes 589832 | tf_op jit(solution)/shard_map/ppermute | solution.py:160
  49.7 14.9 %collective-permute-start.3 = (bf16[256,384]{1,0:T(8,128)(2,1)}, bf16[256,384]{1,0:T(8,128)(2,1)S(1)}, u32[]{:S(2)}, u32[]{:S(2)}) collective-permute-start(bf16[256,384]{1,0:T(8,128)(2,1)} %cross_products.1), channel_id=1, source_target_pairs={{0,6},{2,0},{4,2},{6,4},{1,7},{3,1},{5,3},{7,5},{8,14},{10,8},{12,... | collective-permute-start | bytes 589832 | tf_op jit(solution)/shard_map/ppermute | solution.py:160
  65.6 7.9 %collective-permute-start.7 = (bf16[256,384]{1,0:T(8,128)(2,1)S(1)}, bf16[256,384]{1,0:T(8,128)(2,1)S(1)}, u32[]{:S(2)}, u32[]{:S(2)}) collective-permute-start(bf16[256,384]{1,0:T(8,128)(2,1)S(1)} %add_convert_fusion.refs_0_.m0), channel_id=1, source_target_pairs={{0,128},{128,0},{1,129},{129,1},{2,130},{130,2},{3,131},{131,3},{4... | collective-permute-start | bytes 589832 | tf_op jit(solution)/shard_map/ppermute | solution.py:34
  70.6 17.6 %copy-start.2 = (bf16[1,8192,128]{2,1,0:T(8,128)(2,1)S(1)}, bf16[1,8192,128]{2,1,0:T(8,128)(2,1)}, u32[]{:S(2)}) copy-start(bf16[1,8192,128]{2,1,0:T(8,128)(2,1)} %param.10) | copy-start | bytes 6291460
  70.6 1.0 copy-start.12
  72.7 0.8 copy-start.6
  73.5 10.2 %collective-permute-start.5 = (bf16[128,2048]{1,0:T(8,128)(2,1)}, bf16[128,2048]{1,0:T(8,128)(2,1)}, u32[]{:S(2)}, u32[]{:S(2)}) collective-permute-start(bf16[128,2048]{1,0:T(8,128)(2,1)} %get-tuple-element.21.refs_0_.p0), channel_id=1, source_target_pairs={{0,128},{128,0},{1,129},{129,1},{2,130},{130,2},{3,131},{131,3},{4... | collective-permute-start | bytes 1572872 | tf_op jit(solution)/shard_map/ppermute | solution.py:34
  73.5 0.7 copy-start.8
  74.2 23.8 %all-to-all-start.2 = ((bf16[8,128,256]{2,1,0:T(8,128)(2,1)}), bf16[8,128,256]{2,1,0:T(8,128)(2,1)S(1)}, u32[]{:S(2)}, u32[]{:S(2)}) async-start(bf16[8,128,256]{2,1,0:T(8,128)(2,1)} %ordered.1), calls=%async_computation.2 | async-start | bytes 1048576 | tf_op jit(solution)/shard_map/all_to_all | solution.py:555
  79.2 18.8 %collective-permute-start.4 = (bf16[128,2048]{1,0:T(8,128)(2,1)}, bf16[128,2048]{1,0:T(8,128)(2,1)}, u32[]{:S(2)}, u32[]{:S(2)}) collective-permute-start(bf16[128,2048]{1,0:T(8,128)(2,1)} %get-tuple-element.21.refs_0_.p0), channel_id=1, source_target_pairs={{0,64},{64,0},{1,65},{65,1},{2,66},{66,2},{3,67},{67,3},{4,68},{68... | collective-permute-start | bytes 1572872 | tf_op jit(solution)/shard_map/ppermute | solution.py:34
  83.7 14.2 %collective-permute-start.6 = (bf16[128,2048]{1,0:T(8,128)(2,1)}, bf16[128,2048]{1,0:T(8,128)(2,1)}, u32[]{:S(2)}, u32[]{:S(2)}) collective-permute-start(bf16[128,2048]{1,0:T(8,128)(2,1)} %collective-permute-done.5.p2), channel_id=1, source_target_pairs={{0,64},{64,0},{1,65},{65,1},{2,66},{66,2},{3,67},{67,3},{4,68},{68... | collective-permute-start | bytes 1572872 | tf_op jit(solution)/shard_map/ppermute | solution.py:34
  88.2 20.1 %collective-permute-start.14 = (bf16[256,384]{1,0:T(8,128)(2,1)S(1)}, bf16[256,384]{1,0:T(8,128)(2,1)S(1)}, u32[]{:S(2)}, u32[]{:S(2)}) collective-permute-start(bf16[256,384]{1,0:T(8,128)(2,1)S(1)} %add_convert_fusion.refs_0_.m0), channel_id=1, source_target_pairs={{0,64},{64,0},{1,65},{65,1},{2,66},{66,2},{3,67},{67,3},{4,68},{68... | collective-permute-start | bytes 589832 | tf_op jit(solution)/shard_map/ppermute | solution.py:34
  88.2 2.2 %copy-start = (bf16[1,8192,256]{2,1,0:T(8,128)(2,1)S(1)}, bf16[1,8192,256]{2,1,0:T(8,128)(2,1)}, u32[]{:S(2)}) copy-start(bf16[1,8192,256]{2,1,0:T(8,128)(2,1)} %param.9) | copy-start | bytes 12582916
  90.4 1.6 copy-start.3
  92.0 0.8 copy-start.11
  92.7 5.3 %copy-start.9 = (bf16[256,384]{1,0:T(8,128)(2,1)S(1)}, bf16[256,384]{1,0:T(8,128)(2,1)}, u32[]{:S(2)}) copy-start(bf16[256,384]{1,0:T(8,128)(2,1)} %copy-done.8) | copy-start | bytes 589828
  96.6 1.3 copy-start.4
  98.0 9.8 %collective-permute-start.12 = (bf16[384,256]{1,0:T(8,128)(2,1)S(1)}, bf16[384,256]{1,0:T(8,128)(2,1)}, u32[]{:S(2)}, u32[]{:S(2)}) collective-permute-start(bf16[384,256]{1,0:T(8,128)(2,1)S(1)} %get-tuple-element.26.g0), channel_id=1, source_target_pairs={{0,128},{128,0},{1,129},{129,1},{2,130},{130,2},{3,131},{131,3},{4... | collective-permute-start | bytes 589832 | tf_op jit(solution)/shard_map/ppermute | solution.py:34
  98.0 2.2 %copy-start.1 = (bf16[1,8192,256]{2,1,0:T(8,128)(2,1)S(1)}, bf16[1,8192,256]{2,1,0:T(8,128)(2,1)}, u32[]{:S(2)}) copy-start(bf16[1,8192,256]{2,1,0:T(8,128)(2,1)} %param.9) | copy-start | bytes 12582916
  100.2 1.6 copy-start.5
  101.8 11.9 %copy-start.13 = (bf16[128,256]{1,0:T(8,128)(2,1)S(1)}, bf16[128,256]{1,0:T(8,128)(2,1)}, u32[]{:S(2)}) copy-start(bf16[128,256]{1,0:T(8,128)(2,1)} %cot.1) | copy-start | bytes 196612
  105.2 5.7 %collective-permute-start.9 = (f32[128,384]{1,0:T(8,128)S(1)}, f32[128,384]{1,0:T(8,128)S(1)}, u32[]{:S(2)}, u32[]{:S(2)}) collective-permute-start(f32[128,384]{1,0:T(8,128)S(1)} %get-tuple-element.25.q0), channel_id=1, source_target_pairs={{0,128},{128,0},{1,129},{129,1},{2,130},{130,2},{3,131},{131,3},{4... | collective-permute-start | bytes 589832 | tf_op jit(solution)/shard_map/ppermute | solution.py:34
  106.7 5.9 %collective-permute-start.15 = (bf16[256,384]{1,0:T(8,128)(2,1)S(1)}, bf16[256,384]{1,0:T(8,128)(2,1)S(1)}, u32[]{:S(2)}, u32[]{:S(2)}) collective-permute-start(bf16[256,384]{1,0:T(8,128)(2,1)S(1)} %copy-done.9), channel_id=1, source_target_pairs={{0,64},{64,0},{1,65},{65,1},{2,66},{66,2},{3,67},{67,3},{4,68},{68... | collective-permute-start | bytes 589832 | tf_op jit(solution)/shard_map/ppermute | solution.py:34
  107.8 4.8 %collective-permute-start.11 = (bf16[384,256]{1,0:T(8,128)(2,1)S(1)}, bf16[384,256]{1,0:T(8,128)(2,1)S(1)}, u32[]{:S(2)}, u32[]{:S(2)}) collective-permute-start(bf16[384,256]{1,0:T(8,128)(2,1)S(1)} %get-tuple-element.26.g0), channel_id=1, source_target_pairs={{0,64},{64,0},{1,65},{65,1},{2,66},{66,2},{3,67},{67,3},{4,68},{68... | collective-permute-start | bytes 589832 | tf_op jit(solution)/shard_map/ppermute | solution.py:34
  107.8 4.8 %collective-permute-start.13 = (bf16[384,256]{1,0:T(8,128)(2,1)}, bf16[384,256]{1,0:T(8,128)(2,1)S(1)}, u32[]{:S(2)}, u32[]{:S(2)}) collective-permute-start(bf16[384,256]{1,0:T(8,128)(2,1)} %collective-permute-done.12.g2), channel_id=1, source_target_pairs={{0,64},{64,0},{1,65},{65,1},{2,66},{66,2},{3,67},{67,3},{4,68},{68... | collective-permute-start | bytes 589832 | tf_op jit(solution)/shard_map/ppermute | solution.py:34
  108.3 4.3 %collective-permute-start.8 = (f32[128,384]{1,0:T(8,128)S(1)}, f32[128,384]{1,0:T(8,128)S(1)}, u32[]{:S(2)}, u32[]{:S(2)}) collective-permute-start(f32[128,384]{1,0:T(8,128)S(1)} %get-tuple-element.25.q0), channel_id=1, source_target_pairs={{0,64},{64,0},{1,65},{65,1},{2,66},{66,2},{3,67},{67,3},{4,68},{68... | collective-permute-start | bytes 589832 | tf_op jit(solution)/shard_map/ppermute | solution.py:34
  110.9 2.7 %collective-permute-start.10 = (f32[128,384]{1,0:T(8,128)S(1)}, f32[128,384]{1,0:T(8,128)S(1)}, u32[]{:S(2)}, u32[]{:S(2)}) collective-permute-start(f32[128,384]{1,0:T(8,128)S(1)} %collective-permute-done.9.q2), channel_id=1, source_target_pairs={{0,64},{64,0},{1,65},{65,1},{2,66},{66,2},{3,67},{67,3},{4,68},{68... | collective-permute-start | bytes 589832 | tf_op jit(solution)/shard_map/ppermute | solution.py:34
  117.2 1.1 copy-start.7
  118.3 22.5 %all-to-all-start.3 = ((bf16[8,128,640]{2,1,0:T(8,128)(2,1)}), bf16[8,128,640]{2,1,0:T(8,128)(2,1)}, u32[]{:S(2)}, u32[]{:S(2)}) async-start(bf16[8,128,640]{2,1,0:T(8,128)(2,1)} %copy-done.7), calls=%async_computation.3 | async-start | bytes 2621440 | tf_op jit(solution)/shard_map/all_to_all | solution.py:561
  123.2 12.6 %collective-permute-start.17 = (bf16[1024,256]{1,0:T(8,128)(2,1)S(1)}, bf16[1024,256]{1,0:T(8,128)(2,1)}, u32[]{:S(2)}, u32[]{:S(2)}) collective-permute-start(bf16[1024,256]{1,0:T(8,128)(2,1)S(1)} %bitcast.35), channel_id=1, source_target_pairs={{0,128},{128,0},{1,129},{129,1},{2,130},{130,2},{3,131},{131,3},{4... | collective-permute-start | bytes 1572872 | tf_op jit(solution)/shard_map/ppermute | solution.py:34
  124.7 16.0 %collective-permute-start.16 = (bf16[1024,256]{1,0:T(8,128)(2,1)S(1)}, bf16[1024,256]{1,0:T(8,128)(2,1)}, u32[]{:S(2)}, u32[]{:S(2)}) collective-permute-start(bf16[1024,256]{1,0:T(8,128)(2,1)S(1)} %bitcast.36), channel_id=1, source_target_pairs={{0,64},{64,0},{1,65},{65,1},{2,66},{66,2},{3,67},{67,3},{4,68},{68... | collective-permute-start | bytes 1572872 | tf_op jit(solution)/shard_map/ppermute | solution.py:34
  135.8 4.8 %collective-permute-start.18 = (bf16[1024,256]{1,0:T(8,128)(2,1)}, bf16[1024,256]{1,0:T(8,128)(2,1)}, u32[]{:S(2)}, u32[]{:S(2)}) collective-permute-start(bf16[1024,256]{1,0:T(8,128)(2,1)} %collective-permute-done.17.t2), channel_id=1, source_target_pairs={{0,64},{64,0},{1,65},{65,1},{2,66},{66,2},{3,67},{67,3},{4,68},{68... | collective-permute-start | bytes 1572872 | tf_op jit(solution)/shard_map/ppermute | solution.py:34
  140.8 1.0 copy-start.10
  145.3 25.1 %all-to-all-start.4 = ((bf16[8,256,128]{2,1,0:T(8,128)(2,1)}), bf16[8,256,128]{2,1,0:T(8,128)(2,1)S(1)}, u32[]{:S(2)}, u32[]{:S(2)}) async-start(bf16[8,256,128]{2,1,0:T(8,128)(2,1)} %share.1), calls=%async_computation.4 | async-start | bytes 1048576 | tf_op jit(solution)/shard_map/all_to_all | solution.py:565

commit v5 on v4

--- a/solution.py
+++ b/solution.py
@@ -96,7 +96,7 @@
             jax.ShapeDtypeStruct((r + h, r), BF16),
         ],
         scratch_shapes=[pltpu.VMEM((r + h, r), F32)],
-        compiler_params=pltpu.CompilerParams(vmem_limit_bytes=24 * 2**20),
+        compiler_params=pltpu.CompilerParams(vmem_limit_bytes=GRANT),
         cost_estimate=pl.CostEstimate(
             flops=2 * d * r * (r + h), bytes_accessed=4 * d * (r + h), transcendentals=0
         ),
@@ -544,12 +544,12 @@
     answered = lax.all_to_all(found, DP, split_axis=0, concat_axis=0, tiled=True)
 
     crossed = cross_products(x_at, basis, weight_in, norm_gain, prev_x, found)
+    gained, own = weights(basis, weight_in, norm_gain, weight_out, (crossed,))
+    owns = gather_peers(own)
     crossed = sum_over_x(crossed)
     mats = gather_peers(crossed)
 
-    part, turned = place_rows(place, answered.reshape(shards * CAP, cols), group, (crossed,))
-    gained, own = weights(basis, weight_in, norm_gain, weight_out, (part,))
-    owns = gather_peers(own)
+    part, turned = place_rows(place, answered.reshape(shards * CAP, cols), group, (crossed, gained))
     turned = ordered(turned, mats[2])
     pieces = gather_peers(part)
     turned = lax.all_to_all(turned, GATHER, split_axis=0, concat_axis=0, tiled=True)

time: 173 us -> 168 us (0.971)
  local copies, waits for them, and re-layouts: 19.2 us -> 10.9 us
  waiting for transfers between devices: 50.4 us -> 45.1 us
  starting transfers between devices: 48.1 us -> 53.2 us
  Pallas kernels: 28.3 us -> 32.3 us
    unnamed x28 -> x18, local copies, waits for them, and re-layouts: 14.2 us -> 5.86 us
    all_to_all x1, waiting for transfers between devices: 3.5 us -> 0.01 us  [per_device(): lax.all_to_all(found, DP, split_axis=0, concat_axis=0, tiled=True)]
    pallas_call x1, Pallas kernels: 3.87 us -> 7.12 us  [weights(): pl.pallas_call(weights_kernel, grid=(steps,), in_specs=[pl.BlockSpec((row...]
    ppermute x15, starting transfers between devices: 16.9 us -> 19.1 us  [swap(): return lax.ppermute(x, axis, [(0, 1), (1, 0)])]
  transfers between devices with their start and end apart: 23 -> 23, of which waited for: 9 -> 8; matrix products, arithmetic and copies ran while one was open for 3% -> 4% of each run, Pallas kernels for 8% -> 10%
where the time goes in v5:
time: 168 us; the launch traced here: 167 us
  starting transfers between devices  53.2 us (32%)
  waiting for transfers between devices  45.1 us (27%)
  Pallas kernels  32.3 us (19%)
  blocking collectives  23.6 us (14%)
  local copies, waits for them, and re-layouts  10.9 us (6%)
    all_to_all x1, blocking collectives, per_device(): lax.all_to_all(requests, DP, split_axis=0, concat_axis=0, tiled=True)  23.6 us
    ppermute x15, starting transfers between devices, swap(): return lax.ppermute(x, axis, [(0, 1), (1, 0)])  19.1 us
    all_to_all x1, waiting for transfers between devices, per_device(): lax.all_to_all(shares, REDUCE, split_axis=0, concat_axis=0, tiled=True)  17.1 us
    ppermute x3, waiting for transfers between devices, sum_over_x(): lax.ppermute(v, X, [(i, (i + k) % 4) for i in range(4)]).astype(F32)  13.6 us
    ppermute x15, waiting for transfers between devices, swap(): return lax.ppermute(x, axis, [(0, 1), (1, 0)])  13.5 us
    all_to_all x1, starting transfers between devices, per_device(): lax.all_to_all(shares, REDUCE, split_axis=0, concat_axis=0, tiled=True)  7.35 us
    pallas_call x1, Pallas kernels, weights(): pl.pallas_call(weights_kernel, grid=(steps,), in_specs=[pl.BlockSpec((row...  7.12 us
    all_to_all x1, starting transfers between devices, per_device(): lax.all_to_all(turned, GATHER, split_axis=0, concat_axis=0, tiled=True)  6.22 us
  transfers between devices with their start and end apart: 23, of which 8 were waited for; matrix products, arithmetic and copies ran while one was open for 4% of the time, Pallas kernels for 10%

profile of v5, /device:TPU:33, one launch (start us, length us, event | category | flops | bytes accessed | tf_op | source)
XLA Modules:
  0.0 167.1 jit_solution(18376587605548712746)
XLA Ops:
  0.6 2.9 %request.1 = (s32[128,1]{1,0:T(8,128)}, s32[64,4]{1,0:T(8,128)}, bf16[8,256,256]{2,1,0:T(8,128)(2,1)}) custom-call(s32[1]{0:T(128)} %bitcast.1.at, s32[1,128]{1,0:T(1,128)} %bitcast.41, bf16[8,4,256,256]{3,2,1,0:T(8,128)(2,1)} %bitcast.28), custom_call_target="tpu_custom_call" | custom-call | flops 10000000 | bytes 2097152 | tf_op jit(solution)/shard_map/request/pallas_call | solution.py:213
  3.6 3.8 %collective-permute-start = (bf16[8,256,256]{2,1,0:T(8,128)(2,1)}, bf16[8,256,256]{2,1,0:T(8,128)(2,1)}, u32[]{:S(2)}, u32[]{:S(2)}) collective-permute-start(bf16[8,256,256]{2,1,0:T(8,128)(2,1)} %get-tuple-element.20), channel_id=1, source_target_pairs={{0,64},{64,128},{128,192},{1,65},{65,129},{129,193},{2,66},{66,130... | collective-permute-start | bytes 3145736 | tf_op jit(solution)/shard_map/ppermute | solution.py:541
  7.3 23.6 %all_to_all.31 = s32[64,1,4]{2,1,0:T(1,128)} all-to-all(s32[64,1,4]{2,1,0:T(1,128)} %bitcast.40), channel_id=1, replica_groups=mesh['yl'=2,'co'=2,'zh'=4,'zl'=2,'x'=4,'yh'=2] {'zh','zl','x','yh'}, dimensions={0} | all-to-all | bytes 2048 | tf_op jit(solution)/shard_map/all_to_all | solution.py:542
  30.9 4.6 %pick_rows.1.after = bf16[64,4,2048]{2,1,0:T(4,128)(2,1)} custom-call(s32[64,4]{1,0:T(8,128)} %bitcast.39, bf16[1008,2048]{1,0:T(8,128)(2,1)} %table.1, bf16[8,256,256]{2,1,0:T(8,128)(2,1)} %collective-permute-done.refs_0_.prev), custom_call_target="tpu_custom_call" | custom-call | flops 1056964608 | bytes 5177344 | tf_op jit(solution)/shard_map/pick_rows/pallas_call | solution.py:266
  35.5 5.9 %all-to-all-start.1 = ((bf16[64,4,2048]{2,1,0:T(4,128)(2,1)}), bf16[64,4,2048]{2,1,0:T(4,128)(2,1)}, u32[]{:S(2)}, u32[]{:S(2)}) async-start(bf16[64,4,2048]{2,1,0:T(4,128)(2,1)} %pick_rows.1.after), calls=%async_computation.1 | async-start | bytes 2097152 | tf_op jit(solution)/shard_map/all_to_all | solution.py:544
  41.4 4.7 %cross_products.1.refs_0_ = bf16[256,384]{1,0:T(8,128)(2,1)} custom-call(s32[1]{0:T(128)} %bitcast.1.at, bf16[8,4,256,256]{3,2,1,0:T(8,128)(2,1)} %bitcast.29, bf16[8,4,256,128]{3,2,1,0:T(8,128)(2,1)} %bitcast.35, f32[1,8192]{1,0:T(1,128)} %gain.3, bf16[8,256,256]{2,1,0:T(8,128)(2,1)} %collective-permute-done.refs_0_.prev, bf16[64,4,2048]{2,1,0:T(4,128)(2,1)} %pick_rows.1.after), custom_call_target="tpu_custom_call" | custom-call | flops 402653184 | bytes 2621440 | tf_op jit(solution)/shard_map/cross_products/pallas_call | solution.py:136
  46.1 1.3 collective-permute-start.1
  47.4 2.4 %collective-permute-start.2 = (bf16[256,384]{1,0:T(8,128)(2,1)}, bf16[256,384]{1,0:T(8,128)(2,1)S(1)}, u32[]{:S(2)}, u32[]{:S(2)}) collective-permute-start(bf16[256,384]{1,0:T(8,128)(2,1)} %cross_products.1.refs_0_), channel_id=1, source_target_pairs={{0,4},{2,6},{4,0},{6,2},{1,5},{3,7},{5,1},{7,3},{8,12},{10,14},{12... | collective-permute-start | bytes 589832 | tf_op jit(solution)/shard_map/ppermute | solution.py:160
  49.8 1.2 collective-permute-start.3
  51.0 6.7 %collective-permute-done.1 = bf16[256,384]{1,0:T(8,128)(2,1)S(1)} collective-permute-done((bf16[256,384]{1,0:T(8,128)(2,1)}, bf16[256,384]{1,0:T(8,128)(2,1)S(1)}, u32[]{:S(2)}, u32[]{:S(2)}) %collective-permute-start.1) | collective-permute-done | bytes 196640 | tf_op jit(solution)/shard_map/ppermute | solution.py:160
  57.6 6.9 %collective-permute-done.2 = bf16[256,384]{1,0:T(8,128)(2,1)S(1)} collective-permute-done((bf16[256,384]{1,0:T(8,128)(2,1)}, bf16[256,384]{1,0:T(8,128)(2,1)S(1)}, u32[]{:S(2)}, u32[]{:S(2)}) %collective-permute-start.2) | collective-permute-done | bytes 196640 | tf_op jit(solution)/shard_map/ppermute | solution.py:160
  64.6 0.0 collective-permute-done.3
  64.6 1.0 add_convert_fusion.refs_0_.m0
  65.6 0.1 collective-permute-start.7
  65.7 7.1 %weights.1 = (bf16[8192,128]{1,0:T(8,128)(2,1)}, bf16[384,256]{1,0:T(8,128)(2,1)}) custom-call(bf16[8192,256]{1,0:T(8,128)(2,1)} %bitcast.30, bf16[8192,128]{1,0:T(8,128)(2,1)} %bitcast.36, f32[1,8192]{1,0:T(1,128)} %gain.3, bf16[128,8192]{1,0:T(8,128)(2,1)} %bitcast.37, bf16[256,384]{1,0:T(8,128)(2,1)} %cross_products.1.refs_0_), custom_call_target="tpu_custom_call" | custom-call | flops 1610612736 | bytes 12582912 | tf_op jit(solution)/shard_map/weights/pallas_call | solution.py:83
  72.9 1.5 reshape.35.answered
  74.3 0.4 copy-done.1
  74.8 0.8 copy-done.6
  75.6 1.1 place_rows.1
  76.7 0.8 copy-done.2
  77.5 1.4 collective-permute-start.5
  79.0 0.0 collective-permute-done.7.refs_1_.second.m2
  79.0 0.7 copy-done.3
  79.7 6.2 %all-to-all-start.2 = ((bf16[8,128,256]{2,1,0:T(8,128)(2,1)}), bf16[8,128,256]{2,1,0:T(8,128)(2,1)S(1)}, u32[]{:S(2)}, u32[]{:S(2)}) async-start(bf16[8,128,256]{2,1,0:T(8,128)(2,1)} %ordered.1), calls=%async_computation.2 | async-start | bytes 1048576 | tf_op jit(solution)/shard_map/all_to_all | solution.py:555
  85.9 2.4 %collective-permute-start.4 = (bf16[128,2048]{1,0:T(8,128)(2,1)}, bf16[128,2048]{1,0:T(8,128)(2,1)}, u32[]{:S(2)}, u32[]{:S(2)}) collective-permute-start(bf16[128,2048]{1,0:T(8,128)(2,1)} %get-tuple-element.22.p0), channel_id=1, source_target_pairs={{0,64},{64,0},{1,65},{65,1},{2,66},{66,2},{3,67},{67,3},{4,68},{68... | collective-permute-start | bytes 1572872 | tf_op jit(solution)/shard_map/ppermute | solution.py:34
  88.3 0.2 collective-permute-done.5.p2
  88.5 3.6 %collective-permute-start.6 = (bf16[128,2048]{1,0:T(8,128)(2,1)S(1)}, bf16[128,2048]{1,0:T(8,128)(2,1)}, u32[]{:S(2)}, u32[]{:S(2)}) collective-permute-start(bf16[128,2048]{1,0:T(8,128)(2,1)S(1)} %collective-permute-done.5.p2), channel_id=1, source_target_pairs={{0,64},{64,0},{1,65},{65,1},{2,66},{66,2},{3,67},{67,3},{4,68},{68... | collective-permute-start | bytes 1572872 | tf_op jit(solution)/shard_map/ppermute | solution.py:34
  92.1 1.4 collective-permute-start.12
  93.5 0.3 collective-permute-start.11
  93.8 0.0 collective-permute-done.4.p1
  93.8 0.0 all-to-all-done.2.first
  93.8 0.0 collective-permute-done.6.p3
  93.8 0.0 copy-start
  93.8 2.2 %copy-done = bf16[1,8192,256]{2,1,0:T(8,128)(2,1)S(1)} copy-done((bf16[1,8192,256]{2,1,0:T(8,128)(2,1)S(1)}, bf16[1,8192,256]{2,1,0:T(8,128)(2,1)}, u32[]{:S(2)}) %copy-start) | copy-done | bytes 4194328
  96.0 0.9 copy-done.4
  96.9 3.3 %project.1 = (f32[128,384]{1,0:T(8,128)S(1)}, f32[128,128]{1,0:T(8,128)S(1)}) custom-call(s32[1]{0:T(128)} %bitcast.me.me_ref, bf16[128,2048]{1,0:T(8,128)(2,1)} %get-tuple-element.22.p0, bf16[128,2048]{1,0:T(8,128)(2,1)} %collective-permute-done.4.p1, bf16[128,2048]{1,0:T(8,128)(2,1)S(1)} %collective-permute-done.5.p2, ...), custom_call_target="tpu_custom_call" | custom-call | flops 805306368 | bytes 8388608 | tf_op jit(solution)/shard_map/project/pallas_call | solution.py:342
  100.2 1.5 collective-permute-start.9
  101.7 0.9 collective-permute-start.14
  102.5 0.0 collective-permute-done.12.g2
  102.5 0.0 collective-permute-start.13
  102.5 0.5 collective-permute-start.15
  103.1 0.0 collective-permute-done.11.g1
  103.1 0.0 collective-permute-start.8
  103.1 2.2 %collective-permute-done.9.q2 = f32[128,384]{1,0:T(8,128)S(1)} collective-permute-done((f32[128,384]{1,0:T(8,128)S(1)}, f32[128,384]{1,0:T(8,128)S(1)}, u32[]{:S(2)}, u32[]{:S(2)}) %collective-permute-start.9) | collective-permute-done | bytes 196640 | tf_op jit(solution)/shard_map/ppermute | solution.py:34
  105.3 2.6 %collective-permute-start.10 = (f32[128,384]{1,0:T(8,128)S(1)}, f32[128,384]{1,0:T(8,128)S(1)}, u32[]{:S(2)}, u32[]{:S(2)}) collective-permute-start(f32[128,384]{1,0:T(8,128)S(1)} %collective-permute-done.9.q2), channel_id=1, source_target_pairs={{0,64},{64,0},{1,65},{65,1},{2,66},{66,2},{3,67},{67,3},{4,68},{68... | collective-permute-start | bytes 589832 | tf_op jit(solution)/shard_map/ppermute | solution.py:34
  107.9 0.0 collective-permute-done.14.m1
  107.9 0.0 collective-permute-done.13.g3
  107.9 0.0 collective-permute-done.8.q1
  107.9 1.0 collective-permute-done.10.q3
  109.0 4.7 %chain.1 = (bf16[128,256]{1,0:T(8,128)(2,1)}, bf16[8,128,640]{2,1,0:T(8,128)(2,1)}) custom-call(s32[1]{0:T(128)} %bitcast.me.me_ref, bf16[128,256]{1,0:T(8,128)(2,1)S(1)} %copy-done.8, f32[128,128]{1,0:T(8,128)S(1)} %get-tuple-element.24.square, f32[128,384]{1,0:T(8,128)S(1)} %get-tuple-element.25.q0, f32[128,384]{1,0:T(8,128)S(1)} %collective-permute-done.8.q1, ...), custom_call_target="tpu_custom_call" | custom-call | flops 4000000000 | bytes 6291456 | tf_op jit(solution)/shard_map/chain/pallas_call | solution.py:426
  113.7 5.9 %all-to-all-start.3 = ((bf16[8,128,640]{2,1,0:T(8,128)(2,1)}), bf16[8,128,640]{2,1,0:T(8,128)(2,1)S(1)}, u32[]{:S(2)}, u32[]{:S(2)}) async-start(bf16[8,128,640]{2,1,0:T(8,128)(2,1)} %get-tuple-element.28), calls=%async_computation.3 | async-start | bytes 2621440 | tf_op jit(solution)/shard_map/all_to_all | solution.py:561
  119.6 1.4 collective-permute-start.17
  121.0 1.2 collective-permute-start.16
  122.2 10.0 %collective-permute-done.17.t2 = bf16[1024,256]{1,0:T(8,128)(2,1)} collective-permute-done((bf16[1024,256]{1,0:T(8,128)(2,1)S(1)}, bf16[1024,256]{1,0:T(8,128)(2,1)}, u32[]{:S(2)}, u32[]{:S(2)}) %collective-permute-start.17) | collective-permute-done | bytes 524320 | tf_op jit(solution)/shard_map/ppermute | solution.py:34
  132.2 1.9 %collective-permute-start.18 = (bf16[1024,256]{1,0:T(8,128)(2,1)}, bf16[1024,256]{1,0:T(8,128)(2,1)}, u32[]{:S(2)}, u32[]{:S(2)}) collective-permute-start(bf16[1024,256]{1,0:T(8,128)(2,1)} %collective-permute-done.17.t2), channel_id=1, source_target_pairs={{0,64},{64,0},{1,65},{65,1},{2,66},{66,2},{3,67},{67,3},{4,68},{68... | collective-permute-start | bytes 1572872 | tf_op jit(solution)/shard_map/ppermute | solution.py:34
  134.1 1.1 dynamic-slice_bitcast_fusion.1.rows_own
  135.2 1.1 dynamic-slice_bitcast_fusion.rows_prev
  136.3 0.8 all-to-all-done.3.packed
  137.1 3.1 %share.1 = bf16[8,256,128]{2,1,0:T(8,128)(2,1)} custom-call(s32[1]{0:T(128)} %bitcast.me.me_ref, bf16[8,128,640]{2,1,0:T(8,128)(2,1)S(1)} %all-to-all-done.3.packed, bf16[1024,256]{1,0:T(8,128)(2,1)S(1)} %bitcast.34, bf16[1024,256]{1,0:T(8,128)(2,1)} %collective-permute-done.16.t1, bf16[1024,256]{1,0:T(8,128)(2,1)} %collective-permute-done.17.t2, ...), custom_call_target="tpu_custom_call" | custom-call | flops 2000000000 | bytes 6291456 | tf_op jit(solution)/shard_map/share/pallas_call | solution.py:479
  140.2 7.4 %all-to-all-start.4 = ((bf16[8,256,128]{2,1,0:T(8,128)(2,1)}), bf16[8,256,128]{2,1,0:T(8,128)(2,1)S(1)}, u32[]{:S(2)}, u32[]{:S(2)}) async-start(bf16[8,256,128]{2,1,0:T(8,128)(2,1)} %share.1), calls=%async_computation.4 | async-start | bytes 1048576 | tf_op jit(solution)/shard_map/all_to_all | solution.py:565
  147.5 0.7 constant_dynamic-slice_fusion.gain
  148.2 0.8 dynamic-slice_bitcast_fusion.2.weight_in
  149.0 17.1 %all-to-all-done.4.arrived = bf16[8,256,128]{2,1,0:T(8,128)(2,1)S(1)} async-done(((bf16[8,256,128]{2,1,0:T(8,128)(2,1)}), bf16[8,256,128]{2,1,0:T(8,128)(2,1)S(1)}, u32[]{:S(2)}, u32[]{:S(2)}) %all-to-all-start.4) | async-done | bytes 524320 | tf_op jit(solution)/shard_map/all_to_all | solution.py:565
  166.1 0.8 finish.1
  (17 shorter events, 0.0 us)
Async XLA Ops:
  3.6 27.4 %collective-permute-start = (bf16[8,256,256]{2,1,0:T(8,128)(2,1)}, bf16[8,256,256]{2,1,0:T(8,128)(2,1)}, u32[]{:S(2)}, u32[]{:S(2)}) collective-permute-start(bf16[8,256,256]{2,1,0:T(8,128)(2,1)} %get-tuple-element.20), channel_id=1, source_target_pairs={{0,64},{64,128},{128,192},{1,65},{65,129},{129,193},{2,66},{66,130... | collective-permute-start | bytes 3145736 | tf_op jit(solution)/shard_map/ppermute | solution.py:541
  35.5 37.4 %all-to-all-start.1 = ((bf16[64,4,2048]{2,1,0:T(4,128)(2,1)}), bf16[64,4,2048]{2,1,0:T(4,128)(2,1)}, u32[]{:S(2)}, u32[]{:S(2)}) async-start(bf16[64,4,2048]{2,1,0:T(4,128)(2,1)} %pick_rows.1.after), calls=%async_computation.1 | async-start | bytes 2097152 | tf_op jit(solution)/shard_map/all_to_all | solution.py:544
  46.1 11.5 %collective-permute-start.1 = (bf16[256,384]{1,0:T(8,128)(2,1)}, bf16[256,384]{1,0:T(8,128)(2,1)S(1)}, u32[]{:S(2)}, u32[]{:S(2)}) collective-permute-start(bf16[256,384]{1,0:T(8,128)(2,1)} %cross_products.1.refs_0_), channel_id=1, source_target_pairs={{0,2},{2,4},{4,6},{6,0},{1,3},{3,5},{5,7},{7,1},{8,10},{10,12},{12... | collective-permute-start | bytes 589832 | tf_op jit(solution)/shard_map/ppermute | solution.py:160
  47.4 17.2 %collective-permute-start.2 = (bf16[256,384]{1,0:T(8,128)(2,1)}, bf16[256,384]{1,0:T(8,128)(2,1)S(1)}, u32[]{:S(2)}, u32[]{:S(2)}) collective-permute-start(bf16[256,384]{1,0:T(8,128)(2,1)} %cross_products.1.refs_0_), channel_id=1, source_target_pairs={{0,4},{2,6},{4,0},{6,2},{1,5},{3,7},{5,1},{7,3},{8,12},{10,14},{12... | collective-permute-start | bytes 589832 | tf_op jit(solution)/shard_map/ppermute | solution.py:160
  49.8 14.8 %collective-permute-start.3 = (bf16[256,384]{1,0:T(8,128)(2,1)}, bf16[256,384]{1,0:T(8,128)(2,1)S(1)}, u32[]{:S(2)}, u32[]{:S(2)}) collective-permute-start(bf16[256,384]{1,0:T(8,128)(2,1)} %cross_products.1.refs_0_), channel_id=1, source_target_pairs={{0,6},{2,0},{4,2},{6,4},{1,7},{3,1},{5,3},{7,5},{8,14},{10,8},{12,... | collective-permute-start | bytes 589832 | tf_op jit(solution)/shard_map/ppermute | solution.py:160
  65.6 13.3 %collective-permute-start.7 = (bf16[256,384]{1,0:T(8,128)(2,1)S(1)}, bf16[256,384]{1,0:T(8,128)(2,1)S(1)}, u32[]{:S(2)}, u32[]{:S(2)}) collective-permute-start(bf16[256,384]{1,0:T(8,128)(2,1)S(1)} %add_convert_fusion.refs_0_.m0), channel_id=1, source_target_pairs={{0,128},{128,0},{1,129},{129,1},{2,130},{130,2},{3,131},{131,3},{4... | collective-permute-start | bytes 589832 | tf_op jit(solution)/shard_map/ppermute | solution.py:34
  72.8 1.9 %copy-start.1 = (bf16[8192,128]{1,0:T(8,128)(2,1)S(1)}, bf16[8192,128]{1,0:T(8,128)(2,1)}, u32[]{:S(2)}) copy-start(bf16[8192,128]{1,0:T(8,128)(2,1)} %get-tuple-element.21.refs_1_.gained) | copy-start | bytes 6291460
  74.8 0.8 copy-start.6
  76.7 0.8 copy-start.2
  77.5 11.0 %collective-permute-start.5 = (bf16[128,2048]{1,0:T(8,128)(2,1)}, bf16[128,2048]{1,0:T(8,128)(2,1)S(1)}, u32[]{:S(2)}, u32[]{:S(2)}) collective-permute-start(bf16[128,2048]{1,0:T(8,128)(2,1)} %get-tuple-element.22.p0), channel_id=1, source_target_pairs={{0,128},{128,0},{1,129},{129,1},{2,130},{130,2},{3,131},{131,3},{4... | collective-permute-start | bytes 1572872 | tf_op jit(solution)/shard_map/ppermute | solution.py:34
  79.0 0.7 copy-start.3
  79.7 14.1 %all-to-all-start.2 = ((bf16[8,128,256]{2,1,0:T(8,128)(2,1)}), bf16[8,128,256]{2,1,0:T(8,128)(2,1)S(1)}, u32[]{:S(2)}, u32[]{:S(2)}) async-start(bf16[8,128,256]{2,1,0:T(8,128)(2,1)} %ordered.1), calls=%async_computation.2 | async-start | bytes 1048576 | tf_op jit(solution)/shard_map/all_to_all | solution.py:555
  85.9 7.9 %collective-permute-start.4 = (bf16[128,2048]{1,0:T(8,128)(2,1)}, bf16[128,2048]{1,0:T(8,128)(2,1)}, u32[]{:S(2)}, u32[]{:S(2)}) collective-permute-start(bf16[128,2048]{1,0:T(8,128)(2,1)} %get-tuple-element.22.p0), channel_id=1, source_target_pairs={{0,64},{64,0},{1,65},{65,1},{2,66},{66,2},{3,67},{67,3},{4,68},{68... | collective-permute-start | bytes 1572872 | tf_op jit(solution)/shard_map/ppermute | solution.py:34
  88.5 5.3 %collective-permute-start.6 = (bf16[128,2048]{1,0:T(8,128)(2,1)S(1)}, bf16[128,2048]{1,0:T(8,128)(2,1)}, u32[]{:S(2)}, u32[]{:S(2)}) collective-permute-start(bf16[128,2048]{1,0:T(8,128)(2,1)S(1)} %collective-permute-done.5.p2), channel_id=1, source_target_pairs={{0,64},{64,0},{1,65},{65,1},{2,66},{66,2},{3,67},{67,3},{4,68},{68... | collective-permute-start | bytes 1572872 | tf_op jit(solution)/shard_map/ppermute | solution.py:34
  92.1 10.5 %collective-permute-start.12 = (bf16[384,256]{1,0:T(8,128)(2,1)}, bf16[384,256]{1,0:T(8,128)(2,1)}, u32[]{:S(2)}, u32[]{:S(2)}) collective-permute-start(bf16[384,256]{1,0:T(8,128)(2,1)} %get-tuple-element.26.g0), channel_id=1, source_target_pairs={{0,128},{128,0},{1,129},{129,1},{2,130},{130,2},{3,131},{131,3},{4... | collective-permute-start | bytes 589832 | tf_op jit(solution)/shard_map/ppermute | solution.py:34
  93.5 9.5 %collective-permute-start.11 = (bf16[384,256]{1,0:T(8,128)(2,1)}, bf16[384,256]{1,0:T(8,128)(2,1)}, u32[]{:S(2)}, u32[]{:S(2)}) collective-permute-start(bf16[384,256]{1,0:T(8,128)(2,1)} %get-tuple-element.26.g0), channel_id=1, source_target_pairs={{0,64},{64,0},{1,65},{65,1},{2,66},{66,2},{3,67},{67,3},{4,68},{68... | collective-permute-start | bytes 589832 | tf_op jit(solution)/shard_map/ppermute | solution.py:34
  93.8 2.2 %copy-start = (bf16[1,8192,256]{2,1,0:T(8,128)(2,1)S(1)}, bf16[1,8192,256]{2,1,0:T(8,128)(2,1)}, u32[]{:S(2)}) copy-start(bf16[1,8192,256]{2,1,0:T(8,128)(2,1)} %param.9) | copy-start | bytes 12582916
  96.0 0.9 copy-start.4
  96.9 12.0 %copy-start.5 = (bf16[256,384]{1,0:T(8,128)(2,1)S(1)}, bf16[256,384]{1,0:T(8,128)(2,1)}, u32[]{:S(2)}) copy-start(bf16[256,384]{1,0:T(8,128)(2,1)} %copy-done.3) | copy-start | bytes 589828
  96.9 12.0 %copy-start.7 = (bf16[384,256]{1,0:T(8,128)(2,1)S(1)}, bf16[384,256]{1,0:T(8,128)(2,1)}, u32[]{:S(2)}) copy-start(bf16[384,256]{1,0:T(8,128)(2,1)} %get-tuple-element.26.g0) | copy-start | bytes 589828
  96.9 12.0 %copy-start.8 = (bf16[128,256]{1,0:T(8,128)(2,1)S(1)}, bf16[128,256]{1,0:T(8,128)(2,1)}, u32[]{:S(2)}) copy-start(bf16[128,256]{1,0:T(8,128)(2,1)} %cot.1) | copy-start | bytes 196612
  100.2 5.1 %collective-permute-start.9 = (f32[128,384]{1,0:T(8,128)S(1)}, f32[128,384]{1,0:T(8,128)S(1)}, u32[]{:S(2)}, u32[]{:S(2)}) collective-permute-start(f32[128,384]{1,0:T(8,128)S(1)} %get-tuple-element.25.q0), channel_id=1, source_target_pairs={{0,128},{128,0},{1,129},{129,1},{2,130},{130,2},{3,131},{131,3},{4... | collective-permute-start | bytes 589832 | tf_op jit(solution)/shard_map/ppermute | solution.py:34
  101.7 6.2 %collective-permute-start.14 = (bf16[256,384]{1,0:T(8,128)(2,1)S(1)}, bf16[256,384]{1,0:T(8,128)(2,1)S(1)}, u32[]{:S(2)}, u32[]{:S(2)}) collective-permute-start(bf16[256,384]{1,0:T(8,128)(2,1)S(1)} %add_convert_fusion.refs_0_.m0), channel_id=1, source_target_pairs={{0,64},{64,0},{1,65},{65,1},{2,66},{66,2},{3,67},{67,3},{4,68},{68... | collective-permute-start | bytes 589832 | tf_op jit(solution)/shard_map/ppermute | solution.py:34
  102.5 5.4 %collective-permute-start.13 = (bf16[384,256]{1,0:T(8,128)(2,1)}, bf16[384,256]{1,0:T(8,128)(2,1)S(1)}, u32[]{:S(2)}, u32[]{:S(2)}) collective-permute-start(bf16[384,256]{1,0:T(8,128)(2,1)} %collective-permute-done.12.g2), channel_id=1, source_target_pairs={{0,64},{64,0},{1,65},{65,1},{2,66},{66,2},{3,67},{67,3},{4,68},{68... | collective-permute-start | bytes 589832 | tf_op jit(solution)/shard_map/ppermute | solution.py:34
  102.5 5.4 %collective-permute-start.15 = (bf16[256,384]{1,0:T(8,128)(2,1)S(1)}, bf16[256,384]{1,0:T(8,128)(2,1)S(1)}, u32[]{:S(2)}, u32[]{:S(2)}) collective-permute-start(bf16[256,384]{1,0:T(8,128)(2,1)S(1)} %copy-done.4), channel_id=1, source_target_pairs={{0,64},{64,0},{1,65},{65,1},{2,66},{66,2},{3,67},{67,3},{4,68},{68... | collective-permute-start | bytes 589832 | tf_op jit(solution)/shard_map/ppermute | solution.py:34
  103.1 4.8 %collective-permute-start.8 = (f32[128,384]{1,0:T(8,128)S(1)}, f32[128,384]{1,0:T(8,128)S(1)}, u32[]{:S(2)}, u32[]{:S(2)}) collective-permute-start(f32[128,384]{1,0:T(8,128)S(1)} %get-tuple-element.25.q0), channel_id=1, source_target_pairs={{0,64},{64,0},{1,65},{65,1},{2,66},{66,2},{3,67},{67,3},{4,68},{68... | collective-permute-start | bytes 589832 | tf_op jit(solution)/shard_map/ppermute | solution.py:34
  105.3 3.7 %collective-permute-start.10 = (f32[128,384]{1,0:T(8,128)S(1)}, f32[128,384]{1,0:T(8,128)S(1)}, u32[]{:S(2)}, u32[]{:S(2)}) collective-permute-start(f32[128,384]{1,0:T(8,128)S(1)} %collective-permute-done.9.q2), channel_id=1, source_target_pairs={{0,64},{64,0},{1,65},{65,1},{2,66},{66,2},{3,67},{67,3},{4,68},{68... | collective-permute-start | bytes 589832 | tf_op jit(solution)/shard_map/ppermute | solution.py:34
  113.7 23.4 %all-to-all-start.3 = ((bf16[8,128,640]{2,1,0:T(8,128)(2,1)}), bf16[8,128,640]{2,1,0:T(8,128)(2,1)S(1)}, u32[]{:S(2)}, u32[]{:S(2)}) async-start(bf16[8,128,640]{2,1,0:T(8,128)(2,1)} %get-tuple-element.28), calls=%async_computation.3 | async-start | bytes 2621440 | tf_op jit(solution)/shard_map/all_to_all | solution.py:561
  119.6 12.6 %collective-permute-start.17 = (bf16[1024,256]{1,0:T(8,128)(2,1)S(1)}, bf16[1024,256]{1,0:T(8,128)(2,1)}, u32[]{:S(2)}, u32[]{:S(2)}) collective-permute-start(bf16[1024,256]{1,0:T(8,128)(2,1)S(1)} %bitcast.32), channel_id=1, source_target_pairs={{0,128},{128,0},{1,129},{129,1},{2,130},{130,2},{3,131},{131,3},{4... | collective-permute-start | bytes 1572872 | tf_op jit(solution)/shard_map/ppermute | solution.py:34
  121.0 15.2 %collective-permute-start.16 = (bf16[1024,256]{1,0:T(8,128)(2,1)S(1)}, bf16[1024,256]{1,0:T(8,128)(2,1)}, u32[]{:S(2)}, u32[]{:S(2)}) collective-permute-start(bf16[1024,256]{1,0:T(8,128)(2,1)S(1)} %bitcast.33), channel_id=1, source_target_pairs={{0,64},{64,0},{1,65},{65,1},{2,66},{66,2},{3,67},{67,3},{4,68},{68... | collective-permute-start | bytes 1572872 | tf_op jit(solution)/shard_map/ppermute | solution.py:34
  132.2 4.0 %collective-permute-start.18 = (bf16[1024,256]{1,0:T(8,128)(2,1)}, bf16[1024,256]{1,0:T(8,128)(2,1)}, u32[]{:S(2)}, u32[]{:S(2)}) collective-permute-start(bf16[1024,256]{1,0:T(8,128)(2,1)} %collective-permute-done.17.t2), channel_id=1, source_target_pairs={{0,64},{64,0},{1,65},{65,1},{2,66},{66,2},{3,67},{67,3},{4,68},{68... | collective-permute-start | bytes 1572872 | tf_op jit(solution)/shard_map/ppermute | solution.py:34
  140.2 25.9 %all-to-all-start.4 = ((bf16[8,256,128]{2,1,0:T(8,128)(2,1)}), bf16[8,256,128]{2,1,0:T(8,128)(2,1)S(1)}, u32[]{:S(2)}, u32[]{:S(2)}) async-start(bf16[8,256,128]{2,1,0:T(8,128)(2,1)} %share.1), calls=%async_computation.4 | async-start | bytes 1048576 | tf_op jit(solution)/shard_map/all_to_all | solution.py:565

commit v6 on v5

--- a/solution.py
+++ b/solution.py
@@ -40,20 +40,12 @@
     return x, beside, across, swap(across, CO)
 
 
+def gather_direct(x):
+    return x, swap(x, CO), swap(x, YL), lax.ppermute(x, SEC, [(0, 3), (1, 2), (2, 1), (3, 0)])
+
+
 def full(shape):
     return pl.BlockSpec(shape, lambda *_: (0,) * len(shape))
-
-
-def ordered(x, after):
-    hbm = pl.BlockSpec(memory_space=pl.ANY)
-    return pl.pallas_call(
-        lambda *refs: None,
-        in_specs=[hbm, hbm],
-        out_specs=hbm,
-        out_shape=jax.ShapeDtypeStruct(x.shape, x.dtype),
-        input_output_aliases={0: 0},
-        name="ordered",
-    )(x, after)
 
 
 def weights_kernel(basis, weight_in, gain, weight_out, *refs):
@@ -315,7 +307,7 @@
     )(place, answered, *firsts)
 
 
-def project_kernel(me, p0, p1, p2, p3, basis, gained, first, second, out, square):
+def project_kernel(me, p0, p1, p2, p3, basis, gained, first, second, out, square, acc):
     step = pl.program_id(0)
     r = basis.shape[1]
     for k, piece in enumerate((p0, p1, p2, p3)):
@@ -327,13 +319,17 @@
             q = jnp.broadcast_to(jnp.sum(xf * xf, axis=1, keepdims=True), square.shape)
             a, b = dot_nn(x, basis[...]), dot_nn(x, gained[...])
             if k == 0:
-                out[:, 0:r] = a
-                out[:, r:] = b
+                acc[:, 0:r] = a
+                acc[:, r:] = b
                 square[...] = q
             else:
-                out[:, 0:r] += a
-                out[:, r:] += b
+                acc[:, 0:r] += a
+                acc[:, r:] += b
                 square[...] += q
+
+    @pl.when(step == 3)
+    def _():
+        out[...] = acc[...].astype(BF16)
 
 
 def project(me, pieces, basis, gained, first, second):
@@ -352,9 +348,10 @@
                 pl.BlockSpec(memory_space=pl.ANY),
             ],
             out_specs=[full((tokens, r + h)), full((tokens, 128))],
+            scratch_shapes=[pltpu.VMEM((tokens, r + h), F32)],
         ),
         out_shape=[
-            jax.ShapeDtypeStruct((tokens, r + h), F32),
+            jax.ShapeDtypeStruct((tokens, r + h), BF16),
             jax.ShapeDtypeStruct((tokens, 128), F32),
         ],
         compiler_params=pltpu.CompilerParams(vmem_limit_bytes=24 * 2**20),
@@ -371,7 +368,7 @@
     r = cot.shape[1]
     h = q0.shape[1] - r
     for k, (q, g, m) in enumerate(((q0, g0, m0), (q1, g1, m1), (q2, g2, m2), (q3, g3, m3))):
-        pq[k ^ me] = q[...]
+        pq[k ^ me] = q[...].astype(F32)
         owns[k ^ me] = g[...]
         mats[k ^ me] = m[...]
     squares = square[:, 0:1]
@@ -549,12 +546,11 @@
     crossed = sum_over_x(crossed)
     mats = gather_peers(crossed)
 
-    part, turned = place_rows(place, answered.reshape(shards * CAP, cols), group, (crossed, gained))
-    turned = ordered(turned, mats[2])
+    part, turned = place_rows(place, answered.reshape(shards * CAP, cols), group, (*owns[1:], mats[2]))
     pieces = gather_peers(part)
     turned = lax.all_to_all(turned, GATHER, split_axis=0, concat_axis=0, tiled=True)
     pq, square = project(me, pieces, basis, gained, turned, mats[2])
-    pqs = gather_peers(pq)
+    pqs = gather_direct(pq)
     turned = gather_peers(turned.reshape(group * tokens, cols // group))
 
     sent, packed = chain(me, coef_cotangent, square, pqs, owns, mats, d, group)

time: 168 us -> 164 us (0.976)
  local copies, waits for them, and re-layouts: 10.9 us -> 8.07 us
  starting transfers between devices: 53.2 us -> 50.7 us
    ppermute x3, waiting for transfers between devices: 13.6 us -> 5.18 us  [sum_over_x(): lax.ppermute(v, X, [(i, (i + k) % 4) for i in range(4)]).astype(F32)]
    ppermute x15 -> x14, waiting for transfers between devices: 13.5 us -> 19.4 us  [swap(): return lax.ppermute(x, axis, [(0, 1), (1, 0)])]
    ppermute x15 -> x14, starting transfers between devices: 19.1 us -> 14.8 us  [swap(): return lax.ppermute(x, axis, [(0, 1), (1, 0)])]
    unnamed x18 -> x14, local copies, waits for them, and re-layouts: 5.86 us -> 3.16 us
    ppermute x0 -> x1, waiting for transfers between devices: none -> 2.37 us  [gather_direct(): lax.ppermute(x, SEC, [(0, 3), (1, 2), (2, 1), (3, 0)])]
  transfers between devices with their start and end apart: 23 -> 23, of which waited for: 8 -> 10; matrix products, arithmetic and copies ran while one was open for 4% -> 4% of each run, Pallas kernels for 10% -> 9%
where the time goes in v6:
time: 164 us; the launch traced here: 163 us
  starting transfers between devices  50.7 us (31%)
  waiting for transfers between devices  45.3 us (28%)
  Pallas kernels  32.4 us (20%)
  blocking collectives  23.6 us (14%)
  local copies, waits for them, and re-layouts  8.07 us (5%)
  other arithmetic  1.71 us (1%)
    all_to_all x1, blocking collectives, per_device(): lax.all_to_all(requests, DP, split_axis=0, concat_axis=0, tiled=True)  23.6 us
    ppermute x14, waiting for transfers between devices, swap(): return lax.ppermute(x, axis, [(0, 1), (1, 0)])  19.4 us
    all_to_all x1, waiting for transfers between devices, per_device(): lax.all_to_all(shares, REDUCE, split_axis=0, concat_axis=0, tiled=True)  17.1 us
    ppermute x14, starting transfers between devices, swap(): return lax.ppermute(x, axis, [(0, 1), (1, 0)])  14.8 us
    all_to_all x1, starting transfers between devices, per_device(): lax.all_to_all(shares, REDUCE, split_axis=0, concat_axis=0, tiled=True)  7.85 us
    pallas_call x1, Pallas kernels, weights(): pl.pallas_call(weights_kernel, grid=(steps,), in_specs=[pl.BlockSpec((row...  7.14 us
    all_to_all x1, starting transfers between devices, per_device(): lax.all_to_all(packed, GATHER, split_axis=0, concat_axis=0, tiled=True)  6.14 us
    all_to_all x1, starting transfers between devices, per_device(): lax.all_to_all(turned, GATHER, split_axis=0, concat_axis=0, tiled=True)  6.14 us
  transfers between devices with their start and end apart: 23, of which 10 were waited for; matrix products, arithmetic and copies ran while one was open for 4% of the time, Pallas kernels for 9%

profile of v6, /device:TPU:33, one launch (start us, length us, event | category | flops | bytes accessed | tf_op | source)
XLA Modules:
  0.0 162.7 jit_solution(4382904609985700521)
XLA Ops:
  0.6 2.9 %request.1 = (s32[128,1]{1,0:T(8,128)}, s32[64,4]{1,0:T(8,128)}, bf16[8,256,256]{2,1,0:T(8,128)(2,1)}) custom-call(s32[1]{0:T(128)} %bitcast.1.at, s32[1,128]{1,0:T(1,128)} %bitcast.41, bf16[8,4,256,256]{3,2,1,0:T(8,128)(2,1)} %bitcast.28), custom_call_target="tpu_custom_call" | custom-call | flops 10000000 | bytes 2097152 | tf_op jit(solution)/shard_map/request/pallas_call | solution.py:205
  3.5 3.8 %collective-permute-start = (bf16[8,256,256]{2,1,0:T(8,128)(2,1)}, bf16[8,256,256]{2,1,0:T(8,128)(2,1)}, u32[]{:S(2)}, u32[]{:S(2)}) collective-permute-start(bf16[8,256,256]{2,1,0:T(8,128)(2,1)} %get-tuple-element.20), channel_id=1, source_target_pairs={{0,64},{64,128},{128,192},{1,65},{65,129},{129,193},{2,66},{66,130... | collective-permute-start | bytes 3145736 | tf_op jit(solution)/shard_map/ppermute | solution.py:538
  7.3 23.6 %all_to_all.31 = s32[64,1,4]{2,1,0:T(1,128)} all-to-all(s32[64,1,4]{2,1,0:T(1,128)} %bitcast.40), channel_id=1, replica_groups=mesh['yl'=2,'co'=2,'zh'=4,'zl'=2,'x'=4,'yh'=2] {'zh','zl','x','yh'}, dimensions={0} | all-to-all | bytes 2048 | tf_op jit(solution)/shard_map/all_to_all | solution.py:539
  30.9 0.0 collective-permute-done.refs_0_.prev
  30.9 4.6 %pick_rows.1.after = bf16[64,4,2048]{2,1,0:T(4,128)(2,1)} custom-call(s32[64,4]{1,0:T(8,128)} %bitcast.39, bf16[1008,2048]{1,0:T(8,128)(2,1)} %table.1, bf16[8,256,256]{2,1,0:T(8,128)(2,1)} %collective-permute-done.refs_0_.prev), custom_call_target="tpu_custom_call" | custom-call | flops 1056964608 | bytes 5177344 | tf_op jit(solution)/shard_map/pick_rows/pallas_call | solution.py:258
  35.5 6.1 %all-to-all-start.1 = ((bf16[64,4,2048]{2,1,0:T(4,128)(2,1)}), bf16[64,4,2048]{2,1,0:T(4,128)(2,1)}, u32[]{:S(2)}, u32[]{:S(2)}) async-start(bf16[64,4,2048]{2,1,0:T(4,128)(2,1)} %pick_rows.1.after), calls=%async_computation.1 | async-start | bytes 2097152 | tf_op jit(solution)/shard_map/all_to_all | solution.py:541
  41.6 4.7 %cross_products.1.refs_0_ = bf16[256,384]{1,0:T(8,128)(2,1)} custom-call(s32[1]{0:T(128)} %bitcast.1.at, bf16[8,4,256,256]{3,2,1,0:T(8,128)(2,1)} %bitcast.29, bf16[8,4,256,128]{3,2,1,0:T(8,128)(2,1)} %bitcast.35, f32[1,8192]{1,0:T(1,128)} %gain.3, bf16[8,256,256]{2,1,0:T(8,128)(2,1)} %collective-permute-done.refs_0_.prev, bf16[64,4,2048]{2,1,0:T(4,128)(2,1)} %pick_rows.1.after), custom_call_target="tpu_custom_call" | custom-call | flops 402653184 | bytes 2621440 | tf_op jit(solution)/shard_map/cross_products/pallas_call | solution.py:128
  46.2 1.3 collective-permute-start.4
  47.5 2.4 %collective-permute-start.5 = (bf16[256,384]{1,0:T(8,128)(2,1)}, bf16[256,384]{1,0:T(8,128)(2,1)S(1)}, u32[]{:S(2)}, u32[]{:S(2)}) collective-permute-start(bf16[256,384]{1,0:T(8,128)(2,1)} %cross_products.1.refs_0_), channel_id=1, source_target_pairs={{0,4},{2,6},{4,0},{6,2},{1,5},{3,7},{5,1},{7,3},{8,12},{10,14},{12... | collective-permute-start | bytes 589832 | tf_op jit(solution)/shard_map/ppermute | solution.py:152
  49.9 1.2 collective-permute-start.6
  51.1 7.1 %weights.1 = (bf16[8192,128]{1,0:T(8,128)(2,1)}, bf16[384,256]{1,0:T(8,128)(2,1)}) custom-call(bf16[8192,256]{1,0:T(8,128)(2,1)} %bitcast.30, bf16[8192,128]{1,0:T(8,128)(2,1)} %bitcast.36, f32[1,8192]{1,0:T(1,128)} %gain.3, bf16[128,8192]{1,0:T(8,128)(2,1)} %bitcast.37, bf16[256,384]{1,0:T(8,128)(2,1)} %cross_products.1.refs_0_), custom_call_target="tpu_custom_call" | custom-call | flops 1610612736 | bytes 12582912 | tf_op jit(solution)/shard_map/weights/pallas_call | solution.py:75
  58.3 0.0 collective-permute-start.2
  58.3 2.4 %collective-permute-start.1 = (bf16[384,256]{1,0:T(8,128)(2,1)}, bf16[384,256]{1,0:T(8,128)(2,1)}, u32[]{:S(2)}, u32[]{:S(2)}) collective-permute-start(bf16[384,256]{1,0:T(8,128)(2,1)} %get-tuple-element.21.g0), channel_id=1, source_target_pairs={{0,64},{64,0},{1,65},{65,1},{2,66},{66,2},{3,67},{67,3},{4,68},{68... | collective-permute-start | bytes 589832 | tf_op jit(solution)/shard_map/ppermute | solution.py:34
  60.7 0.0 collective-permute-done.4
  60.7 5.2 %collective-permute-done.5 = bf16[256,384]{1,0:T(8,128)(2,1)S(1)} collective-permute-done((bf16[256,384]{1,0:T(8,128)(2,1)}, bf16[256,384]{1,0:T(8,128)(2,1)S(1)}, u32[]{:S(2)}, u32[]{:S(2)}) %collective-permute-start.5) | collective-permute-done | bytes 196640 | tf_op jit(solution)/shard_map/ppermute | solution.py:152
  65.8 0.0 collective-permute-done.6
  65.9 1.7 %add_convert_fusion.m0 = bf16[256,384]{1,0:T(8,128)(2,1)} fusion(bf16[256,384]{1,0:T(8,128)(2,1)} %collective-permute-done.6, bf16[256,384]{1,0:T(8,128)(2,1)S(1)} %collective-permute-done.5, bf16[256,384]{1,0:T(8,128)(2,1)S(1)} %collective-permute-done.4, bf16[256,384]{1,0:T(8,128)(2,1)S(1)} %copy-done.6), kind=kLoop, calls=%fused_computation.2 | loop fusion | flops 786432 | bytes 983040 | tf_op jit(solution)/shard_map/convert_element_type | solution.py:153
  67.6 0.0 collective-permute-start.7
  67.6 0.0 collective-permute-done.2.refs_1_.g2
  67.6 1.8 %collective-permute-start.3 = (bf16[384,256]{1,0:T(8,128)(2,1)S(1)}, bf16[384,256]{1,0:T(8,128)(2,1)}, u32[]{:S(2)}, u32[]{:S(2)}) collective-permute-start(bf16[384,256]{1,0:T(8,128)(2,1)S(1)} %collective-permute-done.2.refs_1_.g2), channel_id=1, source_target_pairs={{0,64},{64,0},{1,65},{65,1},{2,66},{66,2},{3,67},{67,3},{4,68},{68... | collective-permute-start | bytes 589832 | tf_op jit(solution)/shard_map/ppermute | solution.py:34
  69.4 0.3 all-to-all-done.1
  69.6 1.3 reshape.35.answered
  71.0 0.0 collective-permute-done.1.refs_0_.g1
  71.0 1.7 %collective-permute-done.7.refs_3_.second.m2 = bf16[256,384]{1,0:T(8,128)(2,1)S(1)} collective-permute-done((bf16[256,384]{1,0:T(8,128)(2,1)}, bf16[256,384]{1,0:T(8,128)(2,1)S(1)}, u32[]{:S(2)}, u32[]{:S(2)}) %collective-permute-start.7) | collective-permute-done | bytes 196640 | tf_op jit(solution)/shard_map/ppermute | solution.py:34
  72.7 0.0 collective-permute-done.3.refs_2_.g3
  72.7 0.8 copy-done.3
  73.5 1.2 place_rows.1
  74.7 0.7 collective-permute-start.9
  75.4 0.1 copy-done.2
  75.5 6.1 %all-to-all-start.2 = ((bf16[8,128,256]{2,1,0:T(8,128)(2,1)}), bf16[8,128,256]{2,1,0:T(8,128)(2,1)S(1)}, u32[]{:S(2)}, u32[]{:S(2)}) async-start(bf16[8,128,256]{2,1,0:T(8,128)(2,1)} %copy-done.2), calls=%async_computation.2 | async-start | bytes 1048576 | tf_op jit(solution)/shard_map/all_to_all | solution.py:551
  81.6 1.9 %collective-permute-start.8 = (bf16[128,2048]{1,0:T(8,128)(2,1)}, bf16[128,2048]{1,0:T(8,128)(2,1)}, u32[]{:S(2)}, u32[]{:S(2)}) collective-permute-start(bf16[128,2048]{1,0:T(8,128)(2,1)} %get-tuple-element.22.p0), channel_id=1, source_target_pairs={{0,64},{64,0},{1,65},{65,1},{2,66},{66,2},{3,67},{67,3},{4,68},{68... | collective-permute-start | bytes 1572872 | tf_op jit(solution)/shard_map/ppermute | solution.py:34
  83.6 2.3 %collective-permute-done.9.p2 = bf16[128,2048]{1,0:T(8,128)(2,1)S(1)} collective-permute-done((bf16[128,2048]{1,0:T(8,128)(2,1)}, bf16[128,2048]{1,0:T(8,128)(2,1)S(1)}, u32[]{:S(2)}, u32[]{:S(2)}) %collective-permute-start.9) | collective-permute-done | bytes 524320 | tf_op jit(solution)/shard_map/ppermute | solution.py:34
  85.9 3.4 %collective-permute-start.10 = (bf16[128,2048]{1,0:T(8,128)(2,1)S(1)}, bf16[128,2048]{1,0:T(8,128)(2,1)}, u32[]{:S(2)}, u32[]{:S(2)}) collective-permute-start(bf16[128,2048]{1,0:T(8,128)(2,1)S(1)} %collective-permute-done.9.p2), channel_id=1, source_target_pairs={{0,64},{64,0},{1,65},{65,1},{2,66},{66,2},{3,67},{67,3},{4,68},{68... | collective-permute-start | bytes 1572872 | tf_op jit(solution)/shard_map/ppermute | solution.py:34
  89.2 0.0 collective-permute-start.14
  89.2 0.5 collective-permute-start.15
  89.7 0.0 collective-permute-done.8.p1
  89.8 0.0 all-to-all-done.2.first
  89.8 1.4 collective-permute-done.10.p3
  91.2 2.2 %copy-done = bf16[1,8192,256]{2,1,0:T(8,128)(2,1)S(1)} copy-done((bf16[1,8192,256]{2,1,0:T(8,128)(2,1)S(1)}, bf16[1,8192,256]{2,1,0:T(8,128)(2,1)}, u32[]{:S(2)}) %copy-start) | copy-done | bytes 4194328
  93.4 3.3 %project.1 = (bf16[128,384]{1,0:T(8,128)(2,1)S(1)}, f32[128,128]{1,0:T(8,128)S(1)}) custom-call(s32[1]{0:T(128)} %bitcast.me.me_ref, bf16[128,2048]{1,0:T(8,128)(2,1)} %get-tuple-element.22.p0, bf16[128,2048]{1,0:T(8,128)(2,1)} %collective-permute-done.8.p1, bf16[128,2048]{1,0:T(8,128)(2,1)S(1)} %collective-permute-done.9.p2, ...), custom_call_target="tpu_custom_call" | custom-call | flops 805306368 | bytes 8388608 | tf_op jit(solution)/shard_map/project/pallas_call | solution.py:338
  96.6 0.5 collective-permute-start.11
  97.1 0.7 collective-permute-start.12
  97.8 1.1 collective-permute-start.13
  98.9 0.0 collective-permute-done.14.m1
  98.9 0.0 collective-permute-done.11.q1
  98.9 2.5 %collective-permute-done.12.q2 = bf16[128,384]{1,0:T(8,128)(2,1)S(1)} collective-permute-done((bf16[128,384]{1,0:T(8,128)(2,1)S(1)}, bf16[128,384]{1,0:T(8,128)(2,1)S(1)}, u32[]{:S(2)}, u32[]{:S(2)}) %collective-permute-start.12) | collective-permute-done | bytes 98336 | tf_op jit(solution)/shard_map/ppermute | solution.py:34
  101.4 2.4 %collective-permute-done.13.q3 = bf16[128,384]{1,0:T(8,128)(2,1)S(1)} collective-permute-done((bf16[128,384]{1,0:T(8,128)(2,1)S(1)}, bf16[128,384]{1,0:T(8,128)(2,1)S(1)}, u32[]{:S(2)}, u32[]{:S(2)}) %collective-permute-start.13) | collective-permute-done | bytes 98336 | tf_op jit(solution)/shard_map/ppermute | solution.py:44
  103.7 5.0 %chain.1 = (bf16[128,256]{1,0:T(8,128)(2,1)}, bf16[8,128,640]{2,1,0:T(8,128)(2,1)}) custom-call(s32[1]{0:T(128)} %bitcast.me.me_ref, bf16[128,256]{1,0:T(8,128)(2,1)S(1)} %copy-done.5, f32[128,128]{1,0:T(8,128)S(1)} %get-tuple-element.25.square, bf16[128,384]{1,0:T(8,128)(2,1)S(1)} %get-tuple-element.26.q0, bf16[128,384]{1,0:T(8,128)(2,1)S(1)} %collective-permute-done.11.q1, ...), custom_call_target="tpu_custom_call" | custom-call | flops 4000000000 | bytes 6291456 | tf_op jit(solution)/shard_map/chain/pallas_call | solution.py:423
  108.7 6.1 %all-to-all-start.3 = ((bf16[8,128,640]{2,1,0:T(8,128)(2,1)}), bf16[8,128,640]{2,1,0:T(8,128)(2,1)S(1)}, u32[]{:S(2)}, u32[]{:S(2)}) async-start(bf16[8,128,640]{2,1,0:T(8,128)(2,1)} %get-tuple-element.28), calls=%async_computation.3 | async-start | bytes 2621440 | tf_op jit(solution)/shard_map/all_to_all | solution.py:557
  114.9 0.3 collective-permute-start.17
  115.2 1.0 collective-permute-start.16
  116.2 11.4 %collective-permute-done.17.t2 = bf16[1024,256]{1,0:T(8,128)(2,1)S(1)} collective-permute-done((bf16[1024,256]{1,0:T(8,128)(2,1)S(1)}, bf16[1024,256]{1,0:T(8,128)(2,1)S(1)}, u32[]{:S(2)}, u32[]{:S(2)}) %collective-permute-start.17) | collective-permute-done | bytes 524320 | tf_op jit(solution)/shard_map/ppermute | solution.py:34
  127.6 1.6 collective-permute-start.18
  129.2 1.1 dynamic-slice_bitcast_fusion.1.rows_own
  130.3 1.1 dynamic-slice_bitcast_fusion.rows_prev
  131.4 0.0 collective-permute-done.16.t1
  131.4 0.0 collective-permute-done.18.t3
  131.4 1.0 all-to-all-done.3.packed
  132.4 2.9 %share.1 = bf16[8,256,128]{2,1,0:T(8,128)(2,1)} custom-call(s32[1]{0:T(128)} %bitcast.me.me_ref, bf16[8,128,640]{2,1,0:T(8,128)(2,1)S(1)} %all-to-all-done.3.packed, bf16[1024,256]{1,0:T(8,128)(2,1)S(1)} %bitcast.34, bf16[1024,256]{1,0:T(8,128)(2,1)} %collective-permute-done.16.t1, bf16[1024,256]{1,0:T(8,128)(2,1)S(1)} %collective-permute-done.17.t2, ...), custom_call_target="tpu_custom_call" | custom-call | flops 2000000000 | bytes 6291456 | tf_op jit(solution)/shard_map/share/pallas_call | solution.py:476
  135.3 7.8 %all-to-all-start.4 = ((bf16[8,256,128]{2,1,0:T(8,128)(2,1)}), bf16[8,256,128]{2,1,0:T(8,128)(2,1)S(1)}, u32[]{:S(2)}, u32[]{:S(2)}) async-start(bf16[8,256,128]{2,1,0:T(8,128)(2,1)} %share.1), calls=%async_computation.4 | async-start | bytes 1048576 | tf_op jit(solution)/shard_map/all_to_all | solution.py:561
  143.2 0.7 constant_dynamic-slice_fusion.gain
  143.8 0.8 dynamic-slice_bitcast_fusion.2.weight_in
  144.6 17.1 %all-to-all-done.4.arrived = bf16[8,256,128]{2,1,0:T(8,128)(2,1)S(1)} async-done(((bf16[8,256,128]{2,1,0:T(8,128)(2,1)}), bf16[8,256,128]{2,1,0:T(8,128)(2,1)S(1)}, u32[]{:S(2)}, u32[]{:S(2)}) %all-to-all-start.4) | async-done | bytes 524320 | tf_op jit(solution)/shard_map/all_to_all | solution.py:561
  161.7 0.8 finish.1
  (12 shorter events, 0.0 us)
Async XLA Ops:
  3.5 27.4 %collective-permute-start = (bf16[8,256,256]{2,1,0:T(8,128)(2,1)}, bf16[8,256,256]{2,1,0:T(8,128)(2,1)}, u32[]{:S(2)}, u32[]{:S(2)}) collective-permute-start(bf16[8,256,256]{2,1,0:T(8,128)(2,1)} %get-tuple-element.20), channel_id=1, source_target_pairs={{0,64},{64,128},{128,192},{1,65},{65,129},{129,193},{2,66},{66,130... | collective-permute-start | bytes 3145736 | tf_op jit(solution)/shard_map/ppermute | solution.py:538
  35.5 34.1 %all-to-all-start.1 = ((bf16[64,4,2048]{2,1,0:T(4,128)(2,1)}), bf16[64,4,2048]{2,1,0:T(4,128)(2,1)}, u32[]{:S(2)}, u32[]{:S(2)}) async-start(bf16[64,4,2048]{2,1,0:T(4,128)(2,1)} %pick_rows.1.after), calls=%async_computation.1 | async-start | bytes 2097152 | tf_op jit(solution)/shard_map/all_to_all | solution.py:541
  46.2 14.4 %collective-permute-start.4 = (bf16[256,384]{1,0:T(8,128)(2,1)}, bf16[256,384]{1,0:T(8,128)(2,1)S(1)}, u32[]{:S(2)}, u32[]{:S(2)}) collective-permute-start(bf16[256,384]{1,0:T(8,128)(2,1)} %cross_products.1.refs_0_), channel_id=1, source_target_pairs={{0,2},{2,4},{4,6},{6,0},{1,3},{3,5},{5,7},{7,1},{8,10},{10,12},{12... | collective-permute-start | bytes 589832 | tf_op jit(solution)/shard_map/ppermute | solution.py:152
  47.5 18.3 %collective-permute-start.5 = (bf16[256,384]{1,0:T(8,128)(2,1)}, bf16[256,384]{1,0:T(8,128)(2,1)S(1)}, u32[]{:S(2)}, u32[]{:S(2)}) collective-permute-start(bf16[256,384]{1,0:T(8,128)(2,1)} %cross_products.1.refs_0_), channel_id=1, source_target_pairs={{0,4},{2,6},{4,0},{6,2},{1,5},{3,7},{5,1},{7,3},{8,12},{10,14},{12... | collective-permute-start | bytes 589832 | tf_op jit(solution)/shard_map/ppermute | solution.py:152
  49.9 15.9 %collective-permute-start.6 = (bf16[256,384]{1,0:T(8,128)(2,1)}, bf16[256,384]{1,0:T(8,128)(2,1)}, u32[]{:S(2)}, u32[]{:S(2)}) collective-permute-start(bf16[256,384]{1,0:T(8,128)(2,1)} %cross_products.1.refs_0_), channel_id=1, source_target_pairs={{0,6},{2,0},{4,2},{6,4},{1,7},{3,1},{5,3},{7,5},{8,14},{10,8},{12,... | collective-permute-start | bytes 589832 | tf_op jit(solution)/shard_map/ppermute | solution.py:152
  51.1 14.7 %copy-start.6 = (bf16[256,384]{1,0:T(8,128)(2,1)S(1)}, bf16[256,384]{1,0:T(8,128)(2,1)}, u32[]{:S(2)}) copy-start(bf16[256,384]{1,0:T(8,128)(2,1)} %cross_products.1.refs_0_) | copy-start | bytes 589828
  58.3 9.3 %collective-permute-start.2 = (bf16[384,256]{1,0:T(8,128)(2,1)}, bf16[384,256]{1,0:T(8,128)(2,1)S(1)}, u32[]{:S(2)}, u32[]{:S(2)}) collective-permute-start(bf16[384,256]{1,0:T(8,128)(2,1)} %get-tuple-element.21.g0), channel_id=1, source_target_pairs={{0,128},{128,0},{1,129},{129,1},{2,130},{130,2},{3,131},{131,3},{4... | collective-permute-start | bytes 589832 | tf_op jit(solution)/shard_map/ppermute | solution.py:34
  58.3 12.7 %collective-permute-start.1 = (bf16[384,256]{1,0:T(8,128)(2,1)}, bf16[384,256]{1,0:T(8,128)(2,1)}, u32[]{:S(2)}, u32[]{:S(2)}) collective-permute-start(bf16[384,256]{1,0:T(8,128)(2,1)} %get-tuple-element.21.g0), channel_id=1, source_target_pairs={{0,64},{64,0},{1,65},{65,1},{2,66},{66,2},{3,67},{67,3},{4,68},{68... | collective-permute-start | bytes 589832 | tf_op jit(solution)/shard_map/ppermute | solution.py:34
  67.6 23.6 %copy-start.1 = (bf16[8192,128]{1,0:T(8,128)(2,1)S(1)}, bf16[8192,128]{1,0:T(8,128)(2,1)}, u32[]{:S(2)}) copy-start(bf16[8192,128]{1,0:T(8,128)(2,1)} %get-tuple-element.23.gained) | copy-start | bytes 6291460
  67.6 5.1 %collective-permute-start.7 = (bf16[256,384]{1,0:T(8,128)(2,1)}, bf16[256,384]{1,0:T(8,128)(2,1)S(1)}, u32[]{:S(2)}, u32[]{:S(2)}) collective-permute-start(bf16[256,384]{1,0:T(8,128)(2,1)} %add_convert_fusion.m0), channel_id=1, source_target_pairs={{0,128},{128,0},{1,129},{129,1},{2,130},{130,2},{3,131},{131,3},{4... | collective-permute-start | bytes 589832 | tf_op jit(solution)/shard_map/ppermute | solution.py:34
  67.6 5.1 %collective-permute-start.3 = (bf16[384,256]{1,0:T(8,128)(2,1)S(1)}, bf16[384,256]{1,0:T(8,128)(2,1)}, u32[]{:S(2)}, u32[]{:S(2)}) collective-permute-start(bf16[384,256]{1,0:T(8,128)(2,1)S(1)} %collective-permute-done.2.refs_1_.g2), channel_id=1, source_target_pairs={{0,64},{64,0},{1,65},{65,1},{2,66},{66,2},{3,67},{67,3},{4,68},{68... | collective-permute-start | bytes 589832 | tf_op jit(solution)/shard_map/ppermute | solution.py:34
  72.7 0.8 copy-start.3
  74.7 0.8 copy-start.2
  74.7 11.2 %collective-permute-start.9 = (bf16[128,2048]{1,0:T(8,128)(2,1)}, bf16[128,2048]{1,0:T(8,128)(2,1)S(1)}, u32[]{:S(2)}, u32[]{:S(2)}) collective-permute-start(bf16[128,2048]{1,0:T(8,128)(2,1)} %get-tuple-element.22.p0), channel_id=1, source_target_pairs={{0,128},{128,0},{1,129},{129,1},{2,130},{130,2},{3,131},{131,3},{4... | collective-permute-start | bytes 1572872 | tf_op jit(solution)/shard_map/ppermute | solution.py:34
  75.5 14.3 %all-to-all-start.2 = ((bf16[8,128,256]{2,1,0:T(8,128)(2,1)}), bf16[8,128,256]{2,1,0:T(8,128)(2,1)S(1)}, u32[]{:S(2)}, u32[]{:S(2)}) async-start(bf16[8,128,256]{2,1,0:T(8,128)(2,1)} %copy-done.2), calls=%async_computation.2 | async-start | bytes 1048576 | tf_op jit(solution)/shard_map/all_to_all | solution.py:551
  81.6 8.1 %collective-permute-start.8 = (bf16[128,2048]{1,0:T(8,128)(2,1)}, bf16[128,2048]{1,0:T(8,128)(2,1)}, u32[]{:S(2)}, u32[]{:S(2)}) collective-permute-start(bf16[128,2048]{1,0:T(8,128)(2,1)} %get-tuple-element.22.p0), channel_id=1, source_target_pairs={{0,64},{64,0},{1,65},{65,1},{2,66},{66,2},{3,67},{67,3},{4,68},{68... | collective-permute-start | bytes 1572872 | tf_op jit(solution)/shard_map/ppermute | solution.py:34
  85.9 5.3 %collective-permute-start.10 = (bf16[128,2048]{1,0:T(8,128)(2,1)S(1)}, bf16[128,2048]{1,0:T(8,128)(2,1)}, u32[]{:S(2)}, u32[]{:S(2)}) collective-permute-start(bf16[128,2048]{1,0:T(8,128)(2,1)S(1)} %collective-permute-done.9.p2), channel_id=1, source_target_pairs={{0,64},{64,0},{1,65},{65,1},{2,66},{66,2},{3,67},{67,3},{4,68},{68... | collective-permute-start | bytes 1572872 | tf_op jit(solution)/shard_map/ppermute | solution.py:34
  89.2 9.7 %collective-permute-start.14 = (bf16[256,384]{1,0:T(8,128)(2,1)}, bf16[256,384]{1,0:T(8,128)(2,1)}, u32[]{:S(2)}, u32[]{:S(2)}) collective-permute-start(bf16[256,384]{1,0:T(8,128)(2,1)} %add_convert_fusion.m0), channel_id=1, source_target_pairs={{0,64},{64,0},{1,65},{65,1},{2,66},{66,2},{3,67},{67,3},{4,68},{68... | collective-permute-start | bytes 589832 | tf_op jit(solution)/shard_map/ppermute | solution.py:34
  89.2 9.7 %collective-permute-start.15 = (bf16[256,384]{1,0:T(8,128)(2,1)S(1)}, bf16[256,384]{1,0:T(8,128)(2,1)}, u32[]{:S(2)}, u32[]{:S(2)}) collective-permute-start(bf16[256,384]{1,0:T(8,128)(2,1)S(1)} %collective-permute-done.7.refs_3_.second.m2), channel_id=1, source_target_pairs={{0,64},{64,0},{1,65},{65,1},{2,66},{66,2},{3,67},{67,3},{4,68},{68... | collective-permute-start | bytes 589832 | tf_op jit(solution)/shard_map/ppermute | solution.py:34
  91.2 2.2 %copy-start = (bf16[1,8192,256]{2,1,0:T(8,128)(2,1)S(1)}, bf16[1,8192,256]{2,1,0:T(8,128)(2,1)}, u32[]{:S(2)}) copy-start(bf16[1,8192,256]{2,1,0:T(8,128)(2,1)} %param.9) | copy-start | bytes 12582916
  93.4 10.4 %copy-start.4 = (bf16[384,256]{1,0:T(8,128)(2,1)S(1)}, bf16[384,256]{1,0:T(8,128)(2,1)}, u32[]{:S(2)}) copy-start(bf16[384,256]{1,0:T(8,128)(2,1)} %get-tuple-element.21.g0) | copy-start | bytes 589828
  93.4 10.4 %copy-start.5 = (bf16[128,256]{1,0:T(8,128)(2,1)S(1)}, bf16[128,256]{1,0:T(8,128)(2,1)}, u32[]{:S(2)}) copy-start(bf16[128,256]{1,0:T(8,128)(2,1)} %cot.1) | copy-start | bytes 196612
  96.6 2.3 %collective-permute-start.11 = (bf16[128,384]{1,0:T(8,128)(2,1)S(1)}, bf16[128,384]{1,0:T(8,128)(2,1)S(1)}, u32[]{:S(2)}, u32[]{:S(2)}) collective-permute-start(bf16[128,384]{1,0:T(8,128)(2,1)S(1)} %get-tuple-element.26.q0), channel_id=1, source_target_pairs={{0,64},{64,0},{1,65},{65,1},{2,66},{66,2},{3,67},{67,3},{4,68},{68... | collective-permute-start | bytes 294920 | tf_op jit(solution)/shard_map/ppermute | solution.py:34
  97.1 4.3 %collective-permute-start.12 = (bf16[128,384]{1,0:T(8,128)(2,1)S(1)}, bf16[128,384]{1,0:T(8,128)(2,1)S(1)}, u32[]{:S(2)}, u32[]{:S(2)}) collective-permute-start(bf16[128,384]{1,0:T(8,128)(2,1)S(1)} %get-tuple-element.26.q0), channel_id=1, source_target_pairs={{0,128},{128,0},{1,129},{129,1},{2,130},{130,2},{3,131},{131,3},{4... | collective-permute-start | bytes 294920 | tf_op jit(solution)/shard_map/ppermute | solution.py:34
  97.8 5.9 %collective-permute-start.13 = (bf16[128,384]{1,0:T(8,128)(2,1)S(1)}, bf16[128,384]{1,0:T(8,128)(2,1)S(1)}, u32[]{:S(2)}, u32[]{:S(2)}) collective-permute-start(bf16[128,384]{1,0:T(8,128)(2,1)S(1)} %get-tuple-element.26.q0), channel_id=1, source_target_pairs={{0,192},{64,128},{128,64},{192,0},{1,193},{65,129},{129,65},{193,1... | collective-permute-start | bytes 294920 | tf_op jit(solution)/shard_map/ppermute | solution.py:44
  108.7 23.7 %all-to-all-start.3 = ((bf16[8,128,640]{2,1,0:T(8,128)(2,1)}), bf16[8,128,640]{2,1,0:T(8,128)(2,1)S(1)}, u32[]{:S(2)}, u32[]{:S(2)}) async-start(bf16[8,128,640]{2,1,0:T(8,128)(2,1)} %get-tuple-element.28), calls=%async_computation.3 | async-start | bytes 2621440 | tf_op jit(solution)/shard_map/all_to_all | solution.py:557
  114.9 12.8 %collective-permute-start.17 = (bf16[1024,256]{1,0:T(8,128)(2,1)S(1)}, bf16[1024,256]{1,0:T(8,128)(2,1)S(1)}, u32[]{:S(2)}, u32[]{:S(2)}) collective-permute-start(bf16[1024,256]{1,0:T(8,128)(2,1)S(1)} %bitcast.32), channel_id=1, source_target_pairs={{0,128},{128,0},{1,129},{129,1},{2,130},{130,2},{3,131},{131,3},{4... | collective-permute-start | bytes 1572872 | tf_op jit(solution)/shard_map/ppermute | solution.py:34
  115.2 16.2 %collective-permute-start.16 = (bf16[1024,256]{1,0:T(8,128)(2,1)S(1)}, bf16[1024,256]{1,0:T(8,128)(2,1)}, u32[]{:S(2)}, u32[]{:S(2)}) collective-permute-start(bf16[1024,256]{1,0:T(8,128)(2,1)S(1)} %bitcast.33), channel_id=1, source_target_pairs={{0,64},{64,0},{1,65},{65,1},{2,66},{66,2},{3,67},{67,3},{4,68},{68... | collective-permute-start | bytes 1572872 | tf_op jit(solution)/shard_map/ppermute | solution.py:34
  127.6 3.8 %collective-permute-start.18 = (bf16[1024,256]{1,0:T(8,128)(2,1)S(1)}, bf16[1024,256]{1,0:T(8,128)(2,1)}, u32[]{:S(2)}, u32[]{:S(2)}) collective-permute-start(bf16[1024,256]{1,0:T(8,128)(2,1)S(1)} %collective-permute-done.17.t2), channel_id=1, source_target_pairs={{0,64},{64,0},{1,65},{65,1},{2,66},{66,2},{3,67},{67,3},{4,68},{68... | collective-permute-start | bytes 1572872 | tf_op jit(solution)/shard_map/ppermute | solution.py:34
  135.3 26.4 %all-to-all-start.4 = ((bf16[8,256,128]{2,1,0:T(8,128)(2,1)}), bf16[8,256,128]{2,1,0:T(8,128)(2,1)S(1)}, u32[]{:S(2)}, u32[]{:S(2)}) async-start(bf16[8,256,128]{2,1,0:T(8,128)(2,1)} %share.1), calls=%async_computation.4 | async-start | bytes 1048576 | tf_op jit(solution)/shard_map/all_to_all | solution.py:561

commit v7 on v5

--- a/solution.py
+++ b/solution.py
@@ -154,11 +154,23 @@
     )(at, basis.reshape(blocks, 4, rows, r), weight_in.reshape(blocks, 4, rows, h), gain, prev, after)
 
 
-def sum_over_x(v):
-    total = v.astype(F32)
-    for k in (1, 2, 3):
-        total = total + lax.ppermute(v, X, [(i, (i + k) % 4) for i in range(4)]).astype(F32)
-    return total.astype(BF16)
+def sum_kernel(a, b, c, d, after, out):
+    total = a[...].astype(F32) + b[...].astype(F32) + c[...].astype(F32) + d[...].astype(F32)
+    out[...] = total.astype(BF16)
+
+
+def sum_over_x(v, after):
+    parts = [v] + [lax.ppermute(v, X, [(i, (i + k) % 4) for i in range(4)]) for k in (1, 2, 3)]
+    vmem = pl.BlockSpec(memory_space=pltpu.VMEM)
+    return pl.pallas_call(
+        sum_kernel,
+        in_specs=[vmem] * 4 + [pl.BlockSpec(memory_space=pl.ANY)],
+        out_specs=vmem,
+        out_shape=jax.ShapeDtypeStruct(v.shape, BF16),
+        compiler_params=pltpu.CompilerParams(vmem_limit_bytes=16 * 2**20),
+        cost_estimate=pl.CostEstimate(flops=4 * v.size, bytes_accessed=10 * v.size, transcendentals=0),
+        name="sum_over_x",
+    )(*parts, after)
 
 
 def start_all(copies):
@@ -546,10 +558,10 @@
     crossed = cross_products(x_at, basis, weight_in, norm_gain, prev_x, found)
     gained, own = weights(basis, weight_in, norm_gain, weight_out, (crossed,))
     owns = gather_peers(own)
-    crossed = sum_over_x(crossed)
+    crossed = sum_over_x(crossed, own)
     mats = gather_peers(crossed)
 
-    part, turned = place_rows(place, answered.reshape(shards * CAP, cols), group, (crossed, gained))
+    part, turned = place_rows(place, answered.reshape(shards * CAP, cols), group, (crossed,))
     turned = ordered(turned, mats[2])
     pieces = gather_peers(part)
     turned = lax.all_to_all(turned, GATHER, split_axis=0, concat_axis=0, tiled=True)

time: 168 us -> 163 us (0.970)
  waiting for transfers between devices: 45.1 us -> 40.6 us
  local copies, waits for them, and re-layouts: 10.9 us -> 14.6 us
  starting transfers between devices: 53.2 us -> 49.9 us
    ppermute x3, waiting for transfers between devices: 13.6 us -> 6.57 us  [sum_over_x(): lax.ppermute(v, X, [(i, (i + k) % 4) for i in range(4)])]
    unnamed x18 -> x30, local copies, waits for them, and re-layouts: 5.86 us -> 9.72 us
    ppermute x15, waiting for transfers between devices: 13.5 us -> 15.7 us  [swap(): return lax.ppermute(x, axis, [(0, 1), (1, 0)])]
    ppermute x15, starting transfers between devices: 19.1 us -> 17.3 us  [swap(): return lax.ppermute(x, axis, [(0, 1), (1, 0)])]
  transfers between devices with their start and end apart: 23 -> 23, of which waited for: 8 -> 9; matrix products, arithmetic and copies ran while one was open for 4% -> 3% of each run, Pallas kernels for 10% -> 10%
where the time goes in v7:
time: 163 us; the launch traced here: 162 us
  starting transfers between devices  49.9 us (31%)
  waiting for transfers between devices  40.6 us (25%)
  Pallas kernels  32.2 us (20%)
  blocking collectives  23.6 us (14%)
  local copies, waits for them, and re-layouts  14.6 us (9%)
    all_to_all x1, blocking collectives, per_device(): lax.all_to_all(requests, DP, split_axis=0, concat_axis=0, tiled=True)  23.6 us
    ppermute x15, starting transfers between devices, swap(): return lax.ppermute(x, axis, [(0, 1), (1, 0)])  17.3 us
    all_to_all x1, waiting for transfers between devices, per_device(): lax.all_to_all(shares, REDUCE, split_axis=0, concat_axis=0, tiled=True)  17.1 us
    ppermute x15, waiting for transfers between devices, swap(): return lax.ppermute(x, axis, [(0, 1), (1, 0)])  15.7 us
    unnamed x30, local copies, waits for them, and re-layouts  9.72 us
    all_to_all x1, starting transfers between devices, per_device(): lax.all_to_all(shares, REDUCE, split_axis=0, concat_axis=0, tiled=True)  7.37 us
    pallas_call x1, Pallas kernels, weights(): pl.pallas_call(weights_kernel, grid=(steps,), in_specs=[pl.BlockSpec((row...  7.14 us
    ppermute x3, waiting for transfers between devices, sum_over_x(): lax.ppermute(v, X, [(i, (i + k) % 4) for i in range(4)])  6.57 us
  transfers between devices with their start and end apart: 23, of which 9 were waited for; matrix products, arithmetic and copies ran while one was open for 3% of the time, Pallas kernels for 10%

profile of v7, /device:TPU:33, one launch (start us, length us, event | category | flops | bytes accessed | tf_op | source)
XLA Modules:
  0.0 161.9 jit_solution(3766711361952172212)
XLA Ops:
  0.6 2.9 %request.1 = (s32[128,1]{1,0:T(8,128)}, s32[64,4]{1,0:T(8,128)}, bf16[8,256,256]{2,1,0:T(8,128)(2,1)}) custom-call(s32[1]{0:T(128)} %bitcast.1.at, s32[1,128]{1,0:T(1,128)} %bitcast.41, bf16[8,4,256,256]{3,2,1,0:T(8,128)(2,1)} %bitcast.28), custom_call_target="tpu_custom_call" | custom-call | flops 10000000 | bytes 2097152 | tf_op jit(solution)/shard_map/request/pallas_call | solution.py:225
  3.5 3.8 %collective-permute-start = (bf16[8,256,256]{2,1,0:T(8,128)(2,1)}, bf16[8,256,256]{2,1,0:T(8,128)(2,1)}, u32[]{:S(2)}, u32[]{:S(2)}) collective-permute-start(bf16[8,256,256]{2,1,0:T(8,128)(2,1)} %get-tuple-element.20), channel_id=1, source_target_pairs={{0,64},{64,128},{128,192},{1,65},{65,129},{129,193},{2,66},{66,130... | collective-permute-start | bytes 3145736 | tf_op jit(solution)/shard_map/ppermute | solution.py:553
  7.3 23.6 %all_to_all.31 = s32[64,1,4]{2,1,0:T(1,128)} all-to-all(s32[64,1,4]{2,1,0:T(1,128)} %bitcast.40), channel_id=1, replica_groups=mesh['yl'=2,'co'=2,'zh'=4,'zl'=2,'x'=4,'yh'=2] {'zh','zl','x','yh'}, dimensions={0} | all-to-all | bytes 2048 | tf_op jit(solution)/shard_map/all_to_all | solution.py:554
  30.9 4.5 %pick_rows.1.after = bf16[64,4,2048]{2,1,0:T(4,128)(2,1)} custom-call(s32[64,4]{1,0:T(8,128)} %bitcast.39, bf16[1008,2048]{1,0:T(8,128)(2,1)} %table.1, bf16[8,256,256]{2,1,0:T(8,128)(2,1)} %collective-permute-done.refs_0_.prev), custom_call_target="tpu_custom_call" | custom-call | flops 1056964608 | bytes 5177344 | tf_op jit(solution)/shard_map/pick_rows/pallas_call | solution.py:278
  35.5 5.9 %all-to-all-start.1 = ((bf16[64,4,2048]{2,1,0:T(4,128)(2,1)}), bf16[64,4,2048]{2,1,0:T(4,128)(2,1)}, u32[]{:S(2)}, u32[]{:S(2)}) async-start(bf16[64,4,2048]{2,1,0:T(4,128)(2,1)} %pick_rows.1.after), calls=%async_computation.1 | async-start | bytes 2097152 | tf_op jit(solution)/shard_map/all_to_all | solution.py:556
  41.4 4.7 %cross_products.1.refs_0_.a = bf16[256,384]{1,0:T(8,128)(2,1)} custom-call(s32[1]{0:T(128)} %bitcast.1.at, bf16[8,4,256,256]{3,2,1,0:T(8,128)(2,1)} %bitcast.29, bf16[8,4,256,128]{3,2,1,0:T(8,128)(2,1)} %bitcast.35, f32[1,8192]{1,0:T(1,128)} %gain.3, bf16[8,256,256]{2,1,0:T(8,128)(2,1)} %collective-permute-done.refs_0_.prev, bf16[64,4,2048]{2,1,0:T(4,128)(2,1)} %pick_rows.1.after), custom_call_target="tpu_custom_call" | custom-call | flops 402653184 | bytes 2621440 | tf_op jit(solution)/shard_map/cross_products/pallas_call | solution.py:136
  46.1 1.3 collective-permute-start.1
  47.3 2.4 %collective-permute-start.2 = (bf16[256,384]{1,0:T(8,128)(2,1)}, bf16[256,384]{1,0:T(8,128)(2,1)S(1)}, u32[]{:S(2)}, u32[]{:S(2)}) collective-permute-start(bf16[256,384]{1,0:T(8,128)(2,1)} %cross_products.1.refs_0_.a), channel_id=1, source_target_pairs={{0,4},{2,6},{4,0},{6,2},{1,5},{3,7},{5,1},{7,3},{8,12},{10,14},{12... | collective-permute-start | bytes 589832 | tf_op jit(solution)/shard_map/ppermute | solution.py:163
  49.8 1.2 collective-permute-start.3
  50.9 7.1 %weights.1 = (bf16[8192,128]{1,0:T(8,128)(2,1)}, bf16[384,256]{1,0:T(8,128)(2,1)}) custom-call(bf16[8192,256]{1,0:T(8,128)(2,1)} %bitcast.30, bf16[8192,128]{1,0:T(8,128)(2,1)} %bitcast.36, f32[1,8192]{1,0:T(1,128)} %gain.3, bf16[128,8192]{1,0:T(8,128)(2,1)} %bitcast.37, bf16[256,384]{1,0:T(8,128)(2,1)} %cross_products.1.refs_0_.a), custom_call_target="tpu_custom_call" | custom-call | flops 1610612736 | bytes 12582912 | tf_op jit(solution)/shard_map/weights/pallas_call | solution.py:83
  58.1 0.0 collective-permute-done.1.b
  58.1 6.6 %collective-permute-done.2.c = bf16[256,384]{1,0:T(8,128)(2,1)S(1)} collective-permute-done((bf16[256,384]{1,0:T(8,128)(2,1)}, bf16[256,384]{1,0:T(8,128)(2,1)S(1)}, u32[]{:S(2)}, u32[]{:S(2)}) %collective-permute-start.2) | collective-permute-done | bytes 196640 | tf_op jit(solution)/shard_map/ppermute | solution.py:163
  64.6 0.7 copy-done.9
  65.3 0.0 collective-permute-done.3.d
  65.3 0.7 copy-done.11
  66.0 0.9 copy-done.7
  66.9 0.9 copy-done.10
  67.9 0.9 copy-done.12
  68.8 0.1 sum_over_x.1.refs_0_.m0
  68.9 0.1 collective-permute-start.7
  69.0 0.3 all-to-all-done.1
  69.3 1.3 reshape.35.answered
  70.6 0.0 copy-start.13
  70.6 1.0 copy-done.13
  71.6 1.2 place_rows.1
  72.8 0.8 copy-done.2
  73.6 1.2 collective-permute-start.5
  74.7 0.7 copy-done.4
  75.4 5.7 %all-to-all-start.2 = ((bf16[8,128,256]{2,1,0:T(8,128)(2,1)}), bf16[8,128,256]{2,1,0:T(8,128)(2,1)S(1)}, u32[]{:S(2)}, u32[]{:S(2)}) async-start(bf16[8,128,256]{2,1,0:T(8,128)(2,1)} %ordered.1), calls=%async_computation.2 | async-start | bytes 1048576 | tf_op jit(solution)/shard_map/all_to_all | solution.py:567
  81.1 2.2 %collective-permute-start.4 = (bf16[128,2048]{1,0:T(8,128)(2,1)}, bf16[128,2048]{1,0:T(8,128)(2,1)}, u32[]{:S(2)}, u32[]{:S(2)}) collective-permute-start(bf16[128,2048]{1,0:T(8,128)(2,1)} %get-tuple-element.22.p0), channel_id=1, source_target_pairs={{0,64},{64,0},{1,65},{65,1},{2,66},{66,2},{3,67},{67,3},{4,68},{68... | collective-permute-start | bytes 1572872 | tf_op jit(solution)/shard_map/ppermute | solution.py:34
  83.3 0.9 collective-permute-done.5.p2
  84.2 4.2 %collective-permute-start.6 = (bf16[128,2048]{1,0:T(8,128)(2,1)S(1)}, bf16[128,2048]{1,0:T(8,128)(2,1)}, u32[]{:S(2)}, u32[]{:S(2)}) collective-permute-start(bf16[128,2048]{1,0:T(8,128)(2,1)S(1)} %collective-permute-done.5.p2), channel_id=1, source_target_pairs={{0,64},{64,0},{1,65},{65,1},{2,66},{66,2},{3,67},{67,3},{4,68},{68... | collective-permute-start | bytes 1572872 | tf_op jit(solution)/shard_map/ppermute | solution.py:34
  88.4 0.9 collective-permute-start.12
  89.3 0.3 collective-permute-start.11
  89.6 0.5 collective-permute-done.6.p3
  90.0 2.2 %copy-done = bf16[1,8192,256]{2,1,0:T(8,128)(2,1)S(1)} copy-done((bf16[1,8192,256]{2,1,0:T(8,128)(2,1)S(1)}, bf16[1,8192,256]{2,1,0:T(8,128)(2,1)}, u32[]{:S(2)}) %copy-start) | copy-done | bytes 4194328
  92.2 0.9 copy-done.5
  93.2 3.3 %project.1 = (f32[128,384]{1,0:T(8,128)S(1)}, f32[128,128]{1,0:T(8,128)S(1)}) custom-call(s32[1]{0:T(128)} %bitcast.me.me_ref, bf16[128,2048]{1,0:T(8,128)(2,1)} %get-tuple-element.22.p0, bf16[128,2048]{1,0:T(8,128)(2,1)} %collective-permute-done.4.p1, bf16[128,2048]{1,0:T(8,128)(2,1)S(1)} %collective-permute-done.5.p2, ...), custom_call_target="tpu_custom_call" | custom-call | flops 805306368 | bytes 8388608 | tf_op jit(solution)/shard_map/project/pallas_call | solution.py:354
  96.4 1.0 collective-permute-start.9
  97.4 0.7 collective-permute-start.14
  98.1 0.0 collective-permute-done.12.g2
  98.1 0.0 collective-permute-start.13
  98.1 0.5 collective-permute-start.15
  98.6 0.0 collective-permute-done.11.g1
  98.6 0.0 collective-permute-start.8
  98.6 3.4 %collective-permute-done.9.q2 = f32[128,384]{1,0:T(8,128)S(1)} collective-permute-done((f32[128,384]{1,0:T(8,128)S(1)}, f32[128,384]{1,0:T(8,128)S(1)}, u32[]{:S(2)}, u32[]{:S(2)}) %collective-permute-start.9) | collective-permute-done | bytes 196640 | tf_op jit(solution)/shard_map/ppermute | solution.py:34
  102.0 1.8 %collective-permute-start.10 = (f32[128,384]{1,0:T(8,128)S(1)}, f32[128,384]{1,0:T(8,128)S(1)}, u32[]{:S(2)}, u32[]{:S(2)}) collective-permute-start(f32[128,384]{1,0:T(8,128)S(1)} %collective-permute-done.9.q2), channel_id=1, source_target_pairs={{0,64},{64,0},{1,65},{65,1},{2,66},{66,2},{3,67},{67,3},{4,68},{68... | collective-permute-start | bytes 589832 | tf_op jit(solution)/shard_map/ppermute | solution.py:34
  103.9 0.0 collective-permute-done.8.q1
  103.9 1.0 collective-permute-done.10.q3
  104.9 4.6 %chain.1 = (bf16[128,256]{1,0:T(8,128)(2,1)}, bf16[8,128,640]{2,1,0:T(8,128)(2,1)}) custom-call(s32[1]{0:T(128)} %bitcast.me.me_ref, bf16[128,256]{1,0:T(8,128)(2,1)S(1)} %copy-done.14, f32[128,128]{1,0:T(8,128)S(1)} %get-tuple-element.25.square, f32[128,384]{1,0:T(8,128)S(1)} %get-tuple-element.26.q0, f32[128,384]{1,0:T(8,128)S(1)} %collective-permute-done.8.q1, ...), custom_call_target="tpu_custom_call" | custom-call | flops 4000000000 | bytes 6291456 | tf_op jit(solution)/shard_map/chain/pallas_call | solution.py:438
  109.6 5.0 %all-to-all-start.3 = ((bf16[8,128,640]{2,1,0:T(8,128)(2,1)}), bf16[8,128,640]{2,1,0:T(8,128)(2,1)S(1)}, u32[]{:S(2)}, u32[]{:S(2)}) async-start(bf16[8,128,640]{2,1,0:T(8,128)(2,1)} %get-tuple-element.28), calls=%async_computation.3 | async-start | bytes 2621440 | tf_op jit(solution)/shard_map/all_to_all | solution.py:573
  114.6 1.4 collective-permute-start.17
  116.0 1.2 collective-permute-start.16
  117.2 9.9 %collective-permute-done.17.t2 = bf16[1024,256]{1,0:T(8,128)(2,1)S(1)} collective-permute-done((bf16[1024,256]{1,0:T(8,128)(2,1)S(1)}, bf16[1024,256]{1,0:T(8,128)(2,1)S(1)}, u32[]{:S(2)}, u32[]{:S(2)}) %collective-permute-start.17) | collective-permute-done | bytes 524320 | tf_op jit(solution)/shard_map/ppermute | solution.py:34
  127.1 1.9 %collective-permute-start.18 = (bf16[1024,256]{1,0:T(8,128)(2,1)S(1)}, bf16[1024,256]{1,0:T(8,128)(2,1)}, u32[]{:S(2)}, u32[]{:S(2)}) collective-permute-start(bf16[1024,256]{1,0:T(8,128)(2,1)S(1)} %collective-permute-done.17.t2), channel_id=1, source_target_pairs={{0,64},{64,0},{1,65},{65,1},{2,66},{66,2},{3,67},{67,3},{4,68},{68... | collective-permute-start | bytes 1572872 | tf_op jit(solution)/shard_map/ppermute | solution.py:34
  128.9 1.1 dynamic-slice_bitcast_fusion.1.rows_own
  130.0 1.1 dynamic-slice_bitcast_fusion.rows_prev
  131.1 0.9 all-to-all-done.3.packed
  132.1 2.9 %share.1 = bf16[8,256,128]{2,1,0:T(8,128)(2,1)} custom-call(s32[1]{0:T(128)} %bitcast.me.me_ref, bf16[8,128,640]{2,1,0:T(8,128)(2,1)S(1)} %all-to-all-done.3.packed, bf16[1024,256]{1,0:T(8,128)(2,1)S(1)} %bitcast.34, bf16[1024,256]{1,0:T(8,128)(2,1)} %collective-permute-done.16.t1, bf16[1024,256]{1,0:T(8,128)(2,1)S(1)} %collective-permute-done.17.t2, ...), custom_call_target="tpu_custom_call" | custom-call | flops 2000000000 | bytes 6291456 | tf_op jit(solution)/shard_map/share/pallas_call | solution.py:491
  135.0 7.4 %all-to-all-start.4 = ((bf16[8,256,128]{2,1,0:T(8,128)(2,1)}), bf16[8,256,128]{2,1,0:T(8,128)(2,1)S(1)}, u32[]{:S(2)}, u32[]{:S(2)}) async-start(bf16[8,256,128]{2,1,0:T(8,128)(2,1)} %share.1), calls=%async_computation.4 | async-start | bytes 1048576 | tf_op jit(solution)/shard_map/all_to_all | solution.py:577
  142.4 0.7 constant_dynamic-slice_fusion.gain
  143.0 0.8 dynamic-slice_bitcast_fusion.2.weight_in
  143.8 17.1 %all-to-all-done.4.arrived = bf16[8,256,128]{2,1,0:T(8,128)(2,1)S(1)} async-done(((bf16[8,256,128]{2,1,0:T(8,128)(2,1)}), bf16[8,256,128]{2,1,0:T(8,128)(2,1)S(1)}, u32[]{:S(2)}, u32[]{:S(2)}) %all-to-all-start.4) | async-done | bytes 524320 | tf_op jit(solution)/shard_map/all_to_all | solution.py:577
  160.9 0.8 finish.1
  (29 shorter events, 0.1 us)
Async XLA Ops:
  3.5 27.4 %collective-permute-start = (bf16[8,256,256]{2,1,0:T(8,128)(2,1)}, bf16[8,256,256]{2,1,0:T(8,128)(2,1)}, u32[]{:S(2)}, u32[]{:S(2)}) collective-permute-start(bf16[8,256,256]{2,1,0:T(8,128)(2,1)} %get-tuple-element.20), channel_id=1, source_target_pairs={{0,64},{64,128},{128,192},{1,65},{65,129},{129,193},{2,66},{66,130... | collective-permute-start | bytes 3145736 | tf_op jit(solution)/shard_map/ppermute | solution.py:553
  35.5 33.8 %all-to-all-start.1 = ((bf16[64,4,2048]{2,1,0:T(4,128)(2,1)}), bf16[64,4,2048]{2,1,0:T(4,128)(2,1)}, u32[]{:S(2)}, u32[]{:S(2)}) async-start(bf16[64,4,2048]{2,1,0:T(4,128)(2,1)} %pick_rows.1.after), calls=%async_computation.1 | async-start | bytes 2097152 | tf_op jit(solution)/shard_map/all_to_all | solution.py:556
  46.1 12.0 %collective-permute-start.1 = (bf16[256,384]{1,0:T(8,128)(2,1)}, bf16[256,384]{1,0:T(8,128)(2,1)S(1)}, u32[]{:S(2)}, u32[]{:S(2)}) collective-permute-start(bf16[256,384]{1,0:T(8,128)(2,1)} %cross_products.1.refs_0_.a), channel_id=1, source_target_pairs={{0,2},{2,4},{4,6},{6,0},{1,3},{3,5},{5,7},{7,1},{8,10},{10,12},{12... | collective-permute-start | bytes 589832 | tf_op jit(solution)/shard_map/ppermute | solution.py:163
  47.3 17.3 %collective-permute-start.2 = (bf16[256,384]{1,0:T(8,128)(2,1)}, bf16[256,384]{1,0:T(8,128)(2,1)S(1)}, u32[]{:S(2)}, u32[]{:S(2)}) collective-permute-start(bf16[256,384]{1,0:T(8,128)(2,1)} %cross_products.1.refs_0_.a), channel_id=1, source_target_pairs={{0,4},{2,6},{4,0},{6,2},{1,5},{3,7},{5,1},{7,3},{8,12},{10,14},{12... | collective-permute-start | bytes 589832 | tf_op jit(solution)/shard_map/ppermute | solution.py:163
  49.8 15.6 %collective-permute-start.3 = (bf16[256,384]{1,0:T(8,128)(2,1)}, bf16[256,384]{1,0:T(8,128)(2,1)S(1)}, u32[]{:S(2)}, u32[]{:S(2)}) collective-permute-start(bf16[256,384]{1,0:T(8,128)(2,1)} %cross_products.1.refs_0_.a), channel_id=1, source_target_pairs={{0,6},{2,0},{4,2},{6,4},{1,7},{3,1},{5,3},{7,5},{8,14},{10,8},{12,... | collective-permute-start | bytes 589832 | tf_op jit(solution)/shard_map/ppermute | solution.py:163
  50.9 15.1 %copy-start.3 = (bf16[256,384]{1,0:T(8,128)(2,1)S(1)}, bf16[256,384]{1,0:T(8,128)(2,1)}, u32[]{:S(2)}) copy-start(bf16[256,384]{1,0:T(8,128)(2,1)} %cross_products.1.refs_0_.a) | copy-start | bytes 589828
  64.6 0.7 copy-start.9
  65.3 0.7 copy-start.11
  66.0 0.9 copy-start.7
  66.9 0.9 copy-start.10
  67.9 0.9 copy-start.12
  68.9 5.9 %collective-permute-start.7 = (bf16[256,384]{1,0:T(8,128)(2,1)S(1)}, bf16[256,384]{1,0:T(8,128)(2,1)S(1)}, u32[]{:S(2)}, u32[]{:S(2)}) collective-permute-start(bf16[256,384]{1,0:T(8,128)(2,1)S(1)} %sum_over_x.1.refs_0_.m0), channel_id=1, source_target_pairs={{0,128},{128,0},{1,129},{129,1},{2,130},{130,2},{3,131},{131,3},{4... | collective-permute-start | bytes 589832 | tf_op jit(solution)/shard_map/ppermute | solution.py:34
  70.6 19.4 %copy-start.1 = (bf16[8192,128]{1,0:T(8,128)(2,1)S(1)}, bf16[8192,128]{1,0:T(8,128)(2,1)}, u32[]{:S(2)}) copy-start(bf16[8192,128]{1,0:T(8,128)(2,1)} %get-tuple-element.23.gained) | copy-start | bytes 6291460
  70.6 1.0 copy-start.13
  72.8 0.8 copy-start.2
  73.6 10.6 %collective-permute-start.5 = (bf16[128,2048]{1,0:T(8,128)(2,1)}, bf16[128,2048]{1,0:T(8,128)(2,1)S(1)}, u32[]{:S(2)}, u32[]{:S(2)}) collective-permute-start(bf16[128,2048]{1,0:T(8,128)(2,1)} %get-tuple-element.22.p0), channel_id=1, source_target_pairs={{0,128},{128,0},{1,129},{129,1},{2,130},{130,2},{3,131},{131,3},{4... | collective-permute-start | bytes 1572872 | tf_op jit(solution)/shard_map/ppermute | solution.py:34
  74.7 0.7 copy-start.4
  75.4 14.2 %all-to-all-start.2 = ((bf16[8,128,256]{2,1,0:T(8,128)(2,1)}), bf16[8,128,256]{2,1,0:T(8,128)(2,1)S(1)}, u32[]{:S(2)}, u32[]{:S(2)}) async-start(bf16[8,128,256]{2,1,0:T(8,128)(2,1)} %ordered.1), calls=%async_computation.2 | async-start | bytes 1048576 | tf_op jit(solution)/shard_map/all_to_all | solution.py:567
  81.1 8.5 %collective-permute-start.4 = (bf16[128,2048]{1,0:T(8,128)(2,1)}, bf16[128,2048]{1,0:T(8,128)(2,1)}, u32[]{:S(2)}, u32[]{:S(2)}) collective-permute-start(bf16[128,2048]{1,0:T(8,128)(2,1)} %get-tuple-element.22.p0), channel_id=1, source_target_pairs={{0,64},{64,0},{1,65},{65,1},{2,66},{66,2},{3,67},{67,3},{4,68},{68... | collective-permute-start | bytes 1572872 | tf_op jit(solution)/shard_map/ppermute | solution.py:34
  84.2 5.9 %collective-permute-start.6 = (bf16[128,2048]{1,0:T(8,128)(2,1)S(1)}, bf16[128,2048]{1,0:T(8,128)(2,1)}, u32[]{:S(2)}, u32[]{:S(2)}) collective-permute-start(bf16[128,2048]{1,0:T(8,128)(2,1)S(1)} %collective-permute-done.5.p2), channel_id=1, source_target_pairs={{0,64},{64,0},{1,65},{65,1},{2,66},{66,2},{3,67},{67,3},{4,68},{68... | collective-permute-start | bytes 1572872 | tf_op jit(solution)/shard_map/ppermute | solution.py:34
  88.4 9.7 %collective-permute-start.12 = (bf16[384,256]{1,0:T(8,128)(2,1)}, bf16[384,256]{1,0:T(8,128)(2,1)S(1)}, u32[]{:S(2)}, u32[]{:S(2)}) collective-permute-start(bf16[384,256]{1,0:T(8,128)(2,1)} %get-tuple-element.21.after.g0), channel_id=1, source_target_pairs={{0,128},{128,0},{1,129},{129,1},{2,130},{130,2},{3,131},{131,3},{4... | collective-permute-start | bytes 589832 | tf_op jit(solution)/shard_map/ppermute | solution.py:34
  89.3 9.3 %collective-permute-start.11 = (bf16[384,256]{1,0:T(8,128)(2,1)}, bf16[384,256]{1,0:T(8,128)(2,1)}, u32[]{:S(2)}, u32[]{:S(2)}) collective-permute-start(bf16[384,256]{1,0:T(8,128)(2,1)} %get-tuple-element.21.after.g0), channel_id=1, source_target_pairs={{0,64},{64,0},{1,65},{65,1},{2,66},{66,2},{3,67},{67,3},{4,68},{68... | collective-permute-start | bytes 589832 | tf_op jit(solution)/shard_map/ppermute | solution.py:34
  90.0 2.2 %copy-start = (bf16[1,8192,256]{2,1,0:T(8,128)(2,1)S(1)}, bf16[1,8192,256]{2,1,0:T(8,128)(2,1)}, u32[]{:S(2)}) copy-start(bf16[1,8192,256]{2,1,0:T(8,128)(2,1)} %param.9) | copy-start | bytes 12582916
  92.2 0.9 copy-start.5
  93.2 11.8 %copy-start.6 = (bf16[256,384]{1,0:T(8,128)(2,1)S(1)}, bf16[256,384]{1,0:T(8,128)(2,1)}, u32[]{:S(2)}) copy-start(bf16[256,384]{1,0:T(8,128)(2,1)} %copy-done.4) | copy-start | bytes 589828
  93.2 11.8 %copy-start.8 = (bf16[384,256]{1,0:T(8,128)(2,1)S(1)}, bf16[384,256]{1,0:T(8,128)(2,1)}, u32[]{:S(2)}) copy-start(bf16[384,256]{1,0:T(8,128)(2,1)} %get-tuple-element.21.after.g0) | copy-start | bytes 589828
  93.2 11.8 %copy-start.14 = (bf16[128,256]{1,0:T(8,128)(2,1)S(1)}, bf16[128,256]{1,0:T(8,128)(2,1)}, u32[]{:S(2)}) copy-start(bf16[128,256]{1,0:T(8,128)(2,1)} %cot.1) | copy-start | bytes 196612
  96.4 5.6 %collective-permute-start.9 = (f32[128,384]{1,0:T(8,128)S(1)}, f32[128,384]{1,0:T(8,128)S(1)}, u32[]{:S(2)}, u32[]{:S(2)}) collective-permute-start(f32[128,384]{1,0:T(8,128)S(1)} %get-tuple-element.26.q0), channel_id=1, source_target_pairs={{0,128},{128,0},{1,129},{129,1},{2,130},{130,2},{3,131},{131,3},{4... | collective-permute-start | bytes 589832 | tf_op jit(solution)/shard_map/ppermute | solution.py:34
  97.4 6.4 %collective-permute-start.14 = (bf16[256,384]{1,0:T(8,128)(2,1)S(1)}, bf16[256,384]{1,0:T(8,128)(2,1)S(1)}, u32[]{:S(2)}, u32[]{:S(2)}) collective-permute-start(bf16[256,384]{1,0:T(8,128)(2,1)S(1)} %sum_over_x.1.refs_0_.m0), channel_id=1, source_target_pairs={{0,64},{64,0},{1,65},{65,1},{2,66},{66,2},{3,67},{67,3},{4,68},{68... | collective-permute-start | bytes 589832 | tf_op jit(solution)/shard_map/ppermute | solution.py:34
  98.1 5.8 %collective-permute-start.13 = (bf16[384,256]{1,0:T(8,128)(2,1)S(1)}, bf16[384,256]{1,0:T(8,128)(2,1)S(1)}, u32[]{:S(2)}, u32[]{:S(2)}) collective-permute-start(bf16[384,256]{1,0:T(8,128)(2,1)S(1)} %collective-permute-done.12.g2), channel_id=1, source_target_pairs={{0,64},{64,0},{1,65},{65,1},{2,66},{66,2},{3,67},{67,3},{4,68},{68... | collective-permute-start | bytes 589832 | tf_op jit(solution)/shard_map/ppermute | solution.py:34
  98.1 5.8 %collective-permute-start.15 = (bf16[256,384]{1,0:T(8,128)(2,1)S(1)}, bf16[256,384]{1,0:T(8,128)(2,1)S(1)}, u32[]{:S(2)}, u32[]{:S(2)}) collective-permute-start(bf16[256,384]{1,0:T(8,128)(2,1)S(1)} %copy-done.5), channel_id=1, source_target_pairs={{0,64},{64,0},{1,65},{65,1},{2,66},{66,2},{3,67},{67,3},{4,68},{68... | collective-permute-start | bytes 589832 | tf_op jit(solution)/shard_map/ppermute | solution.py:34
  98.6 5.2 %collective-permute-start.8 = (f32[128,384]{1,0:T(8,128)S(1)}, f32[128,384]{1,0:T(8,128)S(1)}, u32[]{:S(2)}, u32[]{:S(2)}) collective-permute-start(f32[128,384]{1,0:T(8,128)S(1)} %get-tuple-element.26.q0), channel_id=1, source_target_pairs={{0,64},{64,0},{1,65},{65,1},{2,66},{66,2},{3,67},{67,3},{4,68},{68... | collective-permute-start | bytes 589832 | tf_op jit(solution)/shard_map/ppermute | solution.py:34
  102.0 2.9 %collective-permute-start.10 = (f32[128,384]{1,0:T(8,128)S(1)}, f32[128,384]{1,0:T(8,128)S(1)}, u32[]{:S(2)}, u32[]{:S(2)}) collective-permute-start(f32[128,384]{1,0:T(8,128)S(1)} %collective-permute-done.9.q2), channel_id=1, source_target_pairs={{0,64},{64,0},{1,65},{65,1},{2,66},{66,2},{3,67},{67,3},{4,68},{68... | collective-permute-start | bytes 589832 | tf_op jit(solution)/shard_map/ppermute | solution.py:34
  109.6 22.5 %all-to-all-start.3 = ((bf16[8,128,640]{2,1,0:T(8,128)(2,1)}), bf16[8,128,640]{2,1,0:T(8,128)(2,1)S(1)}, u32[]{:S(2)}, u32[]{:S(2)}) async-start(bf16[8,128,640]{2,1,0:T(8,128)(2,1)} %get-tuple-element.28), calls=%async_computation.3 | async-start | bytes 2621440 | tf_op jit(solution)/shard_map/all_to_all | solution.py:573
  114.6 12.5 %collective-permute-start.17 = (bf16[1024,256]{1,0:T(8,128)(2,1)S(1)}, bf16[1024,256]{1,0:T(8,128)(2,1)S(1)}, u32[]{:S(2)}, u32[]{:S(2)}) collective-permute-start(bf16[1024,256]{1,0:T(8,128)(2,1)S(1)} %bitcast.32), channel_id=1, source_target_pairs={{0,128},{128,0},{1,129},{129,1},{2,130},{130,2},{3,131},{131,3},{4... | collective-permute-start | bytes 1572872 | tf_op jit(solution)/shard_map/ppermute | solution.py:34
  116.0 15.1 %collective-permute-start.16 = (bf16[1024,256]{1,0:T(8,128)(2,1)S(1)}, bf16[1024,256]{1,0:T(8,128)(2,1)}, u32[]{:S(2)}, u32[]{:S(2)}) collective-permute-start(bf16[1024,256]{1,0:T(8,128)(2,1)S(1)} %bitcast.33), channel_id=1, source_target_pairs={{0,64},{64,0},{1,65},{65,1},{2,66},{66,2},{3,67},{67,3},{4,68},{68... | collective-permute-start | bytes 1572872 | tf_op jit(solution)/shard_map/ppermute | solution.py:34
  127.1 4.0 %collective-permute-start.18 = (bf16[1024,256]{1,0:T(8,128)(2,1)S(1)}, bf16[1024,256]{1,0:T(8,128)(2,1)}, u32[]{:S(2)}, u32[]{:S(2)}) collective-permute-start(bf16[1024,256]{1,0:T(8,128)(2,1)S(1)} %collective-permute-done.17.t2), channel_id=1, source_target_pairs={{0,64},{64,0},{1,65},{65,1},{2,66},{66,2},{3,67},{67,3},{4,68},{68... | collective-permute-start | bytes 1572872 | tf_op jit(solution)/shard_map/ppermute | solution.py:34
  135.0 25.9 %all-to-all-start.4 = ((bf16[8,256,128]{2,1,0:T(8,128)(2,1)}), bf16[8,256,128]{2,1,0:T(8,128)(2,1)S(1)}, u32[]{:S(2)}, u32[]{:S(2)}) async-start(bf16[8,256,128]{2,1,0:T(8,128)(2,1)} %share.1), calls=%async_computation.4 | async-start | bytes 1048576 | tf_op jit(solution)/shard_map/all_to_all | solution.py:577

commit v8 on v7

--- a/solution.py
+++ b/solution.py
@@ -161,13 +161,12 @@
 
 def sum_over_x(v, after):
     parts = [v] + [lax.ppermute(v, X, [(i, (i + k) % 4) for i in range(4)]) for k in (1, 2, 3)]
-    vmem = pl.BlockSpec(memory_space=pltpu.VMEM)
     return pl.pallas_call(
         sum_kernel,
-        in_specs=[vmem] * 4 + [pl.BlockSpec(memory_space=pl.ANY)],
-        out_specs=vmem,
+        in_specs=[full(v.shape)] * 4 + [pl.BlockSpec(memory_space=pl.ANY)],
+        out_specs=full(v.shape),
         out_shape=jax.ShapeDtypeStruct(v.shape, BF16),
-        compiler_params=pltpu.CompilerParams(vmem_limit_bytes=16 * 2**20),
+        compiler_params=pltpu.CompilerParams(vmem_limit_bytes=GRANT),
         cost_estimate=pl.CostEstimate(flops=4 * v.size, bytes_accessed=10 * v.size, transcendentals=0),
         name="sum_over_x",
     )(*parts, after)
@@ -298,30 +297,32 @@
 
 def place_kernel(place, answered, *refs):
     part, turned = refs[-2:]
-    tokens, slots = part.shape[0], answered.shape[0]
+    shards, cap, cols = answered.shape
     width = turned.shape[2]
-    put = one_hot(place[...], slots).astype(BF16)
+    put = one_hot(place[...], shards * cap).astype(BF16)
     for t in range(turned.shape[0]):
-        rows = dot_nn(put, answered[:, t * width : (t + 1) * width]).astype(BF16)
+        rows = answered[:, :, t * width : (t + 1) * width].reshape(shards * cap, width)
+        rows = dot_nn(put, rows).astype(BF16)
         part[:, t * width : (t + 1) * width] = rows
         turned[t] = rows
 
 
 def place_rows(place, answered, copies, firsts):
     tokens = place.shape[0]
-    slots, cols = answered.shape
-    vmem = pl.BlockSpec(memory_space=pltpu.VMEM)
+    shards, cap, cols = answered.shape
     return pl.pallas_call(
         place_kernel,
-        in_specs=[vmem, vmem] + [pl.BlockSpec(memory_space=pl.ANY)] * len(firsts),
-        out_specs=[vmem, vmem],
+        in_specs=[full(place.shape), full(answered.shape)] + [pl.BlockSpec(memory_space=pl.ANY)] * len(firsts),
+        out_specs=[full((tokens, cols)), full((copies, tokens, cols // copies))],
         out_shape=[
             jax.ShapeDtypeStruct((tokens, cols), BF16),
             jax.ShapeDtypeStruct((copies, tokens, cols // copies), BF16),
         ],
-        compiler_params=pltpu.CompilerParams(vmem_limit_bytes=16 * 2**20),
+        compiler_params=pltpu.CompilerParams(vmem_limit_bytes=GRANT),
         cost_estimate=pl.CostEstimate(
-            flops=2 * slots * tokens * cols, bytes_accessed=2 * cols * (slots + 2 * tokens), transcendentals=0
+            flops=2 * shards * cap * tokens * cols,
+            bytes_accessed=2 * cols * (shards * cap + 2 * tokens),
+            transcendentals=0,
         ),
         name="place_rows",
     )(place, answered, *firsts)
@@ -561,7 +562,7 @@
     crossed = sum_over_x(crossed, own)
     mats = gather_peers(crossed)
 
-    part, turned = place_rows(place, answered.reshape(shards * CAP, cols), group, (crossed,))
+    part, turned = place_rows(place, answered, group, (crossed,))
     turned = ordered(turned, mats[2])
     pieces = gather_peers(part)
     turned = lax.all_to_all(turned, GATHER, split_axis=0, concat_axis=0, tiled=True)

time: 163 us -> 163 us (level)
  local copies, waits for them, and re-layouts: 14.6 us -> 9.17 us
  Pallas kernels: 32.2 us -> 35.3 us
  waiting for transfers between devices: 40.6 us -> 42.5 us
    unnamed x30 -> x24, local copies, waits for them, and re-layouts: 9.72 us -> 5.59 us
    pallas_call x2, Pallas kernels: 1.26 us -> 4.61 us  [the longest x1 2.62 us: place_rows(): pl.pallas_call(place_kernel, in_specs=[full(place.shape), full(answered.s...]
  transfers between devices with their start and end apart: 23 -> 23, of which waited for: 9 -> 9; matrix products, arithmetic and copies ran while one was open for 3% -> 2% of each run, Pallas kernels for 10% -> 12%
where the time goes in v8:
time: 163 us; the launch traced here: 162 us
  starting transfers between devices  50.5 us (31%)
  waiting for transfers between devices  42.5 us (26%)
  Pallas kernels  35.3 us (22%)
  blocking collectives  23.6 us (14%)
  local copies, waits for them, and re-layouts  9.17 us (6%)
    all_to_all x1, blocking collectives, per_device(): lax.all_to_all(requests, DP, split_axis=0, concat_axis=0, tiled=True)  23.6 us
    all_to_all x1, waiting for transfers between devices, per_device(): lax.all_to_all(shares, REDUCE, split_axis=0, concat_axis=0, tiled=True)  17.1 us
    ppermute x15, waiting for transfers between devices, swap(): return lax.ppermute(x, axis, [(0, 1), (1, 0)])  15.9 us
    ppermute x15, starting transfers between devices, swap(): return lax.ppermute(x, axis, [(0, 1), (1, 0)])  15.8 us
    all_to_all x1, starting transfers between devices, per_device(): lax.all_to_all(shares, REDUCE, split_axis=0, concat_axis=0, tiled=True)  7.73 us
    all_to_all x1, starting transfers between devices, per_device(): lax.all_to_all(turned, GATHER, split_axis=0, concat_axis=0, tiled=True)  7.27 us
    pallas_call x1, Pallas kernels, weights(): pl.pallas_call(weights_kernel, grid=(steps,), in_specs=[pl.BlockSpec((row...  7.09 us
    ppermute x3, waiting for transfers between devices, sum_over_x(): lax.ppermute(v, X, [(i, (i + k) % 4) for i in range(4)])  6.64 us
  transfers between devices with their start and end apart: 23, of which 9 were waited for; matrix products, arithmetic and copies ran while one was open for 2% of the time, Pallas kernels for 12%

profile of v8, /device:TPU:33, one launch (start us, length us, event | category | flops | bytes accessed | tf_op | source)
XLA Modules:
  0.0 161.9 jit_solution(17348433574093855236)
XLA Ops:
  0.6 2.9 %request.1 = (s32[128,1]{1,0:T(8,128)}, s32[64,4]{1,0:T(8,128)}, bf16[8,256,256]{2,1,0:T(8,128)(2,1)}) custom-call(s32[1]{0:T(128)} %bitcast.1.at, s32[1,128]{1,0:T(1,128)} %bitcast.41, bf16[8,4,256,256]{3,2,1,0:T(8,128)(2,1)} %bitcast.28), custom_call_target="tpu_custom_call" | custom-call | flops 10000000 | bytes 2097152 | tf_op jit(solution)/shard_map/request/pallas_call | solution.py:224
  3.5 3.8 %collective-permute-start = (bf16[8,256,256]{2,1,0:T(8,128)(2,1)}, bf16[8,256,256]{2,1,0:T(8,128)(2,1)}, u32[]{:S(2)}, u32[]{:S(2)}) collective-permute-start(bf16[8,256,256]{2,1,0:T(8,128)(2,1)} %get-tuple-element.20), channel_id=1, source_target_pairs={{0,64},{64,128},{128,192},{1,65},{65,129},{129,193},{2,66},{66,130... | collective-permute-start | bytes 3145736 | tf_op jit(solution)/shard_map/ppermute | solution.py:554
  7.3 23.6 %all_to_all.31 = s32[64,1,4]{2,1,0:T(1,128)} all-to-all(s32[64,1,4]{2,1,0:T(1,128)} %bitcast.40), channel_id=1, replica_groups=mesh['yl'=2,'co'=2,'zh'=4,'zl'=2,'x'=4,'yh'=2] {'zh','zl','x','yh'}, dimensions={0} | all-to-all | bytes 2048 | tf_op jit(solution)/shard_map/all_to_all | solution.py:555
  30.9 0.0 collective-permute-done.refs_0_.prev
  30.9 4.6 %pick_rows.1.after = bf16[64,4,2048]{2,1,0:T(4,128)(2,1)} custom-call(s32[64,4]{1,0:T(8,128)} %bitcast.39, bf16[1008,2048]{1,0:T(8,128)(2,1)} %table.1, bf16[8,256,256]{2,1,0:T(8,128)(2,1)} %collective-permute-done.refs_0_.prev), custom_call_target="tpu_custom_call" | custom-call | flops 1056964608 | bytes 5177344 | tf_op jit(solution)/shard_map/pick_rows/pallas_call | solution.py:277
  35.5 5.9 %all-to-all-start.1 = ((bf16[64,4,2048]{2,1,0:T(4,128)(2,1)}), bf16[64,4,2048]{2,1,0:T(4,128)(2,1)}, u32[]{:S(2)}, u32[]{:S(2)}) async-start(bf16[64,4,2048]{2,1,0:T(4,128)(2,1)} %pick_rows.1.after), calls=%async_computation.1 | async-start | bytes 2097152 | tf_op jit(solution)/shard_map/all_to_all | solution.py:557
  41.4 4.7 %cross_products.1.refs_0_.a = bf16[256,384]{1,0:T(8,128)(2,1)} custom-call(s32[1]{0:T(128)} %bitcast.1.at, bf16[8,4,256,256]{3,2,1,0:T(8,128)(2,1)} %bitcast.29, bf16[8,4,256,128]{3,2,1,0:T(8,128)(2,1)} %bitcast.35, f32[1,8192]{1,0:T(1,128)} %gain.3, bf16[8,256,256]{2,1,0:T(8,128)(2,1)} %collective-permute-done.refs_0_.prev, bf16[64,4,2048]{2,1,0:T(4,128)(2,1)} %pick_rows.1.after), custom_call_target="tpu_custom_call" | custom-call | flops 402653184 | bytes 2621440 | tf_op jit(solution)/shard_map/cross_products/pallas_call | solution.py:136
  46.1 1.3 collective-permute-start.1
  47.3 2.4 %collective-permute-start.2 = (bf16[256,384]{1,0:T(8,128)(2,1)}, bf16[256,384]{1,0:T(8,128)(2,1)S(1)}, u32[]{:S(2)}, u32[]{:S(2)}) collective-permute-start(bf16[256,384]{1,0:T(8,128)(2,1)} %cross_products.1.refs_0_.a), channel_id=1, source_target_pairs={{0,4},{2,6},{4,0},{6,2},{1,5},{3,7},{5,1},{7,3},{8,12},{10,14},{12... | collective-permute-start | bytes 589832 | tf_op jit(solution)/shard_map/ppermute | solution.py:163
  49.8 1.2 collective-permute-start.3
  50.9 7.1 %weights.1 = (bf16[8192,128]{1,0:T(8,128)(2,1)}, bf16[384,256]{1,0:T(8,128)(2,1)}) custom-call(bf16[8192,256]{1,0:T(8,128)(2,1)} %bitcast.30, bf16[8192,128]{1,0:T(8,128)(2,1)} %bitcast.36, f32[1,8192]{1,0:T(1,128)} %gain.3, bf16[128,8192]{1,0:T(8,128)(2,1)} %bitcast.37, bf16[256,384]{1,0:T(8,128)(2,1)} %cross_products.1.refs_0_.a), custom_call_target="tpu_custom_call" | custom-call | flops 1610612736 | bytes 12582912 | tf_op jit(solution)/shard_map/weights/pallas_call | solution.py:83
  58.0 0.0 collective-permute-done.1.b
  58.1 6.6 %collective-permute-done.2.c = bf16[256,384]{1,0:T(8,128)(2,1)S(1)} collective-permute-done((bf16[256,384]{1,0:T(8,128)(2,1)}, bf16[256,384]{1,0:T(8,128)(2,1)S(1)}, u32[]{:S(2)}, u32[]{:S(2)}) %collective-permute-start.2) | collective-permute-done | bytes 196640 | tf_op jit(solution)/shard_map/ppermute | solution.py:163
  64.7 0.0 collective-permute-done.3.d
  64.7 0.7 copy-done.10
  65.4 0.1 copy-done.11
  65.4 2.0 %sum_over_x.1.refs_0_.m0 = bf16[256,384]{1,0:T(8,128)(2,1)} custom-call(bf16[256,384]{1,0:T(8,128)(2,1)} %cross_products.1.refs_0_.a, bf16[256,384]{1,0:T(8,128)(2,1)} %copy-done.9, bf16[256,384]{1,0:T(8,128)(2,1)} %copy-done.10, bf16[256,384]{1,0:T(8,128)(2,1)} %copy-done.11, bf16[384,256]{1,0:T(8,128)(2,1)} %get-tuple-element.21.after.g0), custom_call_target="tpu_custom_call" | custom-call | flops 393216 | bytes 983040 | tf_op jit(solution)/shard_map/sum_over_x/pallas_call | solution.py:164
  67.4 0.0 collective-permute-start.7
  67.4 1.8 %all-to-all-done.1.answered = bf16[64,4,2048]{2,1,0:T(4,128)(2,1)} async-done(((bf16[64,4,2048]{2,1,0:T(4,128)(2,1)}), bf16[64,4,2048]{2,1,0:T(4,128)(2,1)}, u32[]{:S(2)}, u32[]{:S(2)}) %all-to-all-start.1) | async-done | bytes 1048608 | tf_op jit(solution)/shard_map/all_to_all | solution.py:557
  69.3 2.6 %place_rows.1 = (bf16[128,2048]{1,0:T(8,128)(2,1)}, bf16[8,128,256]{2,1,0:T(8,128)(2,1)}) custom-call(s32[128,1]{1,0:T(8,128)} %get-tuple-element.18.place, bf16[64,4,2048]{2,1,0:T(4,128)(2,1)} %all-to-all-done.1.answered, bf16[256,384]{1,0:T(8,128)(2,1)} %sum_over_x.1.refs_0_.m0), custom_call_target="tpu_custom_call" | custom-call | flops 134217728 | bytes 2097152 | tf_op jit(solution)/shard_map/place_rows/pallas_call | solution.py:313
  71.9 0.0 collective-permute-start.5
  71.9 0.5 collective-permute-done.7.refs_1_.second.m2
  72.4 0.7 copy-done.3
  73.1 7.3 %all-to-all-start.2 = ((bf16[8,128,256]{2,1,0:T(8,128)(2,1)}), bf16[8,128,256]{2,1,0:T(8,128)(2,1)S(1)}, u32[]{:S(2)}, u32[]{:S(2)}) async-start(bf16[8,128,256]{2,1,0:T(8,128)(2,1)} %ordered.1), calls=%async_computation.2 | async-start | bytes 1048576 | tf_op jit(solution)/shard_map/all_to_all | solution.py:568
  80.4 2.9 %collective-permute-start.4 = (bf16[128,2048]{1,0:T(8,128)(2,1)}, bf16[128,2048]{1,0:T(8,128)(2,1)}, u32[]{:S(2)}, u32[]{:S(2)}) collective-permute-start(bf16[128,2048]{1,0:T(8,128)(2,1)} %get-tuple-element.22.p0), channel_id=1, source_target_pairs={{0,64},{64,0},{1,65},{65,1},{2,66},{66,2},{3,67},{67,3},{4,68},{68... | collective-permute-start | bytes 1572872 | tf_op jit(solution)/shard_map/ppermute | solution.py:34
  83.2 0.0 collective-permute-done.5.p2
  83.2 3.8 %collective-permute-start.6 = (bf16[128,2048]{1,0:T(8,128)(2,1)S(1)}, bf16[128,2048]{1,0:T(8,128)(2,1)}, u32[]{:S(2)}, u32[]{:S(2)}) collective-permute-start(bf16[128,2048]{1,0:T(8,128)(2,1)S(1)} %collective-permute-done.5.p2), channel_id=1, source_target_pairs={{0,64},{64,0},{1,65},{65,1},{2,66},{66,2},{3,67},{67,3},{4,68},{68... | collective-permute-start | bytes 1572872 | tf_op jit(solution)/shard_map/ppermute | solution.py:34
  87.0 0.0 collective-permute-start.12
  87.0 0.3 collective-permute-start.11
  87.3 0.0 collective-permute-done.4.p1
  87.3 0.0 all-to-all-done.2.first
  87.3 1.4 collective-permute-done.6.p3
  88.7 2.2 %copy-done = bf16[1,8192,256]{2,1,0:T(8,128)(2,1)S(1)} copy-done((bf16[1,8192,256]{2,1,0:T(8,128)(2,1)S(1)}, bf16[1,8192,256]{2,1,0:T(8,128)(2,1)}, u32[]{:S(2)}) %copy-start) | copy-done | bytes 4194328
  90.9 0.9 copy-done.4
  91.8 1.0 copy-done.6
  92.9 3.1 %project.1 = (f32[128,384]{1,0:T(8,128)S(1)}, f32[128,128]{1,0:T(8,128)S(1)}) custom-call(s32[1]{0:T(128)} %bitcast.me.me_ref, bf16[128,2048]{1,0:T(8,128)(2,1)S(1)} %copy-done.6, bf16[128,2048]{1,0:T(8,128)(2,1)} %collective-permute-done.4.p1, bf16[128,2048]{1,0:T(8,128)(2,1)S(1)} %collective-permute-done.5.p2, ...), custom_call_target="tpu_custom_call" | custom-call | flops 805306368 | bytes 8388608 | tf_op jit(solution)/shard_map/project/pallas_call | solution.py:355
  96.0 0.2 collective-permute-start.9
  96.2 2.0 %collective-permute-start.14 = (bf16[256,384]{1,0:T(8,128)(2,1)S(1)}, bf16[256,384]{1,0:T(8,128)(2,1)S(1)}, u32[]{:S(2)}, u32[]{:S(2)}) collective-permute-start(bf16[256,384]{1,0:T(8,128)(2,1)S(1)} %copy-done.2), channel_id=1, source_target_pairs={{0,64},{64,0},{1,65},{65,1},{2,66},{66,2},{3,67},{67,3},{4,68},{68... | collective-permute-start | bytes 589832 | tf_op jit(solution)/shard_map/ppermute | solution.py:34
  98.2 0.1 collective-permute-start.13
  98.3 0.4 collective-permute-start.15
  98.7 0.0 collective-permute-done.11.g1
  98.7 0.1 collective-permute-start.8
  98.8 1.8 %collective-permute-done.9.q2 = f32[128,384]{1,0:T(8,128)S(1)} collective-permute-done((f32[128,384]{1,0:T(8,128)S(1)}, f32[128,384]{1,0:T(8,128)S(1)}, u32[]{:S(2)}, u32[]{:S(2)}) %collective-permute-start.9) | collective-permute-done | bytes 196640 | tf_op jit(solution)/shard_map/ppermute | solution.py:34
  100.6 2.9 %collective-permute-start.10 = (f32[128,384]{1,0:T(8,128)S(1)}, f32[128,384]{1,0:T(8,128)S(1)}, u32[]{:S(2)}, u32[]{:S(2)}) collective-permute-start(f32[128,384]{1,0:T(8,128)S(1)} %collective-permute-done.9.q2), channel_id=1, source_target_pairs={{0,64},{64,0},{1,65},{65,1},{2,66},{66,2},{3,67},{67,3},{4,68},{68... | collective-permute-start | bytes 589832 | tf_op jit(solution)/shard_map/ppermute | solution.py:34
  103.5 0.0 collective-permute-done.14.m1
  103.5 0.0 collective-permute-done.13.g3
  103.5 0.0 collective-permute-done.15.m3
  103.5 1.0 collective-permute-done.10.q3
  104.6 4.6 %chain.1 = (bf16[128,256]{1,0:T(8,128)(2,1)}, bf16[8,128,640]{2,1,0:T(8,128)(2,1)}) custom-call(s32[1]{0:T(128)} %bitcast.me.me_ref, bf16[128,256]{1,0:T(8,128)(2,1)S(1)} %copy-done.8, f32[128,128]{1,0:T(8,128)S(1)} %get-tuple-element.25.square, f32[128,384]{1,0:T(8,128)S(1)} %get-tuple-element.26.q0, f32[128,384]{1,0:T(8,128)S(1)} %collective-permute-done.8.q1, ...), custom_call_target="tpu_custom_call" | custom-call | flops 4000000000 | bytes 6291456 | tf_op jit(solution)/shard_map/chain/pallas_call | solution.py:439
  109.2 5.1 %all-to-all-start.3 = ((bf16[8,128,640]{2,1,0:T(8,128)(2,1)}), bf16[8,128,640]{2,1,0:T(8,128)(2,1)S(1)}, u32[]{:S(2)}, u32[]{:S(2)}) async-start(bf16[8,128,640]{2,1,0:T(8,128)(2,1)} %get-tuple-element.28), calls=%async_computation.3 | async-start | bytes 2621440 | tf_op jit(solution)/shard_map/all_to_all | solution.py:574
  114.3 0.1 collective-permute-start.17
  114.4 1.2 collective-permute-start.16
  115.6 11.2 %collective-permute-done.17.t2 = bf16[1024,256]{1,0:T(8,128)(2,1)S(1)} collective-permute-done((bf16[1024,256]{1,0:T(8,128)(2,1)S(1)}, bf16[1024,256]{1,0:T(8,128)(2,1)S(1)}, u32[]{:S(2)}, u32[]{:S(2)}) %collective-permute-start.17) | collective-permute-done | bytes 524320 | tf_op jit(solution)/shard_map/ppermute | solution.py:34
  126.8 1.8 %collective-permute-start.18 = (bf16[1024,256]{1,0:T(8,128)(2,1)S(1)}, bf16[1024,256]{1,0:T(8,128)(2,1)}, u32[]{:S(2)}, u32[]{:S(2)}) collective-permute-start(bf16[1024,256]{1,0:T(8,128)(2,1)S(1)} %collective-permute-done.17.t2), channel_id=1, source_target_pairs={{0,64},{64,0},{1,65},{65,1},{2,66},{66,2},{3,67},{67,3},{4,68},{68... | collective-permute-start | bytes 1572872 | tf_op jit(solution)/shard_map/ppermute | solution.py:34
  128.6 1.1 dynamic-slice_bitcast_fusion.1.rows_own
  129.7 1.1 dynamic-slice_bitcast_fusion.rows_prev
  130.8 0.0 collective-permute-done.16.t1
  130.8 1.0 all-to-all-done.3.packed
  131.8 2.9 %share.1 = bf16[8,256,128]{2,1,0:T(8,128)(2,1)} custom-call(s32[1]{0:T(128)} %bitcast.me.me_ref, bf16[8,128,640]{2,1,0:T(8,128)(2,1)S(1)} %all-to-all-done.3.packed, bf16[1024,256]{1,0:T(8,128)(2,1)S(1)} %bitcast.34, bf16[1024,256]{1,0:T(8,128)(2,1)} %collective-permute-done.16.t1, bf16[1024,256]{1,0:T(8,128)(2,1)S(1)} %collective-permute-done.17.t2, ...), custom_call_target="tpu_custom_call" | custom-call | flops 2000000000 | bytes 6291456 | tf_op jit(solution)/shard_map/share/pallas_call | solution.py:492
  134.7 7.7 %all-to-all-start.4 = ((bf16[8,256,128]{2,1,0:T(8,128)(2,1)}), bf16[8,256,128]{2,1,0:T(8,128)(2,1)S(1)}, u32[]{:S(2)}, u32[]{:S(2)}) async-start(bf16[8,256,128]{2,1,0:T(8,128)(2,1)} %share.1), calls=%async_computation.4 | async-start | bytes 1048576 | tf_op jit(solution)/shard_map/all_to_all | solution.py:578
  142.5 0.7 constant_dynamic-slice_fusion.gain
  143.1 0.8 dynamic-slice_bitcast_fusion.2.weight_in
  143.9 17.1 %all-to-all-done.4.arrived = bf16[8,256,128]{2,1,0:T(8,128)(2,1)S(1)} async-done(((bf16[8,256,128]{2,1,0:T(8,128)(2,1)}), bf16[8,256,128]{2,1,0:T(8,128)(2,1)S(1)}, u32[]{:S(2)}, u32[]{:S(2)}) %all-to-all-start.4) | async-done | bytes 524320 | tf_op jit(solution)/shard_map/all_to_all | solution.py:578
  161.0 0.8 finish.1
  (22 shorter events, 0.0 us)
Async XLA Ops:
  3.5 27.4 %collective-permute-start = (bf16[8,256,256]{2,1,0:T(8,128)(2,1)}, bf16[8,256,256]{2,1,0:T(8,128)(2,1)}, u32[]{:S(2)}, u32[]{:S(2)}) collective-permute-start(bf16[8,256,256]{2,1,0:T(8,128)(2,1)} %get-tuple-element.20), channel_id=1, source_target_pairs={{0,64},{64,128},{128,192},{1,65},{65,129},{129,193},{2,66},{66,130... | collective-permute-start | bytes 3145736 | tf_op jit(solution)/shard_map/ppermute | solution.py:554
  35.5 33.8 %all-to-all-start.1 = ((bf16[64,4,2048]{2,1,0:T(4,128)(2,1)}), bf16[64,4,2048]{2,1,0:T(4,128)(2,1)}, u32[]{:S(2)}, u32[]{:S(2)}) async-start(bf16[64,4,2048]{2,1,0:T(4,128)(2,1)} %pick_rows.1.after), calls=%async_computation.1 | async-start | bytes 2097152 | tf_op jit(solution)/shard_map/all_to_all | solution.py:557
  46.1 12.0 %collective-permute-start.1 = (bf16[256,384]{1,0:T(8,128)(2,1)}, bf16[256,384]{1,0:T(8,128)(2,1)S(1)}, u32[]{:S(2)}, u32[]{:S(2)}) collective-permute-start(bf16[256,384]{1,0:T(8,128)(2,1)} %cross_products.1.refs_0_.a), channel_id=1, source_target_pairs={{0,2},{2,4},{4,6},{6,0},{1,3},{3,5},{5,7},{7,1},{8,10},{10,12},{12... | collective-permute-start | bytes 589832 | tf_op jit(solution)/shard_map/ppermute | solution.py:163
  47.3 17.3 %collective-permute-start.2 = (bf16[256,384]{1,0:T(8,128)(2,1)}, bf16[256,384]{1,0:T(8,128)(2,1)S(1)}, u32[]{:S(2)}, u32[]{:S(2)}) collective-permute-start(bf16[256,384]{1,0:T(8,128)(2,1)} %cross_products.1.refs_0_.a), channel_id=1, source_target_pairs={{0,4},{2,6},{4,0},{6,2},{1,5},{3,7},{5,1},{7,3},{8,12},{10,14},{12... | collective-permute-start | bytes 589832 | tf_op jit(solution)/shard_map/ppermute | solution.py:163
  49.8 14.9 %collective-permute-start.3 = (bf16[256,384]{1,0:T(8,128)(2,1)}, bf16[256,384]{1,0:T(8,128)(2,1)S(1)}, u32[]{:S(2)}, u32[]{:S(2)}) collective-permute-start(bf16[256,384]{1,0:T(8,128)(2,1)} %cross_products.1.refs_0_.a), channel_id=1, source_target_pairs={{0,6},{2,0},{4,2},{6,4},{1,7},{3,1},{5,3},{7,5},{8,14},{10,8},{12,... | collective-permute-start | bytes 589832 | tf_op jit(solution)/shard_map/ppermute | solution.py:163
  58.0 6.7 %copy-start.9 = (bf16[256,384]{1,0:T(8,128)(2,1)}, bf16[256,384]{1,0:T(8,128)(2,1)S(1)}, u32[]{:S(2)}) copy-start(bf16[256,384]{1,0:T(8,128)(2,1)S(1)} %collective-permute-done.1.b) | copy-start | bytes 589828
  64.7 0.7 copy-start.10
  64.7 0.8 copy-start.11
  67.4 19.6 %copy-start.7 = (bf16[384,256]{1,0:T(8,128)(2,1)S(1)}, bf16[384,256]{1,0:T(8,128)(2,1)}, u32[]{:S(2)}) copy-start(bf16[384,256]{1,0:T(8,128)(2,1)} %get-tuple-element.21.after.g0) | copy-start | bytes 589828
  67.4 5.0 %collective-permute-start.7 = (bf16[256,384]{1,0:T(8,128)(2,1)}, bf16[256,384]{1,0:T(8,128)(2,1)S(1)}, u32[]{:S(2)}, u32[]{:S(2)}) collective-permute-start(bf16[256,384]{1,0:T(8,128)(2,1)} %sum_over_x.1.refs_0_.m0), channel_id=1, source_target_pairs={{0,128},{128,0},{1,129},{129,1},{2,130},{130,2},{3,131},{131,3},{4... | collective-permute-start | bytes 589832 | tf_op jit(solution)/shard_map/ppermute | solution.py:34
  71.9 16.8 %copy-start.1 = (bf16[8192,128]{1,0:T(8,128)(2,1)S(1)}, bf16[8192,128]{1,0:T(8,128)(2,1)}, u32[]{:S(2)}) copy-start(bf16[8192,128]{1,0:T(8,128)(2,1)} %get-tuple-element.23.gained) | copy-start | bytes 6291460
  71.9 11.3 %collective-permute-start.5 = (bf16[128,2048]{1,0:T(8,128)(2,1)}, bf16[128,2048]{1,0:T(8,128)(2,1)S(1)}, u32[]{:S(2)}, u32[]{:S(2)}) collective-permute-start(bf16[128,2048]{1,0:T(8,128)(2,1)} %get-tuple-element.22.p0), channel_id=1, source_target_pairs={{0,128},{128,0},{1,129},{129,1},{2,130},{130,2},{3,131},{131,3},{4... | collective-permute-start | bytes 1572872 | tf_op jit(solution)/shard_map/ppermute | solution.py:34
  72.4 0.7 copy-start.3
  73.1 14.2 %all-to-all-start.2 = ((bf16[8,128,256]{2,1,0:T(8,128)(2,1)}), bf16[8,128,256]{2,1,0:T(8,128)(2,1)S(1)}, u32[]{:S(2)}, u32[]{:S(2)}) async-start(bf16[8,128,256]{2,1,0:T(8,128)(2,1)} %ordered.1), calls=%async_computation.2 | async-start | bytes 1048576 | tf_op jit(solution)/shard_map/all_to_all | solution.py:568
  80.4 7.0 %collective-permute-start.4 = (bf16[128,2048]{1,0:T(8,128)(2,1)}, bf16[128,2048]{1,0:T(8,128)(2,1)}, u32[]{:S(2)}, u32[]{:S(2)}) collective-permute-start(bf16[128,2048]{1,0:T(8,128)(2,1)} %get-tuple-element.22.p0), channel_id=1, source_target_pairs={{0,64},{64,0},{1,65},{65,1},{2,66},{66,2},{3,67},{67,3},{4,68},{68... | collective-permute-start | bytes 1572872 | tf_op jit(solution)/shard_map/ppermute | solution.py:34
  83.2 5.5 %collective-permute-start.6 = (bf16[128,2048]{1,0:T(8,128)(2,1)S(1)}, bf16[128,2048]{1,0:T(8,128)(2,1)}, u32[]{:S(2)}, u32[]{:S(2)}) collective-permute-start(bf16[128,2048]{1,0:T(8,128)(2,1)S(1)} %collective-permute-done.5.p2), channel_id=1, source_target_pairs={{0,64},{64,0},{1,65},{65,1},{2,66},{66,2},{3,67},{67,3},{4,68},{68... | collective-permute-start | bytes 1572872 | tf_op jit(solution)/shard_map/ppermute | solution.py:34
  87.0 11.2 %collective-permute-start.12 = (bf16[384,256]{1,0:T(8,128)(2,1)S(1)}, bf16[384,256]{1,0:T(8,128)(2,1)S(1)}, u32[]{:S(2)}, u32[]{:S(2)}) collective-permute-start(bf16[384,256]{1,0:T(8,128)(2,1)S(1)} %copy-done.7), channel_id=1, source_target_pairs={{0,128},{128,0},{1,129},{129,1},{2,130},{130,2},{3,131},{131,3},{4... | collective-permute-start | bytes 589832 | tf_op jit(solution)/shard_map/ppermute | solution.py:34
  87.0 11.7 %collective-permute-start.11 = (bf16[384,256]{1,0:T(8,128)(2,1)S(1)}, bf16[384,256]{1,0:T(8,128)(2,1)}, u32[]{:S(2)}, u32[]{:S(2)}) collective-permute-start(bf16[384,256]{1,0:T(8,128)(2,1)S(1)} %copy-done.7), channel_id=1, source_target_pairs={{0,64},{64,0},{1,65},{65,1},{2,66},{66,2},{3,67},{67,3},{4,68},{68... | collective-permute-start | bytes 589832 | tf_op jit(solution)/shard_map/ppermute | solution.py:34
  88.7 2.2 %copy-start = (bf16[1,8192,256]{2,1,0:T(8,128)(2,1)S(1)}, bf16[1,8192,256]{2,1,0:T(8,128)(2,1)}, u32[]{:S(2)}) copy-start(bf16[1,8192,256]{2,1,0:T(8,128)(2,1)} %param.9) | copy-start | bytes 12582916
  90.9 0.9 copy-start.4
  91.8 1.0 copy-start.6
  92.9 3.3 %copy-start.2 = (bf16[256,384]{1,0:T(8,128)(2,1)S(1)}, bf16[256,384]{1,0:T(8,128)(2,1)}, u32[]{:S(2)}) copy-start(bf16[256,384]{1,0:T(8,128)(2,1)} %sum_over_x.1.refs_0_.m0) | copy-start | bytes 589828
  92.9 11.7 %copy-start.5 = (bf16[256,384]{1,0:T(8,128)(2,1)S(1)}, bf16[256,384]{1,0:T(8,128)(2,1)}, u32[]{:S(2)}) copy-start(bf16[256,384]{1,0:T(8,128)(2,1)} %copy-done.3) | copy-start | bytes 589828
  92.9 11.7 %copy-start.8 = (bf16[128,256]{1,0:T(8,128)(2,1)S(1)}, bf16[128,256]{1,0:T(8,128)(2,1)}, u32[]{:S(2)}) copy-start(bf16[128,256]{1,0:T(8,128)(2,1)} %cot.1) | copy-start | bytes 196612
  96.0 4.6 %collective-permute-start.9 = (f32[128,384]{1,0:T(8,128)S(1)}, f32[128,384]{1,0:T(8,128)S(1)}, u32[]{:S(2)}, u32[]{:S(2)}) collective-permute-start(f32[128,384]{1,0:T(8,128)S(1)} %get-tuple-element.26.q0), channel_id=1, source_target_pairs={{0,128},{128,0},{1,129},{129,1},{2,130},{130,2},{3,131},{131,3},{4... | collective-permute-start | bytes 589832 | tf_op jit(solution)/shard_map/ppermute | solution.py:34
  96.2 7.3 %collective-permute-start.14 = (bf16[256,384]{1,0:T(8,128)(2,1)S(1)}, bf16[256,384]{1,0:T(8,128)(2,1)S(1)}, u32[]{:S(2)}, u32[]{:S(2)}) collective-permute-start(bf16[256,384]{1,0:T(8,128)(2,1)S(1)} %copy-done.2), channel_id=1, source_target_pairs={{0,64},{64,0},{1,65},{65,1},{2,66},{66,2},{3,67},{67,3},{4,68},{68... | collective-permute-start | bytes 589832 | tf_op jit(solution)/shard_map/ppermute | solution.py:34
  98.2 5.3 %collective-permute-start.13 = (bf16[384,256]{1,0:T(8,128)(2,1)S(1)}, bf16[384,256]{1,0:T(8,128)(2,1)S(1)}, u32[]{:S(2)}, u32[]{:S(2)}) collective-permute-start(bf16[384,256]{1,0:T(8,128)(2,1)S(1)} %collective-permute-done.12.g2), channel_id=1, source_target_pairs={{0,64},{64,0},{1,65},{65,1},{2,66},{66,2},{3,67},{67,3},{4,68},{68... | collective-permute-start | bytes 589832 | tf_op jit(solution)/shard_map/ppermute | solution.py:34
  98.3 5.2 %collective-permute-start.15 = (bf16[256,384]{1,0:T(8,128)(2,1)S(1)}, bf16[256,384]{1,0:T(8,128)(2,1)S(1)}, u32[]{:S(2)}, u32[]{:S(2)}) collective-permute-start(bf16[256,384]{1,0:T(8,128)(2,1)S(1)} %copy-done.4), channel_id=1, source_target_pairs={{0,64},{64,0},{1,65},{65,1},{2,66},{66,2},{3,67},{67,3},{4,68},{68... | collective-permute-start | bytes 589832 | tf_op jit(solution)/shard_map/ppermute | solution.py:34
  98.7 4.8 %collective-permute-start.8 = (f32[128,384]{1,0:T(8,128)S(1)}, f32[128,384]{1,0:T(8,128)S(1)}, u32[]{:S(2)}, u32[]{:S(2)}) collective-permute-start(f32[128,384]{1,0:T(8,128)S(1)} %get-tuple-element.26.q0), channel_id=1, source_target_pairs={{0,64},{64,0},{1,65},{65,1},{2,66},{66,2},{3,67},{67,3},{4,68},{68... | collective-permute-start | bytes 589832 | tf_op jit(solution)/shard_map/ppermute | solution.py:34
  100.6 4.0 %collective-permute-start.10 = (f32[128,384]{1,0:T(8,128)S(1)}, f32[128,384]{1,0:T(8,128)S(1)}, u32[]{:S(2)}, u32[]{:S(2)}) collective-permute-start(f32[128,384]{1,0:T(8,128)S(1)} %collective-permute-done.9.q2), channel_id=1, source_target_pairs={{0,64},{64,0},{1,65},{65,1},{2,66},{66,2},{3,67},{67,3},{4,68},{68... | collective-permute-start | bytes 589832 | tf_op jit(solution)/shard_map/ppermute | solution.py:34
  109.2 22.6 %all-to-all-start.3 = ((bf16[8,128,640]{2,1,0:T(8,128)(2,1)}), bf16[8,128,640]{2,1,0:T(8,128)(2,1)S(1)}, u32[]{:S(2)}, u32[]{:S(2)}) async-start(bf16[8,128,640]{2,1,0:T(8,128)(2,1)} %get-tuple-element.28), calls=%async_computation.3 | async-start | bytes 2621440 | tf_op jit(solution)/shard_map/all_to_all | solution.py:574
  114.3 12.5 %collective-permute-start.17 = (bf16[1024,256]{1,0:T(8,128)(2,1)S(1)}, bf16[1024,256]{1,0:T(8,128)(2,1)S(1)}, u32[]{:S(2)}, u32[]{:S(2)}) collective-permute-start(bf16[1024,256]{1,0:T(8,128)(2,1)S(1)} %bitcast.32), channel_id=1, source_target_pairs={{0,128},{128,0},{1,129},{129,1},{2,130},{130,2},{3,131},{131,3},{4... | collective-permute-start | bytes 1572872 | tf_op jit(solution)/shard_map/ppermute | solution.py:34
  114.4 16.4 %collective-permute-start.16 = (bf16[1024,256]{1,0:T(8,128)(2,1)S(1)}, bf16[1024,256]{1,0:T(8,128)(2,1)}, u32[]{:S(2)}, u32[]{:S(2)}) collective-permute-start(bf16[1024,256]{1,0:T(8,128)(2,1)S(1)} %bitcast.33), channel_id=1, source_target_pairs={{0,64},{64,0},{1,65},{65,1},{2,66},{66,2},{3,67},{67,3},{4,68},{68... | collective-permute-start | bytes 1572872 | tf_op jit(solution)/shard_map/ppermute | solution.py:34
  126.8 4.0 %collective-permute-start.18 = (bf16[1024,256]{1,0:T(8,128)(2,1)S(1)}, bf16[1024,256]{1,0:T(8,128)(2,1)}, u32[]{:S(2)}, u32[]{:S(2)}) collective-permute-start(bf16[1024,256]{1,0:T(8,128)(2,1)S(1)} %collective-permute-done.17.t2), channel_id=1, source_target_pairs={{0,64},{64,0},{1,65},{65,1},{2,66},{66,2},{3,67},{67,3},{4,68},{68... | collective-permute-start | bytes 1572872 | tf_op jit(solution)/shard_map/ppermute | solution.py:34
  134.7 26.3 %all-to-all-start.4 = ((bf16[8,256,128]{2,1,0:T(8,128)(2,1)}), bf16[8,256,128]{2,1,0:T(8,128)(2,1)S(1)}, u32[]{:S(2)}, u32[]{:S(2)}) async-start(bf16[8,256,128]{2,1,0:T(8,128)(2,1)} %share.1), calls=%async_computation.4 | async-start | bytes 1048576 | tf_op jit(solution)/shard_map/all_to_all | solution.py:578

commit v9 on v8

--- a/solution.py
+++ b/solution.py
@@ -370,7 +370,7 @@
             jax.ShapeDtypeStruct((tokens, r + h), F32),
             jax.ShapeDtypeStruct((tokens, 128), F32),
         ],
-        compiler_params=pltpu.CompilerParams(vmem_limit_bytes=24 * 2**20),
+        compiler_params=pltpu.CompilerParams(vmem_limit_bytes=GRANT),
         cost_estimate=pl.CostEstimate(
             flops=8 * tokens * cols * (r + h), bytes_accessed=8 * cols * (r + h + tokens), transcendentals=0
         ),

time: 163 us -> 164 us (level)
  Pallas kernels: 35.3 us -> 38 us
    pallas_call x1, Pallas kernels: 3.1 us -> 5.63 us  [project(): pl.pallas_call(project_kernel, grid_spec=pltpu.PrefetchScalarGridSpec(num...]
    unnamed x24 -> x30, local copies, waits for them, and re-layouts: 5.59 us -> 4.02 us
  transfers between devices with their start and end apart: 23 -> 23, of which waited for: 9 -> 10; matrix products, arithmetic and copies ran while one was open for 2% -> 2% of each run, Pallas kernels for 12% -> 13%
where the time goes in v9:
time: 164 us; the launch traced here: 163 us
  starting transfers between devices  50.8 us (31%)
  waiting for transfers between devices  42.5 us (26%)
  Pallas kernels  38 us (23%)
  blocking collectives  23.5 us (14%)
  local copies, waits for them, and re-layouts  7.6 us (5%)
    all_to_all x1, blocking collectives, per_device(): lax.all_to_all(requests, DP, split_axis=0, concat_axis=0, tiled=True)  23.5 us
    all_to_all x1, waiting for transfers between devices, per_device(): lax.all_to_all(shares, REDUCE, split_axis=0, concat_axis=0, tiled=True)  17.1 us
    ppermute x15, starting transfers between devices, swap(): return lax.ppermute(x, axis, [(0, 1), (1, 0)])  16.6 us
    ppermute x15, waiting for transfers between devices, swap(): return lax.ppermute(x, axis, [(0, 1), (1, 0)])  15.8 us
    all_to_all x1, starting transfers between devices, per_device(): lax.all_to_all(shares, REDUCE, split_axis=0, concat_axis=0, tiled=True)  7.69 us
    ppermute x3, waiting for transfers between devices, sum_over_x(): lax.ppermute(v, X, [(i, (i + k) % 4) for i in range(4)])  7.62 us
    pallas_call x1, Pallas kernels, weights(): pl.pallas_call(weights_kernel, grid=(steps,), in_specs=[pl.BlockSpec((row...  7.1 us
    all_to_all x1, starting transfers between devices, per_device(): lax.all_to_all(turned, GATHER, split_axis=0, concat_axis=0, tiled=True)  6.64 us
  transfers between devices with their start and end apart: 23, of which 10 were waited for; matrix products, arithmetic and copies ran while one was open for 2% of the time, Pallas kernels for 13%

profile of v9, /device:TPU:33, one launch (start us, length us, event | category | flops | bytes accessed | tf_op | source)
XLA Modules:
  0.0 163.3 jit_solution(10306660183565183574)
XLA Ops:
  0.6 2.9 %request.1 = (s32[128,1]{1,0:T(8,128)}, s32[64,4]{1,0:T(8,128)}, bf16[8,256,256]{2,1,0:T(8,128)(2,1)}) custom-call(s32[1]{0:T(128)} %bitcast.1.at, s32[1,128]{1,0:T(1,128)} %bitcast.41, bf16[8,4,256,256]{3,2,1,0:T(8,128)(2,1)} %bitcast.31), custom_call_target="tpu_custom_call" | custom-call | flops 10000000 | bytes 2097152 | tf_op jit(solution)/shard_map/request/pallas_call | solution.py:224
  3.5 3.8 %collective-permute-start = (bf16[8,256,256]{2,1,0:T(8,128)(2,1)}, bf16[8,256,256]{2,1,0:T(8,128)(2,1)}, u32[]{:S(2)}, u32[]{:S(2)}) collective-permute-start(bf16[8,256,256]{2,1,0:T(8,128)(2,1)} %get-tuple-element.20), channel_id=1, source_target_pairs={{0,64},{64,128},{128,192},{1,65},{65,129},{129,193},{2,66},{66,130... | collective-permute-start | bytes 3145736 | tf_op jit(solution)/shard_map/ppermute | solution.py:554
  7.3 23.5 %all_to_all.31 = s32[64,1,4]{2,1,0:T(1,128)} all-to-all(s32[64,1,4]{2,1,0:T(1,128)} %bitcast.40), channel_id=1, replica_groups=mesh['yl'=2,'co'=2,'zh'=4,'zl'=2,'x'=4,'yh'=2] {'zh','zl','x','yh'}, dimensions={0} | all-to-all | bytes 2048 | tf_op jit(solution)/shard_map/all_to_all | solution.py:555
  30.8 0.0 collective-permute-done.refs_0_.prev
  30.8 4.6 %pick_rows.1.after = bf16[64,4,2048]{2,1,0:T(4,128)(2,1)} custom-call(s32[64,4]{1,0:T(8,128)} %bitcast.39, bf16[1008,2048]{1,0:T(8,128)(2,1)} %table.1, bf16[8,256,256]{2,1,0:T(8,128)(2,1)} %collective-permute-done.refs_0_.prev), custom_call_target="tpu_custom_call" | custom-call | flops 1056964608 | bytes 5177344 | tf_op jit(solution)/shard_map/pick_rows/pallas_call | solution.py:277
  35.3 6.2 %all-to-all-start.1 = ((bf16[64,4,2048]{2,1,0:T(4,128)(2,1)}), bf16[64,4,2048]{2,1,0:T(4,128)(2,1)}, u32[]{:S(2)}, u32[]{:S(2)}) async-start(bf16[64,4,2048]{2,1,0:T(4,128)(2,1)} %pick_rows.1.after), calls=%async_computation.1 | async-start | bytes 2097152 | tf_op jit(solution)/shard_map/all_to_all | solution.py:557
  41.5 4.7 %cross_products.1.refs_0_.a = bf16[256,384]{1,0:T(8,128)(2,1)} custom-call(s32[1]{0:T(128)} %bitcast.1.at, bf16[8,4,256,256]{3,2,1,0:T(8,128)(2,1)} %bitcast.32, bf16[8,4,256,128]{3,2,1,0:T(8,128)(2,1)} %bitcast.35, f32[1,8192]{1,0:T(1,128)} %gain.3, bf16[8,256,256]{2,1,0:T(8,128)(2,1)} %collective-permute-done.refs_0_.prev, bf16[64,4,2048]{2,1,0:T(4,128)(2,1)} %pick_rows.1.after), custom_call_target="tpu_custom_call" | custom-call | flops 402653184 | bytes 2621440 | tf_op jit(solution)/shard_map/cross_products/pallas_call | solution.py:136
  46.2 1.3 collective-permute-start.1
  47.5 2.4 %collective-permute-start.2 = (bf16[256,384]{1,0:T(8,128)(2,1)}, bf16[256,384]{1,0:T(8,128)(2,1)S(1)}, u32[]{:S(2)}, u32[]{:S(2)}) collective-permute-start(bf16[256,384]{1,0:T(8,128)(2,1)} %cross_products.1.refs_0_.a), channel_id=1, source_target_pairs={{0,4},{2,6},{4,0},{6,2},{1,5},{3,7},{5,1},{7,3},{8,12},{10,14},{12... | collective-permute-start | bytes 589832 | tf_op jit(solution)/shard_map/ppermute | solution.py:163
  49.9 1.2 collective-permute-start.3
  51.1 7.1 %weights.1 = (bf16[8192,128]{1,0:T(8,128)(2,1)}, bf16[384,256]{1,0:T(8,128)(2,1)}) custom-call(bf16[8192,256]{1,0:T(8,128)(2,1)} %bitcast.33, bf16[8192,128]{1,0:T(8,128)(2,1)} %bitcast.36, f32[1,8192]{1,0:T(1,128)} %gain.3, bf16[128,8192]{1,0:T(8,128)(2,1)} %bitcast.37, bf16[256,384]{1,0:T(8,128)(2,1)} %cross_products.1.refs_0_.a), custom_call_target="tpu_custom_call" | custom-call | flops 1610612736 | bytes 12582912 | tf_op jit(solution)/shard_map/weights/pallas_call | solution.py:83
  58.2 0.0 collective-permute-done.1.b
  58.2 7.6 %collective-permute-done.2.c = bf16[256,384]{1,0:T(8,128)(2,1)S(1)} collective-permute-done((bf16[256,384]{1,0:T(8,128)(2,1)}, bf16[256,384]{1,0:T(8,128)(2,1)S(1)}, u32[]{:S(2)}, u32[]{:S(2)}) %collective-permute-start.2) | collective-permute-done | bytes 196640 | tf_op jit(solution)/shard_map/ppermute | solution.py:163
  65.8 0.0 collective-permute-done.3.d
  65.8 0.7 copy-done.13
  66.5 0.1 copy-done.14
  66.6 2.0 %sum_over_x.1.refs_0_.m0 = bf16[256,384]{1,0:T(8,128)(2,1)} custom-call(bf16[256,384]{1,0:T(8,128)(2,1)} %cross_products.1.refs_0_.a, bf16[256,384]{1,0:T(8,128)(2,1)} %copy-done.12, bf16[256,384]{1,0:T(8,128)(2,1)} %copy-done.13, bf16[256,384]{1,0:T(8,128)(2,1)} %copy-done.14, bf16[384,256]{1,0:T(8,128)(2,1)} %get-tuple-element.21.after.g0), custom_call_target="tpu_custom_call" | custom-call | flops 393216 | bytes 983040 | tf_op jit(solution)/shard_map/sum_over_x/pallas_call | solution.py:164
  68.6 0.0 collective-permute-start.7
  68.6 1.0 all-to-all-done.1.answered
  69.6 2.6 %place_rows.1 = (bf16[128,2048]{1,0:T(8,128)(2,1)}, bf16[8,128,256]{2,1,0:T(8,128)(2,1)}) custom-call(s32[128,1]{1,0:T(8,128)} %get-tuple-element.18.place, bf16[64,4,2048]{2,1,0:T(4,128)(2,1)} %all-to-all-done.1.answered, bf16[256,384]{1,0:T(8,128)(2,1)} %sum_over_x.1.refs_0_.m0), custom_call_target="tpu_custom_call" | custom-call | flops 134217728 | bytes 2097152 | tf_op jit(solution)/shard_map/place_rows/pallas_call | solution.py:313
  72.2 0.4 collective-permute-start.5
  72.7 0.6 collective-permute-done.7.refs_1_.second.m2
  73.3 0.7 copy-done.3
  74.0 6.6 %all-to-all-start.2 = ((bf16[8,128,256]{2,1,0:T(8,128)(2,1)}), bf16[8,128,256]{2,1,0:T(8,128)(2,1)S(1)}, u32[]{:S(2)}, u32[]{:S(2)}) async-start(bf16[8,128,256]{2,1,0:T(8,128)(2,1)} %ordered.1), calls=%async_computation.2 | async-start | bytes 1048576 | tf_op jit(solution)/shard_map/all_to_all | solution.py:568
  80.6 2.6 %collective-permute-start.4 = (bf16[128,2048]{1,0:T(8,128)(2,1)S(1)}, bf16[128,2048]{1,0:T(8,128)(2,1)S(1)}, u32[]{:S(2)}, u32[]{:S(2)}) collective-permute-start(bf16[128,2048]{1,0:T(8,128)(2,1)S(1)} %copy-done.8), channel_id=1, source_target_pairs={{0,64},{64,0},{1,65},{65,1},{2,66},{66,2},{3,67},{67,3},{4,68},{68... | collective-permute-start | bytes 1572872 | tf_op jit(solution)/shard_map/ppermute | solution.py:34
  83.2 0.4 collective-permute-done.5.p2
  83.6 3.8 %collective-permute-start.6 = (bf16[128,2048]{1,0:T(8,128)(2,1)S(1)}, bf16[128,2048]{1,0:T(8,128)(2,1)S(1)}, u32[]{:S(2)}, u32[]{:S(2)}) collective-permute-start(bf16[128,2048]{1,0:T(8,128)(2,1)S(1)} %collective-permute-done.5.p2), channel_id=1, source_target_pairs={{0,64},{64,0},{1,65},{65,1},{2,66},{66,2},{3,67},{67,3},{4,68},{68... | collective-permute-start | bytes 1572872 | tf_op jit(solution)/shard_map/ppermute | solution.py:34
  87.4 0.0 collective-permute-start.12
  87.4 0.3 collective-permute-start.11
  87.6 0.0 collective-permute-done.4.p1
  87.7 1.2 collective-permute-done.6.p3
  88.9 0.8 copy-done.11
  89.7 5.6 %project.1 = (f32[128,384]{1,0:T(8,128)}, f32[128,128]{1,0:T(8,128)}) custom-call(s32[1]{0:T(128)} %bitcast.me.me_ref, bf16[128,2048]{1,0:T(8,128)(2,1)} %get-tuple-element.22.p0, bf16[128,2048]{1,0:T(8,128)(2,1)} %copy-done.10, bf16[128,2048]{1,0:T(8,128)(2,1)} %copy-done.9, bf16[128,2048]{1,0:T(8,128)(2,1)} %copy-done.11, bf16[8192,256]{1,0:T(8,128)(2,1)} %bitcast.34, ...), custom_call_target="tpu_custom_call" | custom-call | flops 805306368 | bytes 8388608 | tf_op jit(solution)/shard_map/project/pallas_call | solution.py:355
  95.3 0.6 collective-permute-start.9
  95.9 1.8 %collective-permute-start.14 = (bf16[256,384]{1,0:T(8,128)(2,1)S(1)}, bf16[256,384]{1,0:T(8,128)(2,1)S(1)}, u32[]{:S(2)}, u32[]{:S(2)}) collective-permute-start(bf16[256,384]{1,0:T(8,128)(2,1)S(1)} %copy-done.2), channel_id=1, source_target_pairs={{0,64},{64,0},{1,65},{65,1},{2,66},{66,2},{3,67},{67,3},{4,68},{68... | collective-permute-start | bytes 589832 | tf_op jit(solution)/shard_map/ppermute | solution.py:34
  97.7 0.1 collective-permute-start.13
  97.8 0.4 collective-permute-start.15
  98.2 0.0 collective-permute-done.11.g1
  98.2 0.1 collective-permute-start.8
  98.3 1.8 %collective-permute-done.9.q2 = f32[128,384]{1,0:T(8,128)S(1)} collective-permute-done((f32[128,384]{1,0:T(8,128)}, f32[128,384]{1,0:T(8,128)S(1)}, u32[]{:S(2)}, u32[]{:S(2)}) %collective-permute-start.9) | collective-permute-done | bytes 196640 | tf_op jit(solution)/shard_map/ppermute | solution.py:34
  100.1 2.9 %collective-permute-start.10 = (f32[128,384]{1,0:T(8,128)S(1)}, f32[128,384]{1,0:T(8,128)S(1)}, u32[]{:S(2)}, u32[]{:S(2)}) collective-permute-start(f32[128,384]{1,0:T(8,128)S(1)} %collective-permute-done.9.q2), channel_id=1, source_target_pairs={{0,64},{64,0},{1,65},{65,1},{2,66},{66,2},{3,67},{67,3},{4,68},{68... | collective-permute-start | bytes 589832 | tf_op jit(solution)/shard_map/ppermute | solution.py:34
  103.0 0.0 collective-permute-done.14.m1
  103.0 0.0 collective-permute-done.13.g3
  103.0 0.0 collective-permute-done.8.q1
  103.0 1.0 collective-permute-done.10.q3
  104.0 0.9 copy-done.5
  105.0 0.8 copy-done.7
  105.8 4.8 %chain.1 = (bf16[128,256]{1,0:T(8,128)(2,1)}, bf16[8,128,640]{2,1,0:T(8,128)(2,1)}) custom-call(s32[1]{0:T(128)} %bitcast.me.me_ref, bf16[128,256]{1,0:T(8,128)(2,1)S(1)} %copy-done.6, f32[128,128]{1,0:T(8,128)S(1)} %copy-done.7, f32[128,384]{1,0:T(8,128)S(1)} %copy-done.5, f32[128,384]{1,0:T(8,128)S(1)} %collective-permute-done.8.q1, ...), custom_call_target="tpu_custom_call" | custom-call | flops 4000000000 | bytes 6291456 | tf_op jit(solution)/shard_map/chain/pallas_call | solution.py:439
  110.7 5.0 %all-to-all-start.3 = ((bf16[8,128,640]{2,1,0:T(8,128)(2,1)}), bf16[8,128,640]{2,1,0:T(8,128)(2,1)S(1)}, u32[]{:S(2)}, u32[]{:S(2)}) async-start(bf16[8,128,640]{2,1,0:T(8,128)(2,1)} %get-tuple-element.28), calls=%async_computation.3 | async-start | bytes 2621440 | tf_op jit(solution)/shard_map/all_to_all | solution.py:574
  115.7 0.6 collective-permute-start.17
  116.3 1.2 collective-permute-start.16
  117.5 10.7 %collective-permute-done.17.t2 = bf16[1024,256]{1,0:T(8,128)(2,1)S(1)} collective-permute-done((bf16[1024,256]{1,0:T(8,128)(2,1)S(1)}, bf16[1024,256]{1,0:T(8,128)(2,1)S(1)}, u32[]{:S(2)}, u32[]{:S(2)}) %collective-permute-start.17) | collective-permute-done | bytes 524320 | tf_op jit(solution)/shard_map/ppermute | solution.py:34
  128.2 1.8 %collective-permute-start.18 = (bf16[1024,256]{1,0:T(8,128)(2,1)S(1)}, bf16[1024,256]{1,0:T(8,128)(2,1)}, u32[]{:S(2)}, u32[]{:S(2)}) collective-permute-start(bf16[1024,256]{1,0:T(8,128)(2,1)S(1)} %collective-permute-done.17.t2), channel_id=1, source_target_pairs={{0,64},{64,0},{1,65},{65,1},{2,66},{66,2},{3,67},{67,3},{4,68},{68... | collective-permute-start | bytes 1572872 | tf_op jit(solution)/shard_map/ppermute | solution.py:34
  130.0 1.1 dynamic-slice_bitcast_fusion.1.rows_own
  131.1 1.1 dynamic-slice_bitcast_fusion.rows_prev
  132.2 0.0 collective-permute-done.16.t1
  132.2 0.0 collective-permute-done.18.t3
  132.2 1.0 all-to-all-done.3.packed
  133.2 2.9 %share.1 = bf16[8,256,128]{2,1,0:T(8,128)(2,1)} custom-call(s32[1]{0:T(128)} %bitcast.me.me_ref, bf16[8,128,640]{2,1,0:T(8,128)(2,1)S(1)} %all-to-all-done.3.packed, bf16[1024,256]{1,0:T(8,128)(2,1)S(1)} %bitcast.30, bf16[1024,256]{1,0:T(8,128)(2,1)} %collective-permute-done.16.t1, bf16[1024,256]{1,0:T(8,128)(2,1)S(1)} %collective-permute-done.17.t2, ...), custom_call_target="tpu_custom_call" | custom-call | flops 2000000000 | bytes 6291456 | tf_op jit(solution)/shard_map/share/pallas_call | solution.py:492
  136.1 7.7 %all-to-all-start.4 = ((bf16[8,256,128]{2,1,0:T(8,128)(2,1)}), bf16[8,256,128]{2,1,0:T(8,128)(2,1)S(1)}, u32[]{:S(2)}, u32[]{:S(2)}) async-start(bf16[8,256,128]{2,1,0:T(8,128)(2,1)} %share.1), calls=%async_computation.4 | async-start | bytes 1048576 | tf_op jit(solution)/shard_map/all_to_all | solution.py:578
  143.8 0.7 constant_dynamic-slice_fusion.gain
  144.5 0.8 dynamic-slice_bitcast_fusion.2.weight_in
  145.2 17.1 %all-to-all-done.4.arrived = bf16[8,256,128]{2,1,0:T(8,128)(2,1)S(1)} async-done(((bf16[8,256,128]{2,1,0:T(8,128)(2,1)}), bf16[8,256,128]{2,1,0:T(8,128)(2,1)S(1)}, u32[]{:S(2)}, u32[]{:S(2)}) %all-to-all-start.4) | async-done | bytes 524320 | tf_op jit(solution)/shard_map/all_to_all | solution.py:578
  162.4 0.8 finish.1
  (28 shorter events, 0.1 us)
Async XLA Ops:
  3.5 27.2 %collective-permute-start = (bf16[8,256,256]{2,1,0:T(8,128)(2,1)}, bf16[8,256,256]{2,1,0:T(8,128)(2,1)}, u32[]{:S(2)}, u32[]{:S(2)}) collective-permute-start(bf16[8,256,256]{2,1,0:T(8,128)(2,1)} %get-tuple-element.20), channel_id=1, source_target_pairs={{0,64},{64,128},{128,192},{1,65},{65,129},{129,193},{2,66},{66,130... | collective-permute-start | bytes 3145736 | tf_op jit(solution)/shard_map/ppermute | solution.py:554
  35.3 34.3 %all-to-all-start.1 = ((bf16[64,4,2048]{2,1,0:T(4,128)(2,1)}), bf16[64,4,2048]{2,1,0:T(4,128)(2,1)}, u32[]{:S(2)}, u32[]{:S(2)}) async-start(bf16[64,4,2048]{2,1,0:T(4,128)(2,1)} %pick_rows.1.after), calls=%async_computation.1 | async-start | bytes 2097152 | tf_op jit(solution)/shard_map/all_to_all | solution.py:557
  46.2 12.0 %collective-permute-start.1 = (bf16[256,384]{1,0:T(8,128)(2,1)}, bf16[256,384]{1,0:T(8,128)(2,1)S(1)}, u32[]{:S(2)}, u32[]{:S(2)}) collective-permute-start(bf16[256,384]{1,0:T(8,128)(2,1)} %cross_products.1.refs_0_.a), channel_id=1, source_target_pairs={{0,2},{2,4},{4,6},{6,0},{1,3},{3,5},{5,7},{7,1},{8,10},{10,12},{12... | collective-permute-start | bytes 589832 | tf_op jit(solution)/shard_map/ppermute | solution.py:163
  47.5 18.3 %collective-permute-start.2 = (bf16[256,384]{1,0:T(8,128)(2,1)}, bf16[256,384]{1,0:T(8,128)(2,1)S(1)}, u32[]{:S(2)}, u32[]{:S(2)}) collective-permute-start(bf16[256,384]{1,0:T(8,128)(2,1)} %cross_products.1.refs_0_.a), channel_id=1, source_target_pairs={{0,4},{2,6},{4,0},{6,2},{1,5},{3,7},{5,1},{7,3},{8,12},{10,14},{12... | collective-permute-start | bytes 589832 | tf_op jit(solution)/shard_map/ppermute | solution.py:163
  49.9 15.9 %collective-permute-start.3 = (bf16[256,384]{1,0:T(8,128)(2,1)}, bf16[256,384]{1,0:T(8,128)(2,1)S(1)}, u32[]{:S(2)}, u32[]{:S(2)}) collective-permute-start(bf16[256,384]{1,0:T(8,128)(2,1)} %cross_products.1.refs_0_.a), channel_id=1, source_target_pairs={{0,6},{2,0},{4,2},{6,4},{1,7},{3,1},{5,3},{7,5},{8,14},{10,8},{12,... | collective-permute-start | bytes 589832 | tf_op jit(solution)/shard_map/ppermute | solution.py:163
  58.2 7.6 %copy-start.12 = (bf16[256,384]{1,0:T(8,128)(2,1)}, bf16[256,384]{1,0:T(8,128)(2,1)S(1)}, u32[]{:S(2)}) copy-start(bf16[256,384]{1,0:T(8,128)(2,1)S(1)} %collective-permute-done.1.b) | copy-start | bytes 589828
  65.8 0.7 copy-start.13
  65.8 0.8 copy-start.14
  68.6 4.7 %collective-permute-start.7 = (bf16[256,384]{1,0:T(8,128)(2,1)}, bf16[256,384]{1,0:T(8,128)(2,1)S(1)}, u32[]{:S(2)}, u32[]{:S(2)}) collective-permute-start(bf16[256,384]{1,0:T(8,128)(2,1)} %sum_over_x.1.refs_0_.m0), channel_id=1, source_target_pairs={{0,128},{128,0},{1,129},{129,1},{2,130},{130,2},{3,131},{131,3},{4... | collective-permute-start | bytes 589832 | tf_op jit(solution)/shard_map/ppermute | solution.py:34
  72.2 8.4 %copy-start.8 = (bf16[128,2048]{1,0:T(8,128)(2,1)S(1)}, bf16[128,2048]{1,0:T(8,128)(2,1)}, u32[]{:S(2)}) copy-start(bf16[128,2048]{1,0:T(8,128)(2,1)} %get-tuple-element.22.p0) | copy-start | bytes 1572868
  72.2 11.3 %collective-permute-start.5 = (bf16[128,2048]{1,0:T(8,128)(2,1)}, bf16[128,2048]{1,0:T(8,128)(2,1)S(1)}, u32[]{:S(2)}, u32[]{:S(2)}) collective-permute-start(bf16[128,2048]{1,0:T(8,128)(2,1)} %get-tuple-element.22.p0), channel_id=1, source_target_pairs={{0,128},{128,0},{1,129},{129,1},{2,130},{130,2},{3,131},{131,3},{4... | collective-permute-start | bytes 1572872 | tf_op jit(solution)/shard_map/ppermute | solution.py:34
  73.3 0.7 copy-start.3
  74.0 13.7 %all-to-all-start.2 = ((bf16[8,128,256]{2,1,0:T(8,128)(2,1)}), bf16[8,128,256]{2,1,0:T(8,128)(2,1)S(1)}, u32[]{:S(2)}, u32[]{:S(2)}) async-start(bf16[8,128,256]{2,1,0:T(8,128)(2,1)} %ordered.1), calls=%async_computation.2 | async-start | bytes 1048576 | tf_op jit(solution)/shard_map/all_to_all | solution.py:568
  80.6 7.0 %collective-permute-start.4 = (bf16[128,2048]{1,0:T(8,128)(2,1)S(1)}, bf16[128,2048]{1,0:T(8,128)(2,1)S(1)}, u32[]{:S(2)}, u32[]{:S(2)}) collective-permute-start(bf16[128,2048]{1,0:T(8,128)(2,1)S(1)} %copy-done.8), channel_id=1, source_target_pairs={{0,64},{64,0},{1,65},{65,1},{2,66},{66,2},{3,67},{67,3},{4,68},{68... | collective-permute-start | bytes 1572872 | tf_op jit(solution)/shard_map/ppermute | solution.py:34
  83.6 5.3 %copy-start.9 = (bf16[128,2048]{1,0:T(8,128)(2,1)}, bf16[128,2048]{1,0:T(8,128)(2,1)S(1)}, u32[]{:S(2)}) copy-start(bf16[128,2048]{1,0:T(8,128)(2,1)S(1)} %collective-permute-done.5.p2) | copy-start | bytes 1572868
  83.6 5.3 %collective-permute-start.6 = (bf16[128,2048]{1,0:T(8,128)(2,1)S(1)}, bf16[128,2048]{1,0:T(8,128)(2,1)S(1)}, u32[]{:S(2)}, u32[]{:S(2)}) collective-permute-start(bf16[128,2048]{1,0:T(8,128)(2,1)S(1)} %collective-permute-done.5.p2), channel_id=1, source_target_pairs={{0,64},{64,0},{1,65},{65,1},{2,66},{66,2},{3,67},{67,3},{4,68},{68... | collective-permute-start | bytes 1572872 | tf_op jit(solution)/shard_map/ppermute | solution.py:34
  87.4 10.3 %collective-permute-start.12 = (bf16[384,256]{1,0:T(8,128)(2,1)}, bf16[384,256]{1,0:T(8,128)(2,1)}, u32[]{:S(2)}, u32[]{:S(2)}) collective-permute-start(bf16[384,256]{1,0:T(8,128)(2,1)} %get-tuple-element.21.after.g0), channel_id=1, source_target_pairs={{0,128},{128,0},{1,129},{129,1},{2,130},{130,2},{3,131},{131,3},{4... | collective-permute-start | bytes 589832 | tf_op jit(solution)/shard_map/ppermute | solution.py:34
  87.4 10.8 %collective-permute-start.11 = (bf16[384,256]{1,0:T(8,128)(2,1)}, bf16[384,256]{1,0:T(8,128)(2,1)}, u32[]{:S(2)}, u32[]{:S(2)}) collective-permute-start(bf16[384,256]{1,0:T(8,128)(2,1)} %get-tuple-element.21.after.g0), channel_id=1, source_target_pairs={{0,64},{64,0},{1,65},{65,1},{2,66},{66,2},{3,67},{67,3},{4,68},{68... | collective-permute-start | bytes 589832 | tf_op jit(solution)/shard_map/ppermute | solution.py:34
  87.7 1.3 copy-start.10
  87.7 2.0 %copy-start = (bf16[8,128,256]{2,1,0:T(8,128)(2,1)}, bf16[8,128,256]{2,1,0:T(8,128)(2,1)S(1)}, u32[]{:S(2)}) copy-start(bf16[8,128,256]{2,1,0:T(8,128)(2,1)S(1)} %all-to-all-done.2.first) | copy-start | bytes 1572868
  88.9 0.8 copy-start.11
  89.7 6.2 %copy-start.2 = (bf16[256,384]{1,0:T(8,128)(2,1)S(1)}, bf16[256,384]{1,0:T(8,128)(2,1)}, u32[]{:S(2)}) copy-start(bf16[256,384]{1,0:T(8,128)(2,1)} %sum_over_x.1.refs_0_.m0) | copy-start | bytes 589828
  89.7 8.1 %copy-start.4 = (bf16[256,384]{1,0:T(8,128)(2,1)S(1)}, bf16[256,384]{1,0:T(8,128)(2,1)}, u32[]{:S(2)}) copy-start(bf16[256,384]{1,0:T(8,128)(2,1)} %copy-done.3) | copy-start | bytes 589828
  89.7 14.3 %copy-start.6 = (bf16[128,256]{1,0:T(8,128)(2,1)S(1)}, bf16[128,256]{1,0:T(8,128)(2,1)}, u32[]{:S(2)}) copy-start(bf16[128,256]{1,0:T(8,128)(2,1)} %cot.1) | copy-start | bytes 196612
  95.3 4.7 %collective-permute-start.9 = (f32[128,384]{1,0:T(8,128)}, f32[128,384]{1,0:T(8,128)S(1)}, u32[]{:S(2)}, u32[]{:S(2)}) collective-permute-start(f32[128,384]{1,0:T(8,128)} %get-tuple-element.26.q0), channel_id=1, source_target_pairs={{0,128},{128,0},{1,129},{129,1},{2,130},{130,2},{3,131},{131,3},{4... | collective-permute-start | bytes 589832 | tf_op jit(solution)/shard_map/ppermute | solution.py:34
  95.9 7.0 %collective-permute-start.14 = (bf16[256,384]{1,0:T(8,128)(2,1)S(1)}, bf16[256,384]{1,0:T(8,128)(2,1)S(1)}, u32[]{:S(2)}, u32[]{:S(2)}) collective-permute-start(bf16[256,384]{1,0:T(8,128)(2,1)S(1)} %copy-done.2), channel_id=1, source_target_pairs={{0,64},{64,0},{1,65},{65,1},{2,66},{66,2},{3,67},{67,3},{4,68},{68... | collective-permute-start | bytes 589832 | tf_op jit(solution)/shard_map/ppermute | solution.py:34
  97.7 5.3 %collective-permute-start.13 = (bf16[384,256]{1,0:T(8,128)(2,1)}, bf16[384,256]{1,0:T(8,128)(2,1)S(1)}, u32[]{:S(2)}, u32[]{:S(2)}) collective-permute-start(bf16[384,256]{1,0:T(8,128)(2,1)} %collective-permute-done.12.g2), channel_id=1, source_target_pairs={{0,64},{64,0},{1,65},{65,1},{2,66},{66,2},{3,67},{67,3},{4,68},{68... | collective-permute-start | bytes 589832 | tf_op jit(solution)/shard_map/ppermute | solution.py:34
  97.8 5.2 %collective-permute-start.15 = (bf16[256,384]{1,0:T(8,128)(2,1)S(1)}, bf16[256,384]{1,0:T(8,128)(2,1)S(1)}, u32[]{:S(2)}, u32[]{:S(2)}) collective-permute-start(bf16[256,384]{1,0:T(8,128)(2,1)S(1)} %copy-done.4), channel_id=1, source_target_pairs={{0,64},{64,0},{1,65},{65,1},{2,66},{66,2},{3,67},{67,3},{4,68},{68... | collective-permute-start | bytes 589832 | tf_op jit(solution)/shard_map/ppermute | solution.py:34
  98.2 4.8 %collective-permute-start.8 = (f32[128,384]{1,0:T(8,128)}, f32[128,384]{1,0:T(8,128)S(1)}, u32[]{:S(2)}, u32[]{:S(2)}) collective-permute-start(f32[128,384]{1,0:T(8,128)} %get-tuple-element.26.q0), channel_id=1, source_target_pairs={{0,64},{64,0},{1,65},{65,1},{2,66},{66,2},{3,67},{67,3},{4,68},{68... | collective-permute-start | bytes 589832 | tf_op jit(solution)/shard_map/ppermute | solution.py:34
  100.1 4.0 %collective-permute-start.10 = (f32[128,384]{1,0:T(8,128)S(1)}, f32[128,384]{1,0:T(8,128)S(1)}, u32[]{:S(2)}, u32[]{:S(2)}) collective-permute-start(f32[128,384]{1,0:T(8,128)S(1)} %collective-permute-done.9.q2), channel_id=1, source_target_pairs={{0,64},{64,0},{1,65},{65,1},{2,66},{66,2},{3,67},{67,3},{4,68},{68... | collective-permute-start | bytes 589832 | tf_op jit(solution)/shard_map/ppermute | solution.py:34
  104.0 0.9 copy-start.5
  105.0 0.8 copy-start.7
  110.7 5.1 %copy-start.1 = (bf16[8,128,256]{2,1,0:T(8,128)(2,1)S(1)}, bf16[8,128,256]{2,1,0:T(8,128)(2,1)}, u32[]{:S(2)}) copy-start(bf16[8,128,256]{2,1,0:T(8,128)(2,1)} %copy-done) | copy-start | bytes 1572868
  110.7 22.5 %all-to-all-start.3 = ((bf16[8,128,640]{2,1,0:T(8,128)(2,1)}), bf16[8,128,640]{2,1,0:T(8,128)(2,1)S(1)}, u32[]{:S(2)}, u32[]{:S(2)}) async-start(bf16[8,128,640]{2,1,0:T(8,128)(2,1)} %get-tuple-element.28), calls=%async_computation.3 | async-start | bytes 2621440 | tf_op jit(solution)/shard_map/all_to_all | solution.py:574
  115.7 12.5 %collective-permute-start.17 = (bf16[1024,256]{1,0:T(8,128)(2,1)S(1)}, bf16[1024,256]{1,0:T(8,128)(2,1)S(1)}, u32[]{:S(2)}, u32[]{:S(2)}) collective-permute-start(bf16[1024,256]{1,0:T(8,128)(2,1)S(1)} %bitcast.28), channel_id=1, source_target_pairs={{0,128},{128,0},{1,129},{129,1},{2,130},{130,2},{3,131},{131,3},{4... | collective-permute-start | bytes 1572872 | tf_op jit(solution)/shard_map/ppermute | solution.py:34
  116.3 15.9 %collective-permute-start.16 = (bf16[1024,256]{1,0:T(8,128)(2,1)S(1)}, bf16[1024,256]{1,0:T(8,128)(2,1)}, u32[]{:S(2)}, u32[]{:S(2)}) collective-permute-start(bf16[1024,256]{1,0:T(8,128)(2,1)S(1)} %bitcast.29), channel_id=1, source_target_pairs={{0,64},{64,0},{1,65},{65,1},{2,66},{66,2},{3,67},{67,3},{4,68},{68... | collective-permute-start | bytes 1572872 | tf_op jit(solution)/shard_map/ppermute | solution.py:34
  128.2 4.0 %collective-permute-start.18 = (bf16[1024,256]{1,0:T(8,128)(2,1)S(1)}, bf16[1024,256]{1,0:T(8,128)(2,1)}, u32[]{:S(2)}, u32[]{:S(2)}) collective-permute-start(bf16[1024,256]{1,0:T(8,128)(2,1)S(1)} %collective-permute-done.17.t2), channel_id=1, source_target_pairs={{0,64},{64,0},{1,65},{65,1},{2,66},{66,2},{3,67},{67,3},{4,68},{68... | collective-permute-start | bytes 1572872 | tf_op jit(solution)/shard_map/ppermute | solution.py:34
  136.1 26.3 %all-to-all-start.4 = ((bf16[8,256,128]{2,1,0:T(8,128)(2,1)}), bf16[8,256,128]{2,1,0:T(8,128)(2,1)S(1)}, u32[]{:S(2)}, u32[]{:S(2)}) async-start(bf16[8,256,128]{2,1,0:T(8,128)(2,1)} %share.1), calls=%async_computation.4 | async-start | bytes 1048576 | tf_op jit(solution)/shard_map/all_to_all | solution.py:578
